TPU v7x, 128 devices: a whole 4x4x4 slice. The times are simulated.
128 devices in a mesh: dp: 4 (over z), rows: 8 (over x, core), cols: 4 (over y).
Axes of the slice: x: 4, y: 4, z: 4, core: 2. Of those that a mesh axis runs over, the one named last changes fastest.
Arguments:
- gated_hidden_input: bfloat16 [1024, 28672], P('dp', 'rows'), may hold values from -6 to 6
- output_gradient: bfloat16 [1024, 8192], P('dp', 'cols'), may hold values from -6 to 6
- frozen_down_weight: bfloat16 [28672, 8192], P('rows', 'cols'), may hold values from -8 to 8
- input_side_factor: bfloat16 [28672, 64], P('rows'), may hold values from -0.03125 to 0.03125
- output_side_factor: bfloat16 [64, 8192], P(None, 'cols'), may hold values from -0.375 to 0.375
- magnitude: float32 [8192], P('cols'), may hold values from 0.3 to 3
Outputs:
- input_grad: bfloat16 [28672, 1024], P(('rows', 'cols'), 'dp')
- lora_a_grad: float32 [28672, 64], P('rows')
- lora_b_grad: float32 [64, 8192], P(None, 'cols')
- magnitude_grad: float32 [8192], P('cols')
All inputs are finite; a program needn't handle non-finite values.
Results may differ from a plain program's by a relative error of at most 0.0032.
Values sent between devices are 32-bit elements; how exact they have to be, the bound alone decides.
No kernel may reach another device: no remote copies, remote signals or barrier semaphores. Data moves between devices by JAX's collectives and lax.ppermute only.
A program may use at most 192 MiB of HBM per device.

v0:
```python
import jax
import jax.numpy as jnp
from jax import lax
from jax.sharding import PartitionSpec as P

EPS = 1e-06


def shards(
    gated_hidden_input,
    output_gradient,
    frozen_down_weight,
    input_side_factor,
    output_side_factor,
    magnitude,
):
    low_rank_product = jnp.dot(
        input_side_factor, output_side_factor, preferred_element_type=jnp.float32
    )
    merged = (frozen_down_weight.astype(jnp.float32) + 2.0 * low_rank_product).astype(jnp.bfloat16)
    merged_wide = merged.astype(jnp.float32)
    squares_part = jnp.sum(merged_wide * merged_wide, axis=0)
    weight_grad = lax.dot_general(
        gated_hidden_input,
        output_gradient,
        (((0,), (0,)), ((), ())),
        preferred_element_type=jnp.float32,
    )
    inner_part = jnp.sum(weight_grad * merged_wide, axis=0)
    squares = lax.psum(squares_part, "rows") + EPS
    inner = lax.psum(inner_part, ("dp", "rows"))
    norms = jnp.sqrt(squares)
    scale = magnitude / norms
    scaled = (output_gradient.astype(jnp.float32) * scale).astype(jnp.bfloat16)
    input_grad = lax.psum_scatter(
        lax.dot_general(
            merged, scaled, (((1,), (1,)), ((), ())), preferred_element_type=jnp.float32
        ),
        "cols",
        scatter_dimension=0,
        tiled=True,
    ).astype(jnp.bfloat16)
    groups = lax.axis_size("dp")
    full_rows = merged.shape[0] * lax.axis_size("rows")
    gamma = float(gated_hidden_input.shape[0] * groups) ** (-0.5)
    magnitude_grad = gamma * inner / (norms * float(full_rows) ** 0.5)
    direction_gradient = (
        scale * (weight_grad - merged_wide * (inner / (groups * squares)))
    ).astype(jnp.bfloat16)
    a_part = (
        2.0
        * gamma
        * lax.dot_general(
            direction_gradient,
            output_side_factor,
            (((1,), (1,)), ((), ())),
            preferred_element_type=jnp.float32,
        )
    )
    b_part = (
        2.0
        * gamma
        * lax.dot_general(
            input_side_factor,
            direction_gradient,
            (((0,), (0,)), ((), ())),
            preferred_element_type=jnp.float32,
        )
    )
    a_grad = lax.psum(a_part, ("dp", "cols"))
    b_grad = lax.psum(b_part, ("dp", "rows"))
    return (input_grad, a_grad, b_grad, magnitude_grad)


def solution(mesh):
    return jax.shard_map(
        shards,
        mesh=mesh,
        in_specs=(
            P("dp", "rows"),
            P("dp", "cols"),
            P("rows", "cols"),
            P("rows", None),
            P(None, "cols"),
            P("cols"),
        ),
        out_specs=(P(("rows", "cols"), "dp"), P("rows", None), P(None, "cols"), P("cols")),
        check_vma=False,
    )
```

profile of v0, /device:TPU:0, one launch (start us, length us, event | category | flops | bytes accessed | tf_op | source)
XLA Modules:
  0.0 356.0 jit_solution(9056468348397550730)
XLA Ops:
  8.0 0.0 copy-start
  8.0 0.0 copy-start.5
  8.0 0.0 reduce-scatter.2.cloned.1.call-start
  8.1 14.8 %add_convert_fusion = bf16[3584,2048]{1,0:T(8,128)(2,1)} fusion(bf16[3584,2048]{1,0:T(8,128)(2,1)} %param.8, bf16[3584,64]{0,1:T(8,128)(2,1)} %param.9, bf16[64,2048]{1,0:T(8,128)(2,1)} %param.10), kind=kOutput, calls=%fused_computation.8 | convolution fusion | flops 968884224 | bytes 30081024 | tf_op jit(solution)/shard_map/dot_general | solution.py:17
  22.8 0.0 copy-done
  22.8 0.0 copy-done.5
  22.9 15.4 %fusion.1 = (f32[2048]{0:T(1024)S(1)}, f32[2048]{0:T(1024)S(1)}, f32[3584,2048]{1,0:T(8,128)}) fusion(bf16[3584,2048]{1,0:T(8,128)(2,1)} %add_convert_fusion, bf16[256,3584]{1,0:T(8,128)(2,1)S(1)} %copy-done, bf16[256,2048]{1,0:T(8,128)(2,1)S(1)} %copy-done.5), kind=kOutput, calls=%fused_computation.4 | convolution fusion | flops 3794792448 | bytes 46940160 | tf_op jit(solution)/shard_map/dot_general | solution.py:23
  38.3 69.4 %psum.29 = f32[2048]{0:T(1024)S(1)} all-reduce(f32[2048]{0:T(1024)S(1)} %get-tuple-element.4), channel_id=1, replica_groups=mesh['dp'=4,'rows'=8,'cols'=4] {'dp','rows'}, use_global_device_ids=true, to_apply=%region_4.0 | all-reduce | flops 2048 | bytes 16384 | tf_op jit(solution)/shard_map/psum | solution.py:31
  107.7 12.7 %psum.28 = f32[2048]{0:T(1024)S(1)} all-reduce(f32[2048]{0:T(1024)S(1)} %get-tuple-element.5), channel_id=1, replica_groups=mesh['dp'=4,'rows'=8,'cols'=4] {'rows'}, use_global_device_ids=true, to_apply=%region_1.0 | all-reduce | flops 2048 | bytes 16384 | tf_op jit(solution)/shard_map/psum | solution.py:30
  120.4 0.0 copy-done.6
  120.4 0.6 multiply_divide_fusion
  121.0 9.3 %fusion.6 = f32[3584,256]{1,0:T(8,128)} fusion(bf16[3584,2048]{1,0:T(8,128)(2,1)} %add_convert_fusion, bf16[256,2048]{1,0:T(8,128)(2,1)S(1)} %copy-done.5, f32[2048]{0:T(1024)S(1)} %get-tuple-element.8), kind=kOutput, calls=%fused_computation.13 | convolution fusion | flops 3759669248 | bytes 19406848 | tf_op jit(solution)/shard_map/dot_general | solution.py:36
  130.3 0.0 reduce-scatter.2.cloned.1.call-update
  130.3 0.2 all-reduce.5.cloned.1.call-start
  130.5 0.0 copy-start.3
  130.5 15.8 %fusion.4 = bf16[3584,2048]{1,0:T(8,128)(2,1)S(1)} fusion(f32[3584,2048]{1,0:T(8,128)} %get-tuple-element.9, bf16[3584,2048]{1,0:T(8,128)(2,1)} %add_convert_fusion, f32[2048]{0:T(1024)S(1)} %get-tuple-element.7, f32[2048]{0:T(1024)S(1)} %get-tuple-element.8), kind=kLoop, calls=%fused_computation.7 | loop fusion | flops 36700160 | bytes 58736640 | tf_op jit(solution)/shard_map/convert_element_type | solution.py:49
  146.4 0.0 copy-start.2
  146.4 5.2 %copy-done.2 = bf16[3584,2048]{1,0:T(8,128)(2,1)} copy-done((bf16[3584,2048]{1,0:T(8,128)(2,1)}, bf16[3584,2048]{1,0:T(8,128)(2,1)S(1)}, u32[]{:S(2)}) %copy-start.2) | copy-done | bytes 14680088
  151.6 0.0 copy-done.3
  151.6 3.5 fusion.5
  155.0 0.0 all-reduce.5.cloned.1.call-update
  155.1 0.0 all-reduce.3.cloned.1.call-start
  155.1 0.0 copy-done.4
  155.1 10.8 %convolution_multiply_fusion = f32[3584,64]{0,1:T(8,128)} fusion(bf16[3584,2048]{1,0:T(8,128)(2,1)} %copy-done.2, bf16[64,2048]{1,0:T(8,128)(2,1)S(1)} %copy-done.4), kind=kOutput, calls=%fused_computation.9 | convolution fusion | flops 939753472 | bytes 15859712 | tf_op jit(solution)/shard_map/dot_general | solution.py:53
  165.9 0.0 all-reduce.3.cloned.1.call-update
  165.9 3.5 reduce-scatter.2.cloned.1.call-done
  169.4 2.0 convert_element_type.26
  171.4 83.7 %all-reduce.5.cloned.1.call-done = f32[64,2048]{1,0:T(8,128)} async-done(((f32[64,2048]{1,0:T(8,128)}), f32[64,2048]{1,0:T(8,128)}) %all-reduce.5.cloned.1.call-update) | async-done | bytes 524304 | tf_op jit(solution)/shard_map/psum | solution.py:71
  255.2 89.4 %all-reduce.3.cloned.1.call-done = f32[3584,64]{0,1:T(8,128)} async-done(((f32[3584,64]{0,1:T(8,128)}), f32[3584,64]{0,1:T(8,128)}) %all-reduce.3.cloned.1.call-update) | async-done | bytes 917520 | tf_op jit(solution)/shard_map/psum | solution.py:70
  344.5 2.2 copy.12
  346.7 1.9 copy.13
  348.6 0.0 copy-done.1
  (3 shorter events, 0.0 us)
Async XLA Ops:
  8.0 14.8 %copy-start = (bf16[256,3584]{1,0:T(8,128)(2,1)S(1)}, bf16[256,3584]{1,0:T(8,128)(2,1)}, u32[]{:S(2)}) copy-start(bf16[256,3584]{1,0:T(8,128)(2,1)} %param.6) | copy-start | bytes 5505028
  8.0 14.8 %copy-start.5 = (bf16[256,2048]{1,0:T(8,128)(2,1)S(1)}, bf16[256,2048]{1,0:T(8,128)(2,1)}, u32[]{:S(2)}) copy-start(bf16[256,2048]{1,0:T(8,128)(2,1)} %param.7) | copy-start | bytes 3145732
  8.0 161.4 %reduce-scatter.2.cloned.1.call-start = ((), (), s32[]{:S(2)}) async-start(), calls=%async_computation.1 | async-start | bytes 4587520 | tf_op jit(solution)/shard_map/reduce_scatter | solution.py:35
  22.8 97.5 %copy-start.6 = (f32[2048]{0:T(1024)S(1)}, f32[2048]{0:T(1024)}, u32[]{:S(2)}) copy-start(f32[2048]{0:T(1024)} %param.11) | copy-start | bytes 24580
  130.3 124.9 %all-reduce.5.cloned.1.call-start = ((), (), s32[]{:S(2)}) async-start(), calls=%async_computation.3 | async-start | bytes 1048576 | tf_op jit(solution)/shard_map/psum | solution.py:71
  130.5 21.0 %copy-start.3 = (bf16[3584,64]{0,1:T(8,128)(2,1)S(1)}, bf16[3584,64]{0,1:T(8,128)(2,1)}, u32[]{:S(2)}) copy-start(bf16[3584,64]{0,1:T(8,128)(2,1)} %param.9) | copy-start | bytes 1376260
  146.4 5.2 %copy-start.2 = (bf16[3584,2048]{1,0:T(8,128)(2,1)}, bf16[3584,2048]{1,0:T(8,128)(2,1)S(1)}, u32[]{:S(2)}) copy-start(bf16[3584,2048]{1,0:T(8,128)(2,1)S(1)} %fusion.4) | copy-start | bytes 44040196
  151.6 3.5 copy-start.4
  151.6 197.0 %copy-start.1 = (bf16[256,3584]{1,0:T(8,128)(2,1)S(1)}, bf16[256,3584]{1,0:T(8,128)(2,1)}, u32[]{:S(2)}) copy-start(bf16[256,3584]{1,0:T(8,128)(2,1)} %param.6) | copy-start | bytes 5505028
  155.1 189.5 %all-reduce.3.cloned.1.call-start = ((), (), s32[]{:S(2)}) async-start(), calls=%async_computation.2 | async-start | bytes 1835008 | tf_op jit(solution)/shard_map/psum | solution.py:70
Sparse Core Ops, SparseCore 0:
  130.4 38.9 reduce-scatter.1
Sparse Core Ops, SparseCore 1:
  155.1 100.0 all-reduce.4
  259.3 85.2 all-reduce.2
where the time goes:
time: 356 us
  waiting for transfers between devices  177 us (50%)
  blocking collectives  82.1 us (23%)
  matrix products  53.7 us (15%)
  other arithmetic  18.4 us (5%)
  between operations  15.6 us (4%)
  local copies, waits for them, and re-layouts  9.28 us (3%)
    psum x1, waiting for transfers between devices, shards(): a_grad = lax.psum(a_part, ('dp', 'cols'))  89.4 us
    psum x1, waiting for transfers between devices, shards(): b_grad = lax.psum(b_part, ('dp', 'rows'))  83.7 us
    psum x1, blocking collectives, shards(): inner = lax.psum(inner_part, ('dp', 'rows'))  69.4 us
    convert_element_type x1, other arithmetic, shards(): direction_gradient = (scale * (weight_grad - merged_wide * (inner / (grou...  15.8 us
    dot_general x1, matrix products, shards(): lax.dot_general(gated_hidden_input, output_gradient, (((0,), (0,)), ((),...  15.4 us
    dot_general x1, matrix products, shards(): jnp.dot(input_side_factor, output_side_factor, preferred_element_type=jnp...  14.8 us
    psum x1, blocking collectives, shards(): squares = lax.psum(squares_part, 'rows') + EPS  12.7 us
    dot_general x1, matrix products, shards(): lax.dot_general(direction_gradient, output_side_factor, (((1,), (1,)), ((...  10.8 us
  transfers between devices with their start and end apart: 3, of which 3 were waited for; matrix products, arithmetic and copies ran while one was open for 9% of the time, Pallas kernels for 0%

commit v1 on v0

v1 whole, which is shorter than its diff:
```python
import functools

import jax
import jax.numpy as jnp
from jax import lax
from jax.experimental import pallas as pl
from jax.experimental.pallas import tpu as pltpu
from jax.sharding import PartitionSpec as P

EPS = 1e-06
F32 = jnp.float32
BF16 = jnp.bfloat16
MIB = 1024 * 1024

ANY = pl.BlockSpec(memory_space=pl.ANY)
VMEM = pl.BlockSpec(memory_space=pltpu.VMEM)


def nn(a, b):
    return lax.dot_general(a, b, (((1,), (0,)), ((), ())), preferred_element_type=F32)


def nt(a, b):
    return lax.dot_general(a, b, (((1,), (1,)), ((), ())), preferred_element_type=F32)


def tn(a, b):
    return lax.dot_general(a, b, (((0,), (0,)), ((), ())), preferred_element_type=F32)


def hi_lo(value):
    hi = value.astype(BF16)
    lo = (value - hi.astype(F32)).astype(BF16)
    return jnp.concatenate([hi, lo], axis=0)


def fold(value):
    half = value.shape[0] // 2
    return value[:half] + value[half:]


def call(kernel, outs, specs, *args, scratch=(), vmem=16, flops=0, data=0):
    return pl.pallas_call(
        kernel,
        out_shape=outs,
        in_specs=specs,
        out_specs=[VMEM for _ in outs],
        scratch_shapes=list(scratch),
        compiler_params=pltpu.CompilerParams(vmem_limit_bytes=vmem * MIB),
        cost_estimate=pl.CostEstimate(flops=flops, bytes_accessed=data, transcendentals=0),
    )(*args)


def out(shape, dtype=F32):
    return jax.ShapeDtypeStruct(shape, dtype)


def merge_kernel(
    steps, w_ref, x_ref, a_ref, b_ref, dy_ref, m_ref, stat_ref, bq_ref, am_ref,
    xa, b2, dy, acc, qt, sq, w_sem, x_sem, a_sem, b_sem, dy_sem,
):
    rows, cols = w_ref.shape
    toks = x_ref.shape[0]
    step = rows // steps
    tile = 256
    b_copy = pltpu.make_async_copy(b_ref, b2, b_sem)
    dy_copy = pltpu.make_async_copy(dy_ref, dy, dy_sem)
    a_copy = pltpu.make_async_copy(a_ref, xa.at[toks:], a_sem)

    def w_copy(i):
        part = pl.ds(pl.multiple_of(i * step, step), step)
        return pltpu.make_async_copy(w_ref.at[part], m_ref.at[part], w_sem.at[i])

    def x_copy(i):
        part = pl.ds(pl.multiple_of(i * step, step), step)
        return pltpu.make_async_copy(x_ref.at[:, part], xa.at[:toks, part], x_sem.at[i])

    b_copy.start()
    a_copy.start()
    for i in range(steps):
        w_copy(i).start()
        x_copy(i).start()
    dy_copy.start()
    acc[...] = jnp.zeros_like(acc)
    qt[...] = jnp.zeros_like(qt)
    sq[...] = jnp.zeros_like(sq)
    b_copy.wait()
    a_copy.wait()
    b2[...] = b2[...] + b2[...]

    @pl.loop(0, steps)
    def _(i):
        w_copy(i).wait()
        x_copy(i).wait()
        part = pl.ds(pl.multiple_of(i * step, step), step)
        xa_part = xa[:, part]
        a_part = xa_part[toks:]
        for c in range(cols // tile):
            at = slice(c * tile, (c + 1) * tile)
            m = (m_ref[part, at].astype(F32) + tn(a_part, b2[:, at])).astype(BF16)
            m_ref[part, at] = m
            wide = m.astype(F32)
            sq[:, at] += jnp.sum((wide * wide).reshape(step // 8, 8, tile), axis=0)
            acc[:, at] += nn(xa_part, m)
        qt[...] += nt(a_part, xa_part[:toks])

    dy_copy.wait()
    am_ref[...] = acc[toks:]
    stat_ref[0:1] = jnp.sum(sq[...], axis=0, keepdims=True)
    stat_ref[1:2] = jnp.sum(acc[:toks] * dy[...].astype(F32), axis=0, keepdims=True)
    bq_ref[...] = fold(nn(hi_lo(qt[...]), dy[...]))


def merge(w, x, a_t, b, dy):
    rows, cols = w.shape
    toks = x.shape[0]
    rank = b.shape[0]
    steps = rows // 512
    dma = pltpu.SemaphoreType.DMA
    return call(
        functools.partial(merge_kernel, steps),
        [pltpu.VMEM((rows, cols), BF16), out((2, cols)), out((rank, cols)), out((rank, cols))],
        [ANY] * 5,
        w, x, a_t, b, dy,
        scratch=[
            pltpu.VMEM((toks + rank, rows), BF16),
            pltpu.VMEM((rank, cols), BF16),
            pltpu.VMEM((toks, cols), BF16),
            pltpu.VMEM((toks + rank, cols), F32),
            pltpu.VMEM((rank, toks), F32),
            pltpu.VMEM((8, cols), F32),
            dma((steps,)), dma((steps,)), dma, dma, dma,
        ],
        vmem=24,
        flops=2 * rows * cols * (toks + 2 * rank),
        data=rows * cols * 2,
    )


def block(m_ref, index, half=None, count=4):
    size = m_ref.shape[0] // count
    start = lax.rem(index + count, count) * size
    if half is not None:
        size //= 2
        start += half * size
    return m_ref[pl.ds(pl.multiple_of(start, 64), size)]


def far_kernel(stat_ref, r1_ref, r2_ref, r3_ref, mag_ref, dy_ref, m_ref, vec_ref, scaled_ref, h0_ref, h1_ref):
    total = (stat_ref[...] + r2_ref[...]) + (r1_ref[...] + r3_ref[...])
    squares = total[0:1] + EPS
    norms = jnp.sqrt(squares)
    scale = mag_ref[...] / norms
    vec_ref[...] = jnp.concatenate([squares, norms, scale, total[1:2]], axis=0)
    scaled = (dy_ref[...].astype(F32) * scale).astype(BF16)
    scaled_ref[...] = scaled
    y = lax.axis_index("cols")
    h0_ref[...] = nt(block(m_ref, y + 2, 0), scaled)
    h1_ref[...] = nt(block(m_ref, y + 2, 1), scaled)


def near_kernel(m_ref, scaled_ref, up_ref, down_ref):
    y = lax.axis_index("cols")
    up_ref[...] = nt(block(m_ref, y + 1, 1), scaled_ref[...])
    down_ref[...] = nt(block(m_ref, y - 1, 0), scaled_ref[...])


def relay_kernel(m_ref, scaled_ref, u0_ref, u1_ref, up_ref, down_ref):
    y = lax.axis_index("cols")
    up_ref[...] = u0_ref[...] + nt(block(m_ref, y + 1, 0), scaled_ref[...])
    down_ref[...] = u1_ref[...] + nt(block(m_ref, y - 1, 1), scaled_ref[...])


def own_kernel(m_ref, scaled_ref, own_ref):
    own_ref[...] = nt(block(m_ref, lax.axis_index("cols")), scaled_ref[...])


def finish_kernel(own_ref, v0_ref, v1_ref, w0_ref, w1_ref, out_ref):
    half = own_ref.shape[0] // 2
    out_ref[:half] = (own_ref[:half] + (w0_ref[...] + v1_ref[...])).astype(BF16)
    out_ref[half:] = (own_ref[half:] + (w1_ref[...] + v0_ref[...])).astype(BF16)


def a_kernel(factor, vec_ref, dy_ref, b_ref, x_ref, m_ref, *refs):
    outs, whole = refs[:-1], refs[-1]
    scale = vec_ref[2:3] * factor
    wide = b_ref[...].astype(F32) * scale
    p_t = fold(nt(hi_lo(wide), dy_ref[...]))
    left = hi_lo(p_t)
    right = hi_lo(wide * (vec_ref[3:4] / vec_ref[0:1]))
    rows = m_ref.shape[0]
    tile = 512
    for r in range(rows // tile):
        at = slice(r * tile, (r + 1) * tile)
        whole[:, at] = fold(nn(left, x_ref[:, at]) - nt(right, m_ref[at]))
    split(whole, outs, lax.axis_index("dp"), 1)


def split(whole, outs, index, axis):
    count = len(outs)
    size = whole.shape[axis] // count
    for k, ref in enumerate(outs):
        at = pl.ds(pl.multiple_of(lax.rem(index + k, count) * size, 128 if axis else 8), size)
        ref[...] = whole[:, at] if axis else whole[at]


def sum_split_kernel(position, axis, parts, *refs):
    ins, outs, whole = refs[:parts], refs[parts:-1], refs[-1]
    whole[...] = functools.reduce(jnp.add, [ref[...] for ref in ins])
    split(whole, outs, position(), axis)


def sum_split(ins, position, axis, count):
    shape = ins[0].shape
    piece = list(shape)
    piece[axis] //= count
    return call(
        functools.partial(sum_split_kernel, position, axis, len(ins)),
        [out(tuple(piece))] * count,
        [VMEM] * len(ins),
        *ins,
        scratch=[pltpu.VMEM(shape, F32)],
        data=4 * 5 * shape[0] * shape[1],
    )


def join_kernel(position, axis, *refs):
    ins, whole = refs[:-1], refs[-1]
    count = len(ins)
    size = ins[0].shape[axis]
    for k, ref in enumerate(ins):
        start = lax.rem(position() + count - k, count) * size
        at = pl.ds(pl.multiple_of(start, 128 if axis else 8), size)
        if axis:
            whole[:, at] = ref[...]
        else:
            whole[at] = ref[...]


def join(ins, position, axis):
    shape = list(ins[0].shape)
    shape[axis] *= len(ins)
    return call(
        functools.partial(join_kernel, position, axis),
        [out(tuple(shape))],
        [VMEM] * len(ins),
        *ins,
        data=4 * 2 * shape[0] * shape[1],
    )[0]


def b_kernel(factor, vec_ref, bq_ref, am_ref, keep_ref, send_ref, whole):
    ratio = vec_ref[3:4] / vec_ref[0:1]
    whole[...] = (vec_ref[2:3] * factor) * (bq_ref[...] - ratio * am_ref[...])
    split(whole, [keep_ref, send_ref], core_index(), 0)


def b_dp_kernel(vec_ref, *refs):
    ins, outs, whole = refs[:4], refs[4:-1], refs[-1]
    rows = ins[0].shape[0]
    whole[:rows] = functools.reduce(jnp.add, [ref[...] for ref in ins])
    whole[rows:] = jnp.broadcast_to(vec_ref[3:4], (whole.shape[0] - rows, whole.shape[1]))
    split(whole, outs, lax.axis_index("dp"), 1)


def b_join_kernel(factor, vec_ref, i0_ref, i1_ref, i2_ref, i3_ref, b_out_ref, mag_ref, whole):
    join_kernel(dp_index, 1, i0_ref, i1_ref, i2_ref, i3_ref, whole)
    rows = b_out_ref.shape[0]
    b_out_ref[...] = whole[:rows]
    mag_ref[...] = factor * whole[rows:rows + 1] / vec_ref[1:2]


def core_index():
    return lax.rem(lax.axis_index("rows"), 2)


def x_index():
    return lax.div(lax.axis_index("rows"), 2)


def dp_index():
    return lax.axis_index("dp")


def cols_index():
    return lax.axis_index("cols")


def ring(value, axis, k, count=4):
    return lax.ppermute(value, axis, [(i, (i + k) % count) for i in range(count)])


def ring_x(value, k, count=8):
    return lax.ppermute(value, "rows", [(i, (i + 2 * k) % count) for i in range(count)])


def swap_core(value, count=8):
    return lax.ppermute(value, "rows", [(i, i ^ 1) for i in range(count)])


def shards(x, dy, w, a, b, mag):
    rows, cols = w.shape
    toks, rank = x.shape[0], a.shape[1]
    groups, full_rows = 4, rows * 8
    gamma = float(toks * groups) ** (-0.5)
    mag = mag.reshape(1, cols)
    m, stat, bq, am = merge(w, x, a.T, b, dy)

    m = pltpu.with_memory_space_constraint(m, pltpu.VMEM)
    stat = stat + swap_core(stat)
    far = rows // 8
    vec, scaled, h0, h1 = call(
        far_kernel,
        [out((4, cols)), out((toks, cols), BF16), out((far, toks)), out((far, toks))],
        [VMEM] * 7,
        stat, ring_x(stat, 1), ring_x(stat, 2), ring_x(stat, 3), mag, dy, m,
        flops=2 * 2 * far * toks * cols,
    )
    u0, u1 = ring(h0, "cols", 1), ring(h1, "cols", 3)
    up, down = call(near_kernel, [out((far, toks))] * 2, [VMEM] * 2, m, scaled, flops=2 * 2 * far * toks * cols)
    v0, v1 = ring(up, "cols", 1), ring(down, "cols", 3)

    pieces = call(
        functools.partial(a_kernel, 2.0 * gamma),
        [out((rank, rows // 4))] * 4,
        [VMEM] * 5,
        vec, dy, b, x, m,
        scratch=[pltpu.VMEM((rank, rows), F32)],
        flops=2 * 2 * rank * rows * (cols + toks),
    )
    pieces = [pieces[0]] + [ring(pieces[k], "dp", k) for k in (1, 2, 3)]

    keep, send = call(
        functools.partial(b_kernel, 2.0 * gamma),
        [out((rank // 2, cols))] * 2,
        [VMEM] * 3,
        vec, bq, am,
        scratch=[pltpu.VMEM((rank, cols), F32)],
    )
    send = swap_core(send)

    up, down = call(
        relay_kernel, [out((far, toks))] * 2, [VMEM] * 4, m, scaled, u0, u1, flops=2 * 2 * far * toks * cols
    )
    w0, w1 = ring(up, "cols", 1), ring(down, "cols", 3)
    own = call(own_kernel, [out((rows // 4, toks))], [VMEM] * 2, m, scaled, flops=2 * 2 * far * toks * cols)[0]

    pieces = sum_split(pieces, cols_index, 0, 4)
    pieces = [pieces[0]] + [ring(pieces[k], "cols", k) for k in (1, 2, 3)]
    piece = (pieces[0] + pieces[2]) + (pieces[1] + pieces[3])
    piece = join([piece] + [ring(piece, "cols", k) for k in (1, 2, 3)], cols_index, 0)
    a_grad = join([piece] + [ring(piece, "dp", k) for k in (1, 2, 3)], dp_index, 1)

    pieces = sum_split([keep, send], x_index, 0, 4)
    pieces = [pieces[0]] + [ring_x(pieces[k], k) for k in (1, 2, 3)]
    pieces = call(
        b_dp_kernel,
        [out((rank // 4, cols // 4))] * 4,
        [VMEM] * 5,
        vec, *pieces,
        scratch=[pltpu.VMEM((rank // 4, cols), F32)],
    )
    pieces = [pieces[0]] + [ring(pieces[k], "dp", k) for k in (1, 2, 3)]
    piece = (pieces[0] + pieces[2]) + (pieces[1] + pieces[3])
    b_part, mag_grad = call(
        functools.partial(b_join_kernel, gamma / float(full_rows) ** 0.5),
        [out((rank // 8, cols)), out((1, cols))],
        [VMEM] * 5,
        vec, piece, ring(piece, "dp", 1), ring(piece, "dp", 2), ring(piece, "dp", 3),
        scratch=[pltpu.VMEM((rank // 4, cols), F32)],
    )
    b_part = join([b_part] + [ring_x(b_part, k) for k in (1, 2, 3)], x_index, 0)
    b_grad = join([b_part, swap_core(b_part)], core_index, 0)

    grad = call(finish_kernel, [out((rows // 4, toks), BF16)], [VMEM] * 5, own, v0, v1, w0, w1)[0]
    return grad, a_grad.T, b_grad, mag_grad.reshape(cols)


def solution(mesh):
    return jax.shard_map(
        shards,
        mesh=mesh,
        in_specs=(
            P("dp", "rows"),
            P("dp", "cols"),
            P("rows", "cols"),
            P("rows", None),
            P(None, "cols"),
            P("cols"),
        ),
        out_specs=(P(("rows", "cols"), "dp"), P("rows", None), P(None, "cols"), P("cols")),
        check_vma=False,
    )
```

time: 356 us -> 120 us (0.34)
  waiting for transfers between devices: 177 us -> 31.8 us
  blocking collectives: 82.1 us -> 0 us
  matrix products: 53.7 us -> 0 us
  starting transfers between devices: 0.31 us -> 53.4 us
  Pallas kernels: 0 us -> 29.4 us
  other arithmetic: 18.4 us -> 0.04 us
  between operations: 15.6 us -> 0.82 us
  local copies, waits for them, and re-layouts: 9.28 us -> 4.69 us
    psum x2 -> x0, waiting for transfers between devices: 173 us -> none  [the longest x1 89.4 us: shards(): a_grad = lax.psum(a_part, ('dp', 'cols'))]
    psum x2 -> x0, blocking collectives: 82.1 us -> none  [the longest x1 69.4 us: shards(): inner = lax.psum(inner_part, ('dp', 'rows'))]
    dot_general x5 -> x0, matrix products: 53.7 us -> none  [the longest x1 15.4 us: shards(): lax.dot_general(gated_hidden_input, output_gradient, (((0,), (0,)), ((),...]
    ppermute x0 -> x36, starting transfers between devices: none -> 53.4 us  [the longest x24 39 us: ring(): lax.ppermute(value, axis, [(i, (i + k) % count) for i in range(count)])]
    ppermute x0 -> x36, waiting for transfers between devices: none -> 31.8 us  [the longest x24 21.3 us: ring(): lax.ppermute(value, axis, [(i, (i + k) % count) for i in range(count)])]
    pallas_call x0 -> x16, Pallas kernels: none -> 29.4 us  [call(): pl.pallas_call(kernel, out_shape=outs, in_specs=specs, out_specs=[VMEM fo...]
    convert_element_type x2 -> x0, other arithmetic: 17.8 us -> none  [the longest x1 15.8 us: shards(): direction_gradient = (scale * (weight_grad - merged_wide * (inner / (grou...]
    unnamed x16 -> x10, local copies, waits for them, and re-layouts: 9.28 us -> 4.69 us
  transfers between devices with their start and end apart: 3 -> 36, of which waited for: 3 -> 14; matrix products, arithmetic and copies ran while one was open for 9% -> 0% of each run, Pallas kernels for 0% -> 9%
where the time goes in v1:
time: 120 us
  starting transfers between devices  53.4 us (44%)
  waiting for transfers between devices  31.8 us (26%)
  Pallas kernels  29.4 us (24%)
  local copies, waits for them, and re-layouts  4.69 us (4%)
    ppermute x24, starting transfers between devices, ring(): lax.ppermute(value, axis, [(i, (i + k) % count) for i in range(count)])  39 us
    pallas_call x16, Pallas kernels, call(): pl.pallas_call(kernel, out_shape=outs, in_specs=specs, out_specs=[VMEM fo...  29.4 us
    ppermute x24, waiting for transfers between devices, ring(): lax.ppermute(value, axis, [(i, (i + k) % count) for i in range(count)])  21.3 us
    ppermute x9, starting transfers between devices, ring_x(): lax.ppermute(value, 'rows', [(i, (i + 2 * k) % count) for i in range(coun...  14.1 us
    ppermute x9, waiting for transfers between devices, ring_x(): lax.ppermute(value, 'rows', [(i, (i + 2 * k) % count) for i in range(coun...  9.32 us
    unnamed x10, local copies, waits for them, and re-layouts  4.69 us
  transfers between devices with their start and end apart: 36, of which 14 were waited for; matrix products, arithmetic and copies ran while one was open for 0% of the time, Pallas kernels for 9%

profile of v1, /device:TPU:0, one launch (start us, length us, event | category | flops | bytes accessed | tf_op | source)
XLA Modules:
  0.0 120.1 jit_solution(13544944822587534542)
XLA Ops:
  1.9 1.5 %copy-done.1 = bf16[256,3584]{1,0:T(8,128)(2,1)S(1)} copy-done((bf16[256,3584]{1,0:T(8,128)(2,1)S(1)}, bf16[256,3584]{1,0:T(8,128)(2,1)}, u32[]{:S(2)}) %copy-start.1) | copy-done | bytes 1835032
  5.3 15.8 %shard_map.93 = (bf16[3584,2048]{1,0:T(8,128)(2,1)S(1)}, f32[2,2048]{1,0:T(2,128)S(1)}, f32[64,2048]{1,0:T(8,128)S(1)}, f32[64,2048]{1,0:T(8,128)S(1)}) custom-call(bf16[3584,2048]{1,0:T(8,128)(2,1)} %w_ref.1, bf16[256,3584]{1,0:T(8,128)(2,1)S(1)} %copy-done.1, bf16[64,3584]{1,0:T(8,128)(2,1)S(1)} %bitcast.5, bf16[64,2048]{1,0:T(8,128)(2,1)S(1)} %copy-done.2, ...), custom_call_target="tpu_custom_call" | custom-call | flops 5637144576 | bytes 14680064 | tf_op jit(solution)/shard_map/pallas_call | solution.py:43
  22.4 1.6 %collective-permute-start.1 = (f32[2,2048]{1,0:T(2,128)S(1)}, f32[2,2048]{1,0:T(2,128)S(1)}, u32[]{:S(2)}, u32[]{:S(2)}) collective-permute-start(f32[2,2048]{1,0:T(2,128)S(1)} %add.21.stat_ref), channel_id=1, source_target_pairs={{0,8},{4,12},{8,16},{12,20},{16,24},{20,28},{24,0},{28,4},{1,9},{5... | collective-permute-start | bytes 49160 | tf_op jit(solution)/shard_map/ppermute | solution.py:294
  24.0 2.7 %collective-permute-start.2 = (f32[2,2048]{1,0:T(2,128)S(1)}, f32[2,2048]{1,0:T(2,128)S(1)}, u32[]{:S(2)}, u32[]{:S(2)}) collective-permute-start(f32[2,2048]{1,0:T(2,128)S(1)} %add.21.stat_ref), channel_id=1, source_target_pairs={{0,16},{4,20},{8,24},{12,28},{16,0},{20,4},{24,8},{28,12},{1,17},{... | collective-permute-start | bytes 49160 | tf_op jit(solution)/shard_map/ppermute | solution.py:294
  26.8 1.4 %collective-permute-start.3 = (f32[2,2048]{1,0:T(2,128)S(1)}, f32[2,2048]{1,0:T(2,128)S(1)}, u32[]{:S(2)}, u32[]{:S(2)}) collective-permute-start(f32[2,2048]{1,0:T(2,128)S(1)} %add.21.stat_ref), channel_id=1, source_target_pairs={{0,24},{4,28},{8,0},{12,4},{16,8},{20,12},{24,16},{28,20},{1,25},{... | collective-permute-start | bytes 49160 | tf_op jit(solution)/shard_map/ppermute | solution.py:294
  29.3 1.2 %collective-permute-done.3.r3_ref = f32[2,2048]{1,0:T(2,128)S(1)} collective-permute-done((f32[2,2048]{1,0:T(2,128)S(1)}, f32[2,2048]{1,0:T(2,128)S(1)}, u32[]{:S(2)}, u32[]{:S(2)}) %collective-permute-start.3) | collective-permute-done | bytes 16416 | tf_op jit(solution)/shard_map/ppermute | solution.py:294
  32.0 5.3 %shard_map.99 = (f32[64,896]{1,0:T(8,128)S(1)}, f32[64,896]{1,0:T(8,128)S(1)}, f32[64,896]{1,0:T(8,128)S(1)}, f32[64,896]{1,0:T(8,128)S(1)}) custom-call(f32[4,2048]{1,0:T(4,128)S(1)} %get-tuple-element.45.vec_ref, bf16[256,2048]{1,0:T(8,128)(2,1)S(1)} %copy-done, bf16[64,2048]{1,0:T(8,128)(2,1)S(1)} %copy-done.2, bf16[256,3584]{1,0:T(8,128)(2,1)S(1)} %copy-done.1, ...), custom_call_target="tpu_custom_call" | custom-call | flops 2113929216 | tf_op jit(solution)/shard_map/pallas_call | solution.py:43
  37.3 2.0 %collective-permute-start.10 = (f32[64,896]{1,0:T(8,128)S(1)}, f32[64,896]{1,0:T(8,128)S(1)}, u32[]{:S(2)}, u32[]{:S(2)}) collective-permute-start(f32[64,896]{1,0:T(8,128)S(1)} %get-tuple-element.47), channel_id=1, source_target_pairs={{0,32},{32,64},{64,96},{96,0},{1,33},{33,65},{65,97},{97,1},{2,34}... | collective-permute-start | bytes 688136 | tf_op jit(solution)/shard_map/ppermute | solution.py:290
  39.3 3.6 %collective-permute-start.11 = (f32[64,896]{1,0:T(8,128)S(1)}, f32[64,896]{1,0:T(8,128)S(1)}, u32[]{:S(2)}, u32[]{:S(2)}) collective-permute-start(f32[64,896]{1,0:T(8,128)S(1)} %get-tuple-element.48), channel_id=1, source_target_pairs={{0,64},{32,96},{64,0},{96,32},{1,65},{33,97},{65,1},{97,33},{2,66}... | collective-permute-start | bytes 688136 | tf_op jit(solution)/shard_map/ppermute | solution.py:290
  44.3 3.8 %collective-permute-start.24 = (f32[8,2048]{1,0:T(8,128)S(1)}, f32[8,2048]{1,0:T(8,128)S(1)}, u32[]{:S(2)}, u32[]{:S(2)}) collective-permute-start(f32[8,2048]{1,0:T(8,128)S(1)} %get-tuple-element.60), channel_id=1, source_target_pairs={{0,16},{4,20},{8,24},{12,28},{16,0},{20,4},{24,8},{28,12},{1,17},{... | collective-permute-start | bytes 196616 | tf_op jit(solution)/shard_map/ppermute | solution.py:294
  48.1 2.2 %collective-permute-start.25 = (f32[8,2048]{1,0:T(8,128)S(1)}, f32[8,2048]{1,0:T(8,128)S(1)}, u32[]{:S(2)}, u32[]{:S(2)}) collective-permute-start(f32[8,2048]{1,0:T(8,128)S(1)} %get-tuple-element.61), channel_id=1, source_target_pairs={{0,24},{4,28},{8,0},{12,4},{16,8},{20,12},{24,16},{28,20},{1,25},{... | collective-permute-start | bytes 196616 | tf_op jit(solution)/shard_map/ppermute | solution.py:294
  50.3 3.4 %collective-permute-done.11.refs_2_ = f32[64,896]{1,0:T(8,128)S(1)} collective-permute-done((f32[64,896]{1,0:T(8,128)S(1)}, f32[64,896]{1,0:T(8,128)S(1)}, u32[]{:S(2)}, u32[]{:S(2)}) %collective-permute-start.11) | collective-permute-done | bytes 229408 | tf_op jit(solution)/shard_map/ppermute | solution.py:290
  53.8 3.3 %collective-permute-start.13 = (f32[16,896]{1,0:T(8,128)S(1)}, f32[16,896]{1,0:T(8,128)S(1)}, u32[]{:S(2)}, u32[]{:S(2)}) collective-permute-start(f32[16,896]{1,0:T(8,128)S(1)} %get-tuple-element.51), channel_id=1, source_target_pairs={{0,2},{1,3},{2,0},{3,1},{4,6},{5,7},{6,4},{7,5},{8,10},{9,11},{10,... | collective-permute-start | bytes 172040 | tf_op jit(solution)/shard_map/ppermute | solution.py:290
  57.8 2.6 %collective-permute-start.15 = (f32[16,896]{1,0:T(8,128)S(1)}, f32[16,896]{1,0:T(8,128)S(1)}, u32[]{:S(2)}, u32[]{:S(2)}) collective-permute-start(f32[16,896]{1,0:T(8,128)S(1)} %get-tuple-element.53), channel_id=1, source_target_pairs={{0,3},{1,0},{2,1},{3,2},{4,7},{5,4},{6,5},{7,6},{8,11},{9,8},{10,9... | collective-permute-start | bytes 172040 | tf_op jit(solution)/shard_map/ppermute | solution.py:290
  60.4 3.2 %collective-permute-start.7 = (f32[448,256]{1,0:T(8,128)S(1)}, f32[448,256]{1,0:T(8,128)S(1)}, u32[]{:S(2)}, u32[]{:S(2)}) collective-permute-start(f32[448,256]{1,0:T(8,128)S(1)} %get-tuple-element.42), channel_id=1, source_target_pairs={{0,3},{1,0},{2,1},{3,2},{4,7},{5,4},{6,5},{7,6},{8,11},{9,8},{10,9... | collective-permute-start | bytes 1376264 | tf_op jit(solution)/shard_map/ppermute | solution.py:290
  63.6 3.1 %collective-permute-start.26 = (f32[16,512]{1,0:T(8,128)S(1)}, f32[16,512]{1,0:T(8,128)S(1)}, u32[]{:S(2)}, u32[]{:S(2)}) collective-permute-start(f32[16,512]{1,0:T(8,128)S(1)} %get-tuple-element.63), channel_id=1, source_target_pairs={{0,64},{32,96},{64,0},{96,32},{1,65},{33,97},{65,1},{97,33},{2,66}... | collective-permute-start | bytes 98312 | tf_op jit(solution)/shard_map/ppermute | solution.py:290
  66.8 3.2 %collective-permute-start.28 = (f32[16,512]{1,0:T(8,128)S(1)}, f32[16,512]{1,0:T(8,128)S(1)}, u32[]{:S(2)}, u32[]{:S(2)}) collective-permute-start(f32[16,512]{1,0:T(8,128)S(1)} %get-tuple-element.65), channel_id=1, source_target_pairs={{0,96},{32,0},{64,32},{96,64},{1,97},{33,1},{65,33},{97,65},{2,98}... | collective-permute-start | bytes 98312 | tf_op jit(solution)/shard_map/ppermute | solution.py:290
  70.1 1.8 %collective-permute-done.27 = f32[16,512]{1,0:T(8,128)S(1)} collective-permute-done((f32[16,512]{1,0:T(8,128)S(1)}, f32[16,512]{1,0:T(8,128)S(1)}, u32[]{:S(2)}, u32[]{:S(2)}) %collective-permute-start.27) | collective-permute-done | bytes 32800 | tf_op jit(solution)/shard_map/ppermute | solution.py:290
  71.9 1.5 %collective-permute-start.18 = (f32[16,896]{1,0:T(8,128)S(1)}, f32[16,896]{1,0:T(8,128)S(1)}, u32[]{:S(2)}, u32[]{:S(2)}) collective-permute-start(f32[16,896]{1,0:T(8,128)S(1)} %add_add_fusion.refs_0_), channel_id=1, source_target_pairs={{0,3},{1,0},{2,1},{3,2},{4,7},{5,4},{6,5},{7,6},{8,11},{9,8},{10,9... | collective-permute-start | bytes 172040 | tf_op jit(solution)/shard_map/ppermute | solution.py:290
  73.4 2.0 %collective-permute-done.16.refs_1_ = f32[16,896]{1,0:T(8,128)S(1)} collective-permute-done((f32[16,896]{1,0:T(8,128)S(1)}, f32[16,896]{1,0:T(8,128)S(1)}, u32[]{:S(2)}, u32[]{:S(2)}) %collective-permute-start.16) | collective-permute-done | bytes 57376 | tf_op jit(solution)/shard_map/ppermute | solution.py:290
  75.9 1.6 %collective-permute-done.17.refs_2_ = f32[16,896]{1,0:T(8,128)S(1)} collective-permute-done((f32[16,896]{1,0:T(8,128)S(1)}, f32[16,896]{1,0:T(8,128)S(1)}, u32[]{:S(2)}, u32[]{:S(2)}) %collective-permute-start.17) | collective-permute-done | bytes 57376 | tf_op jit(solution)/shard_map/ppermute | solution.py:290
  77.6 1.7 %collective-permute-start.30 = (f32[16,512]{1,0:T(8,128)S(1)}, f32[16,512]{1,0:T(8,128)S(1)}, u32[]{:S(2)}, u32[]{:S(2)}) collective-permute-start(f32[16,512]{1,0:T(8,128)S(1)} %add_add_fusion.1.i0_ref), channel_id=1, source_target_pairs={{0,64},{32,96},{64,0},{96,32},{1,65},{33,97},{65,1},{97,33},{2,66}... | collective-permute-start | bytes 98312 | tf_op jit(solution)/shard_map/ppermute | solution.py:290
  79.7 1.3 %collective-permute-done.29.i1_ref = f32[16,512]{1,0:T(8,128)S(1)} collective-permute-done((f32[16,512]{1,0:T(8,128)S(1)}, f32[16,512]{1,0:T(8,128)S(1)}, u32[]{:S(2)}, u32[]{:S(2)}) %collective-permute-start.29) | collective-permute-done | bytes 32800 | tf_op jit(solution)/shard_map/ppermute | solution.py:290
  81.0 1.5 %collective-permute-start.20 = (f32[64,896]{1,0:T(8,128)S(1)}, f32[64,896]{1,0:T(8,128)S(1)}, u32[]{:S(2)}, u32[]{:S(2)}) collective-permute-start(f32[64,896]{1,0:T(8,128)S(1)} %shard_map.101.refs_0_), channel_id=1, source_target_pairs={{0,64},{32,96},{64,0},{96,32},{1,65},{33,97},{65,1},{97,33},{2,66}... | collective-permute-start | bytes 688136 | tf_op jit(solution)/shard_map/ppermute | solution.py:290
  84.6 3.2 %collective-permute-done.31.i3_ref = f32[16,512]{1,0:T(8,128)S(1)} collective-permute-done((f32[16,512]{1,0:T(8,128)S(1)}, f32[16,512]{1,0:T(8,128)S(1)}, u32[]{:S(2)}, u32[]{:S(2)}) %collective-permute-start.31) | collective-permute-done | bytes 32800 | tf_op jit(solution)/shard_map/ppermute | solution.py:290
  89.9 4.0 %collective-permute-done.32.refs_1_ = f32[8,2048]{1,0:T(8,128)S(1)} collective-permute-done((f32[8,2048]{1,0:T(8,128)S(1)}, f32[8,2048]{1,0:T(8,128)S(1)}, u32[]{:S(2)}, u32[]{:S(2)}) %collective-permute-start.32) | collective-permute-done | bytes 65568 | tf_op jit(solution)/shard_map/ppermute | solution.py:294
  93.9 3.0 %collective-permute-start.21 = (f32[64,896]{1,0:T(8,128)S(1)}, f32[64,896]{1,0:T(8,128)S(1)}, u32[]{:S(2)}, u32[]{:S(2)}) collective-permute-start(f32[64,896]{1,0:T(8,128)S(1)} %shard_map.101.refs_0_), channel_id=1, source_target_pairs={{0,96},{32,0},{64,32},{96,64},{1,97},{33,1},{65,33},{97,65},{2,98}... | collective-permute-start | bytes 688136 | tf_op jit(solution)/shard_map/ppermute | solution.py:290
  99.7 3.0 %collective-permute-done.33.refs_2_ = f32[8,2048]{1,0:T(8,128)S(1)} collective-permute-done((f32[8,2048]{1,0:T(8,128)S(1)}, f32[8,2048]{1,0:T(8,128)S(1)}, u32[]{:S(2)}, u32[]{:S(2)}) %collective-permute-start.33) | collective-permute-done | bytes 65568 | tf_op jit(solution)/shard_map/ppermute | solution.py:294
  102.7 3.2 %collective-permute-start.5 = (f32[448,256]{1,0:T(8,128)S(1)}, f32[448,256]{1,0:T(8,128)S(1)}, u32[]{:S(2)}, u32[]{:S(2)}) collective-permute-start(f32[448,256]{1,0:T(8,128)S(1)} %get-tuple-element.40), channel_id=1, source_target_pairs={{0,3},{1,0},{2,1},{3,2},{4,7},{5,4},{6,5},{7,6},{8,11},{9,8},{10,9... | collective-permute-start | bytes 1376264 | tf_op jit(solution)/shard_map/ppermute | solution.py:290
  106.0 3.2 %collective-permute-start.9 = (f32[448,256]{1,0:T(8,128)S(1)}, f32[448,256]{1,0:T(8,128)S(1)}, u32[]{:S(2)}, u32[]{:S(2)}) collective-permute-start(f32[448,256]{1,0:T(8,128)S(1)} %get-tuple-element.44), channel_id=1, source_target_pairs={{0,3},{1,0},{2,1},{3,2},{4,7},{5,4},{6,5},{7,6},{8,11},{9,8},{10,9... | collective-permute-start | bytes 1376264 | tf_op jit(solution)/shard_map/ppermute | solution.py:290
  112.4 2.0 %collective-permute-done.4.v0_ref = f32[448,256]{1,0:T(8,128)S(1)} collective-permute-done((f32[448,256]{1,0:T(8,128)S(1)}, f32[448,256]{1,0:T(8,128)S(1)}, u32[]{:S(2)}, u32[]{:S(2)}) %collective-permute-start.4) | collective-permute-done | bytes 458784 | tf_op jit(solution)/shard_map/ppermute | solution.py:290
  114.3 4.9 %collective-permute-done.8.w0_ref = f32[448,256]{1,0:T(8,128)S(1)} collective-permute-done((f32[448,256]{1,0:T(8,128)S(1)}, f32[448,256]{1,0:T(8,128)S(1)}, u32[]{:S(2)}, u32[]{:S(2)}) %collective-permute-start.8) | collective-permute-done | bytes 458784 | tf_op jit(solution)/shard_map/ppermute | solution.py:290
  (69 shorter events, 21.1 us)
Async XLA Ops:
  22.4 5.8 %collective-permute-start.1 = (f32[2,2048]{1,0:T(2,128)S(1)}, f32[2,2048]{1,0:T(2,128)S(1)}, u32[]{:S(2)}, u32[]{:S(2)}) collective-permute-start(f32[2,2048]{1,0:T(2,128)S(1)} %add.21.stat_ref), channel_id=1, source_target_pairs={{0,8},{4,12},{8,16},{12,20},{16,24},{20,28},{24,0},{28,4},{1,9},{5... | collective-permute-start | bytes 49160 | tf_op jit(solution)/shard_map/ppermute | solution.py:294
  24.0 5.2 %collective-permute-start.2 = (f32[2,2048]{1,0:T(2,128)S(1)}, f32[2,2048]{1,0:T(2,128)S(1)}, u32[]{:S(2)}, u32[]{:S(2)}) collective-permute-start(f32[2,2048]{1,0:T(2,128)S(1)} %add.21.stat_ref), channel_id=1, source_target_pairs={{0,16},{4,20},{8,24},{12,28},{16,0},{20,4},{24,8},{28,12},{1,17},{... | collective-permute-start | bytes 49160 | tf_op jit(solution)/shard_map/ppermute | solution.py:294
  31.9 12.0 %collective-permute-start.22 = (f32[32,2048]{1,0:T(8,128)S(1)}, f32[32,2048]{1,0:T(8,128)S(1)}, u32[]{:S(2)}, u32[]{:S(2)}) collective-permute-start(f32[32,2048]{1,0:T(8,128)S(1)} %get-tuple-element.57), channel_id=1, source_target_pairs={{0,4},{4,0},{8,12},{12,8},{16,20},{20,16},{24,28},{28,24},{1,5},{5... | collective-permute-start | bytes 786440 | tf_op jit(solution)/shard_map/ppermute | solution.py:298
  37.3 10.8 %collective-permute-start.10 = (f32[64,896]{1,0:T(8,128)S(1)}, f32[64,896]{1,0:T(8,128)S(1)}, u32[]{:S(2)}, u32[]{:S(2)}) collective-permute-start(f32[64,896]{1,0:T(8,128)S(1)} %get-tuple-element.47), channel_id=1, source_target_pairs={{0,32},{32,64},{64,96},{96,0},{1,33},{33,65},{65,97},{97,1},{2,34}... | collective-permute-start | bytes 688136 | tf_op jit(solution)/shard_map/ppermute | solution.py:290
  39.3 14.5 %collective-permute-start.11 = (f32[64,896]{1,0:T(8,128)S(1)}, f32[64,896]{1,0:T(8,128)S(1)}, u32[]{:S(2)}, u32[]{:S(2)}) collective-permute-start(f32[64,896]{1,0:T(8,128)S(1)} %get-tuple-element.48), channel_id=1, source_target_pairs={{0,64},{32,96},{64,0},{96,32},{1,65},{33,97},{65,1},{97,33},{2,66}... | collective-permute-start | bytes 688136 | tf_op jit(solution)/shard_map/ppermute | solution.py:290
  42.9 10.9 %collective-permute-start.12 = (f32[64,896]{1,0:T(8,128)S(1)}, f32[64,896]{1,0:T(8,128)S(1)}, u32[]{:S(2)}, u32[]{:S(2)}) collective-permute-start(f32[64,896]{1,0:T(8,128)S(1)} %get-tuple-element.49), channel_id=1, source_target_pairs={{0,96},{32,0},{64,32},{96,64},{1,97},{33,1},{65,33},{97,65},{2,98}... | collective-permute-start | bytes 688136 | tf_op jit(solution)/shard_map/ppermute | solution.py:290
  43.9 13.9 %collective-permute-start.23 = (f32[8,2048]{1,0:T(8,128)S(1)}, f32[8,2048]{1,0:T(8,128)S(1)}, u32[]{:S(2)}, u32[]{:S(2)}) collective-permute-start(f32[8,2048]{1,0:T(8,128)S(1)} %get-tuple-element.59), channel_id=1, source_target_pairs={{0,8},{4,12},{8,16},{12,20},{16,24},{20,28},{24,0},{28,4},{1,9},{5... | collective-permute-start | bytes 196616 | tf_op jit(solution)/shard_map/ppermute | solution.py:294
  44.3 16.1 %collective-permute-start.24 = (f32[8,2048]{1,0:T(8,128)S(1)}, f32[8,2048]{1,0:T(8,128)S(1)}, u32[]{:S(2)}, u32[]{:S(2)}) collective-permute-start(f32[8,2048]{1,0:T(8,128)S(1)} %get-tuple-element.60), channel_id=1, source_target_pairs={{0,16},{4,20},{8,24},{12,28},{16,0},{20,4},{24,8},{28,12},{1,17},{... | collective-permute-start | bytes 196616 | tf_op jit(solution)/shard_map/ppermute | solution.py:294
  48.1 12.3 %collective-permute-start.25 = (f32[8,2048]{1,0:T(8,128)S(1)}, f32[8,2048]{1,0:T(8,128)S(1)}, u32[]{:S(2)}, u32[]{:S(2)}) collective-permute-start(f32[8,2048]{1,0:T(8,128)S(1)} %get-tuple-element.61), channel_id=1, source_target_pairs={{0,24},{4,28},{8,0},{12,4},{16,8},{20,12},{24,16},{28,20},{1,25},{... | collective-permute-start | bytes 196616 | tf_op jit(solution)/shard_map/ppermute | solution.py:294
  53.8 9.8 %collective-permute-start.13 = (f32[16,896]{1,0:T(8,128)S(1)}, f32[16,896]{1,0:T(8,128)S(1)}, u32[]{:S(2)}, u32[]{:S(2)}) collective-permute-start(f32[16,896]{1,0:T(8,128)S(1)} %get-tuple-element.51), channel_id=1, source_target_pairs={{0,2},{1,3},{2,0},{3,1},{4,6},{5,7},{6,4},{7,5},{8,10},{9,11},{10,... | collective-permute-start | bytes 172040 | tf_op jit(solution)/shard_map/ppermute | solution.py:290
  57.1 9.7 %collective-permute-start.14 = (f32[16,896]{1,0:T(8,128)S(1)}, f32[16,896]{1,0:T(8,128)S(1)}, u32[]{:S(2)}, u32[]{:S(2)}) collective-permute-start(f32[16,896]{1,0:T(8,128)S(1)} %get-tuple-element.52), channel_id=1, source_target_pairs={{0,1},{1,2},{2,3},{3,0},{4,5},{5,6},{6,7},{7,4},{8,9},{9,10},{10,1... | collective-permute-start | bytes 172040 | tf_op jit(solution)/shard_map/ppermute | solution.py:290
  57.8 9.0 %collective-permute-start.15 = (f32[16,896]{1,0:T(8,128)S(1)}, f32[16,896]{1,0:T(8,128)S(1)}, u32[]{:S(2)}, u32[]{:S(2)}) collective-permute-start(f32[16,896]{1,0:T(8,128)S(1)} %get-tuple-element.53), channel_id=1, source_target_pairs={{0,3},{1,0},{2,1},{3,2},{4,7},{5,4},{6,5},{7,6},{8,11},{9,8},{10,9... | collective-permute-start | bytes 172040 | tf_op jit(solution)/shard_map/ppermute | solution.py:290
  60.4 36.6 %collective-permute-start.6 = (f32[448,256]{1,0:T(8,128)S(1)}, f32[448,256]{1,0:T(8,128)S(1)}, u32[]{:S(2)}, u32[]{:S(2)}) collective-permute-start(f32[448,256]{1,0:T(8,128)S(1)} %get-tuple-element.41), channel_id=1, source_target_pairs={{0,1},{1,2},{2,3},{3,0},{4,5},{5,6},{6,7},{7,4},{8,9},{9,10},{10,1... | collective-permute-start | bytes 1376264 | tf_op jit(solution)/shard_map/ppermute | solution.py:290
  60.4 37.1 %collective-permute-start.7 = (f32[448,256]{1,0:T(8,128)S(1)}, f32[448,256]{1,0:T(8,128)S(1)}, u32[]{:S(2)}, u32[]{:S(2)}) collective-permute-start(f32[448,256]{1,0:T(8,128)S(1)} %get-tuple-element.42), channel_id=1, source_target_pairs={{0,3},{1,0},{2,1},{3,2},{4,7},{5,4},{6,5},{7,6},{8,11},{9,8},{10,9... | collective-permute-start | bytes 1376264 | tf_op jit(solution)/shard_map/ppermute | solution.py:290
  63.6 6.4 %collective-permute-start.26 = (f32[16,512]{1,0:T(8,128)S(1)}, f32[16,512]{1,0:T(8,128)S(1)}, u32[]{:S(2)}, u32[]{:S(2)}) collective-permute-start(f32[16,512]{1,0:T(8,128)S(1)} %get-tuple-element.63), channel_id=1, source_target_pairs={{0,64},{32,96},{64,0},{96,32},{1,65},{33,97},{65,1},{97,33},{2,66}... | collective-permute-start | bytes 98312 | tf_op jit(solution)/shard_map/ppermute | solution.py:290
  66.8 5.1 %collective-permute-start.27 = (f32[16,512]{1,0:T(8,128)S(1)}, f32[16,512]{1,0:T(8,128)S(1)}, u32[]{:S(2)}, u32[]{:S(2)}) collective-permute-start(f32[16,512]{1,0:T(8,128)S(1)} %get-tuple-element.64), channel_id=1, source_target_pairs={{0,32},{32,64},{64,96},{96,0},{1,33},{33,65},{65,97},{97,1},{2,34}... | collective-permute-start | bytes 98312 | tf_op jit(solution)/shard_map/ppermute | solution.py:290
  66.8 5.1 %collective-permute-start.28 = (f32[16,512]{1,0:T(8,128)S(1)}, f32[16,512]{1,0:T(8,128)S(1)}, u32[]{:S(2)}, u32[]{:S(2)}) collective-permute-start(f32[16,512]{1,0:T(8,128)S(1)} %get-tuple-element.65), channel_id=1, source_target_pairs={{0,96},{32,0},{64,32},{96,64},{1,97},{33,1},{65,33},{97,65},{2,98}... | collective-permute-start | bytes 98312 | tf_op jit(solution)/shard_map/ppermute | solution.py:290
  70.0 5.5 %collective-permute-start.16 = (f32[16,896]{1,0:T(8,128)S(1)}, f32[16,896]{1,0:T(8,128)S(1)}, u32[]{:S(2)}, u32[]{:S(2)}) collective-permute-start(f32[16,896]{1,0:T(8,128)S(1)} %add_add_fusion.refs_0_), channel_id=1, source_target_pairs={{0,1},{1,2},{2,3},{3,0},{4,5},{5,6},{6,7},{7,4},{8,9},{9,10},{10,1... | collective-permute-start | bytes 172040 | tf_op jit(solution)/shard_map/ppermute | solution.py:290
  71.9 5.7 %collective-permute-start.17 = (f32[16,896]{1,0:T(8,128)S(1)}, f32[16,896]{1,0:T(8,128)S(1)}, u32[]{:S(2)}, u32[]{:S(2)}) collective-permute-start(f32[16,896]{1,0:T(8,128)S(1)} %add_add_fusion.refs_0_), channel_id=1, source_target_pairs={{0,2},{1,3},{2,0},{3,1},{4,6},{5,7},{6,4},{7,5},{8,10},{9,11},{10,... | collective-permute-start | bytes 172040 | tf_op jit(solution)/shard_map/ppermute | solution.py:290
  71.9 7.4 %collective-permute-start.18 = (f32[16,896]{1,0:T(8,128)S(1)}, f32[16,896]{1,0:T(8,128)S(1)}, u32[]{:S(2)}, u32[]{:S(2)}) collective-permute-start(f32[16,896]{1,0:T(8,128)S(1)} %add_add_fusion.refs_0_), channel_id=1, source_target_pairs={{0,3},{1,0},{2,1},{3,2},{4,7},{5,4},{6,5},{7,6},{8,11},{9,8},{10,9... | collective-permute-start | bytes 172040 | tf_op jit(solution)/shard_map/ppermute | solution.py:290
  75.5 5.5 %collective-permute-start.29 = (f32[16,512]{1,0:T(8,128)S(1)}, f32[16,512]{1,0:T(8,128)S(1)}, u32[]{:S(2)}, u32[]{:S(2)}) collective-permute-start(f32[16,512]{1,0:T(8,128)S(1)} %add_add_fusion.1.i0_ref), channel_id=1, source_target_pairs={{0,32},{32,64},{64,96},{96,0},{1,33},{33,65},{65,97},{97,1},{2,34}... | collective-permute-start | bytes 98312 | tf_op jit(solution)/shard_map/ppermute | solution.py:290
  77.6 5.9 %collective-permute-start.30 = (f32[16,512]{1,0:T(8,128)S(1)}, f32[16,512]{1,0:T(8,128)S(1)}, u32[]{:S(2)}, u32[]{:S(2)}) collective-permute-start(f32[16,512]{1,0:T(8,128)S(1)} %add_add_fusion.1.i0_ref), channel_id=1, source_target_pairs={{0,64},{32,96},{64,0},{96,32},{1,65},{33,97},{65,1},{97,33},{2,66}... | collective-permute-start | bytes 98312 | tf_op jit(solution)/shard_map/ppermute | solution.py:290
  79.3 26.7 %collective-permute-start.19 = (f32[64,896]{1,0:T(8,128)S(1)}, f32[64,896]{1,0:T(8,128)S(1)}, u32[]{:S(2)}, u32[]{:S(2)}) collective-permute-start(f32[64,896]{1,0:T(8,128)S(1)} %shard_map.101.refs_0_), channel_id=1, source_target_pairs={{0,32},{32,64},{64,96},{96,0},{1,33},{33,65},{65,97},{97,1},{2,34}... | collective-permute-start | bytes 688136 | tf_op jit(solution)/shard_map/ppermute | solution.py:290
  81.0 25.0 %collective-permute-start.20 = (f32[64,896]{1,0:T(8,128)S(1)}, f32[64,896]{1,0:T(8,128)S(1)}, u32[]{:S(2)}, u32[]{:S(2)}) collective-permute-start(f32[64,896]{1,0:T(8,128)S(1)} %shard_map.101.refs_0_), channel_id=1, source_target_pairs={{0,64},{32,96},{64,0},{96,32},{1,65},{33,97},{65,1},{97,33},{2,66}... | collective-permute-start | bytes 688136 | tf_op jit(solution)/shard_map/ppermute | solution.py:290
  88.4 5.5 %collective-permute-start.32 = (f32[8,2048]{1,0:T(8,128)S(1)}, f32[8,2048]{1,0:T(8,128)S(1)}, u32[]{:S(2)}, u32[]{:S(2)}) collective-permute-start(f32[8,2048]{1,0:T(8,128)S(1)} %get-tuple-element.66.refs_0_), channel_id=1, source_target_pairs={{0,8},{4,12},{8,16},{12,20},{16,24},{20,28},{24,0},{28,4},{1,9},{5... | collective-permute-start | bytes 196616 | tf_op jit(solution)/shard_map/ppermute | solution.py:294
  93.9 15.3 %collective-permute-start.21 = (f32[64,896]{1,0:T(8,128)S(1)}, f32[64,896]{1,0:T(8,128)S(1)}, u32[]{:S(2)}, u32[]{:S(2)}) collective-permute-start(f32[64,896]{1,0:T(8,128)S(1)} %shard_map.101.refs_0_), channel_id=1, source_target_pairs={{0,96},{32,0},{64,32},{96,64},{1,97},{33,1},{65,33},{97,65},{2,98}... | collective-permute-start | bytes 688136 | tf_op jit(solution)/shard_map/ppermute | solution.py:290
  96.9 5.8 %collective-permute-start.33 = (f32[8,2048]{1,0:T(8,128)S(1)}, f32[8,2048]{1,0:T(8,128)S(1)}, u32[]{:S(2)}, u32[]{:S(2)}) collective-permute-start(f32[8,2048]{1,0:T(8,128)S(1)} %get-tuple-element.66.refs_0_), channel_id=1, source_target_pairs={{0,16},{4,20},{8,24},{12,28},{16,0},{20,4},{24,8},{28,12},{1,17},{... | collective-permute-start | bytes 196616 | tf_op jit(solution)/shard_map/ppermute | solution.py:294
  97.4 5.3 %collective-permute-start.34 = (f32[8,2048]{1,0:T(8,128)S(1)}, f32[8,2048]{1,0:T(8,128)S(1)}, u32[]{:S(2)}, u32[]{:S(2)}) collective-permute-start(f32[8,2048]{1,0:T(8,128)S(1)} %get-tuple-element.66.refs_0_), channel_id=1, source_target_pairs={{0,24},{4,28},{8,0},{12,4},{16,8},{20,12},{24,16},{28,20},{1,25},{... | collective-permute-start | bytes 196616 | tf_op jit(solution)/shard_map/ppermute | solution.py:294
  102.7 11.6 %collective-permute-start.4 = (f32[448,256]{1,0:T(8,128)S(1)}, f32[448,256]{1,0:T(8,128)S(1)}, u32[]{:S(2)}, u32[]{:S(2)}) collective-permute-start(f32[448,256]{1,0:T(8,128)S(1)} %get-tuple-element.39), channel_id=1, source_target_pairs={{0,1},{1,2},{2,3},{3,0},{4,5},{5,6},{6,7},{7,4},{8,9},{9,10},{10,1... | collective-permute-start | bytes 1376264 | tf_op jit(solution)/shard_map/ppermute | solution.py:290
  102.7 11.6 %collective-permute-start.5 = (f32[448,256]{1,0:T(8,128)S(1)}, f32[448,256]{1,0:T(8,128)S(1)}, u32[]{:S(2)}, u32[]{:S(2)}) collective-permute-start(f32[448,256]{1,0:T(8,128)S(1)} %get-tuple-element.40), channel_id=1, source_target_pairs={{0,3},{1,0},{2,1},{3,2},{4,7},{5,4},{6,5},{7,6},{8,11},{9,8},{10,9... | collective-permute-start | bytes 1376264 | tf_op jit(solution)/shard_map/ppermute | solution.py:290
  106.0 13.3 %collective-permute-start.8 = (f32[448,256]{1,0:T(8,128)S(1)}, f32[448,256]{1,0:T(8,128)S(1)}, u32[]{:S(2)}, u32[]{:S(2)}) collective-permute-start(f32[448,256]{1,0:T(8,128)S(1)} %get-tuple-element.43), channel_id=1, source_target_pairs={{0,1},{1,2},{2,3},{3,0},{4,5},{5,6},{6,7},{7,4},{8,9},{9,10},{10,1... | collective-permute-start | bytes 1376264 | tf_op jit(solution)/shard_map/ppermute | solution.py:290
  106.0 13.3 %collective-permute-start.9 = (f32[448,256]{1,0:T(8,128)S(1)}, f32[448,256]{1,0:T(8,128)S(1)}, u32[]{:S(2)}, u32[]{:S(2)}) collective-permute-start(f32[448,256]{1,0:T(8,128)S(1)} %get-tuple-element.44), channel_id=1, source_target_pairs={{0,3},{1,0},{2,1},{3,2},{4,7},{5,4},{6,5},{7,6},{8,11},{9,8},{10,9... | collective-permute-start | bytes 1376264 | tf_op jit(solution)/shard_map/ppermute | solution.py:290
  (9 other events, 41.5 us)

commit v2 on v1

--- a/solution.py
+++ b/solution.py
@@ -14,6 +14,7 @@
 
 ANY = pl.BlockSpec(memory_space=pl.ANY)
 VMEM = pl.BlockSpec(memory_space=pltpu.VMEM)
+HBM = pl.BlockSpec(memory_space=pltpu.HBM)
 
 
 def nn(a, b):
@@ -39,16 +40,21 @@
     return value[:half] + value[half:]
 
 
-def call(kernel, outs, specs, *args, scratch=(), vmem=16, flops=0, data=0):
+def call(kernel, outs, specs, *args, scratch=(), vmem=16, flops=1, data=1, after=()):
+    used = len(args)
+
+    def body(*refs):
+        kernel(*refs[:used], *refs[used + len(after):])
+
     return pl.pallas_call(
-        kernel,
+        body,
         out_shape=outs,
-        in_specs=specs,
+        in_specs=list(specs) + [ANY] * len(after),
         out_specs=[VMEM for _ in outs],
         scratch_shapes=list(scratch),
         compiler_params=pltpu.CompilerParams(vmem_limit_bytes=vmem * MIB),
         cost_estimate=pl.CostEstimate(flops=flops, bytes_accessed=data, transcendentals=0),
-    )(*args)
+    )(*args, *after)
 
 
 def out(shape, dtype=F32):
@@ -62,7 +68,7 @@
     rows, cols = w_ref.shape
     toks = x_ref.shape[0]
     step = rows // steps
-    tile = 256
+    tile = 2048
     b_copy = pltpu.make_async_copy(b_ref, b2, b_sem)
     dy_copy = pltpu.make_async_copy(dy_ref, dy, dy_sem)
     a_copy = pltpu.make_async_copy(a_ref, xa.at[toks:], a_sem)
@@ -71,27 +77,25 @@
         part = pl.ds(pl.multiple_of(i * step, step), step)
         return pltpu.make_async_copy(w_ref.at[part], m_ref.at[part], w_sem.at[i])
 
-    def x_copy(i):
-        part = pl.ds(pl.multiple_of(i * step, step), step)
-        return pltpu.make_async_copy(x_ref.at[:, part], xa.at[:toks, part], x_sem.at[i])
-
+    x_copy = pltpu.make_async_copy(x_ref, xa.at[:toks], x_sem)
     b_copy.start()
     a_copy.start()
-    for i in range(steps):
+    w_copy(0).start()
+    x_copy.start()
+    for i in range(1, steps):
         w_copy(i).start()
-        x_copy(i).start()
     dy_copy.start()
     acc[...] = jnp.zeros_like(acc)
     qt[...] = jnp.zeros_like(qt)
     sq[...] = jnp.zeros_like(sq)
     b_copy.wait()
     a_copy.wait()
+    x_copy.wait()
     b2[...] = b2[...] + b2[...]
 
     @pl.loop(0, steps)
     def _(i):
         w_copy(i).wait()
-        x_copy(i).wait()
         part = pl.ds(pl.multiple_of(i * step, step), step)
         xa_part = xa[:, part]
         a_part = xa_part[toks:]
@@ -120,8 +124,8 @@
     return call(
         functools.partial(merge_kernel, steps),
         [pltpu.VMEM((rows, cols), BF16), out((2, cols)), out((rank, cols)), out((rank, cols))],
-        [ANY] * 5,
-        w, x, a_t, b, dy,
+        [HBM] * 5,
+        *[pltpu.with_memory_space_constraint(value, pltpu.HBM) for value in (w, x, a_t, b, dy)],
         scratch=[
             pltpu.VMEM((toks + rank, rows), BF16),
             pltpu.VMEM((rank, cols), BF16),
@@ -129,9 +133,9 @@
             pltpu.VMEM((toks + rank, cols), F32),
             pltpu.VMEM((rank, toks), F32),
             pltpu.VMEM((8, cols), F32),
-            dma((steps,)), dma((steps,)), dma, dma, dma,
+            dma((steps,)), dma, dma, dma, dma,
         ],
-        vmem=24,
+        vmem=32,
         flops=2 * rows * cols * (toks + 2 * rank),
         data=rows * cols * 2,
     )
@@ -175,10 +179,16 @@
     own_ref[...] = nt(block(m_ref, lax.axis_index("cols")), scaled_ref[...])
 
 
-def finish_kernel(own_ref, v0_ref, v1_ref, w0_ref, w1_ref, out_ref):
+def direct_kernel(own_ref, v0_ref, v1_ref, sum_ref):
     half = own_ref.shape[0] // 2
-    out_ref[:half] = (own_ref[:half] + (w0_ref[...] + v1_ref[...])).astype(BF16)
-    out_ref[half:] = (own_ref[half:] + (w1_ref[...] + v0_ref[...])).astype(BF16)
+    sum_ref[:half] = own_ref[:half] + v1_ref[...]
+    sum_ref[half:] = own_ref[half:] + v0_ref[...]
+
+
+def finish_kernel(own_ref, w0_ref, w1_ref, out_ref):
+    half = own_ref.shape[0] // 2
+    out_ref[:half] = (own_ref[:half] + w0_ref[...]).astype(BF16)
+    out_ref[half:] = (own_ref[half:] + w1_ref[...]).astype(BF16)
 
 
 def a_kernel(factor, vec_ref, dy_ref, b_ref, x_ref, m_ref, *refs):
@@ -204,23 +214,28 @@
         ref[...] = whole[:, at] if axis else whole[at]
 
 
-def sum_split_kernel(position, axis, parts, *refs):
-    ins, outs, whole = refs[:parts], refs[parts:-1], refs[-1]
-    whole[...] = functools.reduce(jnp.add, [ref[...] for ref in ins])
-    split(whole, outs, position(), axis)
-
-
-def sum_split(ins, position, axis, count):
-    shape = ins[0].shape
-    piece = list(shape)
-    piece[axis] //= count
+def sum_kernel(*refs):
+    refs[-1][...] = functools.reduce(jnp.add, [ref[...] for ref in refs[:-1]])
+
+
+def add(*ins, after=()):
+    return call(sum_kernel, [out(ins[0].shape)], [VMEM] * len(ins), *ins, after=after)[0]
+
+
+def halve_kernel(position, left_ref, right_ref, keep_ref, send_ref, whole):
+    whole[...] = left_ref[...] + right_ref[...]
+    split(whole, [keep_ref, send_ref], position(), 0)
+
+
+def halve(left, right, position, after=()):
+    rows, cols = left.shape
     return call(
-        functools.partial(sum_split_kernel, position, axis, len(ins)),
-        [out(tuple(piece))] * count,
-        [VMEM] * len(ins),
-        *ins,
-        scratch=[pltpu.VMEM(shape, F32)],
-        data=4 * 5 * shape[0] * shape[1],
+        functools.partial(halve_kernel, position),
+        [out((rows // 2, cols))] * 2,
+        [VMEM] * 2,
+        left, right,
+        scratch=[pltpu.VMEM((rows, cols), F32)],
+        after=after,
     )
 
 
@@ -237,7 +252,7 @@
             whole[at] = ref[...]
 
 
-def join(ins, position, axis):
+def join(ins, position, axis, after=()):
     shape = list(ins[0].shape)
     shape[axis] *= len(ins)
     return call(
@@ -245,53 +260,59 @@
         [out(tuple(shape))],
         [VMEM] * len(ins),
         *ins,
-        data=4 * 2 * shape[0] * shape[1],
+        after=after,
     )[0]
 
 
 def b_kernel(factor, vec_ref, bq_ref, am_ref, keep_ref, send_ref, whole):
     ratio = vec_ref[3:4] / vec_ref[0:1]
     whole[...] = (vec_ref[2:3] * factor) * (bq_ref[...] - ratio * am_ref[...])
-    split(whole, [keep_ref, send_ref], core_index(), 0)
-
-
-def b_dp_kernel(vec_ref, *refs):
-    ins, outs, whole = refs[:4], refs[4:-1], refs[-1]
-    rows = ins[0].shape[0]
-    whole[:rows] = functools.reduce(jnp.add, [ref[...] for ref in ins])
-    whole[rows:] = jnp.broadcast_to(vec_ref[3:4], (whole.shape[0] - rows, whole.shape[1]))
-    split(whole, outs, lax.axis_index("dp"), 1)
-
-
-def b_join_kernel(factor, vec_ref, i0_ref, i1_ref, i2_ref, i3_ref, b_out_ref, mag_ref, whole):
-    join_kernel(dp_index, 1, i0_ref, i1_ref, i2_ref, i3_ref, whole)
-    rows = b_out_ref.shape[0]
-    b_out_ref[...] = whole[:rows]
-    mag_ref[...] = factor * whole[rows:rows + 1] / vec_ref[1:2]
-
-
-def core_index():
+    split(whole, [keep_ref, send_ref], core_bit(), 0)
+
+
+def b_stack_kernel(left_ref, right_ref, vec_ref, out_ref):
+    rows = left_ref.shape[0]
+    out_ref[:rows] = left_ref[...] + right_ref[...]
+    out_ref[rows:] = jnp.broadcast_to(vec_ref[3:4], left_ref.shape)
+
+
+def b_unstack_kernel(factor, left_ref, right_ref, vec_ref, b_ref, mag_ref):
+    rows = b_ref.shape[0]
+    total = left_ref[...] + right_ref[...]
+    b_ref[...] = total[:rows]
+    mag_ref[...] = factor * total[rows:rows + 1] / vec_ref[1:2]
+
+
+def core_bit():
     return lax.rem(lax.axis_index("rows"), 2)
 
 
-def x_index():
-    return lax.div(lax.axis_index("rows"), 2)
+def near_bit():
+    return lax.rem(lax.div(lax.div(lax.axis_index("rows"), 2) + 1, 2), 2)
+
+
+def far_bit():
+    return lax.div(lax.axis_index("rows"), 4)
 
 
 def dp_index():
     return lax.axis_index("dp")
 
 
-def cols_index():
-    return lax.axis_index("cols")
-
-
 def ring(value, axis, k, count=4):
     return lax.ppermute(value, axis, [(i, (i + k) % count) for i in range(count)])
 
 
 def ring_x(value, k, count=8):
     return lax.ppermute(value, "rows", [(i, (i + 2 * k) % count) for i in range(count)])
+
+
+def swap(value, axis, step):
+    return lax.ppermute(value, axis, [(i, i ^ 1 if step == 0 else 3 - i) for i in range(4)])
+
+
+def swap_x(value, step):
+    return lax.ppermute(value, "rows", [(i, i ^ 2 if step == 0 else 6 - 2 * (i // 2) + i % 2) for i in range(8)])
 
 
 def swap_core(value, count=8):
@@ -314,10 +335,9 @@
         [out((4, cols)), out((toks, cols), BF16), out((far, toks)), out((far, toks))],
         [VMEM] * 7,
         stat, ring_x(stat, 1), ring_x(stat, 2), ring_x(stat, 3), mag, dy, m,
-        flops=2 * 2 * far * toks * cols,
     )
     u0, u1 = ring(h0, "cols", 1), ring(h1, "cols", 3)
-    up, down = call(near_kernel, [out((far, toks))] * 2, [VMEM] * 2, m, scaled, flops=2 * 2 * far * toks * cols)
+    up, down = call(near_kernel, [out((far, toks))] * 2, [VMEM] * 2, m, scaled)
     v0, v1 = ring(up, "cols", 1), ring(down, "cols", 3)
 
     pieces = call(
@@ -326,7 +346,7 @@
         [VMEM] * 5,
         vec, dy, b, x, m,
         scratch=[pltpu.VMEM((rank, rows), F32)],
-        flops=2 * 2 * rank * rows * (cols + toks),
+        after=[up],
     )
     pieces = [pieces[0]] + [ring(pieces[k], "dp", k) for k in (1, 2, 3)]
 
@@ -336,43 +356,37 @@
         [VMEM] * 3,
         vec, bq, am,
         scratch=[pltpu.VMEM((rank, cols), F32)],
-    )
-    send = swap_core(send)
-
-    up, down = call(
-        relay_kernel, [out((far, toks))] * 2, [VMEM] * 4, m, scaled, u0, u1, flops=2 * 2 * far * toks * cols
-    )
+        after=[pieces[0]],
+    )
+    keep, send = halve(keep, swap_core(send), near_bit)
+    own = call(own_kernel, [out((rows // 4, toks))], [VMEM] * 2, m, scaled, after=[send])[0]
+    up, down = call(relay_kernel, [out((far, toks))] * 2, [VMEM] * 4, m, scaled, u0, u1, after=[own])
     w0, w1 = ring(up, "cols", 1), ring(down, "cols", 3)
-    own = call(own_kernel, [out((rows // 4, toks))], [VMEM] * 2, m, scaled, flops=2 * 2 * far * toks * cols)[0]
-
-    pieces = sum_split(pieces, cols_index, 0, 4)
-    pieces = [pieces[0]] + [ring(pieces[k], "cols", k) for k in (1, 2, 3)]
-    piece = (pieces[0] + pieces[2]) + (pieces[1] + pieces[3])
-    piece = join([piece] + [ring(piece, "cols", k) for k in (1, 2, 3)], cols_index, 0)
-    a_grad = join([piece] + [ring(piece, "dp", k) for k in (1, 2, 3)], dp_index, 1)
-
-    pieces = sum_split([keep, send], x_index, 0, 4)
-    pieces = [pieces[0]] + [ring_x(pieces[k], k) for k in (1, 2, 3)]
-    pieces = call(
-        b_dp_kernel,
-        [out((rank // 4, cols // 4))] * 4,
-        [VMEM] * 5,
-        vec, *pieces,
-        scratch=[pltpu.VMEM((rank // 4, cols), F32)],
-    )
-    pieces = [pieces[0]] + [ring(pieces[k], "dp", k) for k in (1, 2, 3)]
-    piece = (pieces[0] + pieces[2]) + (pieces[1] + pieces[3])
+
+    keep, send = halve(keep, swap_x(send, 0), far_bit, after=[up])
+    stack = call(
+        b_stack_kernel, [out((rank // 4, cols))], [VMEM] * 3, keep, swap_x(send, 1), vec, after=[keep]
+    )[0]
+    own = call(direct_kernel, [out((rows // 4, toks))], [VMEM] * 3, own, v0, v1, after=[stack])[0]
+
+    piece = add(*pieces, after=[own])
+    stack = add(stack, swap(stack, "dp", 0), after=[piece])
+    piece = add(piece, swap(piece, "cols", 0), after=[stack])
     b_part, mag_grad = call(
-        functools.partial(b_join_kernel, gamma / float(full_rows) ** 0.5),
+        functools.partial(b_unstack_kernel, gamma / float(full_rows) ** 0.5),
         [out((rank // 8, cols)), out((1, cols))],
-        [VMEM] * 5,
-        vec, piece, ring(piece, "dp", 1), ring(piece, "dp", 2), ring(piece, "dp", 3),
-        scratch=[pltpu.VMEM((rank // 4, cols), F32)],
-    )
-    b_part = join([b_part] + [ring_x(b_part, k) for k in (1, 2, 3)], x_index, 0)
-    b_grad = join([b_part, swap_core(b_part)], core_index, 0)
-
-    grad = call(finish_kernel, [out((rows // 4, toks), BF16)], [VMEM] * 5, own, v0, v1, w0, w1)[0]
+        [VMEM] * 3,
+        stack, swap(stack, "dp", 1), vec,
+        after=[piece],
+    )
+    piece = add(piece, swap(piece, "cols", 1), after=[b_part])
+    grad = call(
+        finish_kernel, [out((rows // 4, toks), BF16)], [VMEM] * 3, own, w0, w1, after=[piece]
+    )[0]
+    b_part = join([b_part, swap_x(b_part, 1)], far_bit, 0)
+    b_part = join([b_part, swap_x(b_part, 0)], near_bit, 0)
+    b_grad = join([b_part, swap_core(b_part)], core_bit, 0, after=[grad])
+    a_grad = join([piece] + [ring(piece, "dp", k) for k in (1, 2, 3)], dp_index, 1, after=[b_grad])
     return grad, a_grad.T, b_grad, mag_grad.reshape(cols)
 
 

time: 120 us -> 105 us (0.88)
  starting transfers between devices: 53.4 us -> 34.9 us
  waiting for transfers between devices: 31.8 us -> 36.3 us
  local copies, waits for them, and re-layouts: 4.69 us -> 2.08 us
  Pallas kernels: 29.4 us -> 30.6 us
    ppermute x0 -> x8, waiting for transfers between devices: none -> 17.9 us  [the longest x4 9.89 us: swap(): lax.ppermute(value, axis, [(i, i ^ 1 if step == 0 else 3 - i) for i in ra...]
    ppermute x24 -> x12, starting transfers between devices: 39 us -> 21.3 us  [ring(): lax.ppermute(value, axis, [(i, (i + k) % count) for i in range(count)])]
    ppermute x9 -> x3, starting transfers between devices: 14.1 us -> 4.59 us  [ring_x(): lax.ppermute(value, 'rows', [(i, (i + 2 * k) % count) for i in range(coun...]
    ppermute x0 -> x8, starting transfers between devices: none -> 8.78 us  [the longest x4 5.15 us: swap(): lax.ppermute(value, axis, [(i, i ^ 1 if step == 0 else 3 - i) for i in ra...]
    ppermute x24 -> x12, waiting for transfers between devices: 21.3 us -> 13.2 us  [ring(): lax.ppermute(value, axis, [(i, (i + k) % count) for i in range(count)])]
    ppermute x9 -> x3, waiting for transfers between devices: 9.32 us -> 4.06 us  [ring_x(): lax.ppermute(value, 'rows', [(i, (i + 2 * k) % count) for i in range(coun...]
    unnamed x10 -> x12, local copies, waits for them, and re-layouts: 4.69 us -> 2.08 us
    pallas_call x16 -> x21, Pallas kernels: 29.4 us -> 30.6 us  [call(): pl.pallas_call(body, out_shape=outs, in_specs=list(specs) + [ANY] * len(a...]
  transfers between devices with their start and end apart: 36 -> 26, of which waited for: 14 -> 13; matrix products, arithmetic and copies ran while one was open for 0% -> 0% of each run, Pallas kernels for 9% -> 11%
where the time goes in v2:
time: 105 us
  waiting for transfers between devices  36.3 us (35%)
  starting transfers between devices  34.9 us (33%)
  Pallas kernels  30.6 us (29%)
  local copies, waits for them, and re-layouts  2.08 us (2%)
    pallas_call x21, Pallas kernels, call(): pl.pallas_call(body, out_shape=outs, in_specs=list(specs) + [ANY] * len(a...  30.6 us
    ppermute x12, starting transfers between devices, ring(): lax.ppermute(value, axis, [(i, (i + k) % count) for i in range(count)])  21.3 us
    ppermute x12, waiting for transfers between devices, ring(): lax.ppermute(value, axis, [(i, (i + k) % count) for i in range(count)])  13.2 us
    ppermute x4, waiting for transfers between devices, swap(): lax.ppermute(value, axis, [(i, i ^ 1 if step == 0 else 3 - i) for i in ra...  9.89 us
    ppermute x4, waiting for transfers between devices, swap_x(): lax.ppermute(value, 'rows', [(i, i ^ 2 if step == 0 else 6 - 2 * (i // 2)...  7.97 us
    ppermute x4, starting transfers between devices, swap(): lax.ppermute(value, axis, [(i, i ^ 1 if step == 0 else 3 - i) for i in ra...  5.15 us
    ppermute x3, starting transfers between devices, ring_x(): lax.ppermute(value, 'rows', [(i, (i + 2 * k) % count) for i in range(coun...  4.59 us
    ppermute x3, waiting for transfers between devices, ring_x(): lax.ppermute(value, 'rows', [(i, (i + 2 * k) % count) for i in range(coun...  4.06 us
  transfers between devices with their start and end apart: 26, of which 13 were waited for; matrix products, arithmetic and copies ran while one was open for 0% of the time, Pallas kernels for 11%

profile of v2, /device:TPU:0, one launch (start us, length us, event | category | flops | bytes accessed | tf_op | source)
XLA Modules:
  0.0 104.8 jit_solution(18178642994378432864)
XLA Ops:
  0.7 16.8 %shard_map.93 = (bf16[3584,2048]{1,0:T(8,128)(2,1)S(1)}, f32[2,2048]{1,0:T(2,128)S(1)}, f32[64,2048]{1,0:T(8,128)S(1)}, f32[64,2048]{1,0:T(8,128)S(1)}) custom-call(bf16[3584,2048]{1,0:T(8,128)(2,1)} %refs_0_.1, bf16[256,3584]{1,0:T(8,128)(2,1)} %refs_3_.3, bf16[64,3584]{1,0:T(8,128)(2,1)} %bitcast.6, bf16[64,2048]{1,0:T(8,128)(2,1)} %refs_2_.1, ...), custom_call_target="tpu_custom_call" | custom-call | flops 5637144576 | bytes 14680064 | tf_op jit(solution)/shard_map/pallas_call | solution.py:49
  17.6 1.2 %collective-permute-done = f32[2,2048]{1,0:T(2,128)S(1)} collective-permute-done((f32[2,2048]{1,0:T(2,128)S(1)}, f32[2,2048]{1,0:T(2,128)S(1)}, u32[]{:S(2)}, u32[]{:S(2)}) %collective-permute-start) | collective-permute-done | bytes 16416 | tf_op jit(solution)/shard_map/ppermute | solution.py:319
  18.8 2.9 %collective-permute-start.3 = (f32[2,2048]{1,0:T(2,128)S(1)}, f32[2,2048]{1,0:T(2,128)S(1)}, u32[]{:S(2)}, u32[]{:S(2)}) collective-permute-start(f32[2,2048]{1,0:T(2,128)S(1)} %add.3.refs_0_), channel_id=1, source_target_pairs={{0,24},{4,28},{8,0},{12,4},{16,8},{20,12},{24,16},{28,20},{1,25},{... | collective-permute-start | bytes 49160 | tf_op jit(solution)/shard_map/ppermute | solution.py:307
  22.5 0.9 collective-permute-start.1
  23.4 3.6 %collective-permute-done.2.refs_2_ = f32[2,2048]{1,0:T(2,128)S(1)} collective-permute-done((f32[2,2048]{1,0:T(2,128)S(1)}, f32[2,2048]{1,0:T(2,128)S(1)}, u32[]{:S(2)}, u32[]{:S(2)}) %collective-permute-start.2) | collective-permute-done | bytes 16416 | tf_op jit(solution)/shard_map/ppermute | solution.py:307
  27.4 1.2 %shard_map.94 = (f32[4,2048]{1,0:T(4,128)S(1)}, bf16[256,2048]{1,0:T(8,128)(2,1)S(1)}, f32[448,256]{1,0:T(8,128)S(1)}, f32[448,256]{1,0:T(8,128)S(1)}) custom-call(f32[2,2048]{1,0:T(2,128)S(1)} %add.3.refs_0_, f32[2,2048]{1,0:T(2,128)S(1)} %collective-permute-done.1.refs_1_, f32[2,2048]{1,0:T(2,128)S(1)} %collective-permute-done.2.refs_2_, ...), custom_call_target="tpu_custom_call" | custom-call | flops 1 | bytes 1 | tf_op jit(solution)/shard_map/pallas_call | solution.py:49
  28.6 1.6 %collective-permute-start.8 = (f32[448,256]{1,0:T(8,128)S(1)}, f32[448,256]{1,0:T(8,128)S(1)}, u32[]{:S(2)}, u32[]{:S(2)}) collective-permute-start(f32[448,256]{1,0:T(8,128)S(1)} %get-tuple-element.41), channel_id=1, source_target_pairs={{0,1},{1,2},{2,3},{3,0},{4,5},{5,6},{6,7},{7,4},{8,9},{9,10},{10,1... | collective-permute-start | bytes 1376264 | tf_op jit(solution)/shard_map/ppermute | solution.py:303
  30.3 1.7 %collective-permute-start.9 = (f32[448,256]{1,0:T(8,128)S(1)}, f32[448,256]{1,0:T(8,128)S(1)}, u32[]{:S(2)}, u32[]{:S(2)}) collective-permute-start(f32[448,256]{1,0:T(8,128)S(1)} %get-tuple-element.42), channel_id=1, source_target_pairs={{0,3},{1,0},{2,1},{3,2},{4,7},{5,4},{6,5},{7,6},{8,11},{9,8},{10,9... | collective-permute-start | bytes 1376264 | tf_op jit(solution)/shard_map/ppermute | solution.py:303
  31.9 1.1 %shard_map.95 = (f32[448,256]{1,0:T(8,128)S(1)}, f32[448,256]{1,0:T(8,128)S(1)}) custom-call(bf16[3584,2048]{1,0:T(8,128)(2,1)S(1)} %get-tuple-element.28.refs_6_.refs_0_.refs_4_, bf16[256,2048]{1,0:T(8,128)(2,1)S(1)} %get-tuple-element.30.refs_1_), custom_call_target="tpu_custom_call" | custom-call | flops 1 | bytes 1 | tf_op jit(solution)/shard_map/pallas_call | solution.py:49
  33.1 5.3 %shard_map.96 = (f32[64,896]{1,0:T(8,128)S(1)}, f32[64,896]{1,0:T(8,128)S(1)}, f32[64,896]{1,0:T(8,128)S(1)}, f32[64,896]{1,0:T(8,128)S(1)}) custom-call(f32[4,2048]{1,0:T(4,128)S(1)} %get-tuple-element.31.refs_0_.refs_2_, bf16[256,2048]{1,0:T(8,128)(2,1)S(1)} %copy-done, bf16[64,2048]{1,0:T(8,128)(2,1)S(1)} %copy-done.4, bf16[256,3584]{1,0:T(8,128)(2,1)S(1)} %copy-done.2, ...), custom_call_target="tpu_custom_call" | custom-call | flops 1 | bytes 1 | tf_op jit(solution)/shard_map/pallas_call | solution.py:49
  38.7 1.9 %collective-permute-start.6 = (f32[448,256]{1,0:T(8,128)S(1)}, f32[448,256]{1,0:T(8,128)S(1)}, u32[]{:S(2)}, u32[]{:S(2)}) collective-permute-start(f32[448,256]{1,0:T(8,128)S(1)} %get-tuple-element.39), channel_id=1, source_target_pairs={{0,3},{1,0},{2,1},{3,2},{4,7},{5,4},{6,5},{7,6},{8,11},{9,8},{10,9... | collective-permute-start | bytes 1376264 | tf_op jit(solution)/shard_map/ppermute | solution.py:303
  41.1 1.1 %shard_map.99.refs_4_.refs_0_ = f32[896,256]{1,0:T(8,128)S(1)} custom-call(bf16[3584,2048]{1,0:T(8,128)(2,1)S(1)} %get-tuple-element.28.refs_6_.refs_0_.refs_4_, bf16[256,2048]{1,0:T(8,128)(2,1)S(1)} %get-tuple-element.30.refs_1_, f32[16,2048]{1,0:T(8,128)S(1)} %get-tuple-element.38.refs_2_), custom_call_target="tpu_custom_call" | custom-call | flops 1 | bytes 1 | tf_op jit(solution)/shard_map/pallas_call | solution.py:49
  42.3 1.1 %shard_map.100 = (f32[448,256]{1,0:T(8,128)S(1)}, f32[448,256]{1,0:T(8,128)S(1)}) custom-call(bf16[3584,2048]{1,0:T(8,128)(2,1)S(1)} %get-tuple-element.28.refs_6_.refs_0_.refs_4_, bf16[256,2048]{1,0:T(8,128)(2,1)S(1)} %get-tuple-element.30.refs_1_, f32[448,256]{1,0:T(8,128)S(1)} %collective-permute-done.8.refs_2_, ...), custom_call_target="tpu_custom_call" | custom-call | flops 1 | bytes 1 | tf_op jit(solution)/shard_map/pallas_call | solution.py:49
  43.4 3.0 %collective-permute-done.7.refs_1_ = f32[16,2048]{1,0:T(8,128)S(1)} collective-permute-done((f32[16,2048]{1,0:T(8,128)S(1)}, f32[16,2048]{1,0:T(8,128)S(1)}, u32[]{:S(2)}, u32[]{:S(2)}) %collective-permute-start.7) | collective-permute-done | bytes 131104 | tf_op jit(solution)/shard_map/ppermute | solution.py:315
  46.9 1.9 %collective-permute-start.13 = (f32[64,896]{1,0:T(8,128)S(1)}, f32[64,896]{1,0:T(8,128)S(1)}, u32[]{:S(2)}, u32[]{:S(2)}) collective-permute-start(f32[64,896]{1,0:T(8,128)S(1)} %get-tuple-element.47), channel_id=1, source_target_pairs={{0,32},{32,64},{64,96},{96,0},{1,33},{33,65},{65,97},{97,1},{2,34}... | collective-permute-start | bytes 688136 | tf_op jit(solution)/shard_map/ppermute | solution.py:303
  48.8 3.6 %collective-permute-start.14 = (f32[64,896]{1,0:T(8,128)S(1)}, f32[64,896]{1,0:T(8,128)S(1)}, u32[]{:S(2)}, u32[]{:S(2)}) collective-permute-start(f32[64,896]{1,0:T(8,128)S(1)} %get-tuple-element.48), channel_id=1, source_target_pairs={{0,64},{32,96},{64,0},{96,32},{1,65},{33,97},{65,1},{97,33},{2,66}... | collective-permute-start | bytes 688136 | tf_op jit(solution)/shard_map/ppermute | solution.py:303
  52.4 3.7 %collective-permute-start.15 = (f32[64,896]{1,0:T(8,128)S(1)}, f32[64,896]{1,0:T(8,128)S(1)}, u32[]{:S(2)}, u32[]{:S(2)}) collective-permute-start(f32[64,896]{1,0:T(8,128)S(1)} %get-tuple-element.49), channel_id=1, source_target_pairs={{0,96},{32,0},{64,32},{96,64},{1,97},{33,1},{65,33},{97,65},{2,98}... | collective-permute-start | bytes 688136 | tf_op jit(solution)/shard_map/ppermute | solution.py:303
  56.6 6.5 %collective-permute-done.14.refs_2_ = f32[64,896]{1,0:T(8,128)S(1)} collective-permute-done((f32[64,896]{1,0:T(8,128)S(1)}, f32[64,896]{1,0:T(8,128)S(1)}, u32[]{:S(2)}, u32[]{:S(2)}) %collective-permute-start.14) | collective-permute-done | bytes 229408 | tf_op jit(solution)/shard_map/ppermute | solution.py:303
  63.4 2.8 %collective-permute-start.12 = (f32[448,256]{1,0:T(8,128)S(1)}, f32[448,256]{1,0:T(8,128)S(1)}, u32[]{:S(2)}, u32[]{:S(2)}) collective-permute-start(f32[448,256]{1,0:T(8,128)S(1)} %get-tuple-element.46), channel_id=1, source_target_pairs={{0,3},{1,0},{2,1},{3,2},{4,7},{5,4},{6,5},{7,6},{8,11},{9,8},{10,9... | collective-permute-start | bytes 1376264 | tf_op jit(solution)/shard_map/ppermute | solution.py:303
  66.2 1.5 %collective-permute-start.19 = (f32[16,2048]{1,0:T(8,128)S(1)}, f32[16,2048]{1,0:T(8,128)S(1)}, u32[]{:S(2)}, u32[]{:S(2)}) collective-permute-start(f32[16,2048]{1,0:T(8,128)S(1)} %shard_map.105.refs_2_.refs_0_), channel_id=1, source_target_pairs={{0,96},{32,64},{64,32},{96,0},{1,97},{33,65},{65,33},{97,1},{2,98}... | collective-permute-start | bytes 393224 | tf_op jit(solution)/shard_map/ppermute | solution.py:311
  67.7 4.0 %collective-permute-done.16.refs_1_ = f32[64,896]{1,0:T(8,128)S(1)} collective-permute-done((f32[64,896]{1,0:T(8,128)S(1)}, f32[64,896]{1,0:T(8,128)S(1)}, u32[]{:S(2)}, u32[]{:S(2)}) %collective-permute-start.16) | collective-permute-done | bytes 229408 | tf_op jit(solution)/shard_map/ppermute | solution.py:311
  73.0 2.9 %collective-permute-start.23 = (f32[8,2048]{1,0:T(8,128)S(1)}, f32[8,2048]{1,0:T(8,128)S(1)}, u32[]{:S(2)}, u32[]{:S(2)}) collective-permute-start(f32[8,2048]{1,0:T(8,128)S(1)} %get-tuple-element.50.refs_2_.refs_0_), channel_id=1, source_target_pairs={{0,24},{4,28},{8,16},{12,20},{16,8},{20,12},{24,0},{28,4},{1,25},{... | collective-permute-start | bytes 196616 | tf_op jit(solution)/shard_map/ppermute | solution.py:315
  75.9 3.2 %collective-permute-start.18 = (f32[64,896]{1,0:T(8,128)S(1)}, f32[64,896]{1,0:T(8,128)S(1)}, u32[]{:S(2)}, u32[]{:S(2)}) collective-permute-start(f32[64,896]{1,0:T(8,128)S(1)} %shard_map.106.refs_3_.refs_0_), channel_id=1, source_target_pairs={{0,3},{1,2},{2,1},{3,0},{4,7},{5,6},{6,5},{7,4},{8,11},{9,10},{10,... | collective-permute-start | bytes 688136 | tf_op jit(solution)/shard_map/ppermute | solution.py:311
  79.3 5.0 %collective-permute-done.24.refs_1_ = f32[16,2048]{1,0:T(8,128)S(1)} collective-permute-done((f32[16,2048]{1,0:T(8,128)S(1)}, f32[16,2048]{1,0:T(8,128)S(1)}, u32[]{:S(2)}, u32[]{:S(2)}) %collective-permute-start.24) | collective-permute-done | bytes 131104 | tf_op jit(solution)/shard_map/ppermute | solution.py:315
  84.4 5.2 %collective-permute-done.18.refs_1_ = f32[64,896]{1,0:T(8,128)S(1)} collective-permute-done((f32[64,896]{1,0:T(8,128)S(1)}, f32[64,896]{1,0:T(8,128)S(1)}, u32[]{:S(2)}, u32[]{:S(2)}) %collective-permute-start.18) | collective-permute-done | bytes 229408 | tf_op jit(solution)/shard_map/ppermute | solution.py:311
  89.6 3.0 %collective-permute-start.22 = (f32[64,896]{1,0:T(8,128)S(1)}, f32[64,896]{1,0:T(8,128)S(1)}, u32[]{:S(2)}, u32[]{:S(2)}) collective-permute-start(f32[64,896]{1,0:T(8,128)S(1)} %shard_map.108.refs_3_.refs_0_), channel_id=1, source_target_pairs={{0,96},{32,0},{64,32},{96,64},{1,97},{33,1},{65,33},{97,65},{2,98}... | collective-permute-start | bytes 688136 | tf_op jit(solution)/shard_map/ppermute | solution.py:303
  94.4 1.0 copy-done.3
  96.3 2.7 %collective-permute-done.22.refs_3_ = f32[64,896]{1,0:T(8,128)S(1)} collective-permute-done((f32[64,896]{1,0:T(8,128)S(1)}, f32[64,896]{1,0:T(8,128)S(1)}, u32[]{:S(2)}, u32[]{:S(2)}) %collective-permute-start.22) | collective-permute-done | bytes 229408 | tf_op jit(solution)/shard_map/ppermute | solution.py:303
  99.0 1.4 %collective-permute-done.21.refs_2_ = f32[64,896]{1,0:T(8,128)S(1)} collective-permute-done((f32[64,896]{1,0:T(8,128)S(1)}, f32[64,896]{1,0:T(8,128)S(1)}, u32[]{:S(2)}, u32[]{:S(2)}) %collective-permute-start.21) | collective-permute-done | bytes 229408 | tf_op jit(solution)/shard_map/ppermute | solution.py:303
  100.4 2.4 %collective-permute-done.20.refs_1_ = f32[64,896]{1,0:T(8,128)S(1)} collective-permute-done((f32[64,896]{1,0:T(8,128)S(1)}, f32[64,896]{1,0:T(8,128)S(1)}, u32[]{:S(2)}, u32[]{:S(2)}) %collective-permute-start.20) | collective-permute-done | bytes 229408 | tf_op jit(solution)/shard_map/ppermute | solution.py:303
  102.7 1.0 copy-done.1
  103.8 1.0 shard_map.113
  (54 shorter events, 7.7 us)
Async XLA Ops:
  0.6 26.8 %copy-start = (bf16[256,2048]{1,0:T(8,128)(2,1)S(1)}, bf16[256,2048]{1,0:T(8,128)(2,1)}, u32[]{:S(2)}) copy-start(bf16[256,2048]{1,0:T(8,128)(2,1)} %refs_1_.3) | copy-start | bytes 3145732
  0.6 26.8 %copy-start.5 = (f32[2048]{0:T(1024)S(1)}, f32[2048]{0:T(1024)}, u32[]{:S(2)}) copy-start(f32[2048]{0:T(1024)} %param.11) | copy-start | bytes 24580
  17.5 1.3 %collective-permute-start = (f32[2,2048]{1,0:T(2,128)S(1)}, f32[2,2048]{1,0:T(2,128)S(1)}, u32[]{:S(2)}, u32[]{:S(2)}) collective-permute-start(f32[2,2048]{1,0:T(2,128)S(1)} %get-tuple-element.29), channel_id=1, source_target_pairs={{0,4},{4,0},{8,12},{12,8},{16,20},{20,16},{24,28},{28,24},{1,5},{5... | collective-permute-start | bytes 49160 | tf_op jit(solution)/shard_map/ppermute | solution.py:319
  18.8 4.6 %collective-permute-start.3 = (f32[2,2048]{1,0:T(2,128)S(1)}, f32[2,2048]{1,0:T(2,128)S(1)}, u32[]{:S(2)}, u32[]{:S(2)}) collective-permute-start(f32[2,2048]{1,0:T(2,128)S(1)} %add.3.refs_0_), channel_id=1, source_target_pairs={{0,24},{4,28},{8,0},{12,4},{16,8},{20,12},{24,16},{28,20},{1,25},{... | collective-permute-start | bytes 49160 | tf_op jit(solution)/shard_map/ppermute | solution.py:307
  21.7 5.2 %collective-permute-start.2 = (f32[2,2048]{1,0:T(2,128)S(1)}, f32[2,2048]{1,0:T(2,128)S(1)}, u32[]{:S(2)}, u32[]{:S(2)}) collective-permute-start(f32[2,2048]{1,0:T(2,128)S(1)} %add.3.refs_0_), channel_id=1, source_target_pairs={{0,16},{4,20},{8,24},{12,28},{16,0},{20,4},{24,8},{28,12},{1,17},{... | collective-permute-start | bytes 49160 | tf_op jit(solution)/shard_map/ppermute | solution.py:307
  22.5 4.9 %collective-permute-start.1 = (f32[2,2048]{1,0:T(2,128)S(1)}, f32[2,2048]{1,0:T(2,128)S(1)}, u32[]{:S(2)}, u32[]{:S(2)}) collective-permute-start(f32[2,2048]{1,0:T(2,128)S(1)} %add.3.refs_0_), channel_id=1, source_target_pairs={{0,8},{4,12},{8,16},{12,20},{16,24},{20,28},{24,0},{28,4},{1,9},{5... | collective-permute-start | bytes 49160 | tf_op jit(solution)/shard_map/ppermute | solution.py:307
  27.4 5.6 %copy-start.2 = (bf16[256,3584]{1,0:T(8,128)(2,1)S(1)}, bf16[256,3584]{1,0:T(8,128)(2,1)}, u32[]{:S(2)}) copy-start(bf16[256,3584]{1,0:T(8,128)(2,1)} %refs_3_.3) | copy-start | bytes 5505028
  27.4 5.6 %copy-start.4 = (bf16[64,2048]{1,0:T(8,128)(2,1)S(1)}, bf16[64,2048]{1,0:T(8,128)(2,1)}, u32[]{:S(2)}) copy-start(bf16[64,2048]{1,0:T(8,128)(2,1)} %refs_2_.1) | copy-start | bytes 786436
  28.6 13.6 %collective-permute-start.8 = (f32[448,256]{1,0:T(8,128)S(1)}, f32[448,256]{1,0:T(8,128)S(1)}, u32[]{:S(2)}, u32[]{:S(2)}) collective-permute-start(f32[448,256]{1,0:T(8,128)S(1)} %get-tuple-element.41), channel_id=1, source_target_pairs={{0,1},{1,2},{2,3},{3,0},{4,5},{5,6},{6,7},{7,4},{8,9},{9,10},{10,1... | collective-permute-start | bytes 1376264 | tf_op jit(solution)/shard_map/ppermute | solution.py:303
  30.3 12.0 %collective-permute-start.9 = (f32[448,256]{1,0:T(8,128)S(1)}, f32[448,256]{1,0:T(8,128)S(1)}, u32[]{:S(2)}, u32[]{:S(2)}) collective-permute-start(f32[448,256]{1,0:T(8,128)S(1)} %get-tuple-element.42), channel_id=1, source_target_pairs={{0,3},{1,0},{2,1},{3,2},{4,7},{5,4},{6,5},{7,6},{8,11},{9,8},{10,9... | collective-permute-start | bytes 1376264 | tf_op jit(solution)/shard_map/ppermute | solution.py:303
  38.6 2.2 %collective-permute-start.4 = (f32[32,2048]{1,0:T(8,128)S(1)}, f32[32,2048]{1,0:T(8,128)S(1)}, u32[]{:S(2)}, u32[]{:S(2)}) collective-permute-start(f32[32,2048]{1,0:T(8,128)S(1)} %get-tuple-element.37), channel_id=1, source_target_pairs={{0,4},{4,0},{8,12},{12,8},{16,20},{20,16},{24,28},{28,24},{1,5},{5... | collective-permute-start | bytes 786440 | tf_op jit(solution)/shard_map/ppermute | solution.py:319
  38.7 17.4 %collective-permute-start.6 = (f32[448,256]{1,0:T(8,128)S(1)}, f32[448,256]{1,0:T(8,128)S(1)}, u32[]{:S(2)}, u32[]{:S(2)}) collective-permute-start(f32[448,256]{1,0:T(8,128)S(1)} %get-tuple-element.39), channel_id=1, source_target_pairs={{0,3},{1,0},{2,1},{3,2},{4,7},{5,4},{6,5},{7,6},{8,11},{9,8},{10,9... | collective-permute-start | bytes 1376264 | tf_op jit(solution)/shard_map/ppermute | solution.py:303
  40.6 15.6 %collective-permute-start.5 = (f32[448,256]{1,0:T(8,128)S(1)}, f32[448,256]{1,0:T(8,128)S(1)}, u32[]{:S(2)}, u32[]{:S(2)}) collective-permute-start(f32[448,256]{1,0:T(8,128)S(1)} %get-tuple-element.34.refs_5_), channel_id=1, source_target_pairs={{0,1},{1,2},{2,3},{3,0},{4,5},{5,6},{6,7},{7,4},{8,9},{9,10},{10,1... | collective-permute-start | bytes 1376264 | tf_op jit(solution)/shard_map/ppermute | solution.py:303
  40.8 5.6 %collective-permute-start.7 = (f32[16,2048]{1,0:T(8,128)S(1)}, f32[16,2048]{1,0:T(8,128)S(1)}, u32[]{:S(2)}, u32[]{:S(2)}) collective-permute-start(f32[16,2048]{1,0:T(8,128)S(1)} %get-tuple-element.38.refs_2_), channel_id=1, source_target_pairs={{0,8},{4,12},{8,0},{12,4},{16,24},{20,28},{24,16},{28,20},{1,9},{5... | collective-permute-start | bytes 393224 | tf_op jit(solution)/shard_map/ppermute | solution.py:315
  46.5 5.9 %collective-permute-start.10 = (f32[8,2048]{1,0:T(8,128)S(1)}, f32[8,2048]{1,0:T(8,128)S(1)}, u32[]{:S(2)}, u32[]{:S(2)}) collective-permute-start(f32[8,2048]{1,0:T(8,128)S(1)} %get-tuple-element.45), channel_id=1, source_target_pairs={{0,24},{4,28},{8,16},{12,20},{16,8},{20,12},{24,0},{28,4},{1,25},{... | collective-permute-start | bytes 196616 | tf_op jit(solution)/shard_map/ppermute | solution.py:315
  46.9 9.7 %collective-permute-start.13 = (f32[64,896]{1,0:T(8,128)S(1)}, f32[64,896]{1,0:T(8,128)S(1)}, u32[]{:S(2)}, u32[]{:S(2)}) collective-permute-start(f32[64,896]{1,0:T(8,128)S(1)} %get-tuple-element.47), channel_id=1, source_target_pairs={{0,32},{32,64},{64,96},{96,0},{1,33},{33,65},{65,97},{97,1},{2,34}... | collective-permute-start | bytes 688136 | tf_op jit(solution)/shard_map/ppermute | solution.py:303
  48.8 14.2 %collective-permute-start.14 = (f32[64,896]{1,0:T(8,128)S(1)}, f32[64,896]{1,0:T(8,128)S(1)}, u32[]{:S(2)}, u32[]{:S(2)}) collective-permute-start(f32[64,896]{1,0:T(8,128)S(1)} %get-tuple-element.48), channel_id=1, source_target_pairs={{0,64},{32,96},{64,0},{96,32},{1,65},{33,97},{65,1},{97,33},{2,66}... | collective-permute-start | bytes 688136 | tf_op jit(solution)/shard_map/ppermute | solution.py:303
  52.4 10.6 %collective-permute-start.15 = (f32[64,896]{1,0:T(8,128)S(1)}, f32[64,896]{1,0:T(8,128)S(1)}, u32[]{:S(2)}, u32[]{:S(2)}) collective-permute-start(f32[64,896]{1,0:T(8,128)S(1)} %get-tuple-element.49), channel_id=1, source_target_pairs={{0,96},{32,0},{64,32},{96,64},{1,97},{33,1},{65,33},{97,65},{2,98}... | collective-permute-start | bytes 688136 | tf_op jit(solution)/shard_map/ppermute | solution.py:303
  56.1 10.0 %collective-permute-start.17 = (f32[16,2048]{1,0:T(8,128)S(1)}, f32[16,2048]{1,0:T(8,128)S(1)}, u32[]{:S(2)}, u32[]{:S(2)}) collective-permute-start(f32[16,2048]{1,0:T(8,128)S(1)} %shard_map.102.refs_3_.refs_0_), channel_id=1, source_target_pairs={{0,32},{32,0},{64,96},{96,64},{1,33},{33,1},{65,97},{97,65},{2,34}... | collective-permute-start | bytes 393224 | tf_op jit(solution)/shard_map/ppermute | solution.py:311
  63.1 8.6 %collective-permute-start.16 = (f32[64,896]{1,0:T(8,128)S(1)}, f32[64,896]{1,0:T(8,128)S(1)}, u32[]{:S(2)}, u32[]{:S(2)}) collective-permute-start(f32[64,896]{1,0:T(8,128)S(1)} %shard_map.104.refs_2_.refs_0_), channel_id=1, source_target_pairs={{0,1},{1,0},{2,3},{3,2},{4,5},{5,4},{6,7},{7,6},{8,9},{9,8},{10,11... | collective-permute-start | bytes 688136 | tf_op jit(solution)/shard_map/ppermute | solution.py:311
  63.4 29.9 %collective-permute-start.12 = (f32[448,256]{1,0:T(8,128)S(1)}, f32[448,256]{1,0:T(8,128)S(1)}, u32[]{:S(2)}, u32[]{:S(2)}) collective-permute-start(f32[448,256]{1,0:T(8,128)S(1)} %get-tuple-element.46), channel_id=1, source_target_pairs={{0,3},{1,0},{2,1},{3,2},{4,7},{5,4},{6,5},{7,6},{8,11},{9,8},{10,9... | collective-permute-start | bytes 1376264 | tf_op jit(solution)/shard_map/ppermute | solution.py:303
  66.2 6.3 %collective-permute-start.19 = (f32[16,2048]{1,0:T(8,128)S(1)}, f32[16,2048]{1,0:T(8,128)S(1)}, u32[]{:S(2)}, u32[]{:S(2)}) collective-permute-start(f32[16,2048]{1,0:T(8,128)S(1)} %shard_map.105.refs_2_.refs_0_), channel_id=1, source_target_pairs={{0,96},{32,64},{64,32},{96,0},{1,97},{33,65},{65,33},{97,1},{2,98}... | collective-permute-start | bytes 393224 | tf_op jit(solution)/shard_map/ppermute | solution.py:311
  73.0 6.1 %collective-permute-start.23 = (f32[8,2048]{1,0:T(8,128)S(1)}, f32[8,2048]{1,0:T(8,128)S(1)}, u32[]{:S(2)}, u32[]{:S(2)}) collective-permute-start(f32[8,2048]{1,0:T(8,128)S(1)} %get-tuple-element.50.refs_2_.refs_0_), channel_id=1, source_target_pairs={{0,24},{4,28},{8,16},{12,20},{16,8},{20,12},{24,0},{28,4},{1,25},{... | collective-permute-start | bytes 196616 | tf_op jit(solution)/shard_map/ppermute | solution.py:315
  75.9 17.6 %collective-permute-start.11 = (f32[448,256]{1,0:T(8,128)S(1)}, f32[448,256]{1,0:T(8,128)S(1)}, u32[]{:S(2)}, u32[]{:S(2)}) collective-permute-start(f32[448,256]{1,0:T(8,128)S(1)} %get-tuple-element.43.refs_2_), channel_id=1, source_target_pairs={{0,1},{1,2},{2,3},{3,0},{4,5},{5,6},{6,7},{7,4},{8,9},{9,10},{10,1... | collective-permute-start | bytes 1376264 | tf_op jit(solution)/shard_map/ppermute | solution.py:303
  75.9 13.6 %collective-permute-start.18 = (f32[64,896]{1,0:T(8,128)S(1)}, f32[64,896]{1,0:T(8,128)S(1)}, u32[]{:S(2)}, u32[]{:S(2)}) collective-permute-start(f32[64,896]{1,0:T(8,128)S(1)} %shard_map.106.refs_3_.refs_0_), channel_id=1, source_target_pairs={{0,3},{1,2},{2,1},{3,0},{4,7},{5,6},{6,5},{7,4},{8,11},{9,10},{10,... | collective-permute-start | bytes 688136 | tf_op jit(solution)/shard_map/ppermute | solution.py:311
  79.2 5.0 %collective-permute-start.24 = (f32[16,2048]{1,0:T(8,128)S(1)}, f32[16,2048]{1,0:T(8,128)S(1)}, u32[]{:S(2)}, u32[]{:S(2)}) collective-permute-start(f32[16,2048]{1,0:T(8,128)S(1)} %shard_map.110.refs_0_), channel_id=1, source_target_pairs={{0,8},{4,12},{8,0},{12,4},{16,24},{20,28},{24,16},{28,20},{1,9},{5... | collective-permute-start | bytes 393224 | tf_op jit(solution)/shard_map/ppermute | solution.py:315
  84.3 10.1 %collective-permute-start.25 = (f32[32,2048]{1,0:T(8,128)S(1)}, f32[32,2048]{1,0:T(8,128)S(1)}, u32[]{:S(2)}, u32[]{:S(2)}) collective-permute-start(f32[32,2048]{1,0:T(8,128)S(1)} %shard_map.111.refs_0_), channel_id=1, source_target_pairs={{0,4},{4,0},{8,12},{12,8},{16,20},{20,16},{24,28},{28,24},{1,5},{5... | collective-permute-start | bytes 786440 | tf_op jit(solution)/shard_map/ppermute | solution.py:319
  89.6 9.4 %collective-permute-start.22 = (f32[64,896]{1,0:T(8,128)S(1)}, f32[64,896]{1,0:T(8,128)S(1)}, u32[]{:S(2)}, u32[]{:S(2)}) collective-permute-start(f32[64,896]{1,0:T(8,128)S(1)} %shard_map.108.refs_3_.refs_0_), channel_id=1, source_target_pairs={{0,96},{32,0},{64,32},{96,64},{1,97},{33,1},{65,33},{97,65},{2,98}... | collective-permute-start | bytes 688136 | tf_op jit(solution)/shard_map/ppermute | solution.py:303
  92.6 7.8 %collective-permute-start.21 = (f32[64,896]{1,0:T(8,128)S(1)}, f32[64,896]{1,0:T(8,128)S(1)}, u32[]{:S(2)}, u32[]{:S(2)}) collective-permute-start(f32[64,896]{1,0:T(8,128)S(1)} %shard_map.108.refs_3_.refs_0_), channel_id=1, source_target_pairs={{0,64},{32,96},{64,0},{96,32},{1,65},{33,97},{65,1},{97,33},{2,66}... | collective-permute-start | bytes 688136 | tf_op jit(solution)/shard_map/ppermute | solution.py:303
  93.3 9.5 %collective-permute-start.20 = (f32[64,896]{1,0:T(8,128)S(1)}, f32[64,896]{1,0:T(8,128)S(1)}, u32[]{:S(2)}, u32[]{:S(2)}) collective-permute-start(f32[64,896]{1,0:T(8,128)S(1)} %shard_map.108.refs_3_.refs_0_), channel_id=1, source_target_pairs={{0,32},{32,64},{64,96},{96,0},{1,33},{33,65},{65,97},{97,1},{2,34}... | collective-permute-start | bytes 688136 | tf_op jit(solution)/shard_map/ppermute | solution.py:303
  94.4 1.0 copy-start.3
  102.7 1.0 copy-start.1

commit v3 on v2

--- a/solution.py
+++ b/solution.py
@@ -165,30 +165,25 @@
 
 def near_kernel(m_ref, scaled_ref, up_ref, down_ref):
     y = lax.axis_index("cols")
-    up_ref[...] = nt(block(m_ref, y + 1, 1), scaled_ref[...])
-    down_ref[...] = nt(block(m_ref, y - 1, 0), scaled_ref[...])
-
-
-def relay_kernel(m_ref, scaled_ref, u0_ref, u1_ref, up_ref, down_ref):
-    y = lax.axis_index("cols")
-    up_ref[...] = u0_ref[...] + nt(block(m_ref, y + 1, 0), scaled_ref[...])
-    down_ref[...] = u1_ref[...] + nt(block(m_ref, y - 1, 1), scaled_ref[...])
+    up_ref[...] = nt(block(m_ref, y + 1), scaled_ref[...])
+    down_ref[...] = nt(block(m_ref, y - 1), scaled_ref[...])
+
+
+def relay_kernel(near_up_ref, near_down_ref, u0_ref, u1_ref, up_ref, down_ref):
+    half = u0_ref.shape[0]
+    up_ref[:half] = near_up_ref[:half] + u0_ref[...]
+    up_ref[half:] = near_up_ref[half:]
+    down_ref[:half] = near_down_ref[:half]
+    down_ref[half:] = near_down_ref[half:] + u1_ref[...]
 
 
 def own_kernel(m_ref, scaled_ref, own_ref):
     own_ref[...] = nt(block(m_ref, lax.axis_index("cols")), scaled_ref[...])
 
 
-def direct_kernel(own_ref, v0_ref, v1_ref, sum_ref):
-    half = own_ref.shape[0] // 2
-    sum_ref[:half] = own_ref[:half] + v1_ref[...]
-    sum_ref[half:] = own_ref[half:] + v0_ref[...]
-
-
-def finish_kernel(own_ref, w0_ref, w1_ref, out_ref):
-    half = own_ref.shape[0] // 2
-    out_ref[:half] = (own_ref[:half] + w0_ref[...]).astype(BF16)
-    out_ref[half:] = (own_ref[half:] + w1_ref[...]).astype(BF16)
+def finish_kernel(own_ref, up_ref, down_ref, out_ref, done_ref):
+    out_ref[...] = (own_ref[...] + (up_ref[...] + down_ref[...])).astype(BF16)
+    done_ref[...] = jnp.zeros_like(done_ref)
 
 
 def a_kernel(factor, vec_ref, dy_ref, b_ref, x_ref, m_ref, *refs):
@@ -337,56 +332,53 @@
         stat, ring_x(stat, 1), ring_x(stat, 2), ring_x(stat, 3), mag, dy, m,
     )
     u0, u1 = ring(h0, "cols", 1), ring(h1, "cols", 3)
-    up, down = call(near_kernel, [out((far, toks))] * 2, [VMEM] * 2, m, scaled)
-    v0, v1 = ring(up, "cols", 1), ring(down, "cols", 3)
-
+    keep, send = call(
+        functools.partial(b_kernel, 2.0 * gamma),
+        [out((rank // 2, cols))] * 2,
+        [VMEM] * 3,
+        vec, bq, am,
+        scratch=[pltpu.VMEM((rank, cols), F32)],
+    )
     pieces = call(
         functools.partial(a_kernel, 2.0 * gamma),
         [out((rank, rows // 4))] * 4,
         [VMEM] * 5,
         vec, dy, b, x, m,
         scratch=[pltpu.VMEM((rank, rows), F32)],
-        after=[up],
-    )
-    pieces = [pieces[0]] + [ring(pieces[k], "dp", k) for k in (1, 2, 3)]
-
-    keep, send = call(
-        functools.partial(b_kernel, 2.0 * gamma),
-        [out((rank // 2, cols))] * 2,
-        [VMEM] * 3,
-        vec, bq, am,
-        scratch=[pltpu.VMEM((rank, cols), F32)],
-        after=[pieces[0]],
-    )
-    keep, send = halve(keep, swap_core(send), near_bit)
-    own = call(own_kernel, [out((rows // 4, toks))], [VMEM] * 2, m, scaled, after=[send])[0]
-    up, down = call(relay_kernel, [out((far, toks))] * 2, [VMEM] * 4, m, scaled, u0, u1, after=[own])
+        after=[send],
+    )
+    keep, send = halve(keep, swap_core(send), near_bit, after=[pieces[0]])
+    pieces = [pieces[0]] + [ring(pieces[k], "dp", k) for k in (2, 1, 3)]
+    up, down = call(near_kernel, [out((rows // 4, toks))] * 2, [VMEM] * 2, m, scaled, after=[send])
+    own = call(own_kernel, [out((rows // 4, toks))], [VMEM] * 2, m, scaled, after=[up])[0]
+
+    piece = add(*pieces, after=[own])
+    up, down = call(
+        relay_kernel, [out((rows // 4, toks))] * 2, [VMEM] * 4, up, down, u0, u1, after=[piece]
+    )
     w0, w1 = ring(up, "cols", 1), ring(down, "cols", 3)
-
     keep, send = halve(keep, swap_x(send, 0), far_bit, after=[up])
-    stack = call(
-        b_stack_kernel, [out((rank // 4, cols))], [VMEM] * 3, keep, swap_x(send, 1), vec, after=[keep]
-    )[0]
-    own = call(direct_kernel, [out((rows // 4, toks))], [VMEM] * 3, own, v0, v1, after=[stack])[0]
-
-    piece = add(*pieces, after=[own])
+    stack = call(b_stack_kernel, [out((rank // 4, cols))], [VMEM] * 3, keep, swap_x(send, 1), vec)[0]
+    piece = add(piece, swap(piece, "cols", 0), after=[stack])
     stack = add(stack, swap(stack, "dp", 0), after=[piece])
-    piece = add(piece, swap(piece, "cols", 0), after=[stack])
     b_part, mag_grad = call(
         functools.partial(b_unstack_kernel, gamma / float(full_rows) ** 0.5),
         [out((rank // 8, cols)), out((1, cols))],
         [VMEM] * 3,
         stack, swap(stack, "dp", 1), vec,
-        after=[piece],
-    )
-    piece = add(piece, swap(piece, "cols", 1), after=[b_part])
-    grad = call(
-        finish_kernel, [out((rows // 4, toks), BF16)], [VMEM] * 3, own, w0, w1, after=[piece]
-    )[0]
-    b_part = join([b_part, swap_x(b_part, 1)], far_bit, 0)
+    )
+    grad, done = call(
+        finish_kernel,
+        [out((rows // 4, toks), BF16), out((8, 128))],
+        [VMEM] * 3,
+        own, w0, w1,
+        after=[b_part],
+    )
+    piece = add(piece, swap(piece, "cols", 1), after=[done])
+    b_part = join([b_part, swap_x(b_part, 1)], far_bit, 0, after=[piece])
     b_part = join([b_part, swap_x(b_part, 0)], near_bit, 0)
-    b_grad = join([b_part, swap_core(b_part)], core_bit, 0, after=[grad])
-    a_grad = join([piece] + [ring(piece, "dp", k) for k in (1, 2, 3)], dp_index, 1, after=[b_grad])
+    b_grad = join([b_part, swap_core(b_part)], core_bit, 0)
+    a_grad = join([piece] + [ring(piece, "dp", k) for k in (1, 2, 3)], dp_index, 1, after=[b_part])
     return grad, a_grad.T, b_grad, mag_grad.reshape(cols)
 
 

time: 105 us -> 119 us (1.13)
  waiting for transfers between devices: 36.3 us -> 57.4 us
  starting transfers between devices: 34.9 us -> 29.7 us
  local copies, waits for them, and re-layouts: 2.08 us -> 0.02 us
    ppermute x4, waiting for transfers between devices: 7.97 us -> 18.9 us  [swap_x(): lax.ppermute(value, 'rows', [(i, i ^ 2 if step == 0 else 6 - 2 * (i // 2)...]
    ppermute x4, waiting for transfers between devices: 9.89 us -> 15.7 us  [swap(): lax.ppermute(value, axis, [(i, i ^ 1 if step == 0 else 3 - i) for i in ra...]
    ppermute x12 -> x10, waiting for transfers between devices: 13.2 us -> 17.7 us  [ring(): lax.ppermute(value, axis, [(i, (i + k) % count) for i in range(count)])]
    ppermute x12 -> x10, starting transfers between devices: 21.3 us -> 16.8 us  [ring(): lax.ppermute(value, axis, [(i, (i + k) % count) for i in range(count)])]
    ppermute x4, starting transfers between devices: 3.63 us -> 0.82 us  [swap_x(): lax.ppermute(value, 'rows', [(i, i ^ 2 if step == 0 else 6 - 2 * (i // 2)...]
    ppermute x4, starting transfers between devices: 5.15 us -> 7.22 us  [swap(): lax.ppermute(value, axis, [(i, i ^ 1 if step == 0 else 3 - i) for i in ra...]
    unnamed x12 -> x8, local copies, waits for them, and re-layouts: 2.08 us -> 0.02 us
    pallas_call x21 -> x20, Pallas kernels: 30.6 us -> 30.7 us  [call(): pl.pallas_call(body, out_shape=outs, in_specs=list(specs) + [ANY] * len(a...]
  transfers between devices with their start and end apart: 26 -> 24, of which waited for: 13 -> 13; matrix products, arithmetic and copies ran while one was open for 0% -> 0% of each run, Pallas kernels for 11% -> 10%
where the time goes in v3:
time: 119 us
  waiting for transfers between devices  57.4 us (48%)
  Pallas kernels  30.7 us (26%)
  starting transfers between devices  29.7 us (25%)
    pallas_call x20, Pallas kernels, call(): pl.pallas_call(body, out_shape=outs, in_specs=list(specs) + [ANY] * len(a...  30.7 us
    ppermute x4, waiting for transfers between devices, swap_x(): lax.ppermute(value, 'rows', [(i, i ^ 2 if step == 0 else 6 - 2 * (i // 2)...  18.9 us
    ppermute x10, waiting for transfers between devices, ring(): lax.ppermute(value, axis, [(i, (i + k) % count) for i in range(count)])  17.7 us
    ppermute x10, starting transfers between devices, ring(): lax.ppermute(value, axis, [(i, (i + k) % count) for i in range(count)])  16.8 us
    ppermute x4, waiting for transfers between devices, swap(): lax.ppermute(value, axis, [(i, i ^ 1 if step == 0 else 3 - i) for i in ra...  15.7 us
    ppermute x4, starting transfers between devices, swap(): lax.ppermute(value, axis, [(i, i ^ 1 if step == 0 else 3 - i) for i in ra...  7.22 us
    ppermute x3, starting transfers between devices, ring_x(): lax.ppermute(value, 'rows', [(i, (i + 2 * k) % count) for i in range(coun...  4.59 us
    ppermute x3, waiting for transfers between devices, ring_x(): lax.ppermute(value, 'rows', [(i, (i + 2 * k) % count) for i in range(coun...  4.06 us
  transfers between devices with their start and end apart: 24, of which 13 were waited for; matrix products, arithmetic and copies ran while one was open for 0% of the time, Pallas kernels for 10%

profile of v3, /device:TPU:0, one launch (start us, length us, event | category | flops | bytes accessed | tf_op | source)
XLA Modules:
  0.0 118.7 jit_solution(14665244005202029036)
XLA Ops:
  0.7 16.9 %shard_map.93 = (bf16[3584,2048]{1,0:T(8,128)(2,1)S(1)}, f32[2,2048]{1,0:T(2,128)S(1)}, f32[64,2048]{1,0:T(8,128)S(1)}, f32[64,2048]{1,0:T(8,128)S(1)}) custom-call(bf16[3584,2048]{1,0:T(8,128)(2,1)} %refs_0_.1, bf16[256,3584]{1,0:T(8,128)(2,1)} %refs_3_.3, bf16[64,3584]{1,0:T(8,128)(2,1)} %bitcast.6, bf16[64,2048]{1,0:T(8,128)(2,1)} %refs_2_.1, ...), custom_call_target="tpu_custom_call" | custom-call | flops 5637144576 | bytes 14680064 | tf_op jit(solution)/shard_map/pallas_call | solution.py:49
  17.7 1.2 collective-permute-done
  18.9 2.9 %collective-permute-start.3 = (f32[2,2048]{1,0:T(2,128)S(1)}, f32[2,2048]{1,0:T(2,128)S(1)}, u32[]{:S(2)}, u32[]{:S(2)}) collective-permute-start(f32[2,2048]{1,0:T(2,128)S(1)} %add.3.refs_0_), channel_id=1, source_target_pairs={{0,24},{4,28},{8,0},{12,4},{16,8},{20,12},{24,16},{28,20},{1,25},{... | collective-permute-start | bytes 49160 | tf_op jit(solution)/shard_map/ppermute | solution.py:302
  22.6 0.9 collective-permute-start.1
  23.5 3.6 %collective-permute-done.2.refs_2_ = f32[2,2048]{1,0:T(2,128)S(1)} collective-permute-done((f32[2,2048]{1,0:T(2,128)S(1)}, f32[2,2048]{1,0:T(2,128)S(1)}, u32[]{:S(2)}, u32[]{:S(2)}) %collective-permute-start.2) | collective-permute-done | bytes 16416 | tf_op jit(solution)/shard_map/ppermute | solution.py:302
  27.5 1.2 shard_map.94
  29.0 1.6 %collective-permute-start.5 = (f32[448,256]{1,0:T(8,128)S(1)}, f32[448,256]{1,0:T(8,128)S(1)}, u32[]{:S(2)}, u32[]{:S(2)}) collective-permute-start(f32[448,256]{1,0:T(8,128)S(1)} %get-tuple-element.42), channel_id=1, source_target_pairs={{0,1},{1,2},{2,3},{3,0},{4,5},{5,6},{6,7},{7,4},{8,9},{9,10},{10,1... | collective-permute-start | bytes 1376264 | tf_op jit(solution)/shard_map/ppermute | solution.py:298
  30.6 1.7 %collective-permute-start.6 = (f32[448,256]{1,0:T(8,128)S(1)}, f32[448,256]{1,0:T(8,128)S(1)}, u32[]{:S(2)}, u32[]{:S(2)}) collective-permute-start(f32[448,256]{1,0:T(8,128)S(1)} %get-tuple-element.43), channel_id=1, source_target_pairs={{0,3},{1,0},{2,1},{3,2},{4,7},{5,4},{6,5},{7,6},{8,11},{9,8},{10,9... | collective-permute-start | bytes 1376264 | tf_op jit(solution)/shard_map/ppermute | solution.py:298
  32.3 5.3 %shard_map.96 = (f32[64,896]{1,0:T(8,128)S(1)}, f32[64,896]{1,0:T(8,128)S(1)}, f32[64,896]{1,0:T(8,128)S(1)}, f32[64,896]{1,0:T(8,128)S(1)}) custom-call(f32[4,2048]{1,0:T(4,128)S(1)} %get-tuple-element.33.refs_0_.refs_2_, bf16[256,2048]{1,0:T(8,128)(2,1)S(1)} %copy-done, bf16[64,2048]{1,0:T(8,128)(2,1)S(1)} %copy-done.2, bf16[256,3584]{1,0:T(8,128)(2,1)S(1)} %copy-done.1, ...), custom_call_target="tpu_custom_call" | custom-call | flops 1 | bytes 1 | tf_op jit(solution)/shard_map/pallas_call | solution.py:49
  37.6 4.0 %collective-permute-start.7 = (f32[64,896]{1,0:T(8,128)S(1)}, f32[64,896]{1,0:T(8,128)S(1)}, u32[]{:S(2)}, u32[]{:S(2)}) collective-permute-start(f32[64,896]{1,0:T(8,128)S(1)} %get-tuple-element.44), channel_id=1, source_target_pairs={{0,64},{32,96},{64,0},{96,32},{1,65},{33,97},{65,1},{97,33},{2,66}... | collective-permute-start | bytes 688136 | tf_op jit(solution)/shard_map/ppermute | solution.py:298
  41.6 1.0 collective-permute-start.8
  42.6 2.2 %collective-permute-start.9 = (f32[64,896]{1,0:T(8,128)S(1)}, f32[64,896]{1,0:T(8,128)S(1)}, u32[]{:S(2)}, u32[]{:S(2)}) collective-permute-start(f32[64,896]{1,0:T(8,128)S(1)} %get-tuple-element.46), channel_id=1, source_target_pairs={{0,96},{32,0},{64,32},{96,64},{1,97},{33,1},{65,33},{97,65},{2,98}... | collective-permute-start | bytes 688136 | tf_op jit(solution)/shard_map/ppermute | solution.py:298
  44.8 2.1 %shard_map.98 = (f32[896,256]{1,0:T(8,128)S(1)}, f32[896,256]{1,0:T(8,128)S(1)}) custom-call(bf16[3584,2048]{1,0:T(8,128)(2,1)S(1)} %get-tuple-element.30.refs_6_.refs_4_.refs_0_, bf16[256,2048]{1,0:T(8,128)(2,1)S(1)} %get-tuple-element.32.refs_1_, f32[16,2048]{1,0:T(8,128)S(1)} %get-tuple-element.39.refs_2_), custom_call_target="tpu_custom_call" | custom-call | flops 1 | bytes 1 | tf_op jit(solution)/shard_map/pallas_call | solution.py:49
  46.9 1.1 shard_map.99.refs_4_.refs_0_
  48.1 4.1 %collective-permute-done.8.refs_2_ = f32[64,896]{1,0:T(8,128)S(1)} collective-permute-done((f32[64,896]{1,0:T(8,128)S(1)}, f32[64,896]{1,0:T(8,128)S(1)}, u32[]{:S(2)}, u32[]{:S(2)}) %collective-permute-start.8) | collective-permute-done | bytes 229408 | tf_op jit(solution)/shard_map/ppermute | solution.py:298
  53.1 1.8 %collective-permute-start.11 = (f32[896,256]{1,0:T(8,128)S(1)}, f32[896,256]{1,0:T(8,128)S(1)}, u32[]{:S(2)}, u32[]{:S(2)}) collective-permute-start(f32[896,256]{1,0:T(8,128)S(1)} %get-tuple-element.48), channel_id=1, source_target_pairs={{0,3},{1,0},{2,1},{3,2},{4,7},{5,4},{6,5},{7,6},{8,11},{9,8},{10,9... | collective-permute-start | bytes 2752520 | tf_op jit(solution)/shard_map/ppermute | solution.py:298
  55.6 4.6 %collective-permute-done.12.refs_1_ = f32[16,2048]{1,0:T(8,128)S(1)} collective-permute-done((f32[16,2048]{1,0:T(8,128)S(1)}, f32[16,2048]{1,0:T(8,128)S(1)}, u32[]{:S(2)}, u32[]{:S(2)}) %collective-permute-start.12) | collective-permute-done | bytes 131104 | tf_op jit(solution)/shard_map/ppermute | solution.py:310
  60.7 5.1 %collective-permute-done.13.refs_1_ = f32[8,2048]{1,0:T(8,128)S(1)} collective-permute-done((f32[8,2048]{1,0:T(8,128)S(1)}, f32[8,2048]{1,0:T(8,128)S(1)}, u32[]{:S(2)}, u32[]{:S(2)}) %collective-permute-start.13) | collective-permute-done | bytes 65568 | tf_op jit(solution)/shard_map/ppermute | solution.py:310
  65.8 1.1 collective-permute-start.14
  66.9 12.7 %collective-permute-done.15.refs_1_ = f32[64,896]{1,0:T(8,128)S(1)} collective-permute-done((f32[64,896]{1,0:T(8,128)S(1)}, f32[64,896]{1,0:T(8,128)S(1)}, u32[]{:S(2)}, u32[]{:S(2)}) %collective-permute-start.15) | collective-permute-done | bytes 229408 | tf_op jit(solution)/shard_map/ppermute | solution.py:306
  79.7 2.3 %collective-permute-start.17 = (f32[64,896]{1,0:T(8,128)S(1)}, f32[64,896]{1,0:T(8,128)S(1)}, u32[]{:S(2)}, u32[]{:S(2)}) collective-permute-start(f32[64,896]{1,0:T(8,128)S(1)} %shard_map.104.refs_2_.refs_0_), channel_id=1, source_target_pairs={{0,3},{1,2},{2,1},{3,0},{4,7},{5,6},{6,5},{7,4},{8,11},{9,10},{10,... | collective-permute-start | bytes 688136 | tf_op jit(solution)/shard_map/ppermute | solution.py:306
  82.0 3.5 %collective-permute-start.16 = (f32[16,2048]{1,0:T(8,128)S(1)}, f32[16,2048]{1,0:T(8,128)S(1)}, u32[]{:S(2)}, u32[]{:S(2)}) collective-permute-start(f32[16,2048]{1,0:T(8,128)S(1)} %shard_map.105.refs_0_), channel_id=1, source_target_pairs={{0,96},{32,64},{64,32},{96,0},{1,97},{33,65},{65,33},{97,1},{2,98}... | collective-permute-start | bytes 393224 | tf_op jit(solution)/shard_map/ppermute | solution.py:306
  85.5 2.9 %collective-permute-done.16.refs_1_ = f32[16,2048]{1,0:T(8,128)S(1)} collective-permute-done((f32[16,2048]{1,0:T(8,128)S(1)}, f32[16,2048]{1,0:T(8,128)S(1)}, u32[]{:S(2)}, u32[]{:S(2)}) %collective-permute-start.16) | collective-permute-done | bytes 131104 | tf_op jit(solution)/shard_map/ppermute | solution.py:306
  89.4 1.0 shard_map.107
  90.4 4.1 %collective-permute-done.21.refs_1_ = f32[8,2048]{1,0:T(8,128)S(1)} collective-permute-done((f32[8,2048]{1,0:T(8,128)S(1)}, f32[8,2048]{1,0:T(8,128)S(1)}, u32[]{:S(2)}, u32[]{:S(2)}) %collective-permute-start.21) | collective-permute-done | bytes 65568 | tf_op jit(solution)/shard_map/ppermute | solution.py:310
  94.7 5.0 %collective-permute-done.22.refs_1_ = f32[16,2048]{1,0:T(8,128)S(1)} collective-permute-done((f32[16,2048]{1,0:T(8,128)S(1)}, f32[16,2048]{1,0:T(8,128)S(1)}, u32[]{:S(2)}, u32[]{:S(2)}) %collective-permute-start.22) | collective-permute-done | bytes 131104 | tf_op jit(solution)/shard_map/ppermute | solution.py:310
  99.7 3.3 %collective-permute-start.20 = (f32[64,896]{1,0:T(8,128)S(1)}, f32[64,896]{1,0:T(8,128)S(1)}, u32[]{:S(2)}, u32[]{:S(2)}) collective-permute-start(f32[64,896]{1,0:T(8,128)S(1)} %shard_map.108.refs_2_.refs_0_), channel_id=1, source_target_pairs={{0,96},{32,0},{64,32},{96,64},{1,97},{33,1},{65,33},{97,65},{2,98}... | collective-permute-start | bytes 688136 | tf_op jit(solution)/shard_map/ppermute | solution.py:298
  103.0 0.9 collective-permute-start.18
  104.0 9.4 %collective-permute-done.20.refs_3_ = f32[64,896]{1,0:T(8,128)S(1)} collective-permute-done((f32[64,896]{1,0:T(8,128)S(1)}, f32[64,896]{1,0:T(8,128)S(1)}, u32[]{:S(2)}, u32[]{:S(2)}) %collective-permute-start.20) | collective-permute-done | bytes 229408 | tf_op jit(solution)/shard_map/ppermute | solution.py:298
  113.4 3.4 %collective-permute-done.18.refs_1_ = f32[64,896]{1,0:T(8,128)S(1)} collective-permute-done((f32[64,896]{1,0:T(8,128)S(1)}, f32[64,896]{1,0:T(8,128)S(1)}, u32[]{:S(2)}, u32[]{:S(2)}) %collective-permute-start.18) | collective-permute-done | bytes 229408 | tf_op jit(solution)/shard_map/ppermute | solution.py:298
  116.8 1.0 shard_map.111
  117.9 0.9 shard_map.112
  (45 shorter events, 5.0 us)
Async XLA Ops:
  0.6 26.9 %copy-start = (bf16[256,2048]{1,0:T(8,128)(2,1)S(1)}, bf16[256,2048]{1,0:T(8,128)(2,1)}, u32[]{:S(2)}) copy-start(bf16[256,2048]{1,0:T(8,128)(2,1)} %refs_1_.3) | copy-start | bytes 3145732
  0.6 26.9 %copy-start.3 = (f32[2048]{0:T(1024)S(1)}, f32[2048]{0:T(1024)}, u32[]{:S(2)}) copy-start(f32[2048]{0:T(1024)} %param.11) | copy-start | bytes 24580
  0.7 31.6 %copy-start.1 = (bf16[256,3584]{1,0:T(8,128)(2,1)S(1)}, bf16[256,3584]{1,0:T(8,128)(2,1)}, u32[]{:S(2)}) copy-start(bf16[256,3584]{1,0:T(8,128)(2,1)} %refs_3_.3) | copy-start | bytes 5505028
  0.7 31.6 %copy-start.2 = (bf16[64,2048]{1,0:T(8,128)(2,1)S(1)}, bf16[64,2048]{1,0:T(8,128)(2,1)}, u32[]{:S(2)}) copy-start(bf16[64,2048]{1,0:T(8,128)(2,1)} %refs_2_.1) | copy-start | bytes 786436
  17.6 1.3 %collective-permute-start = (f32[2,2048]{1,0:T(2,128)S(1)}, f32[2,2048]{1,0:T(2,128)S(1)}, u32[]{:S(2)}, u32[]{:S(2)}) collective-permute-start(f32[2,2048]{1,0:T(2,128)S(1)} %get-tuple-element.31), channel_id=1, source_target_pairs={{0,4},{4,0},{8,12},{12,8},{16,20},{20,16},{24,28},{28,24},{1,5},{5... | collective-permute-start | bytes 49160 | tf_op jit(solution)/shard_map/ppermute | solution.py:314
  18.9 4.6 %collective-permute-start.3 = (f32[2,2048]{1,0:T(2,128)S(1)}, f32[2,2048]{1,0:T(2,128)S(1)}, u32[]{:S(2)}, u32[]{:S(2)}) collective-permute-start(f32[2,2048]{1,0:T(2,128)S(1)} %add.3.refs_0_), channel_id=1, source_target_pairs={{0,24},{4,28},{8,0},{12,4},{16,8},{20,12},{24,16},{28,20},{1,25},{... | collective-permute-start | bytes 49160 | tf_op jit(solution)/shard_map/ppermute | solution.py:302
  21.8 5.2 %collective-permute-start.2 = (f32[2,2048]{1,0:T(2,128)S(1)}, f32[2,2048]{1,0:T(2,128)S(1)}, u32[]{:S(2)}, u32[]{:S(2)}) collective-permute-start(f32[2,2048]{1,0:T(2,128)S(1)} %add.3.refs_0_), channel_id=1, source_target_pairs={{0,16},{4,20},{8,24},{12,28},{16,0},{20,4},{24,8},{28,12},{1,17},{... | collective-permute-start | bytes 49160 | tf_op jit(solution)/shard_map/ppermute | solution.py:302
  22.6 4.9 %collective-permute-start.1 = (f32[2,2048]{1,0:T(2,128)S(1)}, f32[2,2048]{1,0:T(2,128)S(1)}, u32[]{:S(2)}, u32[]{:S(2)}) collective-permute-start(f32[2,2048]{1,0:T(2,128)S(1)} %add.3.refs_0_), channel_id=1, source_target_pairs={{0,8},{4,12},{8,16},{12,20},{16,24},{20,28},{24,0},{28,4},{1,9},{5... | collective-permute-start | bytes 49160 | tf_op jit(solution)/shard_map/ppermute | solution.py:302
  28.9 13.7 %collective-permute-start.4 = (f32[32,2048]{1,0:T(8,128)S(1)}, f32[32,2048]{1,0:T(8,128)S(1)}, u32[]{:S(2)}, u32[]{:S(2)}) collective-permute-start(f32[32,2048]{1,0:T(8,128)S(1)} %get-tuple-element.37.refs_5_), channel_id=1, source_target_pairs={{0,4},{4,0},{8,12},{12,8},{16,20},{20,16},{24,28},{28,24},{1,5},{5... | collective-permute-start | bytes 786440 | tf_op jit(solution)/shard_map/ppermute | solution.py:314
  29.0 24.0 %collective-permute-start.5 = (f32[448,256]{1,0:T(8,128)S(1)}, f32[448,256]{1,0:T(8,128)S(1)}, u32[]{:S(2)}, u32[]{:S(2)}) collective-permute-start(f32[448,256]{1,0:T(8,128)S(1)} %get-tuple-element.42), channel_id=1, source_target_pairs={{0,1},{1,2},{2,3},{3,0},{4,5},{5,6},{6,7},{7,4},{8,9},{9,10},{10,1... | collective-permute-start | bytes 1376264 | tf_op jit(solution)/shard_map/ppermute | solution.py:298
  30.6 22.4 %collective-permute-start.6 = (f32[448,256]{1,0:T(8,128)S(1)}, f32[448,256]{1,0:T(8,128)S(1)}, u32[]{:S(2)}, u32[]{:S(2)}) collective-permute-start(f32[448,256]{1,0:T(8,128)S(1)} %get-tuple-element.43), channel_id=1, source_target_pairs={{0,3},{1,0},{2,1},{3,2},{4,7},{5,4},{6,5},{7,6},{8,11},{9,8},{10,9... | collective-permute-start | bytes 1376264 | tf_op jit(solution)/shard_map/ppermute | solution.py:298
  37.6 10.5 %collective-permute-start.7 = (f32[64,896]{1,0:T(8,128)S(1)}, f32[64,896]{1,0:T(8,128)S(1)}, u32[]{:S(2)}, u32[]{:S(2)}) collective-permute-start(f32[64,896]{1,0:T(8,128)S(1)} %get-tuple-element.44), channel_id=1, source_target_pairs={{0,64},{32,96},{64,0},{96,32},{1,65},{33,97},{65,1},{97,33},{2,66}... | collective-permute-start | bytes 688136 | tf_op jit(solution)/shard_map/ppermute | solution.py:298
  41.6 10.6 %collective-permute-start.8 = (f32[64,896]{1,0:T(8,128)S(1)}, f32[64,896]{1,0:T(8,128)S(1)}, u32[]{:S(2)}, u32[]{:S(2)}) collective-permute-start(f32[64,896]{1,0:T(8,128)S(1)} %get-tuple-element.45), channel_id=1, source_target_pairs={{0,32},{32,64},{64,96},{96,0},{1,33},{33,65},{65,97},{97,1},{2,34}... | collective-permute-start | bytes 688136 | tf_op jit(solution)/shard_map/ppermute | solution.py:298
  42.6 10.3 %collective-permute-start.9 = (f32[64,896]{1,0:T(8,128)S(1)}, f32[64,896]{1,0:T(8,128)S(1)}, u32[]{:S(2)}, u32[]{:S(2)}) collective-permute-start(f32[64,896]{1,0:T(8,128)S(1)} %get-tuple-element.46), channel_id=1, source_target_pairs={{0,96},{32,0},{64,32},{96,64},{1,97},{33,1},{65,33},{97,65},{2,98}... | collective-permute-start | bytes 688136 | tf_op jit(solution)/shard_map/ppermute | solution.py:298
  53.1 36.2 %collective-permute-start.11 = (f32[896,256]{1,0:T(8,128)S(1)}, f32[896,256]{1,0:T(8,128)S(1)}, u32[]{:S(2)}, u32[]{:S(2)}) collective-permute-start(f32[896,256]{1,0:T(8,128)S(1)} %get-tuple-element.48), channel_id=1, source_target_pairs={{0,3},{1,0},{2,1},{3,2},{4,7},{5,4},{6,5},{7,6},{8,11},{9,8},{10,9... | collective-permute-start | bytes 2752520 | tf_op jit(solution)/shard_map/ppermute | solution.py:298
  55.0 34.4 %collective-permute-start.10 = (f32[896,256]{1,0:T(8,128)S(1)}, f32[896,256]{1,0:T(8,128)S(1)}, u32[]{:S(2)}, u32[]{:S(2)}) collective-permute-start(f32[896,256]{1,0:T(8,128)S(1)} %get-tuple-element.47.refs_2_), channel_id=1, source_target_pairs={{0,1},{1,2},{2,3},{3,0},{4,5},{5,6},{6,7},{7,4},{8,9},{9,10},{10,1... | collective-permute-start | bytes 2752520 | tf_op jit(solution)/shard_map/ppermute | solution.py:298
  55.2 5.0 %collective-permute-start.12 = (f32[16,2048]{1,0:T(8,128)S(1)}, f32[16,2048]{1,0:T(8,128)S(1)}, u32[]{:S(2)}, u32[]{:S(2)}) collective-permute-start(f32[16,2048]{1,0:T(8,128)S(1)} %get-tuple-element.39.refs_2_), channel_id=1, source_target_pairs={{0,8},{4,12},{8,0},{12,4},{16,24},{20,28},{24,16},{28,20},{1,9},{5... | collective-permute-start | bytes 393224 | tf_op jit(solution)/shard_map/ppermute | solution.py:310
  55.2 24.4 %collective-permute-start.15 = (f32[64,896]{1,0:T(8,128)S(1)}, f32[64,896]{1,0:T(8,128)S(1)}, u32[]{:S(2)}, u32[]{:S(2)}) collective-permute-start(f32[64,896]{1,0:T(8,128)S(1)} %shard_map.100.refs_4_.refs_0_), channel_id=1, source_target_pairs={{0,1},{1,0},{2,3},{3,2},{4,5},{5,4},{6,7},{7,6},{8,9},{9,8},{10,11... | collective-permute-start | bytes 688136 | tf_op jit(solution)/shard_map/ppermute | solution.py:306
  60.2 5.6 %collective-permute-start.13 = (f32[8,2048]{1,0:T(8,128)S(1)}, f32[8,2048]{1,0:T(8,128)S(1)}, u32[]{:S(2)}, u32[]{:S(2)}) collective-permute-start(f32[8,2048]{1,0:T(8,128)S(1)} %get-tuple-element.51), channel_id=1, source_target_pairs={{0,24},{4,28},{8,16},{12,20},{16,8},{20,12},{24,0},{28,4},{1,25},{... | collective-permute-start | bytes 196616 | tf_op jit(solution)/shard_map/ppermute | solution.py:310
  65.8 16.2 %collective-permute-start.14 = (f32[16,2048]{1,0:T(8,128)S(1)}, f32[16,2048]{1,0:T(8,128)S(1)}, u32[]{:S(2)}, u32[]{:S(2)}) collective-permute-start(f32[16,2048]{1,0:T(8,128)S(1)} %shard_map.103.refs_2_.refs_0_), channel_id=1, source_target_pairs={{0,32},{32,0},{64,96},{96,64},{1,33},{33,1},{65,97},{97,65},{2,34}... | collective-permute-start | bytes 393224 | tf_op jit(solution)/shard_map/ppermute | solution.py:306
  79.7 10.7 %collective-permute-start.17 = (f32[64,896]{1,0:T(8,128)S(1)}, f32[64,896]{1,0:T(8,128)S(1)}, u32[]{:S(2)}, u32[]{:S(2)}) collective-permute-start(f32[64,896]{1,0:T(8,128)S(1)} %shard_map.104.refs_2_.refs_0_), channel_id=1, source_target_pairs={{0,3},{1,2},{2,1},{3,0},{4,7},{5,6},{6,5},{7,4},{8,11},{9,10},{10,... | collective-permute-start | bytes 688136 | tf_op jit(solution)/shard_map/ppermute | solution.py:306
  82.0 6.4 %collective-permute-start.16 = (f32[16,2048]{1,0:T(8,128)S(1)}, f32[16,2048]{1,0:T(8,128)S(1)}, u32[]{:S(2)}, u32[]{:S(2)}) collective-permute-start(f32[16,2048]{1,0:T(8,128)S(1)} %shard_map.105.refs_0_), channel_id=1, source_target_pairs={{0,96},{32,64},{64,32},{96,0},{1,97},{33,65},{65,33},{97,1},{2,98}... | collective-permute-start | bytes 393224 | tf_op jit(solution)/shard_map/ppermute | solution.py:306
  89.1 5.5 %collective-permute-start.21 = (f32[8,2048]{1,0:T(8,128)S(1)}, f32[8,2048]{1,0:T(8,128)S(1)}, u32[]{:S(2)}, u32[]{:S(2)}) collective-permute-start(f32[8,2048]{1,0:T(8,128)S(1)} %get-tuple-element.52.refs_3_.refs_0_), channel_id=1, source_target_pairs={{0,24},{4,28},{8,16},{12,20},{16,8},{20,12},{24,0},{28,4},{1,25},{... | collective-permute-start | bytes 196616 | tf_op jit(solution)/shard_map/ppermute | solution.py:310
  94.6 5.0 %collective-permute-start.22 = (f32[16,2048]{1,0:T(8,128)S(1)}, f32[16,2048]{1,0:T(8,128)S(1)}, u32[]{:S(2)}, u32[]{:S(2)}) collective-permute-start(f32[16,2048]{1,0:T(8,128)S(1)} %shard_map.109.refs_0_), channel_id=1, source_target_pairs={{0,8},{4,12},{8,0},{12,4},{16,24},{20,28},{24,16},{28,20},{1,9},{5... | collective-permute-start | bytes 393224 | tf_op jit(solution)/shard_map/ppermute | solution.py:310
  99.7 18.2 %collective-permute-start.23 = (f32[32,2048]{1,0:T(8,128)S(1)}, f32[32,2048]{1,0:T(8,128)S(1)}, u32[]{:S(2)}, u32[]{:S(2)}) collective-permute-start(f32[32,2048]{1,0:T(8,128)S(1)} %shard_map.110.refs_4_.refs_0_), channel_id=1, source_target_pairs={{0,4},{4,0},{8,12},{12,8},{16,20},{20,16},{24,28},{28,24},{1,5},{5... | collective-permute-start | bytes 786440 | tf_op jit(solution)/shard_map/ppermute | solution.py:314
  99.7 13.7 %collective-permute-start.20 = (f32[64,896]{1,0:T(8,128)S(1)}, f32[64,896]{1,0:T(8,128)S(1)}, u32[]{:S(2)}, u32[]{:S(2)}) collective-permute-start(f32[64,896]{1,0:T(8,128)S(1)} %shard_map.108.refs_2_.refs_0_), channel_id=1, source_target_pairs={{0,96},{32,0},{64,32},{96,64},{1,97},{33,1},{65,33},{97,65},{2,98}... | collective-permute-start | bytes 688136 | tf_op jit(solution)/shard_map/ppermute | solution.py:298
  103.0 10.4 %collective-permute-start.19 = (f32[64,896]{1,0:T(8,128)S(1)}, f32[64,896]{1,0:T(8,128)S(1)}, u32[]{:S(2)}, u32[]{:S(2)}) collective-permute-start(f32[64,896]{1,0:T(8,128)S(1)} %shard_map.108.refs_2_.refs_0_), channel_id=1, source_target_pairs={{0,64},{32,96},{64,0},{96,32},{1,65},{33,97},{65,1},{97,33},{2,66}... | collective-permute-start | bytes 688136 | tf_op jit(solution)/shard_map/ppermute | solution.py:298
  103.0 13.8 %collective-permute-start.18 = (f32[64,896]{1,0:T(8,128)S(1)}, f32[64,896]{1,0:T(8,128)S(1)}, u32[]{:S(2)}, u32[]{:S(2)}) collective-permute-start(f32[64,896]{1,0:T(8,128)S(1)} %shard_map.108.refs_2_.refs_0_), channel_id=1, source_target_pairs={{0,32},{32,64},{64,96},{96,0},{1,33},{33,65},{65,97},{97,1},{2,34}... | collective-permute-start | bytes 688136 | tf_op jit(solution)/shard_map/ppermute | solution.py:298

commit v4 on v3

--- a/solution.py
+++ b/solution.py
@@ -165,24 +165,30 @@
 
 def near_kernel(m_ref, scaled_ref, up_ref, down_ref):
     y = lax.axis_index("cols")
-    up_ref[...] = nt(block(m_ref, y + 1), scaled_ref[...])
-    down_ref[...] = nt(block(m_ref, y - 1), scaled_ref[...])
-
-
-def relay_kernel(near_up_ref, near_down_ref, u0_ref, u1_ref, up_ref, down_ref):
-    half = u0_ref.shape[0]
-    up_ref[:half] = near_up_ref[:half] + u0_ref[...]
-    up_ref[half:] = near_up_ref[half:]
-    down_ref[:half] = near_down_ref[:half]
-    down_ref[half:] = near_down_ref[half:] + u1_ref[...]
+    up_ref[...] = nt(block(m_ref, y + 1, 1), scaled_ref[...])
+    down_ref[...] = nt(block(m_ref, y - 1, 0), scaled_ref[...])
+
+
+def relay_kernel(m_ref, scaled_ref, u0_ref, u1_ref, up_ref, down_ref):
+    y = lax.axis_index("cols")
+    up_ref[...] = u0_ref[...] + nt(block(m_ref, y + 1, 0), scaled_ref[...])
+    down_ref[...] = u1_ref[...] + nt(block(m_ref, y - 1, 1), scaled_ref[...])
 
 
 def own_kernel(m_ref, scaled_ref, own_ref):
     own_ref[...] = nt(block(m_ref, lax.axis_index("cols")), scaled_ref[...])
 
 
-def finish_kernel(own_ref, up_ref, down_ref, out_ref, done_ref):
-    out_ref[...] = (own_ref[...] + (up_ref[...] + down_ref[...])).astype(BF16)
+def gather_kernel(own_ref, v0_ref, v1_ref, sum_ref):
+    half = own_ref.shape[0] // 2
+    sum_ref[:half] = own_ref[:half] + v1_ref[...]
+    sum_ref[half:] = own_ref[half:] + v0_ref[...]
+
+
+def finish_kernel(own_ref, w0_ref, w1_ref, out_ref, done_ref):
+    half = own_ref.shape[0] // 2
+    out_ref[:half] = (own_ref[:half] + w0_ref[...]).astype(BF16)
+    out_ref[half:] = (own_ref[half:] + w1_ref[...]).astype(BF16)
     done_ref[...] = jnp.zeros_like(done_ref)
 
 
@@ -265,6 +271,36 @@
     split(whole, [keep_ref, send_ref], core_bit(), 0)
 
 
+def add_halves_kernel(left_ref, right_ref, top_ref, bottom_ref):
+    half = top_ref.shape[0]
+    top_ref[...] = left_ref[:half] + right_ref[:half]
+    bottom_ref[...] = left_ref[half:] + right_ref[half:]
+
+
+def pair_kernel(top_ref, top_more_ref, bottom_ref, bottom_more_ref, top_out_ref, bottom_out_ref):
+    half = top_ref.shape[0]
+    top_out_ref[:half] = top_ref[...]
+    top_out_ref[half:] = top_more_ref[...]
+    bottom_out_ref[:half] = bottom_ref[...]
+    bottom_out_ref[half:] = bottom_more_ref[...]
+
+
+def a_join_kernel(top_ref, top_more_ref, bottom_ref, bottom_more_ref, whole, done_ref):
+    done_ref[...] = jnp.zeros_like(done_ref)
+    z = dp_index()
+    first = z + 1 - 2 * lax.rem(z, 2)
+    second = 3 - z
+    half, size = top_ref.shape[0] // 2, top_ref.shape[1]
+    for row, ref, near, far in (
+        (0, top_ref, z, second),
+        (0, top_more_ref, first, 3 - first),
+        (half, bottom_ref, z, first),
+        (half, bottom_more_ref, second, 3 - first),
+    ):
+        whole[row:row + half, pl.ds(pl.multiple_of(near * size, 128), size)] = ref[:half]
+        whole[row:row + half, pl.ds(pl.multiple_of(far * size, 128), size)] = ref[half:]
+
+
 def b_stack_kernel(left_ref, right_ref, vec_ref, out_ref):
     rows = left_ref.shape[0]
     out_ref[:rows] = left_ref[...] + right_ref[...]
@@ -339,6 +375,10 @@
         vec, bq, am,
         scratch=[pltpu.VMEM((rank, cols), F32)],
     )
+    half = [out((far, toks))] * 2
+    up, down = call(near_kernel, half, [VMEM] * 2, m, scaled, after=[send])
+    v0, v1 = ring(up, "cols", 1), ring(down, "cols", 3)
+    keep, send = halve(keep, swap_core(send), near_bit, after=[up])
     pieces = call(
         functools.partial(a_kernel, 2.0 * gamma),
         [out((rank, rows // 4))] * 4,
@@ -347,26 +387,37 @@
         scratch=[pltpu.VMEM((rank, rows), F32)],
         after=[send],
     )
-    keep, send = halve(keep, swap_core(send), near_bit, after=[pieces[0]])
+    keep, send = halve(keep, swap_x(send, 0), far_bit, after=[pieces[0]])
     pieces = [pieces[0]] + [ring(pieces[k], "dp", k) for k in (2, 1, 3)]
-    up, down = call(near_kernel, [out((rows // 4, toks))] * 2, [VMEM] * 2, m, scaled, after=[send])
-    own = call(own_kernel, [out((rows // 4, toks))], [VMEM] * 2, m, scaled, after=[up])[0]
-
+    own = call(own_kernel, [out((rows // 4, toks))], [VMEM] * 2, m, scaled, after=[send, u0, u1])[0]
+
+    own = call(gather_kernel, [out((rows // 4, toks))], [VMEM] * 3, own, v0, v1)[0]
     piece = add(*pieces, after=[own])
-    up, down = call(
-        relay_kernel, [out((rows // 4, toks))] * 2, [VMEM] * 4, up, down, u0, u1, after=[piece]
-    )
+    stack = call(
+        b_stack_kernel, [out((rank // 4, cols))], [VMEM] * 3, keep, swap_x(send, 1), vec, after=[piece]
+    )[0]
+    piece = add(piece, swap(piece, "cols", 0), after=[stack])
+    last = (piece, swap(piece, "cols", 1))
+    stack = add(stack, swap(stack, "dp", 0), after=[piece])
+    piece = [out((rank // 2, rows // 4))] * 2
+    top, bottom = call(add_halves_kernel, piece, [VMEM] * 2, *last, after=[stack])
+    up, down = call(relay_kernel, half, [VMEM] * 4, m, scaled, u0, u1, after=[top])
     w0, w1 = ring(up, "cols", 1), ring(down, "cols", 3)
-    keep, send = halve(keep, swap_x(send, 0), far_bit, after=[up])
-    stack = call(b_stack_kernel, [out((rank // 4, cols))], [VMEM] * 3, keep, swap_x(send, 1), vec)[0]
-    piece = add(piece, swap(piece, "cols", 0), after=[stack])
-    stack = add(stack, swap(stack, "dp", 0), after=[piece])
     b_part, mag_grad = call(
         functools.partial(b_unstack_kernel, gamma / float(full_rows) ** 0.5),
         [out((rank // 8, cols)), out((1, cols))],
         [VMEM] * 3,
         stack, swap(stack, "dp", 1), vec,
-    )
+        after=[up],
+    )
+    top, bottom = call(
+        pair_kernel,
+        [out((rank, rows // 4))] * 2,
+        [VMEM] * 4,
+        top, swap(top, "dp", 1), bottom, swap(bottom, "dp", 0),
+        after=[b_part],
+    )
+    b_part = join([b_part, swap_x(b_part, 1)], far_bit, 0, after=[top])
     grad, done = call(
         finish_kernel,
         [out((rows // 4, toks), BF16), out((8, 128))],
@@ -374,11 +425,15 @@
         own, w0, w1,
         after=[b_part],
     )
-    piece = add(piece, swap(piece, "cols", 1), after=[done])
-    b_part = join([b_part, swap_x(b_part, 1)], far_bit, 0, after=[piece])
-    b_part = join([b_part, swap_x(b_part, 0)], near_bit, 0)
+    a_grad, done = call(
+        a_join_kernel,
+        [out((rank, rows)), out((8, 128))],
+        [VMEM] * 4,
+        top, swap(top, "dp", 0), bottom, swap(bottom, "dp", 1),
+        after=[done],
+    )
+    b_part = join([b_part, swap_x(b_part, 0)], near_bit, 0, after=[done])
     b_grad = join([b_part, swap_core(b_part)], core_bit, 0)
-    a_grad = join([piece] + [ring(piece, "dp", k) for k in (1, 2, 3)], dp_index, 1, after=[b_part])
     return grad, a_grad.T, b_grad, mag_grad.reshape(cols)
 
 

time: 119 us -> 101 us (0.85); the launches traced: 119 us -> 99.4 us
  waiting for transfers between devices: 57.4 us -> 34.6 us
  starting transfers between devices: 29.7 us -> 33.4 us
    ppermute x10 -> x9, waiting for transfers between devices: 17.7 us -> 6.91 us  [ring(): lax.ppermute(value, axis, [(i, (i + k) % count) for i in range(count)])]
    ppermute x4, waiting for transfers between devices: 18.9 us -> 10.9 us  [swap_x(): lax.ppermute(value, 'rows', [(i, i ^ 2 if step == 0 else 6 - 2 * (i // 2)...]
    ppermute x4 -> x8, waiting for transfers between devices: 15.7 us -> 9.97 us  [swap(): lax.ppermute(value, axis, [(i, i ^ 1 if step == 0 else 3 - i) for i in ra...]
    ppermute x4 -> x8, starting transfers between devices: 7.22 us -> 10.4 us  [swap(): lax.ppermute(value, axis, [(i, i ^ 1 if step == 0 else 3 - i) for i in ra...]
    ppermute x4, starting transfers between devices: 0.82 us -> 3.37 us  [swap_x(): lax.ppermute(value, 'rows', [(i, i ^ 2 if step == 0 else 6 - 2 * (i // 2)...]
    ppermute x10 -> x9, starting transfers between devices: 16.8 us -> 14.9 us  [ring(): lax.ppermute(value, axis, [(i, (i + k) % count) for i in range(count)])]
    ppermute x3, waiting for transfers between devices: 1.18 us -> 2.7 us  [swap_core(): return lax.ppermute(value, 'rows', [(i, i ^ 1) for i in range(count)])]
    pallas_call x20 -> x22, Pallas kernels: 30.7 us -> 30.6 us  [call(): pl.pallas_call(body, out_shape=outs, in_specs=list(specs) + [ANY] * len(a...]
  transfers between devices with their start and end apart: 24 -> 27, of which waited for: 13 -> 16; matrix products, arithmetic and copies ran while one was open for 0% -> 0% of each run, Pallas kernels for 10% -> 11%
where the time goes in v4:
time: 101 us; the launch traced here: 99.4 us
  waiting for transfers between devices  34.6 us (34%)
  starting transfers between devices  33.4 us (33%)
  Pallas kernels  30.6 us (30%)
    pallas_call x22, Pallas kernels, call(): pl.pallas_call(body, out_shape=outs, in_specs=list(specs) + [ANY] * len(a...  30.6 us
    ppermute x9, starting transfers between devices, ring(): lax.ppermute(value, axis, [(i, (i + k) % count) for i in range(count)])  14.9 us
    ppermute x4, waiting for transfers between devices, swap_x(): lax.ppermute(value, 'rows', [(i, i ^ 2 if step == 0 else 6 - 2 * (i // 2)...  10.9 us
    ppermute x8, starting transfers between devices, swap(): lax.ppermute(value, axis, [(i, i ^ 1 if step == 0 else 3 - i) for i in ra...  10.4 us
    ppermute x8, waiting for transfers between devices, swap(): lax.ppermute(value, axis, [(i, i ^ 1 if step == 0 else 3 - i) for i in ra...  9.97 us
    ppermute x9, waiting for transfers between devices, ring(): lax.ppermute(value, axis, [(i, (i + k) % count) for i in range(count)])  6.91 us
    ppermute x3, starting transfers between devices, ring_x(): lax.ppermute(value, 'rows', [(i, (i + 2 * k) % count) for i in range(coun...  4.59 us
    ppermute x3, waiting for transfers between devices, ring_x(): lax.ppermute(value, 'rows', [(i, (i + 2 * k) % count) for i in range(coun...  4.06 us
  transfers between devices with their start and end apart: 27, of which 16 were waited for; matrix products, arithmetic and copies ran while one was open for 0% of the time, Pallas kernels for 11%

profile of v4, /device:TPU:0, one launch (start us, length us, event | category | flops | bytes accessed | tf_op | source)
XLA Modules:
  0.0 99.4 jit_solution(4319060147934427193)
XLA Ops:
  0.7 16.8 %shard_map.93 = (bf16[3584,2048]{1,0:T(8,128)(2,1)S(1)}, f32[2,2048]{1,0:T(2,128)S(1)}, f32[64,2048]{1,0:T(8,128)S(1)}, f32[64,2048]{1,0:T(8,128)S(1)}) custom-call(bf16[3584,2048]{1,0:T(8,128)(2,1)} %refs_0_.1, bf16[256,3584]{1,0:T(8,128)(2,1)} %refs_3_.3, bf16[64,3584]{1,0:T(8,128)(2,1)} %bitcast.6, bf16[64,2048]{1,0:T(8,128)(2,1)} %refs_2_.1, ...), custom_call_target="tpu_custom_call" | custom-call | flops 5637144576 | bytes 14680064 | tf_op jit(solution)/shard_map/pallas_call | solution.py:49
  17.6 1.2 %collective-permute-done = f32[2,2048]{1,0:T(2,128)S(1)} collective-permute-done((f32[2,2048]{1,0:T(2,128)S(1)}, f32[2,2048]{1,0:T(2,128)S(1)}, u32[]{:S(2)}, u32[]{:S(2)}) %collective-permute-start) | collective-permute-done | bytes 16416 | tf_op jit(solution)/shard_map/ppermute | solution.py:350
  18.8 2.9 %collective-permute-start.3 = (f32[2,2048]{1,0:T(2,128)S(1)}, f32[2,2048]{1,0:T(2,128)S(1)}, u32[]{:S(2)}, u32[]{:S(2)}) collective-permute-start(f32[2,2048]{1,0:T(2,128)S(1)} %add.3.refs_0_), channel_id=1, source_target_pairs={{0,24},{4,28},{8,0},{12,4},{16,8},{20,12},{24,16},{28,20},{1,25},{... | collective-permute-start | bytes 49160 | tf_op jit(solution)/shard_map/ppermute | solution.py:338
  23.4 3.6 %collective-permute-done.2.refs_2_ = f32[2,2048]{1,0:T(2,128)S(1)} collective-permute-done((f32[2,2048]{1,0:T(2,128)S(1)}, f32[2,2048]{1,0:T(2,128)S(1)}, u32[]{:S(2)}, u32[]{:S(2)}) %collective-permute-start.2) | collective-permute-done | bytes 16416 | tf_op jit(solution)/shard_map/ppermute | solution.py:338
  27.4 1.2 %shard_map.94 = (f32[4,2048]{1,0:T(4,128)S(1)}, bf16[256,2048]{1,0:T(8,128)(2,1)S(1)}, f32[448,256]{1,0:T(8,128)S(1)}, f32[448,256]{1,0:T(8,128)S(1)}) custom-call(f32[2,2048]{1,0:T(2,128)S(1)} %add.3.refs_0_, f32[2,2048]{1,0:T(2,128)S(1)} %collective-permute-done.1.refs_1_, f32[2,2048]{1,0:T(2,128)S(1)} %collective-permute-done.2.refs_2_, ...), custom_call_target="tpu_custom_call" | custom-call | flops 1 | bytes 1 | tf_op jit(solution)/shard_map/pallas_call | solution.py:49
  28.6 1.6 %collective-permute-start.6 = (f32[448,256]{1,0:T(8,128)S(1)}, f32[448,256]{1,0:T(8,128)S(1)}, u32[]{:S(2)}, u32[]{:S(2)}) collective-permute-start(f32[448,256]{1,0:T(8,128)S(1)} %get-tuple-element.49), channel_id=1, source_target_pairs={{0,1},{1,2},{2,3},{3,0},{4,5},{5,6},{6,7},{7,4},{8,9},{9,10},{10,1... | collective-permute-start | bytes 1376264 | tf_op jit(solution)/shard_map/ppermute | solution.py:334
  30.3 1.7 %collective-permute-start.7 = (f32[448,256]{1,0:T(8,128)S(1)}, f32[448,256]{1,0:T(8,128)S(1)}, u32[]{:S(2)}, u32[]{:S(2)}) collective-permute-start(f32[448,256]{1,0:T(8,128)S(1)} %get-tuple-element.50), channel_id=1, source_target_pairs={{0,3},{1,0},{2,1},{3,2},{4,7},{5,4},{6,5},{7,6},{8,11},{9,8},{10,9... | collective-permute-start | bytes 1376264 | tf_op jit(solution)/shard_map/ppermute | solution.py:334
  32.2 1.1 %shard_map.96 = (f32[448,256]{1,0:T(8,128)S(1)}, f32[448,256]{1,0:T(8,128)S(1)}) custom-call(bf16[3584,2048]{1,0:T(8,128)(2,1)S(1)} %get-tuple-element.36.refs_6_.refs_0_.refs_4_, bf16[256,2048]{1,0:T(8,128)(2,1)S(1)} %get-tuple-element.38.refs_1_, f32[32,2048]{1,0:T(8,128)S(1)} %get-tuple-element.43.refs_2_), custom_call_target="tpu_custom_call" | custom-call | flops 1 | bytes 1 | tf_op jit(solution)/shard_map/pallas_call | solution.py:49
  33.3 1.9 %collective-permute-start.9 = (f32[448,256]{1,0:T(8,128)S(1)}, f32[448,256]{1,0:T(8,128)S(1)}, u32[]{:S(2)}, u32[]{:S(2)}) collective-permute-start(f32[448,256]{1,0:T(8,128)S(1)} %get-tuple-element.51), channel_id=1, source_target_pairs={{0,3},{1,0},{2,1},{3,2},{4,7},{5,4},{6,5},{7,6},{8,11},{9,8},{10,9... | collective-permute-start | bytes 1376264 | tf_op jit(solution)/shard_map/ppermute | solution.py:334
  35.6 5.3 %shard_map.98 = (f32[64,896]{1,0:T(8,128)S(1)}, f32[64,896]{1,0:T(8,128)S(1)}, f32[64,896]{1,0:T(8,128)S(1)}, f32[64,896]{1,0:T(8,128)S(1)}) custom-call(f32[4,2048]{1,0:T(4,128)S(1)} %get-tuple-element.39.refs_0_.refs_2_, bf16[256,2048]{1,0:T(8,128)(2,1)S(1)} %copy-done, bf16[64,2048]{1,0:T(8,128)(2,1)S(1)} %copy-done.2, bf16[256,3584]{1,0:T(8,128)(2,1)S(1)} %copy-done.1, ...), custom_call_target="tpu_custom_call" | custom-call | flops 1 | bytes 1 | tf_op jit(solution)/shard_map/pallas_call | solution.py:49
  41.0 3.9 %collective-permute-start.10 = (f32[64,896]{1,0:T(8,128)S(1)}, f32[64,896]{1,0:T(8,128)S(1)}, u32[]{:S(2)}, u32[]{:S(2)}) collective-permute-start(f32[64,896]{1,0:T(8,128)S(1)} %get-tuple-element.52), channel_id=1, source_target_pairs={{0,64},{32,96},{64,0},{96,32},{1,65},{33,97},{65,1},{97,33},{2,66}... | collective-permute-start | bytes 688136 | tf_op jit(solution)/shard_map/ppermute | solution.py:334
  44.9 1.0 %collective-permute-start.11 = (f32[64,896]{1,0:T(8,128)S(1)}, f32[64,896]{1,0:T(8,128)S(1)}, u32[]{:S(2)}, u32[]{:S(2)}) collective-permute-start(f32[64,896]{1,0:T(8,128)S(1)} %get-tuple-element.53), channel_id=1, source_target_pairs={{0,32},{32,64},{64,96},{96,0},{1,33},{33,65},{65,97},{97,1},{2,34}... | collective-permute-start | bytes 688136 | tf_op jit(solution)/shard_map/ppermute | solution.py:334
  45.9 2.2 %collective-permute-start.12 = (f32[64,896]{1,0:T(8,128)S(1)}, f32[64,896]{1,0:T(8,128)S(1)}, u32[]{:S(2)}, u32[]{:S(2)}) collective-permute-start(f32[64,896]{1,0:T(8,128)S(1)} %get-tuple-element.54), channel_id=1, source_target_pairs={{0,96},{32,0},{64,32},{96,64},{1,97},{33,1},{65,33},{97,65},{2,98}... | collective-permute-start | bytes 688136 | tf_op jit(solution)/shard_map/ppermute | solution.py:334
  48.2 1.1 %shard_map.100.refs_0_ = f32[896,256]{1,0:T(8,128)S(1)} custom-call(bf16[3584,2048]{1,0:T(8,128)(2,1)S(1)} %get-tuple-element.36.refs_6_.refs_0_.refs_4_, bf16[256,2048]{1,0:T(8,128)(2,1)S(1)} %get-tuple-element.38.refs_1_, f32[8,2048]{1,0:T(8,128)S(1)} %get-tuple-element.48.refs_2_, f32[448,256]{1,0:T(8,128)S(1)} %collective-permute-done.6.refs_3_.refs_2_, ...), custom_call_target="tpu_custom_call" | custom-call | flops 1 | bytes 1 | tf_op jit(solution)/shard_map/pallas_call | solution.py:49
  49.3 1.4 %collective-permute-done.9.refs_2_ = f32[448,256]{1,0:T(8,128)S(1)} collective-permute-done((f32[448,256]{1,0:T(8,128)S(1)}, f32[448,256]{1,0:T(8,128)S(1)}, u32[]{:S(2)}, u32[]{:S(2)}) %collective-permute-start.9) | collective-permute-done | bytes 458784 | tf_op jit(solution)/shard_map/ppermute | solution.py:334
  51.3 4.2 %collective-permute-done.11.refs_2_ = f32[64,896]{1,0:T(8,128)S(1)} collective-permute-done((f32[64,896]{1,0:T(8,128)S(1)}, f32[64,896]{1,0:T(8,128)S(1)}, u32[]{:S(2)}, u32[]{:S(2)}) %collective-permute-start.11) | collective-permute-done | bytes 229408 | tf_op jit(solution)/shard_map/ppermute | solution.py:334
  56.8 1.8 %collective-permute-start.14 = (f32[8,2048]{1,0:T(8,128)S(1)}, f32[8,2048]{1,0:T(8,128)S(1)}, u32[]{:S(2)}, u32[]{:S(2)}) collective-permute-start(f32[8,2048]{1,0:T(8,128)S(1)} %get-tuple-element.48.refs_2_), channel_id=1, source_target_pairs={{0,24},{4,28},{8,16},{12,20},{16,8},{20,12},{24,0},{28,4},{1,25},{... | collective-permute-start | bytes 196616 | tf_op jit(solution)/shard_map/ppermute | solution.py:346
  58.5 3.7 %collective-permute-done.14.refs_1_ = f32[8,2048]{1,0:T(8,128)S(1)} collective-permute-done((f32[8,2048]{1,0:T(8,128)S(1)}, f32[8,2048]{1,0:T(8,128)S(1)}, u32[]{:S(2)}, u32[]{:S(2)}) %collective-permute-start.14) | collective-permute-done | bytes 65568 | tf_op jit(solution)/shard_map/ppermute | solution.py:346
  63.3 3.0 %collective-permute-start.15 = (f32[64,896]{1,0:T(8,128)S(1)}, f32[64,896]{1,0:T(8,128)S(1)}, u32[]{:S(2)}, u32[]{:S(2)}) collective-permute-start(f32[64,896]{1,0:T(8,128)S(1)} %shard_map.104.refs_2_.refs_0_), channel_id=1, source_target_pairs={{0,3},{1,2},{2,1},{3,0},{4,7},{5,6},{6,5},{7,4},{8,11},{9,10},{10,... | collective-permute-start | bytes 688136 | tf_op jit(solution)/shard_map/ppermute | solution.py:342
  66.3 1.3 %collective-permute-start.16 = (f32[16,2048]{1,0:T(8,128)S(1)}, f32[16,2048]{1,0:T(8,128)S(1)}, u32[]{:S(2)}, u32[]{:S(2)}) collective-permute-start(f32[16,2048]{1,0:T(8,128)S(1)} %shard_map.103.refs_2_.refs_0_), channel_id=1, source_target_pairs={{0,32},{32,0},{64,96},{96,64},{1,33},{33,1},{65,97},{97,65},{2,34}... | collective-permute-start | bytes 393224 | tf_op jit(solution)/shard_map/ppermute | solution.py:342
  67.6 3.7 %collective-permute-done.16.refs_1_ = f32[16,2048]{1,0:T(8,128)S(1)} collective-permute-done((f32[16,2048]{1,0:T(8,128)S(1)}, f32[16,2048]{1,0:T(8,128)S(1)}, u32[]{:S(2)}, u32[]{:S(2)}) %collective-permute-start.16) | collective-permute-done | bytes 131104 | tf_op jit(solution)/shard_map/ppermute | solution.py:342
  71.3 1.1 %shard_map.107 = (f32[448,256]{1,0:T(8,128)S(1)}, f32[448,256]{1,0:T(8,128)S(1)}) custom-call(bf16[3584,2048]{1,0:T(8,128)(2,1)S(1)} %get-tuple-element.36.refs_6_.refs_0_.refs_4_, bf16[256,2048]{1,0:T(8,128)(2,1)S(1)} %get-tuple-element.38.refs_1_, f32[448,256]{1,0:T(8,128)S(1)} %collective-permute-done.6.refs_3_.refs_2_, ...), custom_call_target="tpu_custom_call" | custom-call | flops 1 | bytes 1 | tf_op jit(solution)/shard_map/pallas_call | solution.py:49
  72.5 2.3 %collective-permute-start.18 = (f32[448,256]{1,0:T(8,128)S(1)}, f32[448,256]{1,0:T(8,128)S(1)}, u32[]{:S(2)}, u32[]{:S(2)}) collective-permute-start(f32[448,256]{1,0:T(8,128)S(1)} %get-tuple-element.58), channel_id=1, source_target_pairs={{0,3},{1,0},{2,1},{3,2},{4,7},{5,4},{6,5},{7,6},{8,11},{9,8},{10,9... | collective-permute-start | bytes 1376264 | tf_op jit(solution)/shard_map/ppermute | solution.py:334
  74.8 4.1 %collective-permute-start.19 = (f32[16,2048]{1,0:T(8,128)S(1)}, f32[16,2048]{1,0:T(8,128)S(1)}, u32[]{:S(2)}, u32[]{:S(2)}) collective-permute-start(f32[16,2048]{1,0:T(8,128)S(1)} %shard_map.105.refs_2_.refs_0_), channel_id=1, source_target_pairs={{0,96},{32,64},{64,32},{96,0},{1,97},{33,65},{65,33},{97,1},{2,98}... | collective-permute-start | bytes 393224 | tf_op jit(solution)/shard_map/ppermute | solution.py:342
  78.9 4.0 %collective-permute-done.19.refs_1_ = f32[16,2048]{1,0:T(8,128)S(1)} collective-permute-done((f32[16,2048]{1,0:T(8,128)S(1)}, f32[16,2048]{1,0:T(8,128)S(1)}, u32[]{:S(2)}, u32[]{:S(2)}) %collective-permute-start.19) | collective-permute-done | bytes 131104 | tf_op jit(solution)/shard_map/ppermute | solution.py:342
  83.6 1.2 %collective-permute-done.21.refs_1_ = f32[32,896]{1,0:T(8,128)S(1)} collective-permute-done((f32[32,896]{1,0:T(8,128)S(1)}, f32[32,896]{1,0:T(8,128)S(1)}, u32[]{:S(2)}, u32[]{:S(2)}) %collective-permute-start.21) | collective-permute-done | bytes 114720 | tf_op jit(solution)/shard_map/ppermute | solution.py:342
  84.9 1.5 %collective-permute-start.24 = (f32[64,896]{1,0:T(8,128)S(1)}, f32[64,896]{1,0:T(8,128)S(1)}, u32[]{:S(2)}, u32[]{:S(2)}) collective-permute-start(f32[64,896]{1,0:T(8,128)S(1)} %get-tuple-element.63.refs_2_), channel_id=1, source_target_pairs={{0,96},{32,64},{64,32},{96,0},{1,97},{33,65},{65,33},{97,1},{2,98}... | collective-permute-start | bytes 688136 | tf_op jit(solution)/shard_map/ppermute | solution.py:342
  86.4 1.4 %collective-permute-start.20 = (f32[8,2048]{1,0:T(8,128)S(1)}, f32[8,2048]{1,0:T(8,128)S(1)}, u32[]{:S(2)}, u32[]{:S(2)}) collective-permute-start(f32[8,2048]{1,0:T(8,128)S(1)} %get-tuple-element.59.refs_4_.refs_0_), channel_id=1, source_target_pairs={{0,24},{4,28},{8,16},{12,20},{16,8},{20,12},{24,0},{28,4},{1,25},{... | collective-permute-start | bytes 196616 | tf_op jit(solution)/shard_map/ppermute | solution.py:346
  87.8 4.1 %collective-permute-done.20.refs_1_ = f32[8,2048]{1,0:T(8,128)S(1)} collective-permute-done((f32[8,2048]{1,0:T(8,128)S(1)}, f32[8,2048]{1,0:T(8,128)S(1)}, u32[]{:S(2)}, u32[]{:S(2)}) %collective-permute-start.20) | collective-permute-done | bytes 65568 | tf_op jit(solution)/shard_map/ppermute | solution.py:346
  92.9 1.0 %shard_map.112 = (f32[64,3584]{1,0:T(8,128)}, f32[8,128]{1,0:T(8,128)S(1)}) custom-call(f32[64,896]{1,0:T(8,128)S(1)} %get-tuple-element.61.refs_2_.refs_0_, f32[64,896]{1,0:T(8,128)S(1)} %collective-permute-done.23.refs_1_, f32[64,896]{1,0:T(8,128)S(1)} %get-tuple-element.63.refs_2_, f32[64,896]{1,0:T(8,128)S(1)} %collective-permute-done.24.refs_3_, ...), custom_call_target="tpu_custom_call" | custom-call | flops 1 | bytes 1 | tf_op jit(solution)/shard_map/pallas_call | solution.py:49
  93.9 3.0 %collective-permute-done.25.refs_1_ = f32[16,2048]{1,0:T(8,128)S(1)} collective-permute-done((f32[16,2048]{1,0:T(8,128)S(1)}, f32[16,2048]{1,0:T(8,128)S(1)}, u32[]{:S(2)}, u32[]{:S(2)}) %collective-permute-start.25) | collective-permute-done | bytes 131104 | tf_op jit(solution)/shard_map/ppermute | solution.py:346
  97.1 1.5 %collective-permute-done.26.refs_1_ = f32[32,2048]{1,0:T(8,128)S(1)} collective-permute-done((f32[32,2048]{1,0:T(8,128)S(1)}, f32[32,2048]{1,0:T(8,128)S(1)}, u32[]{:S(2)}, u32[]{:S(2)}) %collective-permute-start.26) | collective-permute-done | bytes 262176 | tf_op jit(solution)/shard_map/ppermute | solution.py:350
  (53 shorter events, 8.7 us)
Async XLA Ops:
  0.6 26.8 %copy-start = (bf16[256,2048]{1,0:T(8,128)(2,1)S(1)}, bf16[256,2048]{1,0:T(8,128)(2,1)}, u32[]{:S(2)}) copy-start(bf16[256,2048]{1,0:T(8,128)(2,1)} %refs_1_.3) | copy-start | bytes 3145732
  0.6 26.8 %copy-start.3 = (f32[2048]{0:T(1024)S(1)}, f32[2048]{0:T(1024)}, u32[]{:S(2)}) copy-start(f32[2048]{0:T(1024)} %param.11) | copy-start | bytes 24580
  17.5 1.3 %collective-permute-start = (f32[2,2048]{1,0:T(2,128)S(1)}, f32[2,2048]{1,0:T(2,128)S(1)}, u32[]{:S(2)}, u32[]{:S(2)}) collective-permute-start(f32[2,2048]{1,0:T(2,128)S(1)} %get-tuple-element.37), channel_id=1, source_target_pairs={{0,4},{4,0},{8,12},{12,8},{16,20},{20,16},{24,28},{28,24},{1,5},{5... | collective-permute-start | bytes 49160 | tf_op jit(solution)/shard_map/ppermute | solution.py:350
  18.8 4.6 %collective-permute-start.3 = (f32[2,2048]{1,0:T(2,128)S(1)}, f32[2,2048]{1,0:T(2,128)S(1)}, u32[]{:S(2)}, u32[]{:S(2)}) collective-permute-start(f32[2,2048]{1,0:T(2,128)S(1)} %add.3.refs_0_), channel_id=1, source_target_pairs={{0,24},{4,28},{8,0},{12,4},{16,8},{20,12},{24,16},{28,20},{1,25},{... | collective-permute-start | bytes 49160 | tf_op jit(solution)/shard_map/ppermute | solution.py:338
  21.7 5.2 %collective-permute-start.2 = (f32[2,2048]{1,0:T(2,128)S(1)}, f32[2,2048]{1,0:T(2,128)S(1)}, u32[]{:S(2)}, u32[]{:S(2)}) collective-permute-start(f32[2,2048]{1,0:T(2,128)S(1)} %add.3.refs_0_), channel_id=1, source_target_pairs={{0,16},{4,20},{8,24},{12,28},{16,0},{20,4},{24,8},{28,12},{1,17},{... | collective-permute-start | bytes 49160 | tf_op jit(solution)/shard_map/ppermute | solution.py:338
  22.5 4.9 %collective-permute-start.1 = (f32[2,2048]{1,0:T(2,128)S(1)}, f32[2,2048]{1,0:T(2,128)S(1)}, u32[]{:S(2)}, u32[]{:S(2)}) collective-permute-start(f32[2,2048]{1,0:T(2,128)S(1)} %add.3.refs_0_), channel_id=1, source_target_pairs={{0,8},{4,12},{8,16},{12,20},{16,24},{20,28},{24,0},{28,4},{1,9},{5... | collective-permute-start | bytes 49160 | tf_op jit(solution)/shard_map/ppermute | solution.py:338
  27.4 8.1 %copy-start.1 = (bf16[256,3584]{1,0:T(8,128)(2,1)S(1)}, bf16[256,3584]{1,0:T(8,128)(2,1)}, u32[]{:S(2)}) copy-start(bf16[256,3584]{1,0:T(8,128)(2,1)} %refs_3_.3) | copy-start | bytes 5505028
  27.4 8.2 %copy-start.2 = (bf16[64,2048]{1,0:T(8,128)(2,1)S(1)}, bf16[64,2048]{1,0:T(8,128)(2,1)}, u32[]{:S(2)}) copy-start(bf16[64,2048]{1,0:T(8,128)(2,1)} %refs_2_.1) | copy-start | bytes 786436
  28.6 16.3 %collective-permute-start.6 = (f32[448,256]{1,0:T(8,128)S(1)}, f32[448,256]{1,0:T(8,128)S(1)}, u32[]{:S(2)}, u32[]{:S(2)}) collective-permute-start(f32[448,256]{1,0:T(8,128)S(1)} %get-tuple-element.49), channel_id=1, source_target_pairs={{0,1},{1,2},{2,3},{3,0},{4,5},{5,6},{6,7},{7,4},{8,9},{9,10},{10,1... | collective-permute-start | bytes 1376264 | tf_op jit(solution)/shard_map/ppermute | solution.py:334
  30.3 15.6 %collective-permute-start.7 = (f32[448,256]{1,0:T(8,128)S(1)}, f32[448,256]{1,0:T(8,128)S(1)}, u32[]{:S(2)}, u32[]{:S(2)}) collective-permute-start(f32[448,256]{1,0:T(8,128)S(1)} %get-tuple-element.50), channel_id=1, source_target_pairs={{0,3},{1,0},{2,1},{3,2},{4,7},{5,4},{6,5},{7,6},{8,11},{9,8},{10,9... | collective-permute-start | bytes 1376264 | tf_op jit(solution)/shard_map/ppermute | solution.py:334
  32.1 3.3 %collective-permute-start.4 = (f32[32,2048]{1,0:T(8,128)S(1)}, f32[32,2048]{1,0:T(8,128)S(1)}, u32[]{:S(2)}, u32[]{:S(2)}) collective-permute-start(f32[32,2048]{1,0:T(8,128)S(1)} %get-tuple-element.43.refs_2_), channel_id=1, source_target_pairs={{0,4},{4,0},{8,12},{12,8},{16,20},{20,16},{24,28},{28,24},{1,5},{5... | collective-permute-start | bytes 786440 | tf_op jit(solution)/shard_map/ppermute | solution.py:350
  33.3 17.4 %collective-permute-start.9 = (f32[448,256]{1,0:T(8,128)S(1)}, f32[448,256]{1,0:T(8,128)S(1)}, u32[]{:S(2)}, u32[]{:S(2)}) collective-permute-start(f32[448,256]{1,0:T(8,128)S(1)} %get-tuple-element.51), channel_id=1, source_target_pairs={{0,3},{1,0},{2,1},{3,2},{4,7},{5,4},{6,5},{7,6},{8,11},{9,8},{10,9... | collective-permute-start | bytes 1376264 | tf_op jit(solution)/shard_map/ppermute | solution.py:334
  35.2 15.5 %collective-permute-start.8 = (f32[448,256]{1,0:T(8,128)S(1)}, f32[448,256]{1,0:T(8,128)S(1)}, u32[]{:S(2)}, u32[]{:S(2)}) collective-permute-start(f32[448,256]{1,0:T(8,128)S(1)} %get-tuple-element.44.refs_2_), channel_id=1, source_target_pairs={{0,1},{1,2},{2,3},{3,0},{4,5},{5,6},{6,7},{7,4},{8,9},{9,10},{10,1... | collective-permute-start | bytes 1376264 | tf_op jit(solution)/shard_map/ppermute | solution.py:334
  35.5 5.5 %collective-permute-start.5 = (f32[16,2048]{1,0:T(8,128)S(1)}, f32[16,2048]{1,0:T(8,128)S(1)}, u32[]{:S(2)}, u32[]{:S(2)}) collective-permute-start(f32[16,2048]{1,0:T(8,128)S(1)} %get-tuple-element.46.refs_5_), channel_id=1, source_target_pairs={{0,8},{4,12},{8,0},{12,4},{16,24},{20,28},{24,16},{28,20},{1,9},{5... | collective-permute-start | bytes 393224 | tf_op jit(solution)/shard_map/ppermute | solution.py:346
  41.0 10.3 %collective-permute-start.10 = (f32[64,896]{1,0:T(8,128)S(1)}, f32[64,896]{1,0:T(8,128)S(1)}, u32[]{:S(2)}, u32[]{:S(2)}) collective-permute-start(f32[64,896]{1,0:T(8,128)S(1)} %get-tuple-element.52), channel_id=1, source_target_pairs={{0,64},{32,96},{64,0},{96,32},{1,65},{33,97},{65,1},{97,33},{2,66}... | collective-permute-start | bytes 688136 | tf_op jit(solution)/shard_map/ppermute | solution.py:334
  44.9 10.7 %collective-permute-start.11 = (f32[64,896]{1,0:T(8,128)S(1)}, f32[64,896]{1,0:T(8,128)S(1)}, u32[]{:S(2)}, u32[]{:S(2)}) collective-permute-start(f32[64,896]{1,0:T(8,128)S(1)} %get-tuple-element.53), channel_id=1, source_target_pairs={{0,32},{32,64},{64,96},{96,0},{1,33},{33,65},{65,97},{97,1},{2,34}... | collective-permute-start | bytes 688136 | tf_op jit(solution)/shard_map/ppermute | solution.py:334
  45.9 10.4 %collective-permute-start.12 = (f32[64,896]{1,0:T(8,128)S(1)}, f32[64,896]{1,0:T(8,128)S(1)}, u32[]{:S(2)}, u32[]{:S(2)}) collective-permute-start(f32[64,896]{1,0:T(8,128)S(1)} %get-tuple-element.54), channel_id=1, source_target_pairs={{0,96},{32,0},{64,32},{96,64},{1,97},{33,1},{65,33},{97,65},{2,98}... | collective-permute-start | bytes 688136 | tf_op jit(solution)/shard_map/ppermute | solution.py:334
  56.4 6.9 %collective-permute-start.13 = (f32[64,896]{1,0:T(8,128)S(1)}, f32[64,896]{1,0:T(8,128)S(1)}, u32[]{:S(2)}, u32[]{:S(2)}) collective-permute-start(f32[64,896]{1,0:T(8,128)S(1)} %shard_map.102.refs_3_.refs_0_), channel_id=1, source_target_pairs={{0,1},{1,0},{2,3},{3,2},{4,5},{5,4},{6,7},{7,6},{8,9},{9,8},{10,11... | collective-permute-start | bytes 688136 | tf_op jit(solution)/shard_map/ppermute | solution.py:342
  56.8 5.5 %collective-permute-start.14 = (f32[8,2048]{1,0:T(8,128)S(1)}, f32[8,2048]{1,0:T(8,128)S(1)}, u32[]{:S(2)}, u32[]{:S(2)}) collective-permute-start(f32[8,2048]{1,0:T(8,128)S(1)} %get-tuple-element.48.refs_2_), channel_id=1, source_target_pairs={{0,24},{4,28},{8,16},{12,20},{16,8},{20,12},{24,0},{28,4},{1,25},{... | collective-permute-start | bytes 196616 | tf_op jit(solution)/shard_map/ppermute | solution.py:346
  63.3 8.0 %collective-permute-start.15 = (f32[64,896]{1,0:T(8,128)S(1)}, f32[64,896]{1,0:T(8,128)S(1)}, u32[]{:S(2)}, u32[]{:S(2)}) collective-permute-start(f32[64,896]{1,0:T(8,128)S(1)} %shard_map.104.refs_2_.refs_0_), channel_id=1, source_target_pairs={{0,3},{1,2},{2,1},{3,0},{4,7},{5,6},{6,5},{7,4},{8,11},{9,10},{10,... | collective-permute-start | bytes 688136 | tf_op jit(solution)/shard_map/ppermute | solution.py:342
  66.3 5.0 %collective-permute-start.16 = (f32[16,2048]{1,0:T(8,128)S(1)}, f32[16,2048]{1,0:T(8,128)S(1)}, u32[]{:S(2)}, u32[]{:S(2)}) collective-permute-start(f32[16,2048]{1,0:T(8,128)S(1)} %shard_map.103.refs_2_.refs_0_), channel_id=1, source_target_pairs={{0,32},{32,0},{64,96},{96,64},{1,33},{33,1},{65,97},{97,65},{2,34}... | collective-permute-start | bytes 393224 | tf_op jit(solution)/shard_map/ppermute | solution.py:342
  72.5 19.6 %collective-permute-start.18 = (f32[448,256]{1,0:T(8,128)S(1)}, f32[448,256]{1,0:T(8,128)S(1)}, u32[]{:S(2)}, u32[]{:S(2)}) collective-permute-start(f32[448,256]{1,0:T(8,128)S(1)} %get-tuple-element.58), channel_id=1, source_target_pairs={{0,3},{1,0},{2,1},{3,2},{4,7},{5,4},{6,5},{7,6},{8,11},{9,8},{10,9... | collective-permute-start | bytes 1376264 | tf_op jit(solution)/shard_map/ppermute | solution.py:334
  74.8 17.3 %collective-permute-start.17 = (f32[448,256]{1,0:T(8,128)S(1)}, f32[448,256]{1,0:T(8,128)S(1)}, u32[]{:S(2)}, u32[]{:S(2)}) collective-permute-start(f32[448,256]{1,0:T(8,128)S(1)} %get-tuple-element.57.refs_3_), channel_id=1, source_target_pairs={{0,1},{1,2},{2,3},{3,0},{4,5},{5,6},{6,7},{7,4},{8,9},{9,10},{10,1... | collective-permute-start | bytes 1376264 | tf_op jit(solution)/shard_map/ppermute | solution.py:334
  74.8 8.2 %collective-permute-start.19 = (f32[16,2048]{1,0:T(8,128)S(1)}, f32[16,2048]{1,0:T(8,128)S(1)}, u32[]{:S(2)}, u32[]{:S(2)}) collective-permute-start(f32[16,2048]{1,0:T(8,128)S(1)} %shard_map.105.refs_2_.refs_0_), channel_id=1, source_target_pairs={{0,96},{32,64},{64,32},{96,0},{1,97},{33,65},{65,33},{97,1},{2,98}... | collective-permute-start | bytes 393224 | tf_op jit(solution)/shard_map/ppermute | solution.py:342
  78.8 4.8 %collective-permute-start.22 = (f32[32,896]{1,0:T(8,128)S(1)}, f32[32,896]{1,0:T(8,128)S(1)}, u32[]{:S(2)}, u32[]{:S(2)}) collective-permute-start(f32[32,896]{1,0:T(8,128)S(1)} %get-tuple-element.60.refs_2_), channel_id=1, source_target_pairs={{0,32},{32,0},{64,96},{96,64},{1,33},{33,1},{65,97},{97,65},{2,34}... | collective-permute-start | bytes 344072 | tf_op jit(solution)/shard_map/ppermute | solution.py:342
  78.8 6.0 %collective-permute-start.21 = (f32[32,896]{1,0:T(8,128)S(1)}, f32[32,896]{1,0:T(8,128)S(1)}, u32[]{:S(2)}, u32[]{:S(2)}) collective-permute-start(f32[32,896]{1,0:T(8,128)S(1)} %get-tuple-element.56.refs_4_.refs_0_), channel_id=1, source_target_pairs={{0,96},{32,64},{64,32},{96,0},{1,97},{33,65},{65,33},{97,1},{2,98}... | collective-permute-start | bytes 344072 | tf_op jit(solution)/shard_map/ppermute | solution.py:342
  84.9 8.0 %collective-permute-start.24 = (f32[64,896]{1,0:T(8,128)S(1)}, f32[64,896]{1,0:T(8,128)S(1)}, u32[]{:S(2)}, u32[]{:S(2)}) collective-permute-start(f32[64,896]{1,0:T(8,128)S(1)} %get-tuple-element.63.refs_2_), channel_id=1, source_target_pairs={{0,96},{32,64},{64,32},{96,0},{1,97},{33,65},{65,33},{97,1},{2,98}... | collective-permute-start | bytes 688136 | tf_op jit(solution)/shard_map/ppermute | solution.py:342
  86.4 6.6 %collective-permute-start.23 = (f32[64,896]{1,0:T(8,128)S(1)}, f32[64,896]{1,0:T(8,128)S(1)}, u32[]{:S(2)}, u32[]{:S(2)}) collective-permute-start(f32[64,896]{1,0:T(8,128)S(1)} %get-tuple-element.61.refs_2_.refs_0_), channel_id=1, source_target_pairs={{0,32},{32,0},{64,96},{96,64},{1,33},{33,1},{65,97},{97,65},{2,34}... | collective-permute-start | bytes 688136 | tf_op jit(solution)/shard_map/ppermute | solution.py:342
  86.4 5.5 %collective-permute-start.20 = (f32[8,2048]{1,0:T(8,128)S(1)}, f32[8,2048]{1,0:T(8,128)S(1)}, u32[]{:S(2)}, u32[]{:S(2)}) collective-permute-start(f32[8,2048]{1,0:T(8,128)S(1)} %get-tuple-element.59.refs_4_.refs_0_), channel_id=1, source_target_pairs={{0,24},{4,28},{8,16},{12,20},{16,8},{20,12},{24,0},{28,4},{1,25},{... | collective-permute-start | bytes 196616 | tf_op jit(solution)/shard_map/ppermute | solution.py:346
  91.9 5.0 %collective-permute-start.25 = (f32[16,2048]{1,0:T(8,128)S(1)}, f32[16,2048]{1,0:T(8,128)S(1)}, u32[]{:S(2)}, u32[]{:S(2)}) collective-permute-start(f32[16,2048]{1,0:T(8,128)S(1)} %shard_map.110.refs_3_.refs_0_), channel_id=1, source_target_pairs={{0,8},{4,12},{8,0},{12,4},{16,24},{20,28},{24,16},{28,20},{1,9},{5... | collective-permute-start | bytes 393224 | tf_op jit(solution)/shard_map/ppermute | solution.py:346
  97.0 1.6 %collective-permute-start.26 = (f32[32,2048]{1,0:T(8,128)S(1)}, f32[32,2048]{1,0:T(8,128)S(1)}, u32[]{:S(2)}, u32[]{:S(2)}) collective-permute-start(f32[32,2048]{1,0:T(8,128)S(1)} %shard_map.113.refs_0_), channel_id=1, source_target_pairs={{0,4},{4,0},{8,12},{12,8},{16,20},{20,16},{24,28},{28,24},{1,5},{5... | collective-permute-start | bytes 786440 | tf_op jit(solution)/shard_map/ppermute | solution.py:350

commit v5 on v4

--- a/solution.py
+++ b/solution.py
@@ -55,6 +55,18 @@
         compiler_params=pltpu.CompilerParams(vmem_limit_bytes=vmem * MIB),
         cost_estimate=pl.CostEstimate(flops=flops, bytes_accessed=data, transcendentals=0),
     )(*args, *after)
+
+
+def hold(values, after):
+    count = len(values)
+    return pl.pallas_call(
+        lambda *refs: None,
+        out_shape=[out(value.shape, value.dtype) for value in values],
+        in_specs=[ANY] * (count + len(after)),
+        out_specs=[ANY] * count,
+        input_output_aliases={k: k for k in range(count)},
+        compiler_params=pltpu.CompilerParams(vmem_limit_bytes=MIB),
+    )(*values, *after)
 
 
 def out(shape, dtype=F32):
@@ -185,11 +197,10 @@
     sum_ref[half:] = own_ref[half:] + v0_ref[...]
 
 
-def finish_kernel(own_ref, w0_ref, w1_ref, out_ref, done_ref):
+def finish_kernel(own_ref, w0_ref, w1_ref, out_ref):
     half = own_ref.shape[0] // 2
     out_ref[:half] = (own_ref[:half] + w0_ref[...]).astype(BF16)
     out_ref[half:] = (own_ref[half:] + w1_ref[...]).astype(BF16)
-    done_ref[...] = jnp.zeros_like(done_ref)
 
 
 def a_kernel(factor, vec_ref, dy_ref, b_ref, x_ref, m_ref, *refs):
@@ -375,10 +386,6 @@
         vec, bq, am,
         scratch=[pltpu.VMEM((rank, cols), F32)],
     )
-    half = [out((far, toks))] * 2
-    up, down = call(near_kernel, half, [VMEM] * 2, m, scaled, after=[send])
-    v0, v1 = ring(up, "cols", 1), ring(down, "cols", 3)
-    keep, send = halve(keep, swap_core(send), near_bit, after=[up])
     pieces = call(
         functools.partial(a_kernel, 2.0 * gamma),
         [out((rank, rows // 4))] * 4,
@@ -387,29 +394,34 @@
         scratch=[pltpu.VMEM((rank, rows), F32)],
         after=[send],
     )
-    keep, send = halve(keep, swap_x(send, 0), far_bit, after=[pieces[0]])
+    keep, send = halve(keep, swap_core(send), near_bit, after=[pieces[0]])
     pieces = [pieces[0]] + [ring(pieces[k], "dp", k) for k in (2, 1, 3)]
-    own = call(own_kernel, [out((rows // 4, toks))], [VMEM] * 2, m, scaled, after=[send, u0, u1])[0]
-
-    own = call(gather_kernel, [out((rows // 4, toks))], [VMEM] * 3, own, v0, v1)[0]
-    piece = add(*pieces, after=[own])
+    half = [out((far, toks))] * 2
+    up, down = call(near_kernel, half, [VMEM] * 2, m, scaled, after=[send])
+    own = call(own_kernel, [out((rows // 4, toks))], [VMEM] * 2, m, scaled, after=[up])[0]
+    up, down = hold([up, down], [own, u0, u1])
+    v0, v1 = ring(up, "cols", 1), ring(down, "cols", 3)
+    w_up, w_down = call(relay_kernel, half, [VMEM] * 4, m, scaled, u0, u1, after=[up])
+
+    piece = add(*pieces, after=[w_up])
+    keep, send = halve(keep, swap_x(send, 0), far_bit, after=[piece])
+    own = call(gather_kernel, [out((rows // 4, toks))], [VMEM] * 3, own, v0, v1, after=[send])[0]
     stack = call(
-        b_stack_kernel, [out((rank // 4, cols))], [VMEM] * 3, keep, swap_x(send, 1), vec, after=[piece]
+        b_stack_kernel, [out((rank // 4, cols))], [VMEM] * 3, keep, swap_x(send, 1), vec, after=[own]
     )[0]
     piece = add(piece, swap(piece, "cols", 0), after=[stack])
     last = (piece, swap(piece, "cols", 1))
     stack = add(stack, swap(stack, "dp", 0), after=[piece])
     piece = [out((rank // 2, rows // 4))] * 2
     top, bottom = call(add_halves_kernel, piece, [VMEM] * 2, *last, after=[stack])
-    up, down = call(relay_kernel, half, [VMEM] * 4, m, scaled, u0, u1, after=[top])
-    w0, w1 = ring(up, "cols", 1), ring(down, "cols", 3)
     b_part, mag_grad = call(
         functools.partial(b_unstack_kernel, gamma / float(full_rows) ** 0.5),
         [out((rank // 8, cols)), out((1, cols))],
         [VMEM] * 3,
         stack, swap(stack, "dp", 1), vec,
-        after=[up],
-    )
+        after=[top],
+    )
+    b_part = join([b_part, swap_x(b_part, 1)], far_bit, 0)
     top, bottom = call(
         pair_kernel,
         [out((rank, rows // 4))] * 2,
@@ -417,22 +429,17 @@
         top, swap(top, "dp", 1), bottom, swap(bottom, "dp", 0),
         after=[b_part],
     )
-    b_part = join([b_part, swap_x(b_part, 1)], far_bit, 0, after=[top])
-    grad, done = call(
-        finish_kernel,
-        [out((rows // 4, toks), BF16), out((8, 128))],
-        [VMEM] * 3,
-        own, w0, w1,
-        after=[b_part],
-    )
+    w_up, w_down = hold([w_up, w_down], [top])
+    w0, w1 = ring(w_up, "cols", 1), ring(w_down, "cols", 3)
     a_grad, done = call(
         a_join_kernel,
         [out((rank, rows)), out((8, 128))],
         [VMEM] * 4,
         top, swap(top, "dp", 0), bottom, swap(bottom, "dp", 1),
-        after=[done],
+        after=[w_up],
     )
     b_part = join([b_part, swap_x(b_part, 0)], near_bit, 0, after=[done])
+    grad = call(finish_kernel, [out((rows // 4, toks), BF16)], [VMEM] * 3, own, w0, w1, after=[b_part])[0]
     b_grad = join([b_part, swap_core(b_part)], core_bit, 0)
     return grad, a_grad.T, b_grad, mag_grad.reshape(cols)
 

time: 101 us -> 102 us (level)
  waiting for transfers between devices: 34.6 us -> 38.6 us
  starting transfers between devices: 33.4 us -> 31.3 us
    ppermute x4, waiting for transfers between devices: 10.9 us -> 14.9 us  [swap_x(): lax.ppermute(value, 'rows', [(i, i ^ 2 if step == 0 else 6 - 2 * (i // 2)...]
    ppermute x4, starting transfers between devices: 3.37 us -> 0.76 us  [swap_x(): lax.ppermute(value, 'rows', [(i, i ^ 2 if step == 0 else 6 - 2 * (i // 2)...]
    ppermute x3, waiting for transfers between devices: 2.7 us -> 1.18 us  [swap_core(): return lax.ppermute(value, 'rows', [(i, i ^ 1) for i in range(count)])]
    ppermute x8, waiting for transfers between devices: 9.97 us -> 11.2 us  [swap(): lax.ppermute(value, axis, [(i, i ^ 1 if step == 0 else 3 - i) for i in ra...]
  transfers between devices with their start and end apart: 27 -> 27, of which waited for: 16 -> 15; matrix products, arithmetic and copies ran while one was open for 0% -> 0% of each run, Pallas kernels for 11% -> 12%
where the time goes in v5:
time: 102 us; the launch traced here: 101 us
  waiting for transfers between devices  38.6 us (38%)
  starting transfers between devices  31.3 us (31%)
  Pallas kernels  30.7 us (30%)
    pallas_call x22, Pallas kernels, call(): pl.pallas_call(body, out_shape=outs, in_specs=list(specs) + [ANY] * len(a...  30.7 us
    ppermute x4, waiting for transfers between devices, swap_x(): lax.ppermute(value, 'rows', [(i, i ^ 2 if step == 0 else 6 - 2 * (i // 2)...  14.9 us
    ppermute x9, starting transfers between devices, ring(): lax.ppermute(value, axis, [(i, (i + k) % count) for i in range(count)])  14.8 us
    ppermute x8, waiting for transfers between devices, swap(): lax.ppermute(value, axis, [(i, i ^ 1 if step == 0 else 3 - i) for i in ra...  11.2 us
    ppermute x8, starting transfers between devices, swap(): lax.ppermute(value, axis, [(i, i ^ 1 if step == 0 else 3 - i) for i in ra...  10.9 us
    ppermute x9, waiting for transfers between devices, ring(): lax.ppermute(value, axis, [(i, (i + k) % count) for i in range(count)])  7.27 us
    ppermute x3, starting transfers between devices, ring_x(): lax.ppermute(value, 'rows', [(i, (i + 2 * k) % count) for i in range(coun...  4.59 us
    ppermute x3, waiting for transfers between devices, ring_x(): lax.ppermute(value, 'rows', [(i, (i + 2 * k) % count) for i in range(coun...  4.06 us
  transfers between devices with their start and end apart: 27, of which 15 were waited for; matrix products, arithmetic and copies ran while one was open for 0% of the time, Pallas kernels for 12%

profile of v5, /device:TPU:0, one launch (start us, length us, event | category | flops | bytes accessed | tf_op | source)
XLA Modules:
  0.0 101.4 jit_solution(502750072590795707)
XLA Ops:
  0.7 16.9 %shard_map.93 = (bf16[3584,2048]{1,0:T(8,128)(2,1)S(1)}, f32[2,2048]{1,0:T(2,128)S(1)}, f32[64,2048]{1,0:T(8,128)S(1)}, f32[64,2048]{1,0:T(8,128)S(1)}) custom-call(bf16[3584,2048]{1,0:T(8,128)(2,1)} %refs_0_.1, bf16[256,3584]{1,0:T(8,128)(2,1)} %refs_3_.3, bf16[64,3584]{1,0:T(8,128)(2,1)} %bitcast.6, bf16[64,2048]{1,0:T(8,128)(2,1)} %refs_2_.1, ...), custom_call_target="tpu_custom_call" | custom-call | flops 5637144576 | bytes 14680064 | tf_op jit(solution)/shard_map/pallas_call | solution.py:49
  17.7 1.2 %collective-permute-done = f32[2,2048]{1,0:T(2,128)S(1)} collective-permute-done((f32[2,2048]{1,0:T(2,128)S(1)}, f32[2,2048]{1,0:T(2,128)S(1)}, u32[]{:S(2)}, u32[]{:S(2)}) %collective-permute-start) | collective-permute-done | bytes 16416 | tf_op jit(solution)/shard_map/ppermute | solution.py:361
  18.9 2.9 %collective-permute-start.3 = (f32[2,2048]{1,0:T(2,128)S(1)}, f32[2,2048]{1,0:T(2,128)S(1)}, u32[]{:S(2)}, u32[]{:S(2)}) collective-permute-start(f32[2,2048]{1,0:T(2,128)S(1)} %add.3.refs_0_), channel_id=1, source_target_pairs={{0,24},{4,28},{8,0},{12,4},{16,8},{20,12},{24,16},{28,20},{1,25},{... | collective-permute-start | bytes 49160 | tf_op jit(solution)/shard_map/ppermute | solution.py:349
  22.6 0.9 collective-permute-start.1
  23.5 3.6 %collective-permute-done.2.refs_2_ = f32[2,2048]{1,0:T(2,128)S(1)} collective-permute-done((f32[2,2048]{1,0:T(2,128)S(1)}, f32[2,2048]{1,0:T(2,128)S(1)}, u32[]{:S(2)}, u32[]{:S(2)}) %collective-permute-start.2) | collective-permute-done | bytes 16416 | tf_op jit(solution)/shard_map/ppermute | solution.py:349
  27.5 1.2 %shard_map.94 = (f32[4,2048]{1,0:T(4,128)S(1)}, bf16[256,2048]{1,0:T(8,128)(2,1)S(1)}, f32[448,256]{1,0:T(8,128)S(1)}, f32[448,256]{1,0:T(8,128)S(1)}) custom-call(f32[2,2048]{1,0:T(2,128)S(1)} %add.3.refs_0_, f32[2,2048]{1,0:T(2,128)S(1)} %collective-permute-done.1.refs_1_, f32[2,2048]{1,0:T(2,128)S(1)} %collective-permute-done.2.refs_2_, ...), custom_call_target="tpu_custom_call" | custom-call | flops 1 | bytes 1 | tf_op jit(solution)/shard_map/pallas_call | solution.py:49
  28.7 1.6 %collective-permute-start.5 = (f32[448,256]{1,0:T(8,128)S(1)}, f32[448,256]{1,0:T(8,128)S(1)}, u32[]{:S(2)}, u32[]{:S(2)}) collective-permute-start(f32[448,256]{1,0:T(8,128)S(1)} %get-tuple-element.50), channel_id=1, source_target_pairs={{0,1},{1,2},{2,3},{3,0},{4,5},{5,6},{6,7},{7,4},{8,9},{9,10},{10,1... | collective-permute-start | bytes 1376264 | tf_op jit(solution)/shard_map/ppermute | solution.py:345
  30.3 1.7 %collective-permute-start.6 = (f32[448,256]{1,0:T(8,128)S(1)}, f32[448,256]{1,0:T(8,128)S(1)}, u32[]{:S(2)}, u32[]{:S(2)}) collective-permute-start(f32[448,256]{1,0:T(8,128)S(1)} %get-tuple-element.51), channel_id=1, source_target_pairs={{0,3},{1,0},{2,1},{3,2},{4,7},{5,4},{6,5},{7,6},{8,11},{9,8},{10,9... | collective-permute-start | bytes 1376264 | tf_op jit(solution)/shard_map/ppermute | solution.py:345
  32.3 5.3 %shard_map.96 = (f32[64,896]{1,0:T(8,128)S(1)}, f32[64,896]{1,0:T(8,128)S(1)}, f32[64,896]{1,0:T(8,128)S(1)}, f32[64,896]{1,0:T(8,128)S(1)}) custom-call(f32[4,2048]{1,0:T(4,128)S(1)} %get-tuple-element.41.refs_0_.refs_2_, bf16[256,2048]{1,0:T(8,128)(2,1)S(1)} %copy-done, bf16[64,2048]{1,0:T(8,128)(2,1)S(1)} %copy-done.2, bf16[256,3584]{1,0:T(8,128)(2,1)S(1)} %copy-done.1, ...), custom_call_target="tpu_custom_call" | custom-call | flops 1 | bytes 1 | tf_op jit(solution)/shard_map/pallas_call | solution.py:49
  37.6 4.0 %collective-permute-start.10 = (f32[64,896]{1,0:T(8,128)S(1)}, f32[64,896]{1,0:T(8,128)S(1)}, u32[]{:S(2)}, u32[]{:S(2)}) collective-permute-start(f32[64,896]{1,0:T(8,128)S(1)} %get-tuple-element.55), channel_id=1, source_target_pairs={{0,64},{32,96},{64,0},{96,32},{1,65},{33,97},{65,1},{97,33},{2,66}... | collective-permute-start | bytes 688136 | tf_op jit(solution)/shard_map/ppermute | solution.py:345
  41.6 1.0 collective-permute-start.11
  42.6 1.1 %shard_map.98 = (f32[448,256]{1,0:T(8,128)S(1)}, f32[448,256]{1,0:T(8,128)S(1)}) custom-call(bf16[3584,2048]{1,0:T(8,128)(2,1)S(1)} %get-tuple-element.38.refs_6_.refs_4_.refs_0_, bf16[256,2048]{1,0:T(8,128)(2,1)S(1)} %get-tuple-element.40.refs_1_, f32[16,2048]{1,0:T(8,128)S(1)} %get-tuple-element.47.refs_2_), custom_call_target="tpu_custom_call" | custom-call | flops 1 | bytes 1 | tf_op jit(solution)/shard_map/pallas_call | solution.py:49
  43.8 1.2 %shard_map.99.refs_2_.refs_0_ = f32[896,256]{1,0:T(8,128)S(1)} custom-call(bf16[3584,2048]{1,0:T(8,128)(2,1)S(1)} %get-tuple-element.38.refs_6_.refs_4_.refs_0_, bf16[256,2048]{1,0:T(8,128)(2,1)S(1)} %get-tuple-element.40.refs_1_, f32[448,256]{1,0:T(8,128)S(1)} %get-tuple-element.48.refs_2_.refs_0_), custom_call_target="tpu_custom_call" | custom-call | flops 1 | bytes 1 | tf_op jit(solution)/shard_map/pallas_call | solution.py:49
  45.0 2.1 %collective-permute-start.8 = (f32[448,256]{1,0:T(8,128)S(1)}, f32[448,256]{1,0:T(8,128)S(1)}, u32[]{:S(2)}, u32[]{:S(2)}) collective-permute-start(f32[448,256]{1,0:T(8,128)S(1)} %get-tuple-element.53), channel_id=1, source_target_pairs={{0,3},{1,0},{2,1},{3,2},{4,7},{5,4},{6,5},{7,6},{8,11},{9,8},{10,9... | collective-permute-start | bytes 1376264 | tf_op jit(solution)/shard_map/ppermute | solution.py:345
  47.2 2.2 %collective-permute-start.12 = (f32[64,896]{1,0:T(8,128)S(1)}, f32[64,896]{1,0:T(8,128)S(1)}, u32[]{:S(2)}, u32[]{:S(2)}) collective-permute-start(f32[64,896]{1,0:T(8,128)S(1)} %get-tuple-element.57), channel_id=1, source_target_pairs={{0,96},{32,0},{64,32},{96,64},{1,97},{33,1},{65,33},{97,65},{2,98}... | collective-permute-start | bytes 688136 | tf_op jit(solution)/shard_map/ppermute | solution.py:345
  49.5 1.1 %shard_map.101 = (f32[448,256]{1,0:T(8,128)S(1)}, f32[448,256]{1,0:T(8,128)S(1)}) custom-call(bf16[3584,2048]{1,0:T(8,128)(2,1)S(1)} %get-tuple-element.38.refs_6_.refs_4_.refs_0_, bf16[256,2048]{1,0:T(8,128)(2,1)S(1)} %get-tuple-element.40.refs_1_, f32[448,256]{1,0:T(8,128)S(1)} %collective-permute-done.5.refs_3_.refs_2_, ...), custom_call_target="tpu_custom_call" | custom-call | flops 1 | bytes 1 | tf_op jit(solution)/shard_map/pallas_call | solution.py:49
  50.6 2.1 %collective-permute-done.11.refs_2_ = f32[64,896]{1,0:T(8,128)S(1)} collective-permute-done((f32[64,896]{1,0:T(8,128)S(1)}, f32[64,896]{1,0:T(8,128)S(1)}, u32[]{:S(2)}, u32[]{:S(2)}) %collective-permute-start.11) | collective-permute-done | bytes 229408 | tf_op jit(solution)/shard_map/ppermute | solution.py:345
  52.7 1.4 %collective-permute-done.12.refs_3_ = f32[64,896]{1,0:T(8,128)S(1)} collective-permute-done((f32[64,896]{1,0:T(8,128)S(1)}, f32[64,896]{1,0:T(8,128)S(1)}, u32[]{:S(2)}, u32[]{:S(2)}) %collective-permute-start.12) | collective-permute-done | bytes 229408 | tf_op jit(solution)/shard_map/ppermute | solution.py:345
  54.6 5.0 %collective-permute-done.9.refs_1_ = f32[16,2048]{1,0:T(8,128)S(1)} collective-permute-done((f32[16,2048]{1,0:T(8,128)S(1)}, f32[16,2048]{1,0:T(8,128)S(1)}, u32[]{:S(2)}, u32[]{:S(2)}) %collective-permute-start.9) | collective-permute-done | bytes 131104 | tf_op jit(solution)/shard_map/ppermute | solution.py:357
  60.4 4.8 %collective-permute-done.14.refs_1_ = f32[8,2048]{1,0:T(8,128)S(1)} collective-permute-done((f32[8,2048]{1,0:T(8,128)S(1)}, f32[8,2048]{1,0:T(8,128)S(1)}, u32[]{:S(2)}, u32[]{:S(2)}) %collective-permute-start.14) | collective-permute-done | bytes 65568 | tf_op jit(solution)/shard_map/ppermute | solution.py:357
  65.2 2.8 %collective-permute-start.15 = (f32[64,896]{1,0:T(8,128)S(1)}, f32[64,896]{1,0:T(8,128)S(1)}, u32[]{:S(2)}, u32[]{:S(2)}) collective-permute-start(f32[64,896]{1,0:T(8,128)S(1)} %shard_map.106.refs_2_.refs_0_), channel_id=1, source_target_pairs={{0,3},{1,2},{2,1},{3,0},{4,7},{5,6},{6,5},{7,4},{8,11},{9,10},{10,... | collective-permute-start | bytes 688136 | tf_op jit(solution)/shard_map/ppermute | solution.py:353
  68.3 4.7 %collective-permute-done.16.refs_1_ = f32[16,2048]{1,0:T(8,128)S(1)} collective-permute-done((f32[16,2048]{1,0:T(8,128)S(1)}, f32[16,2048]{1,0:T(8,128)S(1)}, u32[]{:S(2)}, u32[]{:S(2)}) %collective-permute-start.16) | collective-permute-done | bytes 131104 | tf_op jit(solution)/shard_map/ppermute | solution.py:353
  73.0 3.7 %collective-permute-start.19 = (f32[16,2048]{1,0:T(8,128)S(1)}, f32[16,2048]{1,0:T(8,128)S(1)}, u32[]{:S(2)}, u32[]{:S(2)}) collective-permute-start(f32[16,2048]{1,0:T(8,128)S(1)} %shard_map.107.refs_2_.refs_0_), channel_id=1, source_target_pairs={{0,96},{32,64},{64,32},{96,0},{1,97},{33,65},{65,33},{97,1},{2,98}... | collective-permute-start | bytes 393224 | tf_op jit(solution)/shard_map/ppermute | solution.py:353
  77.1 2.5 %collective-permute-done.19.refs_1_ = f32[16,2048]{1,0:T(8,128)S(1)} collective-permute-done((f32[16,2048]{1,0:T(8,128)S(1)}, f32[16,2048]{1,0:T(8,128)S(1)}, u32[]{:S(2)}, u32[]{:S(2)}) %collective-permute-start.19) | collective-permute-done | bytes 131104 | tf_op jit(solution)/shard_map/ppermute | solution.py:353
  80.6 5.1 %collective-permute-done.20.refs_1_ = f32[8,2048]{1,0:T(8,128)S(1)} collective-permute-done((f32[8,2048]{1,0:T(8,128)S(1)}, f32[8,2048]{1,0:T(8,128)S(1)}, u32[]{:S(2)}, u32[]{:S(2)}) %collective-permute-start.20) | collective-permute-done | bytes 65568 | tf_op jit(solution)/shard_map/ppermute | solution.py:357
  85.8 3.3 %collective-permute-start.25 = (f32[64,896]{1,0:T(8,128)S(1)}, f32[64,896]{1,0:T(8,128)S(1)}, u32[]{:S(2)}, u32[]{:S(2)}) collective-permute-start(f32[64,896]{1,0:T(8,128)S(1)} %get-tuple-element.68.refs_2_), channel_id=1, source_target_pairs={{0,96},{32,64},{64,32},{96,0},{1,97},{33,65},{65,33},{97,1},{2,98}... | collective-permute-start | bytes 688136 | tf_op jit(solution)/shard_map/ppermute | solution.py:353
  90.0 1.1 %collective-permute-start.21 = (f32[448,256]{1,0:T(8,128)S(1)}, f32[448,256]{1,0:T(8,128)S(1)}, u32[]{:S(2)}, u32[]{:S(2)}) collective-permute-start(f32[448,256]{1,0:T(8,128)S(1)} %get-tuple-element.66.refs_4_), channel_id=1, source_target_pairs={{0,1},{1,2},{2,3},{3,0},{4,5},{5,6},{6,7},{7,4},{8,9},{9,10},{10,1... | collective-permute-start | bytes 1376264 | tf_op jit(solution)/shard_map/ppermute | solution.py:345
  91.2 2.0 %collective-permute-done.25.refs_3_ = f32[64,896]{1,0:T(8,128)S(1)} collective-permute-done((f32[64,896]{1,0:T(8,128)S(1)}, f32[64,896]{1,0:T(8,128)S(1)}, u32[]{:S(2)}, u32[]{:S(2)}) %collective-permute-start.25) | collective-permute-done | bytes 229408 | tf_op jit(solution)/shard_map/ppermute | solution.py:353
  93.2 2.0 %collective-permute-done.24.refs_1_ = f32[64,896]{1,0:T(8,128)S(1)} collective-permute-done((f32[64,896]{1,0:T(8,128)S(1)}, f32[64,896]{1,0:T(8,128)S(1)}, u32[]{:S(2)}, u32[]{:S(2)}) %collective-permute-start.24) | collective-permute-done | bytes 229408 | tf_op jit(solution)/shard_map/ppermute | solution.py:353
  95.2 1.0 shard_map.113
  96.3 1.3 %collective-permute-done.22.refs_2_ = f32[448,256]{1,0:T(8,128)S(1)} collective-permute-done((f32[448,256]{1,0:T(8,128)S(1)}, f32[448,256]{1,0:T(8,128)S(1)}, u32[]{:S(2)}, u32[]{:S(2)}) %collective-permute-start.22) | collective-permute-done | bytes 458784 | tf_op jit(solution)/shard_map/ppermute | solution.py:345
  97.6 2.1 %collective-permute-done.21.refs_1_ = f32[448,256]{1,0:T(8,128)S(1)} collective-permute-done((f32[448,256]{1,0:T(8,128)S(1)}, f32[448,256]{1,0:T(8,128)S(1)}, u32[]{:S(2)}, u32[]{:S(2)}) %collective-permute-start.21) | collective-permute-done | bytes 458784 | tf_op jit(solution)/shard_map/ppermute | solution.py:345
  (55 shorter events, 7.7 us)
Async XLA Ops:
  0.6 26.9 %copy-start = (bf16[256,2048]{1,0:T(8,128)(2,1)S(1)}, bf16[256,2048]{1,0:T(8,128)(2,1)}, u32[]{:S(2)}) copy-start(bf16[256,2048]{1,0:T(8,128)(2,1)} %refs_1_.3) | copy-start | bytes 3145732
  0.6 26.9 %copy-start.3 = (f32[2048]{0:T(1024)S(1)}, f32[2048]{0:T(1024)}, u32[]{:S(2)}) copy-start(f32[2048]{0:T(1024)} %param.11) | copy-start | bytes 24580
  0.7 31.6 %copy-start.1 = (bf16[256,3584]{1,0:T(8,128)(2,1)S(1)}, bf16[256,3584]{1,0:T(8,128)(2,1)}, u32[]{:S(2)}) copy-start(bf16[256,3584]{1,0:T(8,128)(2,1)} %refs_3_.3) | copy-start | bytes 5505028
  0.7 31.6 %copy-start.2 = (bf16[64,2048]{1,0:T(8,128)(2,1)S(1)}, bf16[64,2048]{1,0:T(8,128)(2,1)}, u32[]{:S(2)}) copy-start(bf16[64,2048]{1,0:T(8,128)(2,1)} %refs_2_.1) | copy-start | bytes 786436
  17.6 1.3 %collective-permute-start = (f32[2,2048]{1,0:T(2,128)S(1)}, f32[2,2048]{1,0:T(2,128)S(1)}, u32[]{:S(2)}, u32[]{:S(2)}) collective-permute-start(f32[2,2048]{1,0:T(2,128)S(1)} %get-tuple-element.39), channel_id=1, source_target_pairs={{0,4},{4,0},{8,12},{12,8},{16,20},{20,16},{24,28},{28,24},{1,5},{5... | collective-permute-start | bytes 49160 | tf_op jit(solution)/shard_map/ppermute | solution.py:361
  18.9 4.6 %collective-permute-start.3 = (f32[2,2048]{1,0:T(2,128)S(1)}, f32[2,2048]{1,0:T(2,128)S(1)}, u32[]{:S(2)}, u32[]{:S(2)}) collective-permute-start(f32[2,2048]{1,0:T(2,128)S(1)} %add.3.refs_0_), channel_id=1, source_target_pairs={{0,24},{4,28},{8,0},{12,4},{16,8},{20,12},{24,16},{28,20},{1,25},{... | collective-permute-start | bytes 49160 | tf_op jit(solution)/shard_map/ppermute | solution.py:349
  21.8 5.2 %collective-permute-start.2 = (f32[2,2048]{1,0:T(2,128)S(1)}, f32[2,2048]{1,0:T(2,128)S(1)}, u32[]{:S(2)}, u32[]{:S(2)}) collective-permute-start(f32[2,2048]{1,0:T(2,128)S(1)} %add.3.refs_0_), channel_id=1, source_target_pairs={{0,16},{4,20},{8,24},{12,28},{16,0},{20,4},{24,8},{28,12},{1,17},{... | collective-permute-start | bytes 49160 | tf_op jit(solution)/shard_map/ppermute | solution.py:349
  22.6 4.9 %collective-permute-start.1 = (f32[2,2048]{1,0:T(2,128)S(1)}, f32[2,2048]{1,0:T(2,128)S(1)}, u32[]{:S(2)}, u32[]{:S(2)}) collective-permute-start(f32[2,2048]{1,0:T(2,128)S(1)} %add.3.refs_0_), channel_id=1, source_target_pairs={{0,8},{4,12},{8,16},{12,20},{16,24},{20,28},{24,0},{28,4},{1,9},{5... | collective-permute-start | bytes 49160 | tf_op jit(solution)/shard_map/ppermute | solution.py:349
  28.7 16.2 %collective-permute-start.5 = (f32[448,256]{1,0:T(8,128)S(1)}, f32[448,256]{1,0:T(8,128)S(1)}, u32[]{:S(2)}, u32[]{:S(2)}) collective-permute-start(f32[448,256]{1,0:T(8,128)S(1)} %get-tuple-element.50), channel_id=1, source_target_pairs={{0,1},{1,2},{2,3},{3,0},{4,5},{5,6},{6,7},{7,4},{8,9},{9,10},{10,1... | collective-permute-start | bytes 1376264 | tf_op jit(solution)/shard_map/ppermute | solution.py:345
  30.3 14.6 %collective-permute-start.6 = (f32[448,256]{1,0:T(8,128)S(1)}, f32[448,256]{1,0:T(8,128)S(1)}, u32[]{:S(2)}, u32[]{:S(2)}) collective-permute-start(f32[448,256]{1,0:T(8,128)S(1)} %get-tuple-element.51), channel_id=1, source_target_pairs={{0,3},{1,0},{2,1},{3,2},{4,7},{5,4},{6,5},{7,6},{8,11},{9,8},{10,9... | collective-permute-start | bytes 1376264 | tf_op jit(solution)/shard_map/ppermute | solution.py:345
  32.2 10.4 %collective-permute-start.4 = (f32[32,2048]{1,0:T(8,128)S(1)}, f32[32,2048]{1,0:T(8,128)S(1)}, u32[]{:S(2)}, u32[]{:S(2)}) collective-permute-start(f32[32,2048]{1,0:T(8,128)S(1)} %get-tuple-element.45.refs_5_), channel_id=1, source_target_pairs={{0,4},{4,0},{8,12},{12,8},{16,20},{20,16},{24,28},{28,24},{1,5},{5... | collective-permute-start | bytes 786440 | tf_op jit(solution)/shard_map/ppermute | solution.py:361
  37.6 13.0 %collective-permute-start.10 = (f32[64,896]{1,0:T(8,128)S(1)}, f32[64,896]{1,0:T(8,128)S(1)}, u32[]{:S(2)}, u32[]{:S(2)}) collective-permute-start(f32[64,896]{1,0:T(8,128)S(1)} %get-tuple-element.55), channel_id=1, source_target_pairs={{0,64},{32,96},{64,0},{96,32},{1,65},{33,97},{65,1},{97,33},{2,66}... | collective-permute-start | bytes 688136 | tf_op jit(solution)/shard_map/ppermute | solution.py:345
  41.6 11.2 %collective-permute-start.11 = (f32[64,896]{1,0:T(8,128)S(1)}, f32[64,896]{1,0:T(8,128)S(1)}, u32[]{:S(2)}, u32[]{:S(2)}) collective-permute-start(f32[64,896]{1,0:T(8,128)S(1)} %get-tuple-element.56), channel_id=1, source_target_pairs={{0,32},{32,64},{64,96},{96,0},{1,33},{33,65},{65,97},{97,1},{2,34}... | collective-permute-start | bytes 688136 | tf_op jit(solution)/shard_map/ppermute | solution.py:345
  45.0 15.0 %collective-permute-start.8 = (f32[448,256]{1,0:T(8,128)S(1)}, f32[448,256]{1,0:T(8,128)S(1)}, u32[]{:S(2)}, u32[]{:S(2)}) collective-permute-start(f32[448,256]{1,0:T(8,128)S(1)} %get-tuple-element.53), channel_id=1, source_target_pairs={{0,3},{1,0},{2,1},{3,2},{4,7},{5,4},{6,5},{7,6},{8,11},{9,8},{10,9... | collective-permute-start | bytes 1376264 | tf_op jit(solution)/shard_map/ppermute | solution.py:345
  47.0 13.3 %collective-permute-start.7 = (f32[448,256]{1,0:T(8,128)S(1)}, f32[448,256]{1,0:T(8,128)S(1)}, u32[]{:S(2)}, u32[]{:S(2)}) collective-permute-start(f32[448,256]{1,0:T(8,128)S(1)} %get-tuple-element.52.refs_4_), channel_id=1, source_target_pairs={{0,1},{1,2},{2,3},{3,0},{4,5},{5,6},{6,7},{7,4},{8,9},{9,10},{10,1... | collective-permute-start | bytes 1376264 | tf_op jit(solution)/shard_map/ppermute | solution.py:345
  47.2 6.9 %collective-permute-start.12 = (f32[64,896]{1,0:T(8,128)S(1)}, f32[64,896]{1,0:T(8,128)S(1)}, u32[]{:S(2)}, u32[]{:S(2)}) collective-permute-start(f32[64,896]{1,0:T(8,128)S(1)} %get-tuple-element.57), channel_id=1, source_target_pairs={{0,96},{32,0},{64,32},{96,64},{1,97},{33,1},{65,33},{97,65},{2,98}... | collective-permute-start | bytes 688136 | tf_op jit(solution)/shard_map/ppermute | solution.py:345
  54.2 11.0 %collective-permute-start.13 = (f32[64,896]{1,0:T(8,128)S(1)}, f32[64,896]{1,0:T(8,128)S(1)}, u32[]{:S(2)}, u32[]{:S(2)}) collective-permute-start(f32[64,896]{1,0:T(8,128)S(1)} %shard_map.102.refs_2_.refs_0_), channel_id=1, source_target_pairs={{0,1},{1,0},{2,3},{3,2},{4,5},{5,4},{6,7},{7,6},{8,9},{9,8},{10,11... | collective-permute-start | bytes 688136 | tf_op jit(solution)/shard_map/ppermute | solution.py:353
  54.6 5.0 %collective-permute-start.9 = (f32[16,2048]{1,0:T(8,128)S(1)}, f32[16,2048]{1,0:T(8,128)S(1)}, u32[]{:S(2)}, u32[]{:S(2)}) collective-permute-start(f32[16,2048]{1,0:T(8,128)S(1)} %get-tuple-element.47.refs_2_), channel_id=1, source_target_pairs={{0,8},{4,12},{8,0},{12,4},{16,24},{20,28},{24,16},{28,20},{1,9},{5... | collective-permute-start | bytes 393224 | tf_op jit(solution)/shard_map/ppermute | solution.py:357
  59.6 5.6 %collective-permute-start.14 = (f32[8,2048]{1,0:T(8,128)S(1)}, f32[8,2048]{1,0:T(8,128)S(1)}, u32[]{:S(2)}, u32[]{:S(2)}) collective-permute-start(f32[8,2048]{1,0:T(8,128)S(1)} %get-tuple-element.59.refs_3_), channel_id=1, source_target_pairs={{0,24},{4,28},{8,16},{12,20},{16,8},{20,12},{24,0},{28,4},{1,25},{... | collective-permute-start | bytes 196616 | tf_op jit(solution)/shard_map/ppermute | solution.py:357
  65.2 11.5 %collective-permute-start.15 = (f32[64,896]{1,0:T(8,128)S(1)}, f32[64,896]{1,0:T(8,128)S(1)}, u32[]{:S(2)}, u32[]{:S(2)}) collective-permute-start(f32[64,896]{1,0:T(8,128)S(1)} %shard_map.106.refs_2_.refs_0_), channel_id=1, source_target_pairs={{0,3},{1,2},{2,1},{3,0},{4,7},{5,6},{6,5},{7,4},{8,11},{9,10},{10,... | collective-permute-start | bytes 688136 | tf_op jit(solution)/shard_map/ppermute | solution.py:353
  68.0 5.0 %collective-permute-start.16 = (f32[16,2048]{1,0:T(8,128)S(1)}, f32[16,2048]{1,0:T(8,128)S(1)}, u32[]{:S(2)}, u32[]{:S(2)}) collective-permute-start(f32[16,2048]{1,0:T(8,128)S(1)} %shard_map.105.refs_2_.refs_0_), channel_id=1, source_target_pairs={{0,32},{32,0},{64,96},{96,64},{1,33},{33,1},{65,97},{97,65},{2,34}... | collective-permute-start | bytes 393224 | tf_op jit(solution)/shard_map/ppermute | solution.py:353
  73.0 6.6 %collective-permute-start.19 = (f32[16,2048]{1,0:T(8,128)S(1)}, f32[16,2048]{1,0:T(8,128)S(1)}, u32[]{:S(2)}, u32[]{:S(2)}) collective-permute-start(f32[16,2048]{1,0:T(8,128)S(1)} %shard_map.107.refs_2_.refs_0_), channel_id=1, source_target_pairs={{0,96},{32,64},{64,32},{96,0},{1,97},{33,65},{65,33},{97,1},{2,98}... | collective-permute-start | bytes 393224 | tf_op jit(solution)/shard_map/ppermute | solution.py:353
  76.7 9.0 %collective-permute-start.18 = (f32[32,896]{1,0:T(8,128)S(1)}, f32[32,896]{1,0:T(8,128)S(1)}, u32[]{:S(2)}, u32[]{:S(2)}) collective-permute-start(f32[32,896]{1,0:T(8,128)S(1)} %get-tuple-element.63.refs_2_), channel_id=1, source_target_pairs={{0,32},{32,0},{64,96},{96,64},{1,33},{33,1},{65,97},{97,65},{2,34}... | collective-permute-start | bytes 344072 | tf_op jit(solution)/shard_map/ppermute | solution.py:353
  76.8 9.0 %collective-permute-start.17 = (f32[32,896]{1,0:T(8,128)S(1)}, f32[32,896]{1,0:T(8,128)S(1)}, u32[]{:S(2)}, u32[]{:S(2)}) collective-permute-start(f32[32,896]{1,0:T(8,128)S(1)} %get-tuple-element.62.refs_3_.refs_0_), channel_id=1, source_target_pairs={{0,96},{32,64},{64,32},{96,0},{1,97},{33,65},{65,33},{97,1},{2,98}... | collective-permute-start | bytes 344072 | tf_op jit(solution)/shard_map/ppermute | solution.py:353
  80.3 5.5 %collective-permute-start.20 = (f32[8,2048]{1,0:T(8,128)S(1)}, f32[8,2048]{1,0:T(8,128)S(1)}, u32[]{:S(2)}, u32[]{:S(2)}) collective-permute-start(f32[8,2048]{1,0:T(8,128)S(1)} %get-tuple-element.64.refs_0_), channel_id=1, source_target_pairs={{0,24},{4,28},{8,16},{12,20},{16,8},{20,12},{24,0},{28,4},{1,25},{... | collective-permute-start | bytes 196616 | tf_op jit(solution)/shard_map/ppermute | solution.py:357
  85.8 7.3 %collective-permute-start.25 = (f32[64,896]{1,0:T(8,128)S(1)}, f32[64,896]{1,0:T(8,128)S(1)}, u32[]{:S(2)}, u32[]{:S(2)}) collective-permute-start(f32[64,896]{1,0:T(8,128)S(1)} %get-tuple-element.68.refs_2_), channel_id=1, source_target_pairs={{0,96},{32,64},{64,32},{96,0},{1,97},{33,65},{65,33},{97,1},{2,98}... | collective-permute-start | bytes 688136 | tf_op jit(solution)/shard_map/ppermute | solution.py:353
  89.2 6.0 %collective-permute-start.24 = (f32[64,896]{1,0:T(8,128)S(1)}, f32[64,896]{1,0:T(8,128)S(1)}, u32[]{:S(2)}, u32[]{:S(2)}) collective-permute-start(f32[64,896]{1,0:T(8,128)S(1)} %get-tuple-element.65.refs_2_.refs_0_), channel_id=1, source_target_pairs={{0,32},{32,0},{64,96},{96,64},{1,33},{33,1},{65,97},{97,65},{2,34}... | collective-permute-start | bytes 688136 | tf_op jit(solution)/shard_map/ppermute | solution.py:353
  89.2 8.5 %collective-permute-start.22 = (f32[448,256]{1,0:T(8,128)S(1)}, f32[448,256]{1,0:T(8,128)S(1)}, u32[]{:S(2)}, u32[]{:S(2)}) collective-permute-start(f32[448,256]{1,0:T(8,128)S(1)} %get-tuple-element.67), channel_id=1, source_target_pairs={{0,3},{1,0},{2,1},{3,2},{4,7},{5,4},{6,5},{7,6},{8,11},{9,8},{10,9... | collective-permute-start | bytes 1376264 | tf_op jit(solution)/shard_map/ppermute | solution.py:345
  90.0 9.7 %collective-permute-start.21 = (f32[448,256]{1,0:T(8,128)S(1)}, f32[448,256]{1,0:T(8,128)S(1)}, u32[]{:S(2)}, u32[]{:S(2)}) collective-permute-start(f32[448,256]{1,0:T(8,128)S(1)} %get-tuple-element.66.refs_4_), channel_id=1, source_target_pairs={{0,1},{1,2},{2,3},{3,0},{4,5},{5,6},{6,7},{7,4},{8,9},{9,10},{10,1... | collective-permute-start | bytes 1376264 | tf_op jit(solution)/shard_map/ppermute | solution.py:345
  91.2 5.0 %collective-permute-start.23 = (f32[16,2048]{1,0:T(8,128)S(1)}, f32[16,2048]{1,0:T(8,128)S(1)}, u32[]{:S(2)}, u32[]{:S(2)}) collective-permute-start(f32[16,2048]{1,0:T(8,128)S(1)} %shard_map.110.refs_4_.refs_0_), channel_id=1, source_target_pairs={{0,8},{4,12},{8,0},{12,4},{16,24},{20,28},{24,16},{28,20},{1,9},{5... | collective-permute-start | bytes 393224 | tf_op jit(solution)/shard_map/ppermute | solution.py:357
  96.2 4.4 %collective-permute-start.26 = (f32[32,2048]{1,0:T(8,128)S(1)}, f32[32,2048]{1,0:T(8,128)S(1)}, u32[]{:S(2)}, u32[]{:S(2)}) collective-permute-start(f32[32,2048]{1,0:T(8,128)S(1)} %shard_map.114.refs_3_.refs_0_), channel_id=1, source_target_pairs={{0,4},{4,0},{8,12},{12,8},{16,20},{20,16},{24,28},{28,24},{1,5},{5... | collective-permute-start | bytes 786440 | tf_op jit(solution)/shard_map/ppermute | solution.py:361

commit v6 on v4

--- a/solution.py
+++ b/solution.py
@@ -55,6 +55,18 @@
         compiler_params=pltpu.CompilerParams(vmem_limit_bytes=vmem * MIB),
         cost_estimate=pl.CostEstimate(flops=flops, bytes_accessed=data, transcendentals=0),
     )(*args, *after)
+
+
+def hold(values, after):
+    count = len(values)
+    return pl.pallas_call(
+        lambda *refs: None,
+        out_shape=[out(value.shape, value.dtype) for value in values],
+        in_specs=[ANY] * (count + len(after)),
+        out_specs=[ANY] * count,
+        input_output_aliases={k: k for k in range(count)},
+        compiler_params=pltpu.CompilerParams(vmem_limit_bytes=MIB),
+    )(*values, *after)
 
 
 def out(shape, dtype=F32):
@@ -186,10 +198,10 @@
 
 
 def finish_kernel(own_ref, w0_ref, w1_ref, out_ref, done_ref):
+    done_ref[...] = jnp.zeros_like(done_ref)
     half = own_ref.shape[0] // 2
     out_ref[:half] = (own_ref[:half] + w0_ref[...]).astype(BF16)
     out_ref[half:] = (own_ref[half:] + w1_ref[...]).astype(BF16)
-    done_ref[...] = jnp.zeros_like(done_ref)
 
 
 def a_kernel(factor, vec_ref, dy_ref, b_ref, x_ref, m_ref, *refs):
@@ -390,8 +402,9 @@
     keep, send = halve(keep, swap_x(send, 0), far_bit, after=[pieces[0]])
     pieces = [pieces[0]] + [ring(pieces[k], "dp", k) for k in (2, 1, 3)]
     own = call(own_kernel, [out((rows // 4, toks))], [VMEM] * 2, m, scaled, after=[send, u0, u1])[0]
-
-    own = call(gather_kernel, [out((rows // 4, toks))], [VMEM] * 3, own, v0, v1)[0]
+    up, down = call(relay_kernel, half, [VMEM] * 4, m, scaled, u0, u1, after=[own])
+    own = call(gather_kernel, [out((rows // 4, toks))], [VMEM] * 3, own, v0, v1, after=[up])[0]
+
     piece = add(*pieces, after=[own])
     stack = call(
         b_stack_kernel, [out((rank // 4, cols))], [VMEM] * 3, keep, swap_x(send, 1), vec, after=[piece]
@@ -399,17 +412,18 @@
     piece = add(piece, swap(piece, "cols", 0), after=[stack])
     last = (piece, swap(piece, "cols", 1))
     stack = add(stack, swap(stack, "dp", 0), after=[piece])
+    up, down = hold([up, down], [stack])
+    w0, w1 = ring(up, "cols", 1), ring(down, "cols", 3)
     piece = [out((rank // 2, rows // 4))] * 2
-    top, bottom = call(add_halves_kernel, piece, [VMEM] * 2, *last, after=[stack])
-    up, down = call(relay_kernel, half, [VMEM] * 4, m, scaled, u0, u1, after=[top])
-    w0, w1 = ring(up, "cols", 1), ring(down, "cols", 3)
+    top, bottom = call(add_halves_kernel, piece, [VMEM] * 2, *last, after=[up])
     b_part, mag_grad = call(
         functools.partial(b_unstack_kernel, gamma / float(full_rows) ** 0.5),
         [out((rank // 8, cols)), out((1, cols))],
         [VMEM] * 3,
         stack, swap(stack, "dp", 1), vec,
-        after=[up],
-    )
+        after=[top],
+    )
+    b_part = join([b_part, swap_x(b_part, 1)], far_bit, 0)
     top, bottom = call(
         pair_kernel,
         [out((rank, rows // 4))] * 2,
@@ -417,13 +431,8 @@
         top, swap(top, "dp", 1), bottom, swap(bottom, "dp", 0),
         after=[b_part],
     )
-    b_part = join([b_part, swap_x(b_part, 1)], far_bit, 0, after=[top])
     grad, done = call(
-        finish_kernel,
-        [out((rows // 4, toks), BF16), out((8, 128))],
-        [VMEM] * 3,
-        own, w0, w1,
-        after=[b_part],
+        finish_kernel, [out((rows // 4, toks), BF16), out((8, 128))], [VMEM] * 3, own, w0, w1, after=[top]
     )
     a_grad, done = call(
         a_join_kernel,

time: 101 us -> 96.5 us (0.955)
  waiting for transfers between devices: 34.6 us -> 26.9 us
  starting transfers between devices: 33.4 us -> 36.9 us
    ppermute x8, waiting for transfers between devices: 9.97 us -> 6.71 us  [swap(): lax.ppermute(value, axis, [(i, i ^ 1 if step == 0 else 3 - i) for i in ra...]
    ppermute x4, waiting for transfers between devices: 10.9 us -> 7.69 us  [swap_x(): lax.ppermute(value, 'rows', [(i, i ^ 2 if step == 0 else 6 - 2 * (i // 2)...]
    ppermute x8, starting transfers between devices: 10.4 us -> 13.3 us  [swap(): lax.ppermute(value, axis, [(i, i ^ 1 if step == 0 else 3 - i) for i in ra...]
    ppermute x9, waiting for transfers between devices: 6.91 us -> 5.76 us  [ring(): lax.ppermute(value, axis, [(i, (i + k) % count) for i in range(count)])]
  transfers between devices with their start and end apart: 27 -> 27, of which waited for: 16 -> 15; matrix products, arithmetic and copies ran while one was open for 0% -> 0% of each run, Pallas kernels for 11% -> 12%
where the time goes in v6:
time: 96.5 us; the launch traced here: 95.3 us
  starting transfers between devices  36.9 us (38%)
  Pallas kernels  30.6 us (32%)
  waiting for transfers between devices  26.9 us (28%)
    pallas_call x22, Pallas kernels, call(): pl.pallas_call(body, out_shape=outs, in_specs=list(specs) + [ANY] * len(a...  30.6 us
    ppermute x9, starting transfers between devices, ring(): lax.ppermute(value, axis, [(i, (i + k) % count) for i in range(count)])  15.3 us
    ppermute x8, starting transfers between devices, swap(): lax.ppermute(value, axis, [(i, i ^ 1 if step == 0 else 3 - i) for i in ra...  13.3 us
    ppermute x4, waiting for transfers between devices, swap_x(): lax.ppermute(value, 'rows', [(i, i ^ 2 if step == 0 else 6 - 2 * (i // 2)...  7.69 us
    ppermute x8, waiting for transfers between devices, swap(): lax.ppermute(value, axis, [(i, i ^ 1 if step == 0 else 3 - i) for i in ra...  6.71 us
    ppermute x9, waiting for transfers between devices, ring(): lax.ppermute(value, axis, [(i, (i + k) % count) for i in range(count)])  5.76 us
    ppermute x3, starting transfers between devices, ring_x(): lax.ppermute(value, 'rows', [(i, (i + 2 * k) % count) for i in range(coun...  4.59 us
    ppermute x3, waiting for transfers between devices, ring_x(): lax.ppermute(value, 'rows', [(i, (i + 2 * k) % count) for i in range(coun...  4.06 us
  transfers between devices with their start and end apart: 27, of which 15 were waited for; matrix products, arithmetic and copies ran while one was open for 0% of the time, Pallas kernels for 12%

profile of v6, /device:TPU:0, one launch (start us, length us, event | category | flops | bytes accessed | tf_op | source)
XLA Modules:
  0.0 95.3 jit_solution(8887584442211721075)
XLA Ops:
  0.7 16.8 %shard_map.93 = (bf16[3584,2048]{1,0:T(8,128)(2,1)S(1)}, f32[2,2048]{1,0:T(2,128)S(1)}, f32[64,2048]{1,0:T(8,128)S(1)}, f32[64,2048]{1,0:T(8,128)S(1)}) custom-call(bf16[3584,2048]{1,0:T(8,128)(2,1)} %refs_0_.1, bf16[256,3584]{1,0:T(8,128)(2,1)} %refs_3_.3, bf16[64,3584]{1,0:T(8,128)(2,1)} %bitcast.6, bf16[64,2048]{1,0:T(8,128)(2,1)} %refs_2_.1, ...), custom_call_target="tpu_custom_call" | custom-call | flops 5637144576 | bytes 14680064 | tf_op jit(solution)/shard_map/pallas_call | solution.py:49
  17.6 1.2 %collective-permute-done = f32[2,2048]{1,0:T(2,128)S(1)} collective-permute-done((f32[2,2048]{1,0:T(2,128)S(1)}, f32[2,2048]{1,0:T(2,128)S(1)}, u32[]{:S(2)}, u32[]{:S(2)}) %collective-permute-start) | collective-permute-done | bytes 16416 | tf_op jit(solution)/shard_map/ppermute | solution.py:362
  18.8 2.9 %collective-permute-start.3 = (f32[2,2048]{1,0:T(2,128)S(1)}, f32[2,2048]{1,0:T(2,128)S(1)}, u32[]{:S(2)}, u32[]{:S(2)}) collective-permute-start(f32[2,2048]{1,0:T(2,128)S(1)} %add.3.refs_0_), channel_id=1, source_target_pairs={{0,24},{4,28},{8,0},{12,4},{16,8},{20,12},{24,16},{28,20},{1,25},{... | collective-permute-start | bytes 49160 | tf_op jit(solution)/shard_map/ppermute | solution.py:350
  23.4 3.6 %collective-permute-done.2.refs_2_ = f32[2,2048]{1,0:T(2,128)S(1)} collective-permute-done((f32[2,2048]{1,0:T(2,128)S(1)}, f32[2,2048]{1,0:T(2,128)S(1)}, u32[]{:S(2)}, u32[]{:S(2)}) %collective-permute-start.2) | collective-permute-done | bytes 16416 | tf_op jit(solution)/shard_map/ppermute | solution.py:350
  27.4 1.2 %shard_map.94 = (f32[4,2048]{1,0:T(4,128)S(1)}, bf16[256,2048]{1,0:T(8,128)(2,1)S(1)}, f32[448,256]{1,0:T(8,128)S(1)}, f32[448,256]{1,0:T(8,128)S(1)}) custom-call(f32[2,2048]{1,0:T(2,128)S(1)} %add.3.refs_0_, f32[2,2048]{1,0:T(2,128)S(1)} %collective-permute-done.1.refs_1_, f32[2,2048]{1,0:T(2,128)S(1)} %collective-permute-done.2.refs_2_, ...), custom_call_target="tpu_custom_call" | custom-call | flops 1 | bytes 1 | tf_op jit(solution)/shard_map/pallas_call | solution.py:49
  28.6 1.6 %collective-permute-start.6 = (f32[448,256]{1,0:T(8,128)S(1)}, f32[448,256]{1,0:T(8,128)S(1)}, u32[]{:S(2)}, u32[]{:S(2)}) collective-permute-start(f32[448,256]{1,0:T(8,128)S(1)} %get-tuple-element.51), channel_id=1, source_target_pairs={{0,1},{1,2},{2,3},{3,0},{4,5},{5,6},{6,7},{7,4},{8,9},{9,10},{10,1... | collective-permute-start | bytes 1376264 | tf_op jit(solution)/shard_map/ppermute | solution.py:346
  30.3 1.7 %collective-permute-start.7 = (f32[448,256]{1,0:T(8,128)S(1)}, f32[448,256]{1,0:T(8,128)S(1)}, u32[]{:S(2)}, u32[]{:S(2)}) collective-permute-start(f32[448,256]{1,0:T(8,128)S(1)} %get-tuple-element.52), channel_id=1, source_target_pairs={{0,3},{1,0},{2,1},{3,2},{4,7},{5,4},{6,5},{7,6},{8,11},{9,8},{10,9... | collective-permute-start | bytes 1376264 | tf_op jit(solution)/shard_map/ppermute | solution.py:346
  32.2 1.1 %shard_map.96 = (f32[448,256]{1,0:T(8,128)S(1)}, f32[448,256]{1,0:T(8,128)S(1)}) custom-call(bf16[3584,2048]{1,0:T(8,128)(2,1)S(1)} %get-tuple-element.38.refs_6_.refs_0_.refs_4_, bf16[256,2048]{1,0:T(8,128)(2,1)S(1)} %get-tuple-element.40.refs_1_, f32[32,2048]{1,0:T(8,128)S(1)} %get-tuple-element.45.refs_2_), custom_call_target="tpu_custom_call" | custom-call | flops 1 | bytes 1 | tf_op jit(solution)/shard_map/pallas_call | solution.py:49
  33.3 1.9 %collective-permute-start.9 = (f32[448,256]{1,0:T(8,128)S(1)}, f32[448,256]{1,0:T(8,128)S(1)}, u32[]{:S(2)}, u32[]{:S(2)}) collective-permute-start(f32[448,256]{1,0:T(8,128)S(1)} %get-tuple-element.53), channel_id=1, source_target_pairs={{0,3},{1,0},{2,1},{3,2},{4,7},{5,4},{6,5},{7,6},{8,11},{9,8},{10,9... | collective-permute-start | bytes 1376264 | tf_op jit(solution)/shard_map/ppermute | solution.py:346
  35.6 5.3 %shard_map.98 = (f32[64,896]{1,0:T(8,128)S(1)}, f32[64,896]{1,0:T(8,128)S(1)}, f32[64,896]{1,0:T(8,128)S(1)}, f32[64,896]{1,0:T(8,128)S(1)}) custom-call(f32[4,2048]{1,0:T(4,128)S(1)} %get-tuple-element.41.refs_0_.refs_2_, bf16[256,2048]{1,0:T(8,128)(2,1)S(1)} %copy-done, bf16[64,2048]{1,0:T(8,128)(2,1)S(1)} %copy-done.2, bf16[256,3584]{1,0:T(8,128)(2,1)S(1)} %copy-done.1, ...), custom_call_target="tpu_custom_call" | custom-call | flops 1 | bytes 1 | tf_op jit(solution)/shard_map/pallas_call | solution.py:49
  41.0 3.9 %collective-permute-start.11 = (f32[64,896]{1,0:T(8,128)S(1)}, f32[64,896]{1,0:T(8,128)S(1)}, u32[]{:S(2)}, u32[]{:S(2)}) collective-permute-start(f32[64,896]{1,0:T(8,128)S(1)} %get-tuple-element.57), channel_id=1, source_target_pairs={{0,64},{32,96},{64,0},{96,32},{1,65},{33,97},{65,1},{97,33},{2,66}... | collective-permute-start | bytes 688136 | tf_op jit(solution)/shard_map/ppermute | solution.py:346
  44.9 1.0 %collective-permute-start.12 = (f32[64,896]{1,0:T(8,128)S(1)}, f32[64,896]{1,0:T(8,128)S(1)}, u32[]{:S(2)}, u32[]{:S(2)}) collective-permute-start(f32[64,896]{1,0:T(8,128)S(1)} %get-tuple-element.58), channel_id=1, source_target_pairs={{0,32},{32,64},{64,96},{96,0},{1,33},{33,65},{65,97},{97,1},{2,34}... | collective-permute-start | bytes 688136 | tf_op jit(solution)/shard_map/ppermute | solution.py:346
  45.9 2.2 %collective-permute-start.13 = (f32[64,896]{1,0:T(8,128)S(1)}, f32[64,896]{1,0:T(8,128)S(1)}, u32[]{:S(2)}, u32[]{:S(2)}) collective-permute-start(f32[64,896]{1,0:T(8,128)S(1)} %get-tuple-element.59), channel_id=1, source_target_pairs={{0,96},{32,0},{64,32},{96,64},{1,97},{33,1},{65,33},{97,65},{2,98}... | collective-permute-start | bytes 688136 | tf_op jit(solution)/shard_map/ppermute | solution.py:346
  48.2 1.1 %shard_map.100.refs_4_.refs_0_ = f32[896,256]{1,0:T(8,128)S(1)} custom-call(bf16[3584,2048]{1,0:T(8,128)(2,1)S(1)} %get-tuple-element.38.refs_6_.refs_0_.refs_4_, bf16[256,2048]{1,0:T(8,128)(2,1)S(1)} %get-tuple-element.40.refs_1_, f32[8,2048]{1,0:T(8,128)S(1)} %get-tuple-element.50.refs_2_, f32[448,256]{1,0:T(8,128)S(1)} %collective-permute-done.6.refs_3_.refs_2_, ...), custom_call_target="tpu_custom_call" | custom-call | flops 1 | bytes 1 | tf_op jit(solution)/shard_map/pallas_call | solution.py:49
  49.3 1.1 %shard_map.101 = (f32[448,256]{1,0:T(8,128)S(1)}, f32[448,256]{1,0:T(8,128)S(1)}) custom-call(bf16[3584,2048]{1,0:T(8,128)(2,1)S(1)} %get-tuple-element.38.refs_6_.refs_0_.refs_4_, bf16[256,2048]{1,0:T(8,128)(2,1)S(1)} %get-tuple-element.40.refs_1_, f32[448,256]{1,0:T(8,128)S(1)} %collective-permute-done.6.refs_3_.refs_2_, ...), custom_call_target="tpu_custom_call" | custom-call | flops 1 | bytes 1 | tf_op jit(solution)/shard_map/pallas_call | solution.py:49
  51.3 4.2 %collective-permute-done.12.refs_2_ = f32[64,896]{1,0:T(8,128)S(1)} collective-permute-done((f32[64,896]{1,0:T(8,128)S(1)}, f32[64,896]{1,0:T(8,128)S(1)}, u32[]{:S(2)}, u32[]{:S(2)}) %collective-permute-start.12) | collective-permute-done | bytes 229408 | tf_op jit(solution)/shard_map/ppermute | solution.py:346
  56.8 1.7 %collective-permute-start.10 = (f32[8,2048]{1,0:T(8,128)S(1)}, f32[8,2048]{1,0:T(8,128)S(1)}, u32[]{:S(2)}, u32[]{:S(2)}) collective-permute-start(f32[8,2048]{1,0:T(8,128)S(1)} %get-tuple-element.50.refs_2_), channel_id=1, source_target_pairs={{0,24},{4,28},{8,16},{12,20},{16,8},{20,12},{24,0},{28,4},{1,25},{... | collective-permute-start | bytes 196616 | tf_op jit(solution)/shard_map/ppermute | solution.py:358
  58.5 3.7 %collective-permute-done.10.refs_1_ = f32[8,2048]{1,0:T(8,128)S(1)} collective-permute-done((f32[8,2048]{1,0:T(8,128)S(1)}, f32[8,2048]{1,0:T(8,128)S(1)}, u32[]{:S(2)}, u32[]{:S(2)}) %collective-permute-start.10) | collective-permute-done | bytes 65568 | tf_op jit(solution)/shard_map/ppermute | solution.py:358
  62.3 1.1 %collective-permute-start.14 = (f32[16,2048]{1,0:T(8,128)S(1)}, f32[16,2048]{1,0:T(8,128)S(1)}, u32[]{:S(2)}, u32[]{:S(2)}) collective-permute-start(f32[16,2048]{1,0:T(8,128)S(1)} %shard_map.104.refs_2_.refs_0_), channel_id=1, source_target_pairs={{0,32},{32,0},{64,96},{96,64},{1,33},{33,1},{65,97},{97,65},{2,34}... | collective-permute-start | bytes 393224 | tf_op jit(solution)/shard_map/ppermute | solution.py:354
  63.4 2.9 %collective-permute-start.18 = (f32[64,896]{1,0:T(8,128)S(1)}, f32[64,896]{1,0:T(8,128)S(1)}, u32[]{:S(2)}, u32[]{:S(2)}) collective-permute-start(f32[64,896]{1,0:T(8,128)S(1)} %shard_map.105.refs_2_.refs_0_), channel_id=1, source_target_pairs={{0,3},{1,2},{2,1},{3,0},{4,7},{5,6},{6,5},{7,4},{8,11},{9,10},{10,... | collective-permute-start | bytes 688136 | tf_op jit(solution)/shard_map/ppermute | solution.py:354
  66.3 1.0 %collective-permute-done.14.refs_1_ = f32[16,2048]{1,0:T(8,128)S(1)} collective-permute-done((f32[16,2048]{1,0:T(8,128)S(1)}, f32[16,2048]{1,0:T(8,128)S(1)}, u32[]{:S(2)}, u32[]{:S(2)}) %collective-permute-start.14) | collective-permute-done | bytes 131104 | tf_op jit(solution)/shard_map/ppermute | solution.py:354
  67.3 2.8 %collective-permute-start.17 = (f32[448,256]{1,0:T(8,128)S(1)}, f32[448,256]{1,0:T(8,128)S(1)}, u32[]{:S(2)}, u32[]{:S(2)}) collective-permute-start(f32[448,256]{1,0:T(8,128)S(1)} %get-tuple-element.61), channel_id=1, source_target_pairs={{0,3},{1,0},{2,1},{3,2},{4,7},{5,4},{6,5},{7,6},{8,11},{9,8},{10,9... | collective-permute-start | bytes 1376264 | tf_op jit(solution)/shard_map/ppermute | solution.py:346
  70.1 2.7 %collective-permute-start.21 = (f32[16,2048]{1,0:T(8,128)S(1)}, f32[16,2048]{1,0:T(8,128)S(1)}, u32[]{:S(2)}, u32[]{:S(2)}) collective-permute-start(f32[16,2048]{1,0:T(8,128)S(1)} %shard_map.106.refs_2_.refs_0_), channel_id=1, source_target_pairs={{0,96},{32,64},{64,32},{96,0},{1,97},{33,65},{65,33},{97,1},{2,98}... | collective-permute-start | bytes 393224 | tf_op jit(solution)/shard_map/ppermute | solution.py:354
  72.8 0.9 collective-permute-start.20
  73.7 2.3 %collective-permute-start.19 = (f32[32,896]{1,0:T(8,128)S(1)}, f32[32,896]{1,0:T(8,128)S(1)}, u32[]{:S(2)}, u32[]{:S(2)}) collective-permute-start(f32[32,896]{1,0:T(8,128)S(1)} %get-tuple-element.62.refs_3_.refs_0_), channel_id=1, source_target_pairs={{0,96},{32,64},{64,32},{96,0},{1,97},{33,65},{65,33},{97,1},{2,98}... | collective-permute-start | bytes 344072 | tf_op jit(solution)/shard_map/ppermute | solution.py:354
  77.2 1.6 %collective-permute-start.22 = (f32[8,2048]{1,0:T(8,128)S(1)}, f32[8,2048]{1,0:T(8,128)S(1)}, u32[]{:S(2)}, u32[]{:S(2)}) collective-permute-start(f32[8,2048]{1,0:T(8,128)S(1)} %get-tuple-element.64.refs_0_), channel_id=1, source_target_pairs={{0,24},{4,28},{8,16},{12,20},{16,8},{20,12},{24,0},{28,4},{1,25},{... | collective-permute-start | bytes 196616 | tf_op jit(solution)/shard_map/ppermute | solution.py:358
  78.8 3.9 %collective-permute-done.22.refs_1_ = f32[8,2048]{1,0:T(8,128)S(1)} collective-permute-done((f32[8,2048]{1,0:T(8,128)S(1)}, f32[8,2048]{1,0:T(8,128)S(1)}, u32[]{:S(2)}, u32[]{:S(2)}) %collective-permute-start.22) | collective-permute-done | bytes 65568 | tf_op jit(solution)/shard_map/ppermute | solution.py:358
  82.8 3.0 %collective-permute-start.24 = (f32[64,896]{1,0:T(8,128)S(1)}, f32[64,896]{1,0:T(8,128)S(1)}, u32[]{:S(2)}, u32[]{:S(2)}) collective-permute-start(f32[64,896]{1,0:T(8,128)S(1)} %get-tuple-element.67.refs_2_), channel_id=1, source_target_pairs={{0,96},{32,64},{64,32},{96,0},{1,97},{33,65},{65,33},{97,1},{2,98}... | collective-permute-start | bytes 688136 | tf_op jit(solution)/shard_map/ppermute | solution.py:354
  86.7 3.4 %collective-permute-done.24.refs_3_ = f32[64,896]{1,0:T(8,128)S(1)} collective-permute-done((f32[64,896]{1,0:T(8,128)S(1)}, f32[64,896]{1,0:T(8,128)S(1)}, u32[]{:S(2)}, u32[]{:S(2)}) %collective-permute-start.24) | collective-permute-done | bytes 229408 | tf_op jit(solution)/shard_map/ppermute | solution.py:354
  90.1 1.7 %collective-permute-done.23.refs_1_ = f32[64,896]{1,0:T(8,128)S(1)} collective-permute-done((f32[64,896]{1,0:T(8,128)S(1)}, f32[64,896]{1,0:T(8,128)S(1)}, u32[]{:S(2)}, u32[]{:S(2)}) %collective-permute-start.23) | collective-permute-done | bytes 229408 | tf_op jit(solution)/shard_map/ppermute | solution.py:354
  91.8 1.0 %shard_map.113 = (f32[64,3584]{1,0:T(8,128)}, f32[8,128]{1,0:T(8,128)S(1)}) custom-call(f32[64,896]{1,0:T(8,128)S(1)} %get-tuple-element.65.refs_3_.refs_0_, f32[64,896]{1,0:T(8,128)S(1)} %collective-permute-done.23.refs_1_, f32[64,896]{1,0:T(8,128)S(1)} %get-tuple-element.67.refs_2_, f32[64,896]{1,0:T(8,128)S(1)} %collective-permute-done.24.refs_3_, ...), custom_call_target="tpu_custom_call" | custom-call | flops 1 | bytes 1 | tf_op jit(solution)/shard_map/pallas_call | solution.py:49
  92.9 1.5 %collective-permute-done.26.refs_1_ = f32[32,2048]{1,0:T(8,128)S(1)} collective-permute-done((f32[32,2048]{1,0:T(8,128)S(1)}, f32[32,2048]{1,0:T(8,128)S(1)}, u32[]{:S(2)}, u32[]{:S(2)}) %collective-permute-start.26) | collective-permute-done | bytes 262176 | tf_op jit(solution)/shard_map/ppermute | solution.py:362
  (54 shorter events, 8.2 us)
Async XLA Ops:
  0.6 26.8 %copy-start = (bf16[256,2048]{1,0:T(8,128)(2,1)S(1)}, bf16[256,2048]{1,0:T(8,128)(2,1)}, u32[]{:S(2)}) copy-start(bf16[256,2048]{1,0:T(8,128)(2,1)} %refs_1_.3) | copy-start | bytes 3145732
  0.6 26.8 %copy-start.3 = (f32[2048]{0:T(1024)S(1)}, f32[2048]{0:T(1024)}, u32[]{:S(2)}) copy-start(f32[2048]{0:T(1024)} %param.11) | copy-start | bytes 24580
  17.5 1.3 %collective-permute-start = (f32[2,2048]{1,0:T(2,128)S(1)}, f32[2,2048]{1,0:T(2,128)S(1)}, u32[]{:S(2)}, u32[]{:S(2)}) collective-permute-start(f32[2,2048]{1,0:T(2,128)S(1)} %get-tuple-element.39), channel_id=1, source_target_pairs={{0,4},{4,0},{8,12},{12,8},{16,20},{20,16},{24,28},{28,24},{1,5},{5... | collective-permute-start | bytes 49160 | tf_op jit(solution)/shard_map/ppermute | solution.py:362
  18.8 4.6 %collective-permute-start.3 = (f32[2,2048]{1,0:T(2,128)S(1)}, f32[2,2048]{1,0:T(2,128)S(1)}, u32[]{:S(2)}, u32[]{:S(2)}) collective-permute-start(f32[2,2048]{1,0:T(2,128)S(1)} %add.3.refs_0_), channel_id=1, source_target_pairs={{0,24},{4,28},{8,0},{12,4},{16,8},{20,12},{24,16},{28,20},{1,25},{... | collective-permute-start | bytes 49160 | tf_op jit(solution)/shard_map/ppermute | solution.py:350
  21.7 5.2 %collective-permute-start.2 = (f32[2,2048]{1,0:T(2,128)S(1)}, f32[2,2048]{1,0:T(2,128)S(1)}, u32[]{:S(2)}, u32[]{:S(2)}) collective-permute-start(f32[2,2048]{1,0:T(2,128)S(1)} %add.3.refs_0_), channel_id=1, source_target_pairs={{0,16},{4,20},{8,24},{12,28},{16,0},{20,4},{24,8},{28,12},{1,17},{... | collective-permute-start | bytes 49160 | tf_op jit(solution)/shard_map/ppermute | solution.py:350
  22.5 4.9 %collective-permute-start.1 = (f32[2,2048]{1,0:T(2,128)S(1)}, f32[2,2048]{1,0:T(2,128)S(1)}, u32[]{:S(2)}, u32[]{:S(2)}) collective-permute-start(f32[2,2048]{1,0:T(2,128)S(1)} %add.3.refs_0_), channel_id=1, source_target_pairs={{0,8},{4,12},{8,16},{12,20},{16,24},{20,28},{24,0},{28,4},{1,9},{5... | collective-permute-start | bytes 49160 | tf_op jit(solution)/shard_map/ppermute | solution.py:350
  27.4 8.1 %copy-start.1 = (bf16[256,3584]{1,0:T(8,128)(2,1)S(1)}, bf16[256,3584]{1,0:T(8,128)(2,1)}, u32[]{:S(2)}) copy-start(bf16[256,3584]{1,0:T(8,128)(2,1)} %refs_3_.3) | copy-start | bytes 5505028
  27.4 8.2 %copy-start.2 = (bf16[64,2048]{1,0:T(8,128)(2,1)S(1)}, bf16[64,2048]{1,0:T(8,128)(2,1)}, u32[]{:S(2)}) copy-start(bf16[64,2048]{1,0:T(8,128)(2,1)} %refs_2_.1) | copy-start | bytes 786436
  28.6 16.3 %collective-permute-start.6 = (f32[448,256]{1,0:T(8,128)S(1)}, f32[448,256]{1,0:T(8,128)S(1)}, u32[]{:S(2)}, u32[]{:S(2)}) collective-permute-start(f32[448,256]{1,0:T(8,128)S(1)} %get-tuple-element.51), channel_id=1, source_target_pairs={{0,1},{1,2},{2,3},{3,0},{4,5},{5,6},{6,7},{7,4},{8,9},{9,10},{10,1... | collective-permute-start | bytes 1376264 | tf_op jit(solution)/shard_map/ppermute | solution.py:346
  30.3 15.6 %collective-permute-start.7 = (f32[448,256]{1,0:T(8,128)S(1)}, f32[448,256]{1,0:T(8,128)S(1)}, u32[]{:S(2)}, u32[]{:S(2)}) collective-permute-start(f32[448,256]{1,0:T(8,128)S(1)} %get-tuple-element.52), channel_id=1, source_target_pairs={{0,3},{1,0},{2,1},{3,2},{4,7},{5,4},{6,5},{7,6},{8,11},{9,8},{10,9... | collective-permute-start | bytes 1376264 | tf_op jit(solution)/shard_map/ppermute | solution.py:346
  32.1 3.3 %collective-permute-start.4 = (f32[32,2048]{1,0:T(8,128)S(1)}, f32[32,2048]{1,0:T(8,128)S(1)}, u32[]{:S(2)}, u32[]{:S(2)}) collective-permute-start(f32[32,2048]{1,0:T(8,128)S(1)} %get-tuple-element.45.refs_2_), channel_id=1, source_target_pairs={{0,4},{4,0},{8,12},{12,8},{16,20},{20,16},{24,28},{28,24},{1,5},{5... | collective-permute-start | bytes 786440 | tf_op jit(solution)/shard_map/ppermute | solution.py:362
  33.3 17.4 %collective-permute-start.9 = (f32[448,256]{1,0:T(8,128)S(1)}, f32[448,256]{1,0:T(8,128)S(1)}, u32[]{:S(2)}, u32[]{:S(2)}) collective-permute-start(f32[448,256]{1,0:T(8,128)S(1)} %get-tuple-element.53), channel_id=1, source_target_pairs={{0,3},{1,0},{2,1},{3,2},{4,7},{5,4},{6,5},{7,6},{8,11},{9,8},{10,9... | collective-permute-start | bytes 1376264 | tf_op jit(solution)/shard_map/ppermute | solution.py:346
  35.2 15.5 %collective-permute-start.8 = (f32[448,256]{1,0:T(8,128)S(1)}, f32[448,256]{1,0:T(8,128)S(1)}, u32[]{:S(2)}, u32[]{:S(2)}) collective-permute-start(f32[448,256]{1,0:T(8,128)S(1)} %get-tuple-element.46.refs_2_), channel_id=1, source_target_pairs={{0,1},{1,2},{2,3},{3,0},{4,5},{5,6},{6,7},{7,4},{8,9},{9,10},{10,1... | collective-permute-start | bytes 1376264 | tf_op jit(solution)/shard_map/ppermute | solution.py:346
  35.5 5.5 %collective-permute-start.5 = (f32[16,2048]{1,0:T(8,128)S(1)}, f32[16,2048]{1,0:T(8,128)S(1)}, u32[]{:S(2)}, u32[]{:S(2)}) collective-permute-start(f32[16,2048]{1,0:T(8,128)S(1)} %get-tuple-element.48.refs_5_), channel_id=1, source_target_pairs={{0,8},{4,12},{8,0},{12,4},{16,24},{20,28},{24,16},{28,20},{1,9},{5... | collective-permute-start | bytes 393224 | tf_op jit(solution)/shard_map/ppermute | solution.py:358
  41.0 10.3 %collective-permute-start.11 = (f32[64,896]{1,0:T(8,128)S(1)}, f32[64,896]{1,0:T(8,128)S(1)}, u32[]{:S(2)}, u32[]{:S(2)}) collective-permute-start(f32[64,896]{1,0:T(8,128)S(1)} %get-tuple-element.57), channel_id=1, source_target_pairs={{0,64},{32,96},{64,0},{96,32},{1,65},{33,97},{65,1},{97,33},{2,66}... | collective-permute-start | bytes 688136 | tf_op jit(solution)/shard_map/ppermute | solution.py:346
  44.9 10.7 %collective-permute-start.12 = (f32[64,896]{1,0:T(8,128)S(1)}, f32[64,896]{1,0:T(8,128)S(1)}, u32[]{:S(2)}, u32[]{:S(2)}) collective-permute-start(f32[64,896]{1,0:T(8,128)S(1)} %get-tuple-element.58), channel_id=1, source_target_pairs={{0,32},{32,64},{64,96},{96,0},{1,33},{33,65},{65,97},{97,1},{2,34}... | collective-permute-start | bytes 688136 | tf_op jit(solution)/shard_map/ppermute | solution.py:346
  45.9 10.4 %collective-permute-start.13 = (f32[64,896]{1,0:T(8,128)S(1)}, f32[64,896]{1,0:T(8,128)S(1)}, u32[]{:S(2)}, u32[]{:S(2)}) collective-permute-start(f32[64,896]{1,0:T(8,128)S(1)} %get-tuple-element.59), channel_id=1, source_target_pairs={{0,96},{32,0},{64,32},{96,64},{1,97},{33,1},{65,33},{97,65},{2,98}... | collective-permute-start | bytes 688136 | tf_op jit(solution)/shard_map/ppermute | solution.py:346
  56.4 7.0 %collective-permute-start.15 = (f32[64,896]{1,0:T(8,128)S(1)}, f32[64,896]{1,0:T(8,128)S(1)}, u32[]{:S(2)}, u32[]{:S(2)}) collective-permute-start(f32[64,896]{1,0:T(8,128)S(1)} %shard_map.103.refs_3_.refs_0_), channel_id=1, source_target_pairs={{0,1},{1,0},{2,3},{3,2},{4,5},{5,4},{6,7},{7,6},{8,9},{9,8},{10,11... | collective-permute-start | bytes 688136 | tf_op jit(solution)/shard_map/ppermute | solution.py:354
  56.8 5.5 %collective-permute-start.10 = (f32[8,2048]{1,0:T(8,128)S(1)}, f32[8,2048]{1,0:T(8,128)S(1)}, u32[]{:S(2)}, u32[]{:S(2)}) collective-permute-start(f32[8,2048]{1,0:T(8,128)S(1)} %get-tuple-element.50.refs_2_), channel_id=1, source_target_pairs={{0,24},{4,28},{8,16},{12,20},{16,8},{20,12},{24,0},{28,4},{1,25},{... | collective-permute-start | bytes 196616 | tf_op jit(solution)/shard_map/ppermute | solution.py:358
  62.3 5.0 %collective-permute-start.14 = (f32[16,2048]{1,0:T(8,128)S(1)}, f32[16,2048]{1,0:T(8,128)S(1)}, u32[]{:S(2)}, u32[]{:S(2)}) collective-permute-start(f32[16,2048]{1,0:T(8,128)S(1)} %shard_map.104.refs_2_.refs_0_), channel_id=1, source_target_pairs={{0,32},{32,0},{64,96},{96,64},{1,33},{33,1},{65,97},{97,65},{2,34}... | collective-permute-start | bytes 393224 | tf_op jit(solution)/shard_map/ppermute | solution.py:354
  63.4 9.4 %collective-permute-start.18 = (f32[64,896]{1,0:T(8,128)S(1)}, f32[64,896]{1,0:T(8,128)S(1)}, u32[]{:S(2)}, u32[]{:S(2)}) collective-permute-start(f32[64,896]{1,0:T(8,128)S(1)} %shard_map.105.refs_2_.refs_0_), channel_id=1, source_target_pairs={{0,3},{1,2},{2,1},{3,0},{4,7},{5,6},{6,5},{7,4},{8,11},{9,10},{10,... | collective-permute-start | bytes 688136 | tf_op jit(solution)/shard_map/ppermute | solution.py:354
  67.3 18.5 %collective-permute-start.17 = (f32[448,256]{1,0:T(8,128)S(1)}, f32[448,256]{1,0:T(8,128)S(1)}, u32[]{:S(2)}, u32[]{:S(2)}) collective-permute-start(f32[448,256]{1,0:T(8,128)S(1)} %get-tuple-element.61), channel_id=1, source_target_pairs={{0,3},{1,0},{2,1},{3,2},{4,7},{5,4},{6,5},{7,6},{8,11},{9,8},{10,9... | collective-permute-start | bytes 1376264 | tf_op jit(solution)/shard_map/ppermute | solution.py:346
  70.1 15.7 %collective-permute-start.16 = (f32[448,256]{1,0:T(8,128)S(1)}, f32[448,256]{1,0:T(8,128)S(1)}, u32[]{:S(2)}, u32[]{:S(2)}) collective-permute-start(f32[448,256]{1,0:T(8,128)S(1)} %get-tuple-element.60.refs_2_), channel_id=1, source_target_pairs={{0,1},{1,2},{2,3},{3,0},{4,5},{5,6},{6,7},{7,4},{8,9},{9,10},{10,1... | collective-permute-start | bytes 1376264 | tf_op jit(solution)/shard_map/ppermute | solution.py:346
  70.1 6.5 %collective-permute-start.21 = (f32[16,2048]{1,0:T(8,128)S(1)}, f32[16,2048]{1,0:T(8,128)S(1)}, u32[]{:S(2)}, u32[]{:S(2)}) collective-permute-start(f32[16,2048]{1,0:T(8,128)S(1)} %shard_map.106.refs_2_.refs_0_), channel_id=1, source_target_pairs={{0,96},{32,64},{64,32},{96,0},{1,97},{33,65},{65,33},{97,1},{2,98}... | collective-permute-start | bytes 393224 | tf_op jit(solution)/shard_map/ppermute | solution.py:354
  72.8 9.9 %collective-permute-start.20 = (f32[32,896]{1,0:T(8,128)S(1)}, f32[32,896]{1,0:T(8,128)S(1)}, u32[]{:S(2)}, u32[]{:S(2)}) collective-permute-start(f32[32,896]{1,0:T(8,128)S(1)} %get-tuple-element.63.refs_2_), channel_id=1, source_target_pairs={{0,32},{32,0},{64,96},{96,64},{1,33},{33,1},{65,97},{97,65},{2,34}... | collective-permute-start | bytes 344072 | tf_op jit(solution)/shard_map/ppermute | solution.py:354
  73.7 9.0 %collective-permute-start.19 = (f32[32,896]{1,0:T(8,128)S(1)}, f32[32,896]{1,0:T(8,128)S(1)}, u32[]{:S(2)}, u32[]{:S(2)}) collective-permute-start(f32[32,896]{1,0:T(8,128)S(1)} %get-tuple-element.62.refs_3_.refs_0_), channel_id=1, source_target_pairs={{0,96},{32,64},{64,32},{96,0},{1,97},{33,65},{65,33},{97,1},{2,98}... | collective-permute-start | bytes 344072 | tf_op jit(solution)/shard_map/ppermute | solution.py:354
  77.2 5.5 %collective-permute-start.22 = (f32[8,2048]{1,0:T(8,128)S(1)}, f32[8,2048]{1,0:T(8,128)S(1)}, u32[]{:S(2)}, u32[]{:S(2)}) collective-permute-start(f32[8,2048]{1,0:T(8,128)S(1)} %get-tuple-element.64.refs_0_), channel_id=1, source_target_pairs={{0,24},{4,28},{8,16},{12,20},{16,8},{20,12},{24,0},{28,4},{1,25},{... | collective-permute-start | bytes 196616 | tf_op jit(solution)/shard_map/ppermute | solution.py:358
  82.8 7.3 %collective-permute-start.24 = (f32[64,896]{1,0:T(8,128)S(1)}, f32[64,896]{1,0:T(8,128)S(1)}, u32[]{:S(2)}, u32[]{:S(2)}) collective-permute-start(f32[64,896]{1,0:T(8,128)S(1)} %get-tuple-element.67.refs_2_), channel_id=1, source_target_pairs={{0,96},{32,64},{64,32},{96,0},{1,97},{33,65},{65,33},{97,1},{2,98}... | collective-permute-start | bytes 688136 | tf_op jit(solution)/shard_map/ppermute | solution.py:354
  85.8 6.0 %collective-permute-start.23 = (f32[64,896]{1,0:T(8,128)S(1)}, f32[64,896]{1,0:T(8,128)S(1)}, u32[]{:S(2)}, u32[]{:S(2)}) collective-permute-start(f32[64,896]{1,0:T(8,128)S(1)} %get-tuple-element.65.refs_3_.refs_0_), channel_id=1, source_target_pairs={{0,32},{32,0},{64,96},{96,64},{1,33},{33,1},{65,97},{97,65},{2,34}... | collective-permute-start | bytes 688136 | tf_op jit(solution)/shard_map/ppermute | solution.py:354
  85.8 7.0 %collective-permute-start.25 = (f32[16,2048]{1,0:T(8,128)S(1)}, f32[16,2048]{1,0:T(8,128)S(1)}, u32[]{:S(2)}, u32[]{:S(2)}) collective-permute-start(f32[16,2048]{1,0:T(8,128)S(1)} %shard_map.110.refs_4_.refs_0_), channel_id=1, source_target_pairs={{0,8},{4,12},{8,0},{12,4},{16,24},{20,28},{24,16},{28,20},{1,9},{5... | collective-permute-start | bytes 393224 | tf_op jit(solution)/shard_map/ppermute | solution.py:358
  92.8 1.6 %collective-permute-start.26 = (f32[32,2048]{1,0:T(8,128)S(1)}, f32[32,2048]{1,0:T(8,128)S(1)}, u32[]{:S(2)}, u32[]{:S(2)}) collective-permute-start(f32[32,2048]{1,0:T(8,128)S(1)} %shard_map.114.refs_0_), channel_id=1, source_target_pairs={{0,4},{4,0},{8,12},{12,8},{16,20},{20,16},{24,28},{28,24},{1,5},{5... | collective-permute-start | bytes 786440 | tf_op jit(solution)/shard_map/ppermute | solution.py:362

commit v7 on v6

--- a/solution.py
+++ b/solution.py
@@ -74,8 +74,8 @@
 
 
 def merge_kernel(
-    steps, w_ref, x_ref, a_ref, b_ref, dy_ref, m_ref, stat_ref, bq_ref, am_ref,
-    xa, b2, dy, acc, qt, sq, w_sem, x_sem, a_sem, b_sem, dy_sem,
+    steps, w_ref, x_ref, a_ref, b_ref, dy_ref, m_ref, stat_ref, am_ref,
+    xa, b2, dy, acc, sq, w_sem, x_sem, a_sem, b_sem, dy_sem,
 ):
     rows, cols = w_ref.shape
     toks = x_ref.shape[0]
@@ -98,7 +98,6 @@
         w_copy(i).start()
     dy_copy.start()
     acc[...] = jnp.zeros_like(acc)
-    qt[...] = jnp.zeros_like(qt)
     sq[...] = jnp.zeros_like(sq)
     b_copy.wait()
     a_copy.wait()
@@ -118,13 +117,11 @@
             wide = m.astype(F32)
             sq[:, at] += jnp.sum((wide * wide).reshape(step // 8, 8, tile), axis=0)
             acc[:, at] += nn(xa_part, m)
-        qt[...] += nt(a_part, xa_part[:toks])
 
     dy_copy.wait()
     am_ref[...] = acc[toks:]
     stat_ref[0:1] = jnp.sum(sq[...], axis=0, keepdims=True)
     stat_ref[1:2] = jnp.sum(acc[:toks] * dy[...].astype(F32), axis=0, keepdims=True)
-    bq_ref[...] = fold(nn(hi_lo(qt[...]), dy[...]))
 
 
 def merge(w, x, a_t, b, dy):
@@ -135,7 +132,7 @@
     dma = pltpu.SemaphoreType.DMA
     return call(
         functools.partial(merge_kernel, steps),
-        [pltpu.VMEM((rows, cols), BF16), out((2, cols)), out((rank, cols)), out((rank, cols))],
+        [pltpu.VMEM((rows, cols), BF16), out((2, cols)), out((rank, cols))],
         [HBM] * 5,
         *[pltpu.with_memory_space_constraint(value, pltpu.HBM) for value in (w, x, a_t, b, dy)],
         scratch=[
@@ -143,7 +140,6 @@
             pltpu.VMEM((rank, cols), BF16),
             pltpu.VMEM((toks, cols), BF16),
             pltpu.VMEM((toks + rank, cols), F32),
-            pltpu.VMEM((rank, toks), F32),
             pltpu.VMEM((8, cols), F32),
             dma((steps,)), dma, dma, dma, dma,
         ],
@@ -151,6 +147,10 @@
         flops=2 * rows * cols * (toks + 2 * rank),
         data=rows * cols * 2,
     )
+
+
+def q_kernel(a_ref, x_ref, dy_ref, bq_ref):
+    bq_ref[...] = fold(nn(hi_lo(nt(a_ref[...], x_ref[...])), dy_ref[...]))
 
 
 def block(m_ref, index, half=None, count=4):
@@ -297,8 +297,7 @@
     bottom_out_ref[half:] = bottom_more_ref[...]
 
 
-def a_join_kernel(top_ref, top_more_ref, bottom_ref, bottom_more_ref, whole, done_ref):
-    done_ref[...] = jnp.zeros_like(done_ref)
+def a_join_kernel(top_ref, top_more_ref, bottom_ref, bottom_more_ref, whole):
     z = dp_index()
     first = z + 1 - 2 * lax.rem(z, 2)
     second = 3 - z
@@ -368,7 +367,8 @@
     groups, full_rows = 4, rows * 8
     gamma = float(toks * groups) ** (-0.5)
     mag = mag.reshape(1, cols)
-    m, stat, bq, am = merge(w, x, a.T, b, dy)
+    m, stat, am = merge(w, x, a.T, b, dy)
+    bq = call(q_kernel, [out((rank, cols))], [VMEM] * 3, a.T, x, dy, after=[stat])[0]
 
     m = pltpu.with_memory_space_constraint(m, pltpu.VMEM)
     stat = stat + swap_core(stat)
@@ -378,6 +378,7 @@
         [out((4, cols)), out((toks, cols), BF16), out((far, toks)), out((far, toks))],
         [VMEM] * 7,
         stat, ring_x(stat, 1), ring_x(stat, 2), ring_x(stat, 3), mag, dy, m,
+        after=[bq],
     )
     u0, u1 = ring(h0, "cols", 1), ring(h1, "cols", 3)
     keep, send = call(
@@ -434,14 +435,9 @@
     grad, done = call(
         finish_kernel, [out((rows // 4, toks), BF16), out((8, 128))], [VMEM] * 3, own, w0, w1, after=[top]
     )
-    a_grad, done = call(
-        a_join_kernel,
-        [out((rank, rows)), out((8, 128))],
-        [VMEM] * 4,
-        top, swap(top, "dp", 0), bottom, swap(bottom, "dp", 1),
-        after=[done],
-    )
-    b_part = join([b_part, swap_x(b_part, 0)], near_bit, 0, after=[done])
+    top_more, bottom_more = hold([swap(top, "dp", 0), swap(bottom, "dp", 1)], [done])
+    b_part = join([b_part, swap_x(b_part, 0)], near_bit, 0, after=[top_more])
+    a_grad = call(a_join_kernel, [out((rank, rows))], [VMEM] * 4, top, top_more, bottom, bottom_more, after=[b_part])[0]
     b_grad = join([b_part, swap_core(b_part)], core_bit, 0)
     return grad, a_grad.T, b_grad, mag_grad.reshape(cols)
 

time: 96.5 us -> 95.1 us (0.985)
  waiting for transfers between devices: 26.9 us -> 24.7 us
    ppermute x3, waiting for transfers between devices: 4.06 us -> 2.88 us  [ring_x(): lax.ppermute(value, 'rows', [(i, (i + 2 * k) % count) for i in range(coun...]
    ppermute x3, waiting for transfers between devices: 2.7 us -> 1.7 us  [swap_core(): return lax.ppermute(value, 'rows', [(i, i ^ 1) for i in range(count)])]
    pallas_call x22 -> x23, Pallas kernels: 30.6 us -> 31.4 us  [call(): pl.pallas_call(body, out_shape=outs, in_specs=list(specs) + [ANY] * len(a...]
  transfers between devices with their start and end apart: 27 -> 27, of which waited for: 15 -> 15; matrix products, arithmetic and copies ran while one was open for 0% -> 0% of each run, Pallas kernels for 12% -> 14%
where the time goes in v7:
time: 95.1 us; the launch traced here: 93.9 us
  starting transfers between devices  37 us (39%)
  Pallas kernels  31.4 us (33%)
  waiting for transfers between devices  24.7 us (26%)
    pallas_call x23, Pallas kernels, call(): pl.pallas_call(body, out_shape=outs, in_specs=list(specs) + [ANY] * len(a...  31.4 us
    ppermute x9, starting transfers between devices, ring(): lax.ppermute(value, axis, [(i, (i + k) % count) for i in range(count)])  15.3 us
    ppermute x8, starting transfers between devices, swap(): lax.ppermute(value, axis, [(i, i ^ 1 if step == 0 else 3 - i) for i in ra...  13.2 us
    ppermute x4, waiting for transfers between devices, swap_x(): lax.ppermute(value, 'rows', [(i, i ^ 2 if step == 0 else 6 - 2 * (i // 2)...  7.63 us
    ppermute x8, waiting for transfers between devices, swap(): lax.ppermute(value, axis, [(i, i ^ 1 if step == 0 else 3 - i) for i in ra...  6.7 us
    ppermute x9, waiting for transfers between devices, ring(): lax.ppermute(value, axis, [(i, (i + k) % count) for i in range(count)])  5.76 us
    ppermute x3, starting transfers between devices, ring_x(): lax.ppermute(value, 'rows', [(i, (i + 2 * k) % count) for i in range(coun...  4.59 us
    ppermute x4, starting transfers between devices, swap_x(): lax.ppermute(value, 'rows', [(i, i ^ 2 if step == 0 else 6 - 2 * (i // 2)...  3.52 us
  transfers between devices with their start and end apart: 27, of which 15 were waited for; matrix products, arithmetic and copies ran while one was open for 0% of the time, Pallas kernels for 14%

profile of v7, /device:TPU:0, one launch (start us, length us, event | category | flops | bytes accessed | tf_op | source)
XLA Modules:
  0.0 93.9 jit_solution(6796802386627013272)
XLA Ops:
  0.7 16.5 %shard_map.93 = (bf16[3584,2048]{1,0:T(8,128)(2,1)S(1)}, f32[2,2048]{1,0:T(2,128)S(1)}, f32[64,2048]{1,0:T(8,128)S(1)}) custom-call(bf16[3584,2048]{1,0:T(8,128)(2,1)} %refs_0_.1, bf16[256,3584]{1,0:T(8,128)(2,1)} %refs_3_.3, bf16[64,3584]{1,0:T(8,128)(2,1)} %bitcast.4, bf16[64,2048]{1,0:T(8,128)(2,1)} %refs_2_.3, bf16[256,2048]{1,0:T(8,128)(2,1)} %refs_1_.5), custom_call_target="tpu_custom_call" | custom-call | flops 5637144576 | bytes 14680064 | tf_op jit(solution)/shard_map/pallas_call | solution.py:49
  17.2 1.2 %collective-permute-done = f32[2,2048]{1,0:T(2,128)S(1)} collective-permute-done((f32[2,2048]{1,0:T(2,128)S(1)}, f32[2,2048]{1,0:T(2,128)S(1)}, u32[]{:S(2)}, u32[]{:S(2)}) %collective-permute-start) | collective-permute-done | bytes 16416 | tf_op jit(solution)/shard_map/ppermute | solution.py:361
  18.4 2.9 %collective-permute-start.3 = (f32[2,2048]{1,0:T(2,128)S(1)}, f32[2,2048]{1,0:T(2,128)S(1)}, u32[]{:S(2)}, u32[]{:S(2)}) collective-permute-start(f32[2,2048]{1,0:T(2,128)S(1)} %add.3.refs_0_), channel_id=1, source_target_pairs={{0,24},{4,28},{8,0},{12,4},{16,8},{20,12},{24,16},{28,20},{1,25},{... | collective-permute-start | bytes 49160 | tf_op jit(solution)/shard_map/ppermute | solution.py:349
  23.0 1.2 %shard_map.94.refs_7_.refs_1_ = f32[64,2048]{1,0:T(8,128)S(1)} custom-call(bf16[64,3584]{1,0:T(8,128)(2,1)S(1)} %bitcast.5, bf16[256,3584]{1,0:T(8,128)(2,1)S(1)} %copy-done.1, bf16[256,2048]{1,0:T(8,128)(2,1)S(1)} %copy-done, f32[2,2048]{1,0:T(2,128)S(1)} %get-tuple-element.38.refs_3_), custom_call_target="tpu_custom_call" | custom-call | flops 1 | bytes 1 | tf_op jit(solution)/shard_map/pallas_call | solution.py:49
  24.2 2.4 %collective-permute-done.2.refs_2_ = f32[2,2048]{1,0:T(2,128)S(1)} collective-permute-done((f32[2,2048]{1,0:T(2,128)S(1)}, f32[2,2048]{1,0:T(2,128)S(1)}, u32[]{:S(2)}, u32[]{:S(2)}) %collective-permute-start.2) | collective-permute-done | bytes 16416 | tf_op jit(solution)/shard_map/ppermute | solution.py:349
  27.1 1.2 %shard_map.95 = (f32[4,2048]{1,0:T(4,128)S(1)}, bf16[256,2048]{1,0:T(8,128)(2,1)S(1)}, f32[448,256]{1,0:T(8,128)S(1)}, f32[448,256]{1,0:T(8,128)S(1)}) custom-call(f32[2,2048]{1,0:T(2,128)S(1)} %add.3.refs_0_, f32[2,2048]{1,0:T(2,128)S(1)} %collective-permute-done.1.refs_1_, f32[2,2048]{1,0:T(2,128)S(1)} %collective-permute-done.2.refs_2_, ...), custom_call_target="tpu_custom_call" | custom-call | flops 1 | bytes 1 | tf_op jit(solution)/shard_map/pallas_call | solution.py:49
  28.3 1.6 %collective-permute-start.6 = (f32[448,256]{1,0:T(8,128)S(1)}, f32[448,256]{1,0:T(8,128)S(1)}, u32[]{:S(2)}, u32[]{:S(2)}) collective-permute-start(f32[448,256]{1,0:T(8,128)S(1)} %get-tuple-element.49), channel_id=1, source_target_pairs={{0,1},{1,2},{2,3},{3,0},{4,5},{5,6},{6,7},{7,4},{8,9},{9,10},{10,1... | collective-permute-start | bytes 1376264 | tf_op jit(solution)/shard_map/ppermute | solution.py:345
  29.9 1.7 %collective-permute-start.7 = (f32[448,256]{1,0:T(8,128)S(1)}, f32[448,256]{1,0:T(8,128)S(1)}, u32[]{:S(2)}, u32[]{:S(2)}) collective-permute-start(f32[448,256]{1,0:T(8,128)S(1)} %get-tuple-element.50), channel_id=1, source_target_pairs={{0,3},{1,0},{2,1},{3,2},{4,7},{5,4},{6,5},{7,6},{8,11},{9,8},{10,9... | collective-permute-start | bytes 1376264 | tf_op jit(solution)/shard_map/ppermute | solution.py:345
  31.8 1.1 %shard_map.97 = (f32[448,256]{1,0:T(8,128)S(1)}, f32[448,256]{1,0:T(8,128)S(1)}) custom-call(bf16[3584,2048]{1,0:T(8,128)(2,1)S(1)} %get-tuple-element.37.refs_6_.refs_0_.refs_4_, bf16[256,2048]{1,0:T(8,128)(2,1)S(1)} %get-tuple-element.39.refs_1_, f32[32,2048]{1,0:T(8,128)S(1)} %get-tuple-element.43.refs_2_), custom_call_target="tpu_custom_call" | custom-call | flops 1 | bytes 1 | tf_op jit(solution)/shard_map/pallas_call | solution.py:49
  33.0 1.9 %collective-permute-start.9 = (f32[448,256]{1,0:T(8,128)S(1)}, f32[448,256]{1,0:T(8,128)S(1)}, u32[]{:S(2)}, u32[]{:S(2)}) collective-permute-start(f32[448,256]{1,0:T(8,128)S(1)} %get-tuple-element.51), channel_id=1, source_target_pairs={{0,3},{1,0},{2,1},{3,2},{4,7},{5,4},{6,5},{7,6},{8,11},{9,8},{10,9... | collective-permute-start | bytes 1376264 | tf_op jit(solution)/shard_map/ppermute | solution.py:345
  35.2 5.3 %shard_map.99 = (f32[64,896]{1,0:T(8,128)S(1)}, f32[64,896]{1,0:T(8,128)S(1)}, f32[64,896]{1,0:T(8,128)S(1)}, f32[64,896]{1,0:T(8,128)S(1)}) custom-call(f32[4,2048]{1,0:T(4,128)S(1)} %get-tuple-element.40.refs_0_.refs_2_, bf16[256,2048]{1,0:T(8,128)(2,1)S(1)} %copy-done, bf16[64,2048]{1,0:T(8,128)(2,1)S(1)} %copy-done.3, bf16[256,3584]{1,0:T(8,128)(2,1)S(1)} %copy-done.1, ...), custom_call_target="tpu_custom_call" | custom-call | flops 1 | bytes 1 | tf_op jit(solution)/shard_map/pallas_call | solution.py:49
  40.6 3.9 %collective-permute-start.11 = (f32[64,896]{1,0:T(8,128)S(1)}, f32[64,896]{1,0:T(8,128)S(1)}, u32[]{:S(2)}, u32[]{:S(2)}) collective-permute-start(f32[64,896]{1,0:T(8,128)S(1)} %get-tuple-element.55), channel_id=1, source_target_pairs={{0,64},{32,96},{64,0},{96,32},{1,65},{33,97},{65,1},{97,33},{2,66}... | collective-permute-start | bytes 688136 | tf_op jit(solution)/shard_map/ppermute | solution.py:345
  44.5 1.0 %collective-permute-start.12 = (f32[64,896]{1,0:T(8,128)S(1)}, f32[64,896]{1,0:T(8,128)S(1)}, u32[]{:S(2)}, u32[]{:S(2)}) collective-permute-start(f32[64,896]{1,0:T(8,128)S(1)} %get-tuple-element.56), channel_id=1, source_target_pairs={{0,32},{32,64},{64,96},{96,0},{1,33},{33,65},{65,97},{97,1},{2,34}... | collective-permute-start | bytes 688136 | tf_op jit(solution)/shard_map/ppermute | solution.py:345
  45.5 2.2 %collective-permute-start.13 = (f32[64,896]{1,0:T(8,128)S(1)}, f32[64,896]{1,0:T(8,128)S(1)}, u32[]{:S(2)}, u32[]{:S(2)}) collective-permute-start(f32[64,896]{1,0:T(8,128)S(1)} %get-tuple-element.57), channel_id=1, source_target_pairs={{0,96},{32,0},{64,32},{96,64},{1,97},{33,1},{65,33},{97,65},{2,98}... | collective-permute-start | bytes 688136 | tf_op jit(solution)/shard_map/ppermute | solution.py:345
  47.8 1.1 %shard_map.101.refs_4_.refs_0_ = f32[896,256]{1,0:T(8,128)S(1)} custom-call(bf16[3584,2048]{1,0:T(8,128)(2,1)S(1)} %get-tuple-element.37.refs_6_.refs_0_.refs_4_, bf16[256,2048]{1,0:T(8,128)(2,1)S(1)} %get-tuple-element.39.refs_1_, f32[8,2048]{1,0:T(8,128)S(1)} %get-tuple-element.48.refs_2_, f32[448,256]{1,0:T(8,128)S(1)} %collective-permute-done.6.refs_3_.refs_2_, ...), custom_call_target="tpu_custom_call" | custom-call | flops 1 | bytes 1 | tf_op jit(solution)/shard_map/pallas_call | solution.py:49
  49.0 1.1 %shard_map.102 = (f32[448,256]{1,0:T(8,128)S(1)}, f32[448,256]{1,0:T(8,128)S(1)}) custom-call(bf16[3584,2048]{1,0:T(8,128)(2,1)S(1)} %get-tuple-element.37.refs_6_.refs_0_.refs_4_, bf16[256,2048]{1,0:T(8,128)(2,1)S(1)} %get-tuple-element.39.refs_1_, f32[448,256]{1,0:T(8,128)S(1)} %collective-permute-done.6.refs_3_.refs_2_, ...), custom_call_target="tpu_custom_call" | custom-call | flops 1 | bytes 1 | tf_op jit(solution)/shard_map/pallas_call | solution.py:49
  51.0 4.2 %collective-permute-done.12.refs_2_ = f32[64,896]{1,0:T(8,128)S(1)} collective-permute-done((f32[64,896]{1,0:T(8,128)S(1)}, f32[64,896]{1,0:T(8,128)S(1)}, u32[]{:S(2)}, u32[]{:S(2)}) %collective-permute-start.12) | collective-permute-done | bytes 229408 | tf_op jit(solution)/shard_map/ppermute | solution.py:345
  56.4 1.8 %collective-permute-start.10 = (f32[8,2048]{1,0:T(8,128)S(1)}, f32[8,2048]{1,0:T(8,128)S(1)}, u32[]{:S(2)}, u32[]{:S(2)}) collective-permute-start(f32[8,2048]{1,0:T(8,128)S(1)} %get-tuple-element.48.refs_2_), channel_id=1, source_target_pairs={{0,24},{4,28},{8,16},{12,20},{16,8},{20,12},{24,0},{28,4},{1,25},{... | collective-permute-start | bytes 196616 | tf_op jit(solution)/shard_map/ppermute | solution.py:357
  58.1 3.7 %collective-permute-done.10.refs_1_ = f32[8,2048]{1,0:T(8,128)S(1)} collective-permute-done((f32[8,2048]{1,0:T(8,128)S(1)}, f32[8,2048]{1,0:T(8,128)S(1)}, u32[]{:S(2)}, u32[]{:S(2)}) %collective-permute-start.10) | collective-permute-done | bytes 65568 | tf_op jit(solution)/shard_map/ppermute | solution.py:357
  61.9 1.1 %collective-permute-start.14 = (f32[16,2048]{1,0:T(8,128)S(1)}, f32[16,2048]{1,0:T(8,128)S(1)}, u32[]{:S(2)}, u32[]{:S(2)}) collective-permute-start(f32[16,2048]{1,0:T(8,128)S(1)} %shard_map.105.refs_2_.refs_0_), channel_id=1, source_target_pairs={{0,32},{32,0},{64,96},{96,64},{1,33},{33,1},{65,97},{97,65},{2,34}... | collective-permute-start | bytes 393224 | tf_op jit(solution)/shard_map/ppermute | solution.py:353
  63.0 2.9 %collective-permute-start.18 = (f32[64,896]{1,0:T(8,128)S(1)}, f32[64,896]{1,0:T(8,128)S(1)}, u32[]{:S(2)}, u32[]{:S(2)}) collective-permute-start(f32[64,896]{1,0:T(8,128)S(1)} %shard_map.106.refs_2_.refs_0_), channel_id=1, source_target_pairs={{0,3},{1,2},{2,1},{3,0},{4,7},{5,6},{6,5},{7,4},{8,11},{9,10},{10,... | collective-permute-start | bytes 688136 | tf_op jit(solution)/shard_map/ppermute | solution.py:353
  65.9 1.0 %collective-permute-done.14.refs_1_ = f32[16,2048]{1,0:T(8,128)S(1)} collective-permute-done((f32[16,2048]{1,0:T(8,128)S(1)}, f32[16,2048]{1,0:T(8,128)S(1)}, u32[]{:S(2)}, u32[]{:S(2)}) %collective-permute-start.14) | collective-permute-done | bytes 131104 | tf_op jit(solution)/shard_map/ppermute | solution.py:353
  67.0 2.8 %collective-permute-start.17 = (f32[448,256]{1,0:T(8,128)S(1)}, f32[448,256]{1,0:T(8,128)S(1)}, u32[]{:S(2)}, u32[]{:S(2)}) collective-permute-start(f32[448,256]{1,0:T(8,128)S(1)} %get-tuple-element.59), channel_id=1, source_target_pairs={{0,3},{1,0},{2,1},{3,2},{4,7},{5,4},{6,5},{7,6},{8,11},{9,8},{10,9... | collective-permute-start | bytes 1376264 | tf_op jit(solution)/shard_map/ppermute | solution.py:345
  69.8 2.7 %collective-permute-start.21 = (f32[16,2048]{1,0:T(8,128)S(1)}, f32[16,2048]{1,0:T(8,128)S(1)}, u32[]{:S(2)}, u32[]{:S(2)}) collective-permute-start(f32[16,2048]{1,0:T(8,128)S(1)} %shard_map.107.refs_2_.refs_0_), channel_id=1, source_target_pairs={{0,96},{32,64},{64,32},{96,0},{1,97},{33,65},{65,33},{97,1},{2,98}... | collective-permute-start | bytes 393224 | tf_op jit(solution)/shard_map/ppermute | solution.py:353
  72.5 0.9 collective-permute-start.20
  73.4 2.3 %collective-permute-start.19 = (f32[32,896]{1,0:T(8,128)S(1)}, f32[32,896]{1,0:T(8,128)S(1)}, u32[]{:S(2)}, u32[]{:S(2)}) collective-permute-start(f32[32,896]{1,0:T(8,128)S(1)} %get-tuple-element.60.refs_3_.refs_0_), channel_id=1, source_target_pairs={{0,96},{32,64},{64,32},{96,0},{1,97},{33,65},{65,33},{97,1},{2,98}... | collective-permute-start | bytes 344072 | tf_op jit(solution)/shard_map/ppermute | solution.py:353
  76.8 1.6 %collective-permute-start.22 = (f32[8,2048]{1,0:T(8,128)S(1)}, f32[8,2048]{1,0:T(8,128)S(1)}, u32[]{:S(2)}, u32[]{:S(2)}) collective-permute-start(f32[8,2048]{1,0:T(8,128)S(1)} %get-tuple-element.62.refs_0_), channel_id=1, source_target_pairs={{0,24},{4,28},{8,16},{12,20},{16,8},{20,12},{24,0},{28,4},{1,25},{... | collective-permute-start | bytes 196616 | tf_op jit(solution)/shard_map/ppermute | solution.py:357
  78.5 3.8 %collective-permute-done.22.refs_1_ = f32[8,2048]{1,0:T(8,128)S(1)} collective-permute-done((f32[8,2048]{1,0:T(8,128)S(1)}, f32[8,2048]{1,0:T(8,128)S(1)}, u32[]{:S(2)}, u32[]{:S(2)}) %collective-permute-start.22) | collective-permute-done | bytes 65568 | tf_op jit(solution)/shard_map/ppermute | solution.py:357
  82.4 3.0 %collective-permute-start.24 = (f32[64,896]{1,0:T(8,128)S(1)}, f32[64,896]{1,0:T(8,128)S(1)}, u32[]{:S(2)}, u32[]{:S(2)}) collective-permute-start(f32[64,896]{1,0:T(8,128)S(1)} %get-tuple-element.65.refs_2_), channel_id=1, source_target_pairs={{0,96},{32,64},{64,32},{96,0},{1,97},{33,65},{65,33},{97,1},{2,98}... | collective-permute-start | bytes 688136 | tf_op jit(solution)/shard_map/ppermute | solution.py:353
  86.3 3.4 %collective-permute-done.24.refs_1_ = f32[64,896]{1,0:T(8,128)S(1)} collective-permute-done((f32[64,896]{1,0:T(8,128)S(1)}, f32[64,896]{1,0:T(8,128)S(1)}, u32[]{:S(2)}, u32[]{:S(2)}) %collective-permute-start.24) | collective-permute-done | bytes 229408 | tf_op jit(solution)/shard_map/ppermute | solution.py:353
  89.7 1.7 %collective-permute-done.23.refs_0_ = f32[64,896]{1,0:T(8,128)S(1)} collective-permute-done((f32[64,896]{1,0:T(8,128)S(1)}, f32[64,896]{1,0:T(8,128)S(1)}, u32[]{:S(2)}, u32[]{:S(2)}) %collective-permute-start.23) | collective-permute-done | bytes 229408 | tf_op jit(solution)/shard_map/ppermute | solution.py:353
  91.6 1.0 %shard_map.116 = f32[64,3584]{1,0:T(8,128)} custom-call(f32[64,896]{1,0:T(8,128)S(1)} %get-tuple-element.63.refs_3_.refs_0_, f32[64,896]{1,0:T(8,128)S(1)} %get-tuple-element.67.refs_2_.refs_1_, f32[64,896]{1,0:T(8,128)S(1)} %get-tuple-element.65.refs_2_, f32[64,896]{1,0:T(8,128)S(1)} %get-tuple-element.68.refs_3_, f32[32,2048]{1,0:T(8,128)S(1)} %shard_map.115.refs_4_.refs_0_), custom_call_target="tpu_custom_call" | custom-call | flops 1 | bytes 1 | tf_op jit(solution)/shard_map/pallas_call | solution.py:49
  (58 shorter events, 8.8 us)
Async XLA Ops:
  0.6 22.4 %copy-start = (bf16[256,2048]{1,0:T(8,128)(2,1)S(1)}, bf16[256,2048]{1,0:T(8,128)(2,1)}, u32[]{:S(2)}) copy-start(bf16[256,2048]{1,0:T(8,128)(2,1)} %refs_1_.5) | copy-start | bytes 3145732
  0.6 22.4 %copy-start.1 = (bf16[256,3584]{1,0:T(8,128)(2,1)S(1)}, bf16[256,3584]{1,0:T(8,128)(2,1)}, u32[]{:S(2)}) copy-start(bf16[256,3584]{1,0:T(8,128)(2,1)} %refs_3_.3) | copy-start | bytes 5505028
  0.7 22.4 %copy-start.2 = (bf16[3584,64]{0,1:T(8,128)(2,1)S(1)}, bf16[3584,64]{0,1:T(8,128)(2,1)}, u32[]{:S(2)}) copy-start(bf16[3584,64]{0,1:T(8,128)(2,1)} %param.9) | copy-start | bytes 1376260
  0.7 26.4 %copy-start.4 = (f32[2048]{0:T(1024)S(1)}, f32[2048]{0:T(1024)}, u32[]{:S(2)}) copy-start(f32[2048]{0:T(1024)} %param.11) | copy-start | bytes 24580
  17.1 1.3 %collective-permute-start = (f32[2,2048]{1,0:T(2,128)S(1)}, f32[2,2048]{1,0:T(2,128)S(1)}, u32[]{:S(2)}, u32[]{:S(2)}) collective-permute-start(f32[2,2048]{1,0:T(2,128)S(1)} %get-tuple-element.38.refs_3_), channel_id=1, source_target_pairs={{0,4},{4,0},{8,12},{12,8},{16,20},{20,16},{24,28},{28,24},{1,5},{5... | collective-permute-start | bytes 49160 | tf_op jit(solution)/shard_map/ppermute | solution.py:361
  18.4 5.8 %collective-permute-start.3 = (f32[2,2048]{1,0:T(2,128)S(1)}, f32[2,2048]{1,0:T(2,128)S(1)}, u32[]{:S(2)}, u32[]{:S(2)}) collective-permute-start(f32[2,2048]{1,0:T(2,128)S(1)} %add.3.refs_0_), channel_id=1, source_target_pairs={{0,24},{4,28},{8,0},{12,4},{16,8},{20,12},{24,16},{28,20},{1,25},{... | collective-permute-start | bytes 49160 | tf_op jit(solution)/shard_map/ppermute | solution.py:349
  21.3 5.2 %collective-permute-start.2 = (f32[2,2048]{1,0:T(2,128)S(1)}, f32[2,2048]{1,0:T(2,128)S(1)}, u32[]{:S(2)}, u32[]{:S(2)}) collective-permute-start(f32[2,2048]{1,0:T(2,128)S(1)} %add.3.refs_0_), channel_id=1, source_target_pairs={{0,16},{4,20},{8,24},{12,28},{16,0},{20,4},{24,8},{28,12},{1,17},{... | collective-permute-start | bytes 49160 | tf_op jit(solution)/shard_map/ppermute | solution.py:349
  22.1 4.9 %collective-permute-start.1 = (f32[2,2048]{1,0:T(2,128)S(1)}, f32[2,2048]{1,0:T(2,128)S(1)}, u32[]{:S(2)}, u32[]{:S(2)}) collective-permute-start(f32[2,2048]{1,0:T(2,128)S(1)} %add.3.refs_0_), channel_id=1, source_target_pairs={{0,8},{4,12},{8,16},{12,20},{16,24},{20,28},{24,0},{28,4},{1,9},{5... | collective-permute-start | bytes 49160 | tf_op jit(solution)/shard_map/ppermute | solution.py:349
  27.1 8.2 %copy-start.3 = (bf16[64,2048]{1,0:T(8,128)(2,1)S(1)}, bf16[64,2048]{1,0:T(8,128)(2,1)}, u32[]{:S(2)}) copy-start(bf16[64,2048]{1,0:T(8,128)(2,1)} %refs_2_.3) | copy-start | bytes 786436
  28.3 16.3 %collective-permute-start.6 = (f32[448,256]{1,0:T(8,128)S(1)}, f32[448,256]{1,0:T(8,128)S(1)}, u32[]{:S(2)}, u32[]{:S(2)}) collective-permute-start(f32[448,256]{1,0:T(8,128)S(1)} %get-tuple-element.49), channel_id=1, source_target_pairs={{0,1},{1,2},{2,3},{3,0},{4,5},{5,6},{6,7},{7,4},{8,9},{9,10},{10,1... | collective-permute-start | bytes 1376264 | tf_op jit(solution)/shard_map/ppermute | solution.py:345
  29.9 15.6 %collective-permute-start.7 = (f32[448,256]{1,0:T(8,128)S(1)}, f32[448,256]{1,0:T(8,128)S(1)}, u32[]{:S(2)}, u32[]{:S(2)}) collective-permute-start(f32[448,256]{1,0:T(8,128)S(1)} %get-tuple-element.50), channel_id=1, source_target_pairs={{0,3},{1,0},{2,1},{3,2},{4,7},{5,4},{6,5},{7,6},{8,11},{9,8},{10,9... | collective-permute-start | bytes 1376264 | tf_op jit(solution)/shard_map/ppermute | solution.py:345
  31.8 3.3 %collective-permute-start.4 = (f32[32,2048]{1,0:T(8,128)S(1)}, f32[32,2048]{1,0:T(8,128)S(1)}, u32[]{:S(2)}, u32[]{:S(2)}) collective-permute-start(f32[32,2048]{1,0:T(8,128)S(1)} %get-tuple-element.43.refs_2_), channel_id=1, source_target_pairs={{0,4},{4,0},{8,12},{12,8},{16,20},{20,16},{24,28},{28,24},{1,5},{5... | collective-permute-start | bytes 786440 | tf_op jit(solution)/shard_map/ppermute | solution.py:361
  33.0 17.3 %collective-permute-start.9 = (f32[448,256]{1,0:T(8,128)S(1)}, f32[448,256]{1,0:T(8,128)S(1)}, u32[]{:S(2)}, u32[]{:S(2)}) collective-permute-start(f32[448,256]{1,0:T(8,128)S(1)} %get-tuple-element.51), channel_id=1, source_target_pairs={{0,3},{1,0},{2,1},{3,2},{4,7},{5,4},{6,5},{7,6},{8,11},{9,8},{10,9... | collective-permute-start | bytes 1376264 | tf_op jit(solution)/shard_map/ppermute | solution.py:345
  34.9 15.5 %collective-permute-start.8 = (f32[448,256]{1,0:T(8,128)S(1)}, f32[448,256]{1,0:T(8,128)S(1)}, u32[]{:S(2)}, u32[]{:S(2)}) collective-permute-start(f32[448,256]{1,0:T(8,128)S(1)} %get-tuple-element.44.refs_2_), channel_id=1, source_target_pairs={{0,1},{1,2},{2,3},{3,0},{4,5},{5,6},{6,7},{7,4},{8,9},{9,10},{10,1... | collective-permute-start | bytes 1376264 | tf_op jit(solution)/shard_map/ppermute | solution.py:345
  35.1 5.5 %collective-permute-start.5 = (f32[16,2048]{1,0:T(8,128)S(1)}, f32[16,2048]{1,0:T(8,128)S(1)}, u32[]{:S(2)}, u32[]{:S(2)}) collective-permute-start(f32[16,2048]{1,0:T(8,128)S(1)} %get-tuple-element.46.refs_5_), channel_id=1, source_target_pairs={{0,8},{4,12},{8,0},{12,4},{16,24},{20,28},{24,16},{28,20},{1,9},{5... | collective-permute-start | bytes 393224 | tf_op jit(solution)/shard_map/ppermute | solution.py:357
  40.6 10.3 %collective-permute-start.11 = (f32[64,896]{1,0:T(8,128)S(1)}, f32[64,896]{1,0:T(8,128)S(1)}, u32[]{:S(2)}, u32[]{:S(2)}) collective-permute-start(f32[64,896]{1,0:T(8,128)S(1)} %get-tuple-element.55), channel_id=1, source_target_pairs={{0,64},{32,96},{64,0},{96,32},{1,65},{33,97},{65,1},{97,33},{2,66}... | collective-permute-start | bytes 688136 | tf_op jit(solution)/shard_map/ppermute | solution.py:345
  44.5 10.7 %collective-permute-start.12 = (f32[64,896]{1,0:T(8,128)S(1)}, f32[64,896]{1,0:T(8,128)S(1)}, u32[]{:S(2)}, u32[]{:S(2)}) collective-permute-start(f32[64,896]{1,0:T(8,128)S(1)} %get-tuple-element.56), channel_id=1, source_target_pairs={{0,32},{32,64},{64,96},{96,0},{1,33},{33,65},{65,97},{97,1},{2,34}... | collective-permute-start | bytes 688136 | tf_op jit(solution)/shard_map/ppermute | solution.py:345
  45.5 10.4 %collective-permute-start.13 = (f32[64,896]{1,0:T(8,128)S(1)}, f32[64,896]{1,0:T(8,128)S(1)}, u32[]{:S(2)}, u32[]{:S(2)}) collective-permute-start(f32[64,896]{1,0:T(8,128)S(1)} %get-tuple-element.57), channel_id=1, source_target_pairs={{0,96},{32,0},{64,32},{96,64},{1,97},{33,1},{65,33},{97,65},{2,98}... | collective-permute-start | bytes 688136 | tf_op jit(solution)/shard_map/ppermute | solution.py:345
  56.0 7.0 %collective-permute-start.15 = (f32[64,896]{1,0:T(8,128)S(1)}, f32[64,896]{1,0:T(8,128)S(1)}, u32[]{:S(2)}, u32[]{:S(2)}) collective-permute-start(f32[64,896]{1,0:T(8,128)S(1)} %shard_map.104.refs_3_.refs_0_), channel_id=1, source_target_pairs={{0,1},{1,0},{2,3},{3,2},{4,5},{5,4},{6,7},{7,6},{8,9},{9,8},{10,11... | collective-permute-start | bytes 688136 | tf_op jit(solution)/shard_map/ppermute | solution.py:353
  56.4 5.5 %collective-permute-start.10 = (f32[8,2048]{1,0:T(8,128)S(1)}, f32[8,2048]{1,0:T(8,128)S(1)}, u32[]{:S(2)}, u32[]{:S(2)}) collective-permute-start(f32[8,2048]{1,0:T(8,128)S(1)} %get-tuple-element.48.refs_2_), channel_id=1, source_target_pairs={{0,24},{4,28},{8,16},{12,20},{16,8},{20,12},{24,0},{28,4},{1,25},{... | collective-permute-start | bytes 196616 | tf_op jit(solution)/shard_map/ppermute | solution.py:357
  61.9 5.0 %collective-permute-start.14 = (f32[16,2048]{1,0:T(8,128)S(1)}, f32[16,2048]{1,0:T(8,128)S(1)}, u32[]{:S(2)}, u32[]{:S(2)}) collective-permute-start(f32[16,2048]{1,0:T(8,128)S(1)} %shard_map.105.refs_2_.refs_0_), channel_id=1, source_target_pairs={{0,32},{32,0},{64,96},{96,64},{1,33},{33,1},{65,97},{97,65},{2,34}... | collective-permute-start | bytes 393224 | tf_op jit(solution)/shard_map/ppermute | solution.py:353
  63.0 9.4 %collective-permute-start.18 = (f32[64,896]{1,0:T(8,128)S(1)}, f32[64,896]{1,0:T(8,128)S(1)}, u32[]{:S(2)}, u32[]{:S(2)}) collective-permute-start(f32[64,896]{1,0:T(8,128)S(1)} %shard_map.106.refs_2_.refs_0_), channel_id=1, source_target_pairs={{0,3},{1,2},{2,1},{3,0},{4,7},{5,6},{6,5},{7,4},{8,11},{9,10},{10,... | collective-permute-start | bytes 688136 | tf_op jit(solution)/shard_map/ppermute | solution.py:353
  67.0 18.5 %collective-permute-start.17 = (f32[448,256]{1,0:T(8,128)S(1)}, f32[448,256]{1,0:T(8,128)S(1)}, u32[]{:S(2)}, u32[]{:S(2)}) collective-permute-start(f32[448,256]{1,0:T(8,128)S(1)} %get-tuple-element.59), channel_id=1, source_target_pairs={{0,3},{1,0},{2,1},{3,2},{4,7},{5,4},{6,5},{7,6},{8,11},{9,8},{10,9... | collective-permute-start | bytes 1376264 | tf_op jit(solution)/shard_map/ppermute | solution.py:345
  69.8 15.7 %collective-permute-start.16 = (f32[448,256]{1,0:T(8,128)S(1)}, f32[448,256]{1,0:T(8,128)S(1)}, u32[]{:S(2)}, u32[]{:S(2)}) collective-permute-start(f32[448,256]{1,0:T(8,128)S(1)} %get-tuple-element.58.refs_2_), channel_id=1, source_target_pairs={{0,1},{1,2},{2,3},{3,0},{4,5},{5,6},{6,7},{7,4},{8,9},{9,10},{10,1... | collective-permute-start | bytes 1376264 | tf_op jit(solution)/shard_map/ppermute | solution.py:345
  69.8 6.5 %collective-permute-start.21 = (f32[16,2048]{1,0:T(8,128)S(1)}, f32[16,2048]{1,0:T(8,128)S(1)}, u32[]{:S(2)}, u32[]{:S(2)}) collective-permute-start(f32[16,2048]{1,0:T(8,128)S(1)} %shard_map.107.refs_2_.refs_0_), channel_id=1, source_target_pairs={{0,96},{32,64},{64,32},{96,0},{1,97},{33,65},{65,33},{97,1},{2,98}... | collective-permute-start | bytes 393224 | tf_op jit(solution)/shard_map/ppermute | solution.py:353
  72.5 9.9 %collective-permute-start.20 = (f32[32,896]{1,0:T(8,128)S(1)}, f32[32,896]{1,0:T(8,128)S(1)}, u32[]{:S(2)}, u32[]{:S(2)}) collective-permute-start(f32[32,896]{1,0:T(8,128)S(1)} %get-tuple-element.61.refs_2_), channel_id=1, source_target_pairs={{0,32},{32,0},{64,96},{96,64},{1,33},{33,1},{65,97},{97,65},{2,34}... | collective-permute-start | bytes 344072 | tf_op jit(solution)/shard_map/ppermute | solution.py:353
  73.4 9.0 %collective-permute-start.19 = (f32[32,896]{1,0:T(8,128)S(1)}, f32[32,896]{1,0:T(8,128)S(1)}, u32[]{:S(2)}, u32[]{:S(2)}) collective-permute-start(f32[32,896]{1,0:T(8,128)S(1)} %get-tuple-element.60.refs_3_.refs_0_), channel_id=1, source_target_pairs={{0,96},{32,64},{64,32},{96,0},{1,97},{33,65},{65,33},{97,1},{2,98}... | collective-permute-start | bytes 344072 | tf_op jit(solution)/shard_map/ppermute | solution.py:353
  76.8 5.5 %collective-permute-start.22 = (f32[8,2048]{1,0:T(8,128)S(1)}, f32[8,2048]{1,0:T(8,128)S(1)}, u32[]{:S(2)}, u32[]{:S(2)}) collective-permute-start(f32[8,2048]{1,0:T(8,128)S(1)} %get-tuple-element.62.refs_0_), channel_id=1, source_target_pairs={{0,24},{4,28},{8,16},{12,20},{16,8},{20,12},{24,0},{28,4},{1,25},{... | collective-permute-start | bytes 196616 | tf_op jit(solution)/shard_map/ppermute | solution.py:357
  82.4 7.3 %collective-permute-start.24 = (f32[64,896]{1,0:T(8,128)S(1)}, f32[64,896]{1,0:T(8,128)S(1)}, u32[]{:S(2)}, u32[]{:S(2)}) collective-permute-start(f32[64,896]{1,0:T(8,128)S(1)} %get-tuple-element.65.refs_2_), channel_id=1, source_target_pairs={{0,96},{32,64},{64,32},{96,0},{1,97},{33,65},{65,33},{97,1},{2,98}... | collective-permute-start | bytes 688136 | tf_op jit(solution)/shard_map/ppermute | solution.py:353
  85.4 6.0 %collective-permute-start.23 = (f32[64,896]{1,0:T(8,128)S(1)}, f32[64,896]{1,0:T(8,128)S(1)}, u32[]{:S(2)}, u32[]{:S(2)}) collective-permute-start(f32[64,896]{1,0:T(8,128)S(1)} %get-tuple-element.63.refs_3_.refs_0_), channel_id=1, source_target_pairs={{0,32},{32,0},{64,96},{96,64},{1,33},{33,1},{65,97},{97,65},{2,34}... | collective-permute-start | bytes 688136 | tf_op jit(solution)/shard_map/ppermute | solution.py:353
  85.4 6.0 %collective-permute-start.25 = (f32[16,2048]{1,0:T(8,128)S(1)}, f32[16,2048]{1,0:T(8,128)S(1)}, u32[]{:S(2)}, u32[]{:S(2)}) collective-permute-start(f32[16,2048]{1,0:T(8,128)S(1)} %shard_map.111.refs_4_.refs_0_), channel_id=1, source_target_pairs={{0,8},{4,12},{8,0},{12,4},{16,24},{20,28},{24,16},{28,20},{1,9},{5... | collective-permute-start | bytes 393224 | tf_op jit(solution)/shard_map/ppermute | solution.py:357
  91.5 1.6 %collective-permute-start.26 = (f32[32,2048]{1,0:T(8,128)S(1)}, f32[32,2048]{1,0:T(8,128)S(1)}, u32[]{:S(2)}, u32[]{:S(2)}) collective-permute-start(f32[32,2048]{1,0:T(8,128)S(1)} %shard_map.115.refs_4_.refs_0_), channel_id=1, source_target_pairs={{0,4},{4,0},{8,12},{12,8},{16,20},{20,16},{24,28},{28,24},{1,5},{5... | collective-permute-start | bytes 786440 | tf_op jit(solution)/shard_map/ppermute | solution.py:361

commit v8 on v7

--- a/solution.py
+++ b/solution.py
@@ -162,8 +162,10 @@
     return m_ref[pl.ds(pl.multiple_of(start, 64), size)]
 
 
-def far_kernel(stat_ref, r1_ref, r2_ref, r3_ref, mag_ref, dy_ref, m_ref, vec_ref, scaled_ref, h0_ref, h1_ref):
-    total = (stat_ref[...] + r2_ref[...]) + (r1_ref[...] + r3_ref[...])
+def far_kernel(*refs):
+    stats, (mag_ref, dy_ref, m_ref, vec_ref, scaled_ref, h0_ref, h1_ref) = refs[:8], refs[8:]
+    chips = [stats[k][...] + stats[k + 4][...] for k in range(4)]
+    total = (chips[0] + chips[2]) + (chips[1] + chips[3])
     squares = total[0:1] + EPS
     norms = jnp.sqrt(squares)
     scale = mag_ref[...] / norms
@@ -345,8 +347,8 @@
     return lax.ppermute(value, axis, [(i, (i + k) % count) for i in range(count)])
 
 
-def ring_x(value, k, count=8):
-    return lax.ppermute(value, "rows", [(i, (i + 2 * k) % count) for i in range(count)])
+def ring_x(value, k, core=0, count=8):
+    return lax.ppermute(value, "rows", [(i, (i + 2 * k) % count ^ core) for i in range(count)])
 
 
 def swap(value, axis, step):
@@ -371,13 +373,13 @@
     bq = call(q_kernel, [out((rank, cols))], [VMEM] * 3, a.T, x, dy, after=[stat])[0]
 
     m = pltpu.with_memory_space_constraint(m, pltpu.VMEM)
-    stat = stat + swap_core(stat)
+    stats = [stat] + [ring_x(stat, k) for k in (1, 2, 3)] + [ring_x(stat, k, 1) for k in range(4)]
     far = rows // 8
     vec, scaled, h0, h1 = call(
         far_kernel,
         [out((4, cols)), out((toks, cols), BF16), out((far, toks)), out((far, toks))],
-        [VMEM] * 7,
-        stat, ring_x(stat, 1), ring_x(stat, 2), ring_x(stat, 3), mag, dy, m,
+        [VMEM] * 11,
+        *stats, mag, dy, m,
         after=[bq],
     )
     u0, u1 = ring(h0, "cols", 1), ring(h1, "cols", 3)

time: 95.1 us -> 98.6 us (1.037)
  starting transfers between devices: 37 us -> 39.3 us
  waiting for transfers between devices: 24.7 us -> 25.8 us
    ppermute x3 -> x7, starting transfers between devices: 4.59 us -> 8.31 us  [ring_x(): lax.ppermute(value, 'rows', [(i, (i + 2 * k) % count ^ core) for i in ran...]
    ppermute x4, waiting for transfers between devices: 7.63 us -> 9.1 us  [swap_x(): lax.ppermute(value, 'rows', [(i, i ^ 2 if step == 0 else 6 - 2 * (i // 2)...]
    ppermute x4, starting transfers between devices: 3.52 us -> 2.21 us  [swap_x(): lax.ppermute(value, 'rows', [(i, i ^ 2 if step == 0 else 6 - 2 * (i // 2)...]
    ppermute x3 -> x2, waiting for transfers between devices: 1.7 us -> 0.53 us  [swap_core(): return lax.ppermute(value, 'rows', [(i, i ^ 1) for i in range(count)])]
    ppermute x3 -> x7, waiting for transfers between devices: 2.88 us -> 3.73 us  [ring_x(): lax.ppermute(value, 'rows', [(i, (i + 2 * k) % count ^ core) for i in ran...]
  transfers between devices with their start and end apart: 27 -> 30, of which waited for: 15 -> 14; matrix products, arithmetic and copies ran while one was open for 0% -> 0% of each run, Pallas kernels for 14% -> 13%
where the time goes in v8:
time: 98.6 us; the launch traced here: 97.5 us
  starting transfers between devices  39.3 us (40%)
  Pallas kernels  31.4 us (32%)
  waiting for transfers between devices  25.8 us (26%)
    pallas_call x23, Pallas kernels, call(): pl.pallas_call(body, out_shape=outs, in_specs=list(specs) + [ANY] * len(a...  31.4 us
    ppermute x9, starting transfers between devices, ring(): lax.ppermute(value, axis, [(i, (i + k) % count) for i in range(count)])  15.4 us
    ppermute x8, starting transfers between devices, swap(): lax.ppermute(value, axis, [(i, i ^ 1 if step == 0 else 3 - i) for i in ra...  13.3 us
    ppermute x4, waiting for transfers between devices, swap_x(): lax.ppermute(value, 'rows', [(i, i ^ 2 if step == 0 else 6 - 2 * (i // 2)...  9.1 us
    ppermute x7, starting transfers between devices, ring_x(): lax.ppermute(value, 'rows', [(i, (i + 2 * k) % count ^ core) for i in ran...  8.31 us
    ppermute x8, waiting for transfers between devices, swap(): lax.ppermute(value, axis, [(i, i ^ 1 if step == 0 else 3 - i) for i in ra...  6.71 us
    ppermute x9, waiting for transfers between devices, ring(): lax.ppermute(value, axis, [(i, (i + k) % count) for i in range(count)])  5.77 us
    ppermute x7, waiting for transfers between devices, ring_x(): lax.ppermute(value, 'rows', [(i, (i + 2 * k) % count ^ core) for i in ran...  3.73 us
  transfers between devices with their start and end apart: 30, of which 14 were waited for; matrix products, arithmetic and copies ran while one was open for 0% of the time, Pallas kernels for 13%

profile of v8, /device:TPU:0, one launch (start us, length us, event | category | flops | bytes accessed | tf_op | source)
XLA Modules:
  0.0 97.5 jit_solution(8273611451118700841)
XLA Ops:
  0.7 16.5 %shard_map.93 = (bf16[3584,2048]{1,0:T(8,128)(2,1)S(1)}, f32[2,2048]{1,0:T(2,128)S(1)}, f32[64,2048]{1,0:T(8,128)S(1)}) custom-call(bf16[3584,2048]{1,0:T(8,128)(2,1)} %refs_0_.1, bf16[256,3584]{1,0:T(8,128)(2,1)} %refs_3_.3, bf16[64,3584]{1,0:T(8,128)(2,1)} %bitcast.4, bf16[64,2048]{1,0:T(8,128)(2,1)} %refs_2_.3, bf16[256,2048]{1,0:T(8,128)(2,1)} %refs_1_.5), custom_call_target="tpu_custom_call" | custom-call | flops 5637144576 | bytes 14680064 | tf_op jit(solution)/shard_map/pallas_call | solution.py:49
  17.1 2.3 %collective-permute-start.6 = (f32[2,2048]{1,0:T(2,128)S(1)}, f32[2,2048]{1,0:T(2,128)S(1)}, u32[]{:S(2)}, u32[]{:S(2)}) collective-permute-start(f32[2,2048]{1,0:T(2,128)S(1)} %get-tuple-element.38.refs_3_.refs_0_), channel_id=1, source_target_pairs={{0,28},{4,24},{8,4},{12,0},{16,12},{20,8},{24,20},{28,16},{1,29},{... | collective-permute-start | bytes 49160 | tf_op jit(solution)/shard_map/ppermute | solution.py:351
  19.5 1.1 %collective-permute-start.5 = (f32[2,2048]{1,0:T(2,128)S(1)}, f32[2,2048]{1,0:T(2,128)S(1)}, u32[]{:S(2)}, u32[]{:S(2)}) collective-permute-start(f32[2,2048]{1,0:T(2,128)S(1)} %get-tuple-element.38.refs_3_.refs_0_), channel_id=1, source_target_pairs={{0,20},{4,16},{8,28},{12,24},{16,4},{20,0},{24,12},{28,8},{1,21},{... | collective-permute-start | bytes 49160 | tf_op jit(solution)/shard_map/ppermute | solution.py:351
  21.6 2.4 %collective-permute-start.2 = (f32[2,2048]{1,0:T(2,128)S(1)}, f32[2,2048]{1,0:T(2,128)S(1)}, u32[]{:S(2)}, u32[]{:S(2)}) collective-permute-start(f32[2,2048]{1,0:T(2,128)S(1)} %get-tuple-element.38.refs_3_.refs_0_), channel_id=1, source_target_pairs={{0,24},{4,28},{8,0},{12,4},{16,8},{20,12},{24,16},{28,20},{1,25},{... | collective-permute-start | bytes 49160 | tf_op jit(solution)/shard_map/ppermute | solution.py:351
  23.9 1.5 %collective-permute-start.1 = (f32[2,2048]{1,0:T(2,128)S(1)}, f32[2,2048]{1,0:T(2,128)S(1)}, u32[]{:S(2)}, u32[]{:S(2)}) collective-permute-start(f32[2,2048]{1,0:T(2,128)S(1)} %get-tuple-element.38.refs_3_.refs_0_), channel_id=1, source_target_pairs={{0,16},{4,20},{8,24},{12,28},{16,0},{20,4},{24,8},{28,12},{1,17},{... | collective-permute-start | bytes 49160 | tf_op jit(solution)/shard_map/ppermute | solution.py:351
  25.5 1.2 %shard_map.94.refs_11_.refs_1_ = f32[64,2048]{1,0:T(8,128)S(1)} custom-call(bf16[64,3584]{1,0:T(8,128)(2,1)S(1)} %bitcast.5, bf16[256,3584]{1,0:T(8,128)(2,1)S(1)} %copy-done.1, bf16[256,2048]{1,0:T(8,128)(2,1)S(1)} %copy-done, f32[2,2048]{1,0:T(2,128)S(1)} %get-tuple-element.38.refs_3_.refs_0_), custom_call_target="tpu_custom_call" | custom-call | flops 1 | bytes 1 | tf_op jit(solution)/shard_map/pallas_call | solution.py:49
  26.7 2.5 %collective-permute-done.1.refs_2_ = f32[2,2048]{1,0:T(2,128)S(1)} collective-permute-done((f32[2,2048]{1,0:T(2,128)S(1)}, f32[2,2048]{1,0:T(2,128)S(1)}, u32[]{:S(2)}, u32[]{:S(2)}) %collective-permute-start.1) | collective-permute-done | bytes 16416 | tf_op jit(solution)/shard_map/ppermute | solution.py:351
  29.2 1.2 %collective-permute-done.refs_1_ = f32[2,2048]{1,0:T(2,128)S(1)} collective-permute-done((f32[2,2048]{1,0:T(2,128)S(1)}, f32[2,2048]{1,0:T(2,128)S(1)}, u32[]{:S(2)}, u32[]{:S(2)}) %collective-permute-start) | collective-permute-done | bytes 16416 | tf_op jit(solution)/shard_map/ppermute | solution.py:351
  30.4 1.2 %shard_map.95 = (f32[4,2048]{1,0:T(4,128)S(1)}, bf16[256,2048]{1,0:T(8,128)(2,1)S(1)}, f32[448,256]{1,0:T(8,128)S(1)}, f32[448,256]{1,0:T(8,128)S(1)}) custom-call(f32[2,2048]{1,0:T(2,128)S(1)} %get-tuple-element.38.refs_3_.refs_0_, f32[2,2048]{1,0:T(2,128)S(1)} %collective-permute-done.refs_1_, f32[2,2048]{1,0:T(2,128)S(1)} %collective-permute-done.1.refs_2_, ...), custom_call_target="tpu_custom_call" | custom-call | flops 1 | bytes 1 | tf_op jit(solution)/shard_map/pallas_call | solution.py:49
  31.6 1.6 %collective-permute-start.9 = (f32[448,256]{1,0:T(8,128)S(1)}, f32[448,256]{1,0:T(8,128)S(1)}, u32[]{:S(2)}, u32[]{:S(2)}) collective-permute-start(f32[448,256]{1,0:T(8,128)S(1)} %get-tuple-element.49), channel_id=1, source_target_pairs={{0,1},{1,2},{2,3},{3,0},{4,5},{5,6},{6,7},{7,4},{8,9},{9,10},{10,1... | collective-permute-start | bytes 1376264 | tf_op jit(solution)/shard_map/ppermute | solution.py:347
  33.2 1.7 %collective-permute-start.10 = (f32[448,256]{1,0:T(8,128)S(1)}, f32[448,256]{1,0:T(8,128)S(1)}, u32[]{:S(2)}, u32[]{:S(2)}) collective-permute-start(f32[448,256]{1,0:T(8,128)S(1)} %get-tuple-element.50), channel_id=1, source_target_pairs={{0,3},{1,0},{2,1},{3,2},{4,7},{5,4},{6,5},{7,6},{8,11},{9,8},{10,9... | collective-permute-start | bytes 1376264 | tf_op jit(solution)/shard_map/ppermute | solution.py:347
  35.2 1.1 %shard_map.97 = (f32[448,256]{1,0:T(8,128)S(1)}, f32[448,256]{1,0:T(8,128)S(1)}) custom-call(bf16[3584,2048]{1,0:T(8,128)(2,1)S(1)} %get-tuple-element.37.refs_10_.refs_0_.refs_4_, bf16[256,2048]{1,0:T(8,128)(2,1)S(1)} %get-tuple-element.39.refs_1_, f32[32,2048]{1,0:T(8,128)S(1)} %get-tuple-element.43.refs_2_), custom_call_target="tpu_custom_call" | custom-call | flops 1 | bytes 1 | tf_op jit(solution)/shard_map/pallas_call | solution.py:49
  36.3 1.9 %collective-permute-start.12 = (f32[448,256]{1,0:T(8,128)S(1)}, f32[448,256]{1,0:T(8,128)S(1)}, u32[]{:S(2)}, u32[]{:S(2)}) collective-permute-start(f32[448,256]{1,0:T(8,128)S(1)} %get-tuple-element.51), channel_id=1, source_target_pairs={{0,3},{1,0},{2,1},{3,2},{4,7},{5,4},{6,5},{7,6},{8,11},{9,8},{10,9... | collective-permute-start | bytes 1376264 | tf_op jit(solution)/shard_map/ppermute | solution.py:347
  38.7 5.3 %shard_map.99 = (f32[64,896]{1,0:T(8,128)S(1)}, f32[64,896]{1,0:T(8,128)S(1)}, f32[64,896]{1,0:T(8,128)S(1)}, f32[64,896]{1,0:T(8,128)S(1)}) custom-call(f32[4,2048]{1,0:T(4,128)S(1)} %get-tuple-element.40.refs_0_.refs_2_, bf16[256,2048]{1,0:T(8,128)(2,1)S(1)} %copy-done, bf16[64,2048]{1,0:T(8,128)(2,1)S(1)} %copy-done.3, bf16[256,3584]{1,0:T(8,128)(2,1)S(1)} %copy-done.1, ...), custom_call_target="tpu_custom_call" | custom-call | flops 1 | bytes 1 | tf_op jit(solution)/shard_map/pallas_call | solution.py:49
  44.1 3.9 %collective-permute-start.14 = (f32[64,896]{1,0:T(8,128)S(1)}, f32[64,896]{1,0:T(8,128)S(1)}, u32[]{:S(2)}, u32[]{:S(2)}) collective-permute-start(f32[64,896]{1,0:T(8,128)S(1)} %get-tuple-element.55), channel_id=1, source_target_pairs={{0,64},{32,96},{64,0},{96,32},{1,65},{33,97},{65,1},{97,33},{2,66}... | collective-permute-start | bytes 688136 | tf_op jit(solution)/shard_map/ppermute | solution.py:347
  48.0 1.0 %collective-permute-start.15 = (f32[64,896]{1,0:T(8,128)S(1)}, f32[64,896]{1,0:T(8,128)S(1)}, u32[]{:S(2)}, u32[]{:S(2)}) collective-permute-start(f32[64,896]{1,0:T(8,128)S(1)} %get-tuple-element.56), channel_id=1, source_target_pairs={{0,32},{32,64},{64,96},{96,0},{1,33},{33,65},{65,97},{97,1},{2,34}... | collective-permute-start | bytes 688136 | tf_op jit(solution)/shard_map/ppermute | solution.py:347
  49.0 2.2 %collective-permute-start.16 = (f32[64,896]{1,0:T(8,128)S(1)}, f32[64,896]{1,0:T(8,128)S(1)}, u32[]{:S(2)}, u32[]{:S(2)}) collective-permute-start(f32[64,896]{1,0:T(8,128)S(1)} %get-tuple-element.57), channel_id=1, source_target_pairs={{0,96},{32,0},{64,32},{96,64},{1,97},{33,1},{65,33},{97,65},{2,98}... | collective-permute-start | bytes 688136 | tf_op jit(solution)/shard_map/ppermute | solution.py:347
  51.3 1.1 %shard_map.101.refs_4_.refs_0_ = f32[896,256]{1,0:T(8,128)S(1)} custom-call(bf16[3584,2048]{1,0:T(8,128)(2,1)S(1)} %get-tuple-element.37.refs_10_.refs_0_.refs_4_, bf16[256,2048]{1,0:T(8,128)(2,1)S(1)} %get-tuple-element.39.refs_1_, f32[8,2048]{1,0:T(8,128)S(1)} %get-tuple-element.48.refs_2_, f32[448,256]{1,0:T(8,128)S(1)} %collective-permute-done.9.refs_3_.refs_2_, ...), custom_call_target="tpu_custom_call" | custom-call | flops 1 | bytes 1 | tf_op jit(solution)/shard_map/pallas_call | solution.py:49
  52.4 1.1 %shard_map.102 = (f32[448,256]{1,0:T(8,128)S(1)}, f32[448,256]{1,0:T(8,128)S(1)}) custom-call(bf16[3584,2048]{1,0:T(8,128)(2,1)S(1)} %get-tuple-element.37.refs_10_.refs_0_.refs_4_, bf16[256,2048]{1,0:T(8,128)(2,1)S(1)} %get-tuple-element.39.refs_1_, f32[448,256]{1,0:T(8,128)S(1)} %collective-permute-done.9.refs_3_.refs_2_, ...), custom_call_target="tpu_custom_call" | custom-call | flops 1 | bytes 1 | tf_op jit(solution)/shard_map/pallas_call | solution.py:49
  54.4 4.3 %collective-permute-done.15.refs_2_ = f32[64,896]{1,0:T(8,128)S(1)} collective-permute-done((f32[64,896]{1,0:T(8,128)S(1)}, f32[64,896]{1,0:T(8,128)S(1)}, u32[]{:S(2)}, u32[]{:S(2)}) %collective-permute-start.15) | collective-permute-done | bytes 229408 | tf_op jit(solution)/shard_map/ppermute | solution.py:347
  59.9 1.0 %collective-permute-start.13 = (f32[8,2048]{1,0:T(8,128)S(1)}, f32[8,2048]{1,0:T(8,128)S(1)}, u32[]{:S(2)}, u32[]{:S(2)}) collective-permute-start(f32[8,2048]{1,0:T(8,128)S(1)} %get-tuple-element.48.refs_2_), channel_id=1, source_target_pairs={{0,24},{4,28},{8,16},{12,20},{16,8},{20,12},{24,0},{28,4},{1,25},{... | collective-permute-start | bytes 196616 | tf_op jit(solution)/shard_map/ppermute | solution.py:359
  60.9 4.4 %collective-permute-done.13.refs_1_ = f32[8,2048]{1,0:T(8,128)S(1)} collective-permute-done((f32[8,2048]{1,0:T(8,128)S(1)}, f32[8,2048]{1,0:T(8,128)S(1)}, u32[]{:S(2)}, u32[]{:S(2)}) %collective-permute-start.13) | collective-permute-done | bytes 65568 | tf_op jit(solution)/shard_map/ppermute | solution.py:359
  65.4 1.1 %collective-permute-start.17 = (f32[16,2048]{1,0:T(8,128)S(1)}, f32[16,2048]{1,0:T(8,128)S(1)}, u32[]{:S(2)}, u32[]{:S(2)}) collective-permute-start(f32[16,2048]{1,0:T(8,128)S(1)} %shard_map.105.refs_2_.refs_0_), channel_id=1, source_target_pairs={{0,32},{32,0},{64,96},{96,64},{1,33},{33,1},{65,97},{97,65},{2,34}... | collective-permute-start | bytes 393224 | tf_op jit(solution)/shard_map/ppermute | solution.py:355
  66.5 2.9 %collective-permute-start.21 = (f32[64,896]{1,0:T(8,128)S(1)}, f32[64,896]{1,0:T(8,128)S(1)}, u32[]{:S(2)}, u32[]{:S(2)}) collective-permute-start(f32[64,896]{1,0:T(8,128)S(1)} %shard_map.106.refs_2_.refs_0_), channel_id=1, source_target_pairs={{0,3},{1,2},{2,1},{3,0},{4,7},{5,6},{6,5},{7,4},{8,11},{9,10},{10,... | collective-permute-start | bytes 688136 | tf_op jit(solution)/shard_map/ppermute | solution.py:355
  69.4 1.0 %collective-permute-done.17.refs_1_ = f32[16,2048]{1,0:T(8,128)S(1)} collective-permute-done((f32[16,2048]{1,0:T(8,128)S(1)}, f32[16,2048]{1,0:T(8,128)S(1)}, u32[]{:S(2)}, u32[]{:S(2)}) %collective-permute-start.17) | collective-permute-done | bytes 131104 | tf_op jit(solution)/shard_map/ppermute | solution.py:355
  70.5 2.8 %collective-permute-start.20 = (f32[448,256]{1,0:T(8,128)S(1)}, f32[448,256]{1,0:T(8,128)S(1)}, u32[]{:S(2)}, u32[]{:S(2)}) collective-permute-start(f32[448,256]{1,0:T(8,128)S(1)} %get-tuple-element.59), channel_id=1, source_target_pairs={{0,3},{1,0},{2,1},{3,2},{4,7},{5,4},{6,5},{7,6},{8,11},{9,8},{10,9... | collective-permute-start | bytes 1376264 | tf_op jit(solution)/shard_map/ppermute | solution.py:347
  73.3 2.6 %collective-permute-start.24 = (f32[16,2048]{1,0:T(8,128)S(1)}, f32[16,2048]{1,0:T(8,128)S(1)}, u32[]{:S(2)}, u32[]{:S(2)}) collective-permute-start(f32[16,2048]{1,0:T(8,128)S(1)} %shard_map.107.refs_2_.refs_0_), channel_id=1, source_target_pairs={{0,96},{32,64},{64,32},{96,0},{1,97},{33,65},{65,33},{97,1},{2,98}... | collective-permute-start | bytes 393224 | tf_op jit(solution)/shard_map/ppermute | solution.py:355
  76.9 2.3 %collective-permute-start.22 = (f32[32,896]{1,0:T(8,128)S(1)}, f32[32,896]{1,0:T(8,128)S(1)}, u32[]{:S(2)}, u32[]{:S(2)}) collective-permute-start(f32[32,896]{1,0:T(8,128)S(1)} %get-tuple-element.60.refs_3_.refs_0_), channel_id=1, source_target_pairs={{0,96},{32,64},{64,32},{96,0},{1,97},{33,65},{65,33},{97,1},{2,98}... | collective-permute-start | bytes 344072 | tf_op jit(solution)/shard_map/ppermute | solution.py:355
  81.2 4.6 %collective-permute-done.25.refs_1_ = f32[8,2048]{1,0:T(8,128)S(1)} collective-permute-done((f32[8,2048]{1,0:T(8,128)S(1)}, f32[8,2048]{1,0:T(8,128)S(1)}, u32[]{:S(2)}, u32[]{:S(2)}) %collective-permute-start.25) | collective-permute-done | bytes 65568 | tf_op jit(solution)/shard_map/ppermute | solution.py:359
  85.9 3.0 %collective-permute-start.27 = (f32[64,896]{1,0:T(8,128)S(1)}, f32[64,896]{1,0:T(8,128)S(1)}, u32[]{:S(2)}, u32[]{:S(2)}) collective-permute-start(f32[64,896]{1,0:T(8,128)S(1)} %get-tuple-element.65.refs_2_), channel_id=1, source_target_pairs={{0,96},{32,64},{64,32},{96,0},{1,97},{33,65},{65,33},{97,1},{2,98}... | collective-permute-start | bytes 688136 | tf_op jit(solution)/shard_map/ppermute | solution.py:355
  89.8 3.4 %collective-permute-done.27.refs_1_ = f32[64,896]{1,0:T(8,128)S(1)} collective-permute-done((f32[64,896]{1,0:T(8,128)S(1)}, f32[64,896]{1,0:T(8,128)S(1)}, u32[]{:S(2)}, u32[]{:S(2)}) %collective-permute-start.27) | collective-permute-done | bytes 229408 | tf_op jit(solution)/shard_map/ppermute | solution.py:355
  93.2 1.7 %collective-permute-done.26.refs_0_ = f32[64,896]{1,0:T(8,128)S(1)} collective-permute-done((f32[64,896]{1,0:T(8,128)S(1)}, f32[64,896]{1,0:T(8,128)S(1)}, u32[]{:S(2)}, u32[]{:S(2)}) %collective-permute-start.26) | collective-permute-done | bytes 229408 | tf_op jit(solution)/shard_map/ppermute | solution.py:355
  (63 shorter events, 10.4 us)
Async XLA Ops:
  0.6 24.8 %copy-start = (bf16[256,2048]{1,0:T(8,128)(2,1)S(1)}, bf16[256,2048]{1,0:T(8,128)(2,1)}, u32[]{:S(2)}) copy-start(bf16[256,2048]{1,0:T(8,128)(2,1)} %refs_1_.5) | copy-start | bytes 3145732
  0.7 29.7 %copy-start.4 = (f32[2048]{0:T(1024)S(1)}, f32[2048]{0:T(1024)}, u32[]{:S(2)}) copy-start(f32[2048]{0:T(1024)} %param.11) | copy-start | bytes 24580
  17.1 6.8 %collective-permute-start.6 = (f32[2,2048]{1,0:T(2,128)S(1)}, f32[2,2048]{1,0:T(2,128)S(1)}, u32[]{:S(2)}, u32[]{:S(2)}) collective-permute-start(f32[2,2048]{1,0:T(2,128)S(1)} %get-tuple-element.38.refs_3_.refs_0_), channel_id=1, source_target_pairs={{0,28},{4,24},{8,4},{12,0},{16,12},{20,8},{24,20},{28,16},{1,29},{... | collective-permute-start | bytes 49160 | tf_op jit(solution)/shard_map/ppermute | solution.py:351
  19.5 6.0 %collective-permute-start.5 = (f32[2,2048]{1,0:T(2,128)S(1)}, f32[2,2048]{1,0:T(2,128)S(1)}, u32[]{:S(2)}, u32[]{:S(2)}) collective-permute-start(f32[2,2048]{1,0:T(2,128)S(1)} %get-tuple-element.38.refs_3_.refs_0_), channel_id=1, source_target_pairs={{0,20},{4,16},{8,28},{12,24},{16,4},{20,0},{24,12},{28,8},{1,21},{... | collective-permute-start | bytes 49160 | tf_op jit(solution)/shard_map/ppermute | solution.py:351
  20.6 6.1 %collective-permute-start.4 = (f32[2,2048]{1,0:T(2,128)S(1)}, f32[2,2048]{1,0:T(2,128)S(1)}, u32[]{:S(2)}, u32[]{:S(2)}) collective-permute-start(f32[2,2048]{1,0:T(2,128)S(1)} %get-tuple-element.38.refs_3_.refs_0_), channel_id=1, source_target_pairs={{0,12},{4,8},{8,20},{12,16},{16,28},{20,24},{24,4},{28,0},{1,13},{... | collective-permute-start | bytes 49160 | tf_op jit(solution)/shard_map/ppermute | solution.py:351
  20.9 5.8 %collective-permute-start.3 = (f32[2,2048]{1,0:T(2,128)S(1)}, f32[2,2048]{1,0:T(2,128)S(1)}, u32[]{:S(2)}, u32[]{:S(2)}) collective-permute-start(f32[2,2048]{1,0:T(2,128)S(1)} %get-tuple-element.38.refs_3_.refs_0_), channel_id=1, source_target_pairs={{0,4},{4,0},{8,12},{12,8},{16,20},{20,16},{24,28},{28,24},{1,5},{5... | collective-permute-start | bytes 49160 | tf_op jit(solution)/shard_map/ppermute | solution.py:351
  21.6 5.1 %collective-permute-start.2 = (f32[2,2048]{1,0:T(2,128)S(1)}, f32[2,2048]{1,0:T(2,128)S(1)}, u32[]{:S(2)}, u32[]{:S(2)}) collective-permute-start(f32[2,2048]{1,0:T(2,128)S(1)} %get-tuple-element.38.refs_3_.refs_0_), channel_id=1, source_target_pairs={{0,24},{4,28},{8,0},{12,4},{16,8},{20,12},{24,16},{28,20},{1,25},{... | collective-permute-start | bytes 49160 | tf_op jit(solution)/shard_map/ppermute | solution.py:351
  23.9 5.2 %collective-permute-start.1 = (f32[2,2048]{1,0:T(2,128)S(1)}, f32[2,2048]{1,0:T(2,128)S(1)}, u32[]{:S(2)}, u32[]{:S(2)}) collective-permute-start(f32[2,2048]{1,0:T(2,128)S(1)} %get-tuple-element.38.refs_3_.refs_0_), channel_id=1, source_target_pairs={{0,16},{4,20},{8,24},{12,28},{16,0},{20,4},{24,8},{28,12},{1,17},{... | collective-permute-start | bytes 49160 | tf_op jit(solution)/shard_map/ppermute | solution.py:351
  25.4 5.0 %collective-permute-start = (f32[2,2048]{1,0:T(2,128)S(1)}, f32[2,2048]{1,0:T(2,128)S(1)}, u32[]{:S(2)}, u32[]{:S(2)}) collective-permute-start(f32[2,2048]{1,0:T(2,128)S(1)} %get-tuple-element.38.refs_3_.refs_0_), channel_id=1, source_target_pairs={{0,8},{4,12},{8,16},{12,20},{16,24},{20,28},{24,0},{28,4},{1,9},{5... | collective-permute-start | bytes 49160 | tf_op jit(solution)/shard_map/ppermute | solution.py:351
  31.6 16.4 %collective-permute-start.9 = (f32[448,256]{1,0:T(8,128)S(1)}, f32[448,256]{1,0:T(8,128)S(1)}, u32[]{:S(2)}, u32[]{:S(2)}) collective-permute-start(f32[448,256]{1,0:T(8,128)S(1)} %get-tuple-element.49), channel_id=1, source_target_pairs={{0,1},{1,2},{2,3},{3,0},{4,5},{5,6},{6,7},{7,4},{8,9},{9,10},{10,1... | collective-permute-start | bytes 1376264 | tf_op jit(solution)/shard_map/ppermute | solution.py:347
  33.2 15.8 %collective-permute-start.10 = (f32[448,256]{1,0:T(8,128)S(1)}, f32[448,256]{1,0:T(8,128)S(1)}, u32[]{:S(2)}, u32[]{:S(2)}) collective-permute-start(f32[448,256]{1,0:T(8,128)S(1)} %get-tuple-element.50), channel_id=1, source_target_pairs={{0,3},{1,0},{2,1},{3,2},{4,7},{5,4},{6,5},{7,6},{8,11},{9,8},{10,9... | collective-permute-start | bytes 1376264 | tf_op jit(solution)/shard_map/ppermute | solution.py:347
  35.1 3.3 %collective-permute-start.7 = (f32[32,2048]{1,0:T(8,128)S(1)}, f32[32,2048]{1,0:T(8,128)S(1)}, u32[]{:S(2)}, u32[]{:S(2)}) collective-permute-start(f32[32,2048]{1,0:T(8,128)S(1)} %get-tuple-element.43.refs_2_), channel_id=1, source_target_pairs={{0,4},{4,0},{8,12},{12,8},{16,20},{20,16},{24,28},{28,24},{1,5},{5... | collective-permute-start | bytes 786440 | tf_op jit(solution)/shard_map/ppermute | solution.py:363
  36.3 17.5 %collective-permute-start.12 = (f32[448,256]{1,0:T(8,128)S(1)}, f32[448,256]{1,0:T(8,128)S(1)}, u32[]{:S(2)}, u32[]{:S(2)}) collective-permute-start(f32[448,256]{1,0:T(8,128)S(1)} %get-tuple-element.51), channel_id=1, source_target_pairs={{0,3},{1,0},{2,1},{3,2},{4,7},{5,4},{6,5},{7,6},{8,11},{9,8},{10,9... | collective-permute-start | bytes 1376264 | tf_op jit(solution)/shard_map/ppermute | solution.py:347
  38.2 15.7 %collective-permute-start.11 = (f32[448,256]{1,0:T(8,128)S(1)}, f32[448,256]{1,0:T(8,128)S(1)}, u32[]{:S(2)}, u32[]{:S(2)}) collective-permute-start(f32[448,256]{1,0:T(8,128)S(1)} %get-tuple-element.44.refs_2_), channel_id=1, source_target_pairs={{0,1},{1,2},{2,3},{3,0},{4,5},{5,6},{6,7},{7,4},{8,9},{9,10},{10,1... | collective-permute-start | bytes 1376264 | tf_op jit(solution)/shard_map/ppermute | solution.py:347
  38.5 5.6 %collective-permute-start.8 = (f32[16,2048]{1,0:T(8,128)S(1)}, f32[16,2048]{1,0:T(8,128)S(1)}, u32[]{:S(2)}, u32[]{:S(2)}) collective-permute-start(f32[16,2048]{1,0:T(8,128)S(1)} %get-tuple-element.46.refs_5_), channel_id=1, source_target_pairs={{0,8},{4,12},{8,0},{12,4},{16,24},{20,28},{24,16},{28,20},{1,9},{5... | collective-permute-start | bytes 393224 | tf_op jit(solution)/shard_map/ppermute | solution.py:359
  44.1 10.3 %collective-permute-start.14 = (f32[64,896]{1,0:T(8,128)S(1)}, f32[64,896]{1,0:T(8,128)S(1)}, u32[]{:S(2)}, u32[]{:S(2)}) collective-permute-start(f32[64,896]{1,0:T(8,128)S(1)} %get-tuple-element.55), channel_id=1, source_target_pairs={{0,64},{32,96},{64,0},{96,32},{1,65},{33,97},{65,1},{97,33},{2,66}... | collective-permute-start | bytes 688136 | tf_op jit(solution)/shard_map/ppermute | solution.py:347
  48.0 10.7 %collective-permute-start.15 = (f32[64,896]{1,0:T(8,128)S(1)}, f32[64,896]{1,0:T(8,128)S(1)}, u32[]{:S(2)}, u32[]{:S(2)}) collective-permute-start(f32[64,896]{1,0:T(8,128)S(1)} %get-tuple-element.56), channel_id=1, source_target_pairs={{0,32},{32,64},{64,96},{96,0},{1,33},{33,65},{65,97},{97,1},{2,34}... | collective-permute-start | bytes 688136 | tf_op jit(solution)/shard_map/ppermute | solution.py:347
  49.0 10.4 %collective-permute-start.16 = (f32[64,896]{1,0:T(8,128)S(1)}, f32[64,896]{1,0:T(8,128)S(1)}, u32[]{:S(2)}, u32[]{:S(2)}) collective-permute-start(f32[64,896]{1,0:T(8,128)S(1)} %get-tuple-element.57), channel_id=1, source_target_pairs={{0,96},{32,0},{64,32},{96,64},{1,97},{33,1},{65,33},{97,65},{2,98}... | collective-permute-start | bytes 688136 | tf_op jit(solution)/shard_map/ppermute | solution.py:347
  59.5 7.0 %collective-permute-start.18 = (f32[64,896]{1,0:T(8,128)S(1)}, f32[64,896]{1,0:T(8,128)S(1)}, u32[]{:S(2)}, u32[]{:S(2)}) collective-permute-start(f32[64,896]{1,0:T(8,128)S(1)} %shard_map.104.refs_3_.refs_0_), channel_id=1, source_target_pairs={{0,1},{1,0},{2,3},{3,2},{4,5},{5,4},{6,7},{7,6},{8,9},{9,8},{10,11... | collective-permute-start | bytes 688136 | tf_op jit(solution)/shard_map/ppermute | solution.py:355
  59.9 5.5 %collective-permute-start.13 = (f32[8,2048]{1,0:T(8,128)S(1)}, f32[8,2048]{1,0:T(8,128)S(1)}, u32[]{:S(2)}, u32[]{:S(2)}) collective-permute-start(f32[8,2048]{1,0:T(8,128)S(1)} %get-tuple-element.48.refs_2_), channel_id=1, source_target_pairs={{0,24},{4,28},{8,16},{12,20},{16,8},{20,12},{24,0},{28,4},{1,25},{... | collective-permute-start | bytes 196616 | tf_op jit(solution)/shard_map/ppermute | solution.py:359
  65.4 5.0 %collective-permute-start.17 = (f32[16,2048]{1,0:T(8,128)S(1)}, f32[16,2048]{1,0:T(8,128)S(1)}, u32[]{:S(2)}, u32[]{:S(2)}) collective-permute-start(f32[16,2048]{1,0:T(8,128)S(1)} %shard_map.105.refs_2_.refs_0_), channel_id=1, source_target_pairs={{0,32},{32,0},{64,96},{96,64},{1,33},{33,1},{65,97},{97,65},{2,34}... | collective-permute-start | bytes 393224 | tf_op jit(solution)/shard_map/ppermute | solution.py:355
  66.5 9.4 %collective-permute-start.21 = (f32[64,896]{1,0:T(8,128)S(1)}, f32[64,896]{1,0:T(8,128)S(1)}, u32[]{:S(2)}, u32[]{:S(2)}) collective-permute-start(f32[64,896]{1,0:T(8,128)S(1)} %shard_map.106.refs_2_.refs_0_), channel_id=1, source_target_pairs={{0,3},{1,2},{2,1},{3,0},{4,7},{5,6},{6,5},{7,4},{8,11},{9,10},{10,... | collective-permute-start | bytes 688136 | tf_op jit(solution)/shard_map/ppermute | solution.py:355
  70.5 18.5 %collective-permute-start.20 = (f32[448,256]{1,0:T(8,128)S(1)}, f32[448,256]{1,0:T(8,128)S(1)}, u32[]{:S(2)}, u32[]{:S(2)}) collective-permute-start(f32[448,256]{1,0:T(8,128)S(1)} %get-tuple-element.59), channel_id=1, source_target_pairs={{0,3},{1,0},{2,1},{3,2},{4,7},{5,4},{6,5},{7,6},{8,11},{9,8},{10,9... | collective-permute-start | bytes 1376264 | tf_op jit(solution)/shard_map/ppermute | solution.py:347
  73.3 15.7 %collective-permute-start.19 = (f32[448,256]{1,0:T(8,128)S(1)}, f32[448,256]{1,0:T(8,128)S(1)}, u32[]{:S(2)}, u32[]{:S(2)}) collective-permute-start(f32[448,256]{1,0:T(8,128)S(1)} %get-tuple-element.58.refs_2_), channel_id=1, source_target_pairs={{0,1},{1,2},{2,3},{3,0},{4,5},{5,6},{6,7},{7,4},{8,9},{9,10},{10,1... | collective-permute-start | bytes 1376264 | tf_op jit(solution)/shard_map/ppermute | solution.py:347
  73.3 6.5 %collective-permute-start.24 = (f32[16,2048]{1,0:T(8,128)S(1)}, f32[16,2048]{1,0:T(8,128)S(1)}, u32[]{:S(2)}, u32[]{:S(2)}) collective-permute-start(f32[16,2048]{1,0:T(8,128)S(1)} %shard_map.107.refs_2_.refs_0_), channel_id=1, source_target_pairs={{0,96},{32,64},{64,32},{96,0},{1,97},{33,65},{65,33},{97,1},{2,98}... | collective-permute-start | bytes 393224 | tf_op jit(solution)/shard_map/ppermute | solution.py:355
  76.0 9.9 %collective-permute-start.23 = (f32[32,896]{1,0:T(8,128)S(1)}, f32[32,896]{1,0:T(8,128)S(1)}, u32[]{:S(2)}, u32[]{:S(2)}) collective-permute-start(f32[32,896]{1,0:T(8,128)S(1)} %get-tuple-element.61.refs_2_), channel_id=1, source_target_pairs={{0,32},{32,0},{64,96},{96,64},{1,33},{33,1},{65,97},{97,65},{2,34}... | collective-permute-start | bytes 344072 | tf_op jit(solution)/shard_map/ppermute | solution.py:355
  76.9 9.0 %collective-permute-start.22 = (f32[32,896]{1,0:T(8,128)S(1)}, f32[32,896]{1,0:T(8,128)S(1)}, u32[]{:S(2)}, u32[]{:S(2)}) collective-permute-start(f32[32,896]{1,0:T(8,128)S(1)} %get-tuple-element.60.refs_3_.refs_0_), channel_id=1, source_target_pairs={{0,96},{32,64},{64,32},{96,0},{1,97},{33,65},{65,33},{97,1},{2,98}... | collective-permute-start | bytes 344072 | tf_op jit(solution)/shard_map/ppermute | solution.py:355
  80.3 5.5 %collective-permute-start.25 = (f32[8,2048]{1,0:T(8,128)S(1)}, f32[8,2048]{1,0:T(8,128)S(1)}, u32[]{:S(2)}, u32[]{:S(2)}) collective-permute-start(f32[8,2048]{1,0:T(8,128)S(1)} %get-tuple-element.62.refs_0_), channel_id=1, source_target_pairs={{0,24},{4,28},{8,16},{12,20},{16,8},{20,12},{24,0},{28,4},{1,25},{... | collective-permute-start | bytes 196616 | tf_op jit(solution)/shard_map/ppermute | solution.py:359
  85.9 7.3 %collective-permute-start.27 = (f32[64,896]{1,0:T(8,128)S(1)}, f32[64,896]{1,0:T(8,128)S(1)}, u32[]{:S(2)}, u32[]{:S(2)}) collective-permute-start(f32[64,896]{1,0:T(8,128)S(1)} %get-tuple-element.65.refs_2_), channel_id=1, source_target_pairs={{0,96},{32,64},{64,32},{96,0},{1,97},{33,65},{65,33},{97,1},{2,98}... | collective-permute-start | bytes 688136 | tf_op jit(solution)/shard_map/ppermute | solution.py:355
  88.9 6.0 %collective-permute-start.26 = (f32[64,896]{1,0:T(8,128)S(1)}, f32[64,896]{1,0:T(8,128)S(1)}, u32[]{:S(2)}, u32[]{:S(2)}) collective-permute-start(f32[64,896]{1,0:T(8,128)S(1)} %get-tuple-element.63.refs_3_.refs_0_), channel_id=1, source_target_pairs={{0,32},{32,0},{64,96},{96,64},{1,33},{33,1},{65,97},{97,65},{2,34}... | collective-permute-start | bytes 688136 | tf_op jit(solution)/shard_map/ppermute | solution.py:355
  88.9 6.0 %collective-permute-start.28 = (f32[16,2048]{1,0:T(8,128)S(1)}, f32[16,2048]{1,0:T(8,128)S(1)}, u32[]{:S(2)}, u32[]{:S(2)}) collective-permute-start(f32[16,2048]{1,0:T(8,128)S(1)} %shard_map.111.refs_4_.refs_0_), channel_id=1, source_target_pairs={{0,8},{4,12},{8,0},{12,4},{16,24},{20,28},{24,16},{28,20},{1,9},{5... | collective-permute-start | bytes 393224 | tf_op jit(solution)/shard_map/ppermute | solution.py:359
  95.0 1.6 %collective-permute-start.29 = (f32[32,2048]{1,0:T(8,128)S(1)}, f32[32,2048]{1,0:T(8,128)S(1)}, u32[]{:S(2)}, u32[]{:S(2)}) collective-permute-start(f32[32,2048]{1,0:T(8,128)S(1)} %shard_map.115.refs_4_.refs_0_), channel_id=1, source_target_pairs={{0,4},{4,0},{8,12},{12,8},{16,20},{20,16},{24,28},{28,24},{1,5},{5... | collective-permute-start | bytes 786440 | tf_op jit(solution)/shard_map/ppermute | solution.py:363
  (3 other events, 58.0 us)

commit v9 on v7

--- a/solution.py
+++ b/solution.py
@@ -388,10 +388,7 @@
         vec, bq, am,
         scratch=[pltpu.VMEM((rank, cols), F32)],
     )
-    half = [out((far, toks))] * 2
-    up, down = call(near_kernel, half, [VMEM] * 2, m, scaled, after=[send])
-    v0, v1 = ring(up, "cols", 1), ring(down, "cols", 3)
-    keep, send = halve(keep, swap_core(send), near_bit, after=[up])
+    keep, send = halve(keep, swap_core(send), near_bit)
     pieces = call(
         functools.partial(a_kernel, 2.0 * gamma),
         [out((rank, rows // 4))] * 4,
@@ -402,15 +399,19 @@
     )
     keep, send = halve(keep, swap_x(send, 0), far_bit, after=[pieces[0]])
     pieces = [pieces[0]] + [ring(pieces[k], "dp", k) for k in (2, 1, 3)]
-    own = call(own_kernel, [out((rows // 4, toks))], [VMEM] * 2, m, scaled, after=[send, u0, u1])[0]
-    up, down = call(relay_kernel, half, [VMEM] * 4, m, scaled, u0, u1, after=[own])
-    own = call(gather_kernel, [out((rows // 4, toks))], [VMEM] * 3, own, v0, v1, after=[up])[0]
-
-    piece = add(*pieces, after=[own])
+    half = [out((far, toks))] * 2
+    v_up, v_down = call(near_kernel, half, [VMEM] * 2, m, scaled, after=[send])
+    own = call(own_kernel, [out((rows // 4, toks))], [VMEM] * 2, m, scaled, after=[v_up])[0]
+    v_up, v_down = hold([v_up, v_down], [own, u0, u1])
+    v0, v1 = ring(v_up, "cols", 1), ring(v_down, "cols", 3)
+    up, down = call(relay_kernel, half, [VMEM] * 4, m, scaled, u0, u1, after=[v_up])
+
+    piece = add(*pieces, after=[up])
     stack = call(
         b_stack_kernel, [out((rank // 4, cols))], [VMEM] * 3, keep, swap_x(send, 1), vec, after=[piece]
     )[0]
-    piece = add(piece, swap(piece, "cols", 0), after=[stack])
+    own = call(gather_kernel, [out((rows // 4, toks))], [VMEM] * 3, own, v0, v1, after=[stack])[0]
+    piece = add(piece, swap(piece, "cols", 0), after=[own])
     last = (piece, swap(piece, "cols", 1))
     stack = add(stack, swap(stack, "dp", 0), after=[piece])
     up, down = hold([up, down], [stack])

time: 95.1 us -> 94.1 us (0.989)
  starting transfers between devices: 37 us -> 31.5 us
  waiting for transfers between devices: 24.7 us -> 29.1 us
    ppermute x8, starting transfers between devices: 13.2 us -> 7.96 us  [swap(): lax.ppermute(value, axis, [(i, i ^ 1 if step == 0 else 3 - i) for i in ra...]
    ppermute x8, waiting for transfers between devices: 6.7 us -> 11.1 us  [swap(): lax.ppermute(value, axis, [(i, i ^ 1 if step == 0 else 3 - i) for i in ra...]
    ppermute x9, waiting for transfers between devices: 5.76 us -> 4.19 us  [ring(): lax.ppermute(value, axis, [(i, (i + k) % count) for i in range(count)])]
    ppermute x3, waiting for transfers between devices: 1.7 us -> 3.22 us  [swap_core(): return lax.ppermute(value, 'rows', [(i, i ^ 1) for i in range(count)])]
  transfers between devices with their start and end apart: 27 -> 27, of which waited for: 15 -> 16; matrix products, arithmetic and copies ran while one was open for 0% -> 0% of each run, Pallas kernels for 14% -> 14%
where the time goes in v9:
time: 94.1 us; the launch traced here: 93 us
  starting transfers between devices  31.5 us (33%)
  Pallas kernels  31.4 us (33%)
  waiting for transfers between devices  29.1 us (31%)
    pallas_call x23, Pallas kernels, call(): pl.pallas_call(body, out_shape=outs, in_specs=list(specs) + [ANY] * len(a...  31.4 us
    ppermute x9, starting transfers between devices, ring(): lax.ppermute(value, axis, [(i, (i + k) % count) for i in range(count)])  14.7 us
    ppermute x8, waiting for transfers between devices, swap(): lax.ppermute(value, axis, [(i, i ^ 1 if step == 0 else 3 - i) for i in ra...  11.1 us
    ppermute x8, starting transfers between devices, swap(): lax.ppermute(value, axis, [(i, i ^ 1 if step == 0 else 3 - i) for i in ra...  7.96 us
    ppermute x4, waiting for transfers between devices, swap_x(): lax.ppermute(value, 'rows', [(i, i ^ 2 if step == 0 else 6 - 2 * (i // 2)...  7.71 us
    ppermute x3, starting transfers between devices, ring_x(): lax.ppermute(value, 'rows', [(i, (i + 2 * k) % count) for i in range(coun...  4.59 us
    ppermute x9, waiting for transfers between devices, ring(): lax.ppermute(value, axis, [(i, (i + k) % count) for i in range(count)])  4.19 us
    ppermute x4, starting transfers between devices, swap_x(): lax.ppermute(value, 'rows', [(i, i ^ 2 if step == 0 else 6 - 2 * (i // 2)...  4.02 us
  transfers between devices with their start and end apart: 27, of which 16 were waited for; matrix products, arithmetic and copies ran while one was open for 0% of the time, Pallas kernels for 14%

profile of v9, /device:TPU:0, one launch (start us, length us, event | category | flops | bytes accessed | tf_op | source)
XLA Modules:
  0.0 93.0 jit_solution(2504570970991699758)
XLA Ops:
  0.7 16.5 %shard_map.93 = (bf16[3584,2048]{1,0:T(8,128)(2,1)S(1)}, f32[2,2048]{1,0:T(2,128)S(1)}, f32[64,2048]{1,0:T(8,128)S(1)}) custom-call(bf16[3584,2048]{1,0:T(8,128)(2,1)} %refs_0_.1, bf16[256,3584]{1,0:T(8,128)(2,1)} %refs_3_.3, bf16[64,3584]{1,0:T(8,128)(2,1)} %bitcast.4, bf16[64,2048]{1,0:T(8,128)(2,1)} %refs_2_.3, bf16[256,2048]{1,0:T(8,128)(2,1)} %refs_1_.5), custom_call_target="tpu_custom_call" | custom-call | flops 5637144576 | bytes 14680064 | tf_op jit(solution)/shard_map/pallas_call | solution.py:49
  17.2 1.2 %collective-permute-done = f32[2,2048]{1,0:T(2,128)S(1)} collective-permute-done((f32[2,2048]{1,0:T(2,128)S(1)}, f32[2,2048]{1,0:T(2,128)S(1)}, u32[]{:S(2)}, u32[]{:S(2)}) %collective-permute-start) | collective-permute-done | bytes 16416 | tf_op jit(solution)/shard_map/ppermute | solution.py:361
  18.4 2.9 %collective-permute-start.3 = (f32[2,2048]{1,0:T(2,128)S(1)}, f32[2,2048]{1,0:T(2,128)S(1)}, u32[]{:S(2)}, u32[]{:S(2)}) collective-permute-start(f32[2,2048]{1,0:T(2,128)S(1)} %add.3.refs_0_), channel_id=1, source_target_pairs={{0,24},{4,28},{8,0},{12,4},{16,8},{20,12},{24,16},{28,20},{1,25},{... | collective-permute-start | bytes 49160 | tf_op jit(solution)/shard_map/ppermute | solution.py:349
  23.0 1.2 %shard_map.94.refs_7_.refs_1_ = f32[64,2048]{1,0:T(8,128)S(1)} custom-call(bf16[64,3584]{1,0:T(8,128)(2,1)S(1)} %bitcast.5, bf16[256,3584]{1,0:T(8,128)(2,1)S(1)} %copy-done.1, bf16[256,2048]{1,0:T(8,128)(2,1)S(1)} %copy-done, f32[2,2048]{1,0:T(2,128)S(1)} %get-tuple-element.40.refs_3_), custom_call_target="tpu_custom_call" | custom-call | flops 1 | bytes 1 | tf_op jit(solution)/shard_map/pallas_call | solution.py:49
  24.2 2.4 %collective-permute-done.2.refs_2_ = f32[2,2048]{1,0:T(2,128)S(1)} collective-permute-done((f32[2,2048]{1,0:T(2,128)S(1)}, f32[2,2048]{1,0:T(2,128)S(1)}, u32[]{:S(2)}, u32[]{:S(2)}) %collective-permute-start.2) | collective-permute-done | bytes 16416 | tf_op jit(solution)/shard_map/ppermute | solution.py:349
  27.1 1.2 %shard_map.95 = (f32[4,2048]{1,0:T(4,128)S(1)}, bf16[256,2048]{1,0:T(8,128)(2,1)S(1)}, f32[448,256]{1,0:T(8,128)S(1)}, f32[448,256]{1,0:T(8,128)S(1)}) custom-call(f32[2,2048]{1,0:T(2,128)S(1)} %add.3.refs_0_, f32[2,2048]{1,0:T(2,128)S(1)} %collective-permute-done.1.refs_1_, f32[2,2048]{1,0:T(2,128)S(1)} %collective-permute-done.2.refs_2_, ...), custom_call_target="tpu_custom_call" | custom-call | flops 1 | bytes 1 | tf_op jit(solution)/shard_map/pallas_call | solution.py:49
  28.3 1.6 %collective-permute-start.6 = (f32[448,256]{1,0:T(8,128)S(1)}, f32[448,256]{1,0:T(8,128)S(1)}, u32[]{:S(2)}, u32[]{:S(2)}) collective-permute-start(f32[448,256]{1,0:T(8,128)S(1)} %get-tuple-element.52), channel_id=1, source_target_pairs={{0,1},{1,2},{2,3},{3,0},{4,5},{5,6},{6,7},{7,4},{8,9},{9,10},{10,1... | collective-permute-start | bytes 1376264 | tf_op jit(solution)/shard_map/ppermute | solution.py:345
  29.9 1.7 %collective-permute-start.7 = (f32[448,256]{1,0:T(8,128)S(1)}, f32[448,256]{1,0:T(8,128)S(1)}, u32[]{:S(2)}, u32[]{:S(2)}) collective-permute-start(f32[448,256]{1,0:T(8,128)S(1)} %get-tuple-element.53), channel_id=1, source_target_pairs={{0,3},{1,0},{2,1},{3,2},{4,7},{5,4},{6,5},{7,6},{8,11},{9,8},{10,9... | collective-permute-start | bytes 1376264 | tf_op jit(solution)/shard_map/ppermute | solution.py:345
  31.9 1.5 %collective-permute-done.4.refs_1_ = f32[32,2048]{1,0:T(8,128)S(1)} collective-permute-done((f32[32,2048]{1,0:T(8,128)S(1)}, f32[32,2048]{1,0:T(8,128)S(1)}, u32[]{:S(2)}, u32[]{:S(2)}) %collective-permute-start.4) | collective-permute-done | bytes 262176 | tf_op jit(solution)/shard_map/ppermute | solution.py:361
  33.5 5.3 %shard_map.98 = (f32[64,896]{1,0:T(8,128)S(1)}, f32[64,896]{1,0:T(8,128)S(1)}, f32[64,896]{1,0:T(8,128)S(1)}, f32[64,896]{1,0:T(8,128)S(1)}) custom-call(f32[4,2048]{1,0:T(4,128)S(1)} %get-tuple-element.42.refs_0_.refs_2_, bf16[256,2048]{1,0:T(8,128)(2,1)S(1)} %copy-done, bf16[64,2048]{1,0:T(8,128)(2,1)S(1)} %copy-done.3, bf16[256,3584]{1,0:T(8,128)(2,1)S(1)} %copy-done.1, ...), custom_call_target="tpu_custom_call" | custom-call | flops 1 | bytes 1 | tf_op jit(solution)/shard_map/pallas_call | solution.py:49
  38.8 4.0 %collective-permute-start.11 = (f32[64,896]{1,0:T(8,128)S(1)}, f32[64,896]{1,0:T(8,128)S(1)}, u32[]{:S(2)}, u32[]{:S(2)}) collective-permute-start(f32[64,896]{1,0:T(8,128)S(1)} %get-tuple-element.57), channel_id=1, source_target_pairs={{0,64},{32,96},{64,0},{96,32},{1,65},{33,97},{65,1},{97,33},{2,66}... | collective-permute-start | bytes 688136 | tf_op jit(solution)/shard_map/ppermute | solution.py:345
  42.8 1.0 %collective-permute-start.12 = (f32[64,896]{1,0:T(8,128)S(1)}, f32[64,896]{1,0:T(8,128)S(1)}, u32[]{:S(2)}, u32[]{:S(2)}) collective-permute-start(f32[64,896]{1,0:T(8,128)S(1)} %get-tuple-element.58), channel_id=1, source_target_pairs={{0,32},{32,64},{64,96},{96,0},{1,33},{33,65},{65,97},{97,1},{2,34}... | collective-permute-start | bytes 688136 | tf_op jit(solution)/shard_map/ppermute | solution.py:345
  43.8 2.2 %collective-permute-start.13 = (f32[64,896]{1,0:T(8,128)S(1)}, f32[64,896]{1,0:T(8,128)S(1)}, u32[]{:S(2)}, u32[]{:S(2)}) collective-permute-start(f32[64,896]{1,0:T(8,128)S(1)} %get-tuple-element.59), channel_id=1, source_target_pairs={{0,96},{32,0},{64,32},{96,64},{1,97},{33,1},{65,33},{97,65},{2,98}... | collective-permute-start | bytes 688136 | tf_op jit(solution)/shard_map/ppermute | solution.py:345
  46.1 1.1 %shard_map.100 = (f32[448,256]{1,0:T(8,128)S(1)}, f32[448,256]{1,0:T(8,128)S(1)}) custom-call(bf16[3584,2048]{1,0:T(8,128)(2,1)S(1)} %get-tuple-element.39.refs_6_.refs_4_.refs_0_, bf16[256,2048]{1,0:T(8,128)(2,1)S(1)} %get-tuple-element.41.refs_1_, f32[8,2048]{1,0:T(8,128)S(1)} %get-tuple-element.49.refs_2_), custom_call_target="tpu_custom_call" | custom-call | flops 1 | bytes 1 | tf_op jit(solution)/shard_map/pallas_call | solution.py:49
  47.2 1.1 %shard_map.101.refs_2_.refs_0_ = f32[896,256]{1,0:T(8,128)S(1)} custom-call(bf16[3584,2048]{1,0:T(8,128)(2,1)S(1)} %get-tuple-element.39.refs_6_.refs_4_.refs_0_, bf16[256,2048]{1,0:T(8,128)(2,1)S(1)} %get-tuple-element.41.refs_1_, f32[448,256]{1,0:T(8,128)S(1)} %get-tuple-element.50.refs_2_.refs_0_), custom_call_target="tpu_custom_call" | custom-call | flops 1 | bytes 1 | tf_op jit(solution)/shard_map/pallas_call | solution.py:49
  48.4 1.9 %collective-permute-start.9 = (f32[448,256]{1,0:T(8,128)S(1)}, f32[448,256]{1,0:T(8,128)S(1)}, u32[]{:S(2)}, u32[]{:S(2)}) collective-permute-start(f32[448,256]{1,0:T(8,128)S(1)} %get-tuple-element.55), channel_id=1, source_target_pairs={{0,3},{1,0},{2,1},{3,2},{4,7},{5,4},{6,5},{7,6},{8,11},{9,8},{10,9... | collective-permute-start | bytes 1376264 | tf_op jit(solution)/shard_map/ppermute | solution.py:345
  50.5 1.1 %shard_map.103 = (f32[448,256]{1,0:T(8,128)S(1)}, f32[448,256]{1,0:T(8,128)S(1)}) custom-call(bf16[3584,2048]{1,0:T(8,128)(2,1)S(1)} %get-tuple-element.39.refs_6_.refs_4_.refs_0_, bf16[256,2048]{1,0:T(8,128)(2,1)S(1)} %get-tuple-element.41.refs_1_, f32[448,256]{1,0:T(8,128)S(1)} %collective-permute-done.6.refs_3_.refs_2_, ...), custom_call_target="tpu_custom_call" | custom-call | flops 1 | bytes 1 | tf_op jit(solution)/shard_map/pallas_call | solution.py:49
  51.7 2.0 %collective-permute-done.12.refs_2_ = f32[64,896]{1,0:T(8,128)S(1)} collective-permute-done((f32[64,896]{1,0:T(8,128)S(1)}, f32[64,896]{1,0:T(8,128)S(1)}, u32[]{:S(2)}, u32[]{:S(2)}) %collective-permute-start.12) | collective-permute-done | bytes 229408 | tf_op jit(solution)/shard_map/ppermute | solution.py:345
  54.9 1.8 %collective-permute-start.10 = (f32[8,2048]{1,0:T(8,128)S(1)}, f32[8,2048]{1,0:T(8,128)S(1)}, u32[]{:S(2)}, u32[]{:S(2)}) collective-permute-start(f32[8,2048]{1,0:T(8,128)S(1)} %get-tuple-element.49.refs_2_), channel_id=1, source_target_pairs={{0,24},{4,28},{8,16},{12,20},{16,8},{20,12},{24,0},{28,4},{1,25},{... | collective-permute-start | bytes 196616 | tf_op jit(solution)/shard_map/ppermute | solution.py:357
  56.6 3.7 %collective-permute-done.10.refs_1_ = f32[8,2048]{1,0:T(8,128)S(1)} collective-permute-done((f32[8,2048]{1,0:T(8,128)S(1)}, f32[8,2048]{1,0:T(8,128)S(1)}, u32[]{:S(2)}, u32[]{:S(2)}) %collective-permute-start.10) | collective-permute-done | bytes 65568 | tf_op jit(solution)/shard_map/ppermute | solution.py:357
  60.4 1.1 %collective-permute-start.14 = (f32[16,2048]{1,0:T(8,128)S(1)}, f32[16,2048]{1,0:T(8,128)S(1)}, u32[]{:S(2)}, u32[]{:S(2)}) collective-permute-start(f32[16,2048]{1,0:T(8,128)S(1)} %shard_map.105.refs_3_.refs_0_), channel_id=1, source_target_pairs={{0,32},{32,0},{64,96},{96,64},{1,33},{33,1},{65,97},{97,65},{2,34}... | collective-permute-start | bytes 393224 | tf_op jit(solution)/shard_map/ppermute | solution.py:353
  61.9 1.0 %collective-permute-done.8.refs_1_ = f32[448,256]{1,0:T(8,128)S(1)} collective-permute-done((f32[448,256]{1,0:T(8,128)S(1)}, f32[448,256]{1,0:T(8,128)S(1)}, u32[]{:S(2)}, u32[]{:S(2)}) %collective-permute-start.8) | collective-permute-done | bytes 458784 | tf_op jit(solution)/shard_map/ppermute | solution.py:345
  63.0 2.1 %collective-permute-done.15.refs_1_ = f32[64,896]{1,0:T(8,128)S(1)} collective-permute-done((f32[64,896]{1,0:T(8,128)S(1)}, f32[64,896]{1,0:T(8,128)S(1)}, u32[]{:S(2)}, u32[]{:S(2)}) %collective-permute-start.15) | collective-permute-done | bytes 229408 | tf_op jit(solution)/shard_map/ppermute | solution.py:353
  65.1 2.3 %collective-permute-start.18 = (f32[64,896]{1,0:T(8,128)S(1)}, f32[64,896]{1,0:T(8,128)S(1)}, u32[]{:S(2)}, u32[]{:S(2)}) collective-permute-start(f32[64,896]{1,0:T(8,128)S(1)} %shard_map.107.refs_2_.refs_0_), channel_id=1, source_target_pairs={{0,3},{1,2},{2,1},{3,0},{4,7},{5,6},{6,5},{7,4},{8,11},{9,10},{10,... | collective-permute-start | bytes 688136 | tf_op jit(solution)/shard_map/ppermute | solution.py:353
  67.5 1.0 %collective-permute-start.17 = (f32[448,256]{1,0:T(8,128)S(1)}, f32[448,256]{1,0:T(8,128)S(1)}, u32[]{:S(2)}, u32[]{:S(2)}) collective-permute-start(f32[448,256]{1,0:T(8,128)S(1)} %get-tuple-element.63), channel_id=1, source_target_pairs={{0,3},{1,0},{2,1},{3,2},{4,7},{5,4},{6,5},{7,6},{8,11},{9,8},{10,9... | collective-permute-start | bytes 1376264 | tf_op jit(solution)/shard_map/ppermute | solution.py:345
  68.6 1.0 %collective-permute-start.16 = (f32[448,256]{1,0:T(8,128)S(1)}, f32[448,256]{1,0:T(8,128)S(1)}, u32[]{:S(2)}, u32[]{:S(2)}) collective-permute-start(f32[448,256]{1,0:T(8,128)S(1)} %get-tuple-element.62.refs_2_), channel_id=1, source_target_pairs={{0,1},{1,2},{2,3},{3,0},{4,5},{5,6},{6,7},{7,4},{8,9},{9,10},{10,1... | collective-permute-start | bytes 1376264 | tf_op jit(solution)/shard_map/ppermute | solution.py:345
  70.3 4.4 %collective-permute-done.18.refs_1_ = f32[64,896]{1,0:T(8,128)S(1)} collective-permute-done((f32[64,896]{1,0:T(8,128)S(1)}, f32[64,896]{1,0:T(8,128)S(1)}, u32[]{:S(2)}, u32[]{:S(2)}) %collective-permute-start.18) | collective-permute-done | bytes 229408 | tf_op jit(solution)/shard_map/ppermute | solution.py:353
  76.9 1.5 %collective-permute-start.22 = (f32[8,2048]{1,0:T(8,128)S(1)}, f32[8,2048]{1,0:T(8,128)S(1)}, u32[]{:S(2)}, u32[]{:S(2)}) collective-permute-start(f32[8,2048]{1,0:T(8,128)S(1)} %get-tuple-element.66.refs_0_), channel_id=1, source_target_pairs={{0,24},{4,28},{8,16},{12,20},{16,8},{20,12},{24,0},{28,4},{1,25},{... | collective-permute-start | bytes 196616 | tf_op jit(solution)/shard_map/ppermute | solution.py:357
  78.4 4.0 %collective-permute-done.22.refs_1_ = f32[8,2048]{1,0:T(8,128)S(1)} collective-permute-done((f32[8,2048]{1,0:T(8,128)S(1)}, f32[8,2048]{1,0:T(8,128)S(1)}, u32[]{:S(2)}, u32[]{:S(2)}) %collective-permute-start.22) | collective-permute-done | bytes 65568 | tf_op jit(solution)/shard_map/ppermute | solution.py:357
  82.5 1.9 %collective-permute-start.24 = (f32[64,896]{1,0:T(8,128)S(1)}, f32[64,896]{1,0:T(8,128)S(1)}, u32[]{:S(2)}, u32[]{:S(2)}) collective-permute-start(f32[64,896]{1,0:T(8,128)S(1)} %get-tuple-element.69.refs_2_), channel_id=1, source_target_pairs={{0,96},{32,64},{64,32},{96,0},{1,97},{33,65},{65,33},{97,1},{2,98}... | collective-permute-start | bytes 688136 | tf_op jit(solution)/shard_map/ppermute | solution.py:353
  86.7 3.1 %collective-permute-done.24.refs_1_ = f32[64,896]{1,0:T(8,128)S(1)} collective-permute-done((f32[64,896]{1,0:T(8,128)S(1)}, f32[64,896]{1,0:T(8,128)S(1)}, u32[]{:S(2)}, u32[]{:S(2)}) %collective-permute-start.24) | collective-permute-done | bytes 229408 | tf_op jit(solution)/shard_map/ppermute | solution.py:353
  90.6 1.0 %shard_map.117 = f32[64,3584]{1,0:T(8,128)} custom-call(f32[64,896]{1,0:T(8,128)S(1)} %get-tuple-element.67.refs_3_.refs_0_, f32[64,896]{1,0:T(8,128)S(1)} %get-tuple-element.71.refs_2_.refs_1_, f32[64,896]{1,0:T(8,128)S(1)} %get-tuple-element.69.refs_2_, f32[64,896]{1,0:T(8,128)S(1)} %get-tuple-element.72.refs_3_, f32[32,2048]{1,0:T(8,128)S(1)} %shard_map.116.refs_4_.refs_0_), custom_call_target="tpu_custom_call" | custom-call | flops 1 | bytes 1 | tf_op jit(solution)/shard_map/pallas_call | solution.py:49
  (59 shorter events, 12.2 us)
Async XLA Ops:
  0.6 22.4 %copy-start = (bf16[256,2048]{1,0:T(8,128)(2,1)S(1)}, bf16[256,2048]{1,0:T(8,128)(2,1)}, u32[]{:S(2)}) copy-start(bf16[256,2048]{1,0:T(8,128)(2,1)} %refs_1_.5) | copy-start | bytes 3145732
  0.6 22.4 %copy-start.1 = (bf16[256,3584]{1,0:T(8,128)(2,1)S(1)}, bf16[256,3584]{1,0:T(8,128)(2,1)}, u32[]{:S(2)}) copy-start(bf16[256,3584]{1,0:T(8,128)(2,1)} %refs_3_.3) | copy-start | bytes 5505028
  0.7 22.4 %copy-start.2 = (bf16[3584,64]{0,1:T(8,128)(2,1)S(1)}, bf16[3584,64]{0,1:T(8,128)(2,1)}, u32[]{:S(2)}) copy-start(bf16[3584,64]{0,1:T(8,128)(2,1)} %param.9) | copy-start | bytes 1376260
  0.7 26.4 %copy-start.4 = (f32[2048]{0:T(1024)S(1)}, f32[2048]{0:T(1024)}, u32[]{:S(2)}) copy-start(f32[2048]{0:T(1024)} %param.11) | copy-start | bytes 24580
  17.1 16.4 %copy-start.3 = (bf16[64,2048]{1,0:T(8,128)(2,1)S(1)}, bf16[64,2048]{1,0:T(8,128)(2,1)}, u32[]{:S(2)}) copy-start(bf16[64,2048]{1,0:T(8,128)(2,1)} %refs_2_.3) | copy-start | bytes 786436
  17.1 1.3 %collective-permute-start = (f32[2,2048]{1,0:T(2,128)S(1)}, f32[2,2048]{1,0:T(2,128)S(1)}, u32[]{:S(2)}, u32[]{:S(2)}) collective-permute-start(f32[2,2048]{1,0:T(2,128)S(1)} %get-tuple-element.40.refs_3_), channel_id=1, source_target_pairs={{0,4},{4,0},{8,12},{12,8},{16,20},{20,16},{24,28},{28,24},{1,5},{5... | collective-permute-start | bytes 49160 | tf_op jit(solution)/shard_map/ppermute | solution.py:361
  18.4 5.8 %collective-permute-start.3 = (f32[2,2048]{1,0:T(2,128)S(1)}, f32[2,2048]{1,0:T(2,128)S(1)}, u32[]{:S(2)}, u32[]{:S(2)}) collective-permute-start(f32[2,2048]{1,0:T(2,128)S(1)} %add.3.refs_0_), channel_id=1, source_target_pairs={{0,24},{4,28},{8,0},{12,4},{16,8},{20,12},{24,16},{28,20},{1,25},{... | collective-permute-start | bytes 49160 | tf_op jit(solution)/shard_map/ppermute | solution.py:349
  21.3 5.2 %collective-permute-start.2 = (f32[2,2048]{1,0:T(2,128)S(1)}, f32[2,2048]{1,0:T(2,128)S(1)}, u32[]{:S(2)}, u32[]{:S(2)}) collective-permute-start(f32[2,2048]{1,0:T(2,128)S(1)} %add.3.refs_0_), channel_id=1, source_target_pairs={{0,16},{4,20},{8,24},{12,28},{16,0},{20,4},{24,8},{28,12},{1,17},{... | collective-permute-start | bytes 49160 | tf_op jit(solution)/shard_map/ppermute | solution.py:349
  22.1 4.9 %collective-permute-start.1 = (f32[2,2048]{1,0:T(2,128)S(1)}, f32[2,2048]{1,0:T(2,128)S(1)}, u32[]{:S(2)}, u32[]{:S(2)}) collective-permute-start(f32[2,2048]{1,0:T(2,128)S(1)} %add.3.refs_0_), channel_id=1, source_target_pairs={{0,8},{4,12},{8,16},{12,20},{16,24},{20,28},{24,0},{28,4},{1,9},{5... | collective-permute-start | bytes 49160 | tf_op jit(solution)/shard_map/ppermute | solution.py:349
  28.3 20.1 %collective-permute-start.6 = (f32[448,256]{1,0:T(8,128)S(1)}, f32[448,256]{1,0:T(8,128)S(1)}, u32[]{:S(2)}, u32[]{:S(2)}) collective-permute-start(f32[448,256]{1,0:T(8,128)S(1)} %get-tuple-element.52), channel_id=1, source_target_pairs={{0,1},{1,2},{2,3},{3,0},{4,5},{5,6},{6,7},{7,4},{8,9},{9,10},{10,1... | collective-permute-start | bytes 1376264 | tf_op jit(solution)/shard_map/ppermute | solution.py:345
  29.9 18.5 %collective-permute-start.7 = (f32[448,256]{1,0:T(8,128)S(1)}, f32[448,256]{1,0:T(8,128)S(1)}, u32[]{:S(2)}, u32[]{:S(2)}) collective-permute-start(f32[448,256]{1,0:T(8,128)S(1)} %get-tuple-element.53), channel_id=1, source_target_pairs={{0,3},{1,0},{2,1},{3,2},{4,7},{5,4},{6,5},{7,6},{8,11},{9,8},{10,9... | collective-permute-start | bytes 1376264 | tf_op jit(solution)/shard_map/ppermute | solution.py:345
  31.8 1.6 %collective-permute-start.4 = (f32[32,2048]{1,0:T(8,128)S(1)}, f32[32,2048]{1,0:T(8,128)S(1)}, u32[]{:S(2)}, u32[]{:S(2)}) collective-permute-start(f32[32,2048]{1,0:T(8,128)S(1)} %get-tuple-element.45), channel_id=1, source_target_pairs={{0,4},{4,0},{8,12},{12,8},{16,20},{20,16},{24,28},{28,24},{1,5},{5... | collective-permute-start | bytes 786440 | tf_op jit(solution)/shard_map/ppermute | solution.py:361
  33.4 10.4 %collective-permute-start.5 = (f32[16,2048]{1,0:T(8,128)S(1)}, f32[16,2048]{1,0:T(8,128)S(1)}, u32[]{:S(2)}, u32[]{:S(2)}) collective-permute-start(f32[16,2048]{1,0:T(8,128)S(1)} %get-tuple-element.47.refs_5_), channel_id=1, source_target_pairs={{0,8},{4,12},{8,0},{12,4},{16,24},{20,28},{24,16},{28,20},{1,9},{5... | collective-permute-start | bytes 393224 | tf_op jit(solution)/shard_map/ppermute | solution.py:357
  38.8 12.8 %collective-permute-start.11 = (f32[64,896]{1,0:T(8,128)S(1)}, f32[64,896]{1,0:T(8,128)S(1)}, u32[]{:S(2)}, u32[]{:S(2)}) collective-permute-start(f32[64,896]{1,0:T(8,128)S(1)} %get-tuple-element.57), channel_id=1, source_target_pairs={{0,64},{32,96},{64,0},{96,32},{1,65},{33,97},{65,1},{97,33},{2,66}... | collective-permute-start | bytes 688136 | tf_op jit(solution)/shard_map/ppermute | solution.py:345
  42.8 10.8 %collective-permute-start.12 = (f32[64,896]{1,0:T(8,128)S(1)}, f32[64,896]{1,0:T(8,128)S(1)}, u32[]{:S(2)}, u32[]{:S(2)}) collective-permute-start(f32[64,896]{1,0:T(8,128)S(1)} %get-tuple-element.58), channel_id=1, source_target_pairs={{0,32},{32,64},{64,96},{96,0},{1,33},{33,65},{65,97},{97,1},{2,34}... | collective-permute-start | bytes 688136 | tf_op jit(solution)/shard_map/ppermute | solution.py:345
  43.8 10.6 %collective-permute-start.13 = (f32[64,896]{1,0:T(8,128)S(1)}, f32[64,896]{1,0:T(8,128)S(1)}, u32[]{:S(2)}, u32[]{:S(2)}) collective-permute-start(f32[64,896]{1,0:T(8,128)S(1)} %get-tuple-element.59), channel_id=1, source_target_pairs={{0,96},{32,0},{64,32},{96,64},{1,97},{33,1},{65,33},{97,65},{2,98}... | collective-permute-start | bytes 688136 | tf_op jit(solution)/shard_map/ppermute | solution.py:345
  48.4 13.5 %collective-permute-start.9 = (f32[448,256]{1,0:T(8,128)S(1)}, f32[448,256]{1,0:T(8,128)S(1)}, u32[]{:S(2)}, u32[]{:S(2)}) collective-permute-start(f32[448,256]{1,0:T(8,128)S(1)} %get-tuple-element.55), channel_id=1, source_target_pairs={{0,3},{1,0},{2,1},{3,2},{4,7},{5,4},{6,5},{7,6},{8,11},{9,8},{10,9... | collective-permute-start | bytes 1376264 | tf_op jit(solution)/shard_map/ppermute | solution.py:345
  50.3 12.6 %collective-permute-start.8 = (f32[448,256]{1,0:T(8,128)S(1)}, f32[448,256]{1,0:T(8,128)S(1)}, u32[]{:S(2)}, u32[]{:S(2)}) collective-permute-start(f32[448,256]{1,0:T(8,128)S(1)} %get-tuple-element.54.refs_4_), channel_id=1, source_target_pairs={{0,1},{1,2},{2,3},{3,0},{4,5},{5,6},{6,7},{7,4},{8,9},{9,10},{10,1... | collective-permute-start | bytes 1376264 | tf_op jit(solution)/shard_map/ppermute | solution.py:345
  54.4 10.7 %collective-permute-start.15 = (f32[64,896]{1,0:T(8,128)S(1)}, f32[64,896]{1,0:T(8,128)S(1)}, u32[]{:S(2)}, u32[]{:S(2)}) collective-permute-start(f32[64,896]{1,0:T(8,128)S(1)} %shard_map.104.refs_3_.refs_0_), channel_id=1, source_target_pairs={{0,1},{1,0},{2,3},{3,2},{4,5},{5,4},{6,7},{7,6},{8,9},{9,8},{10,11... | collective-permute-start | bytes 688136 | tf_op jit(solution)/shard_map/ppermute | solution.py:353
  54.9 5.5 %collective-permute-start.10 = (f32[8,2048]{1,0:T(8,128)S(1)}, f32[8,2048]{1,0:T(8,128)S(1)}, u32[]{:S(2)}, u32[]{:S(2)}) collective-permute-start(f32[8,2048]{1,0:T(8,128)S(1)} %get-tuple-element.49.refs_2_), channel_id=1, source_target_pairs={{0,24},{4,28},{8,16},{12,20},{16,8},{20,12},{24,0},{28,4},{1,25},{... | collective-permute-start | bytes 196616 | tf_op jit(solution)/shard_map/ppermute | solution.py:357
  60.4 7.1 %collective-permute-start.14 = (f32[16,2048]{1,0:T(8,128)S(1)}, f32[16,2048]{1,0:T(8,128)S(1)}, u32[]{:S(2)}, u32[]{:S(2)}) collective-permute-start(f32[16,2048]{1,0:T(8,128)S(1)} %shard_map.105.refs_3_.refs_0_), channel_id=1, source_target_pairs={{0,32},{32,0},{64,96},{96,64},{1,33},{33,1},{65,97},{97,65},{2,34}... | collective-permute-start | bytes 393224 | tf_op jit(solution)/shard_map/ppermute | solution.py:353
  65.1 9.6 %collective-permute-start.18 = (f32[64,896]{1,0:T(8,128)S(1)}, f32[64,896]{1,0:T(8,128)S(1)}, u32[]{:S(2)}, u32[]{:S(2)}) collective-permute-start(f32[64,896]{1,0:T(8,128)S(1)} %shard_map.107.refs_2_.refs_0_), channel_id=1, source_target_pairs={{0,3},{1,2},{2,1},{3,0},{4,7},{5,6},{6,5},{7,4},{8,11},{9,10},{10,... | collective-permute-start | bytes 688136 | tf_op jit(solution)/shard_map/ppermute | solution.py:353
  67.5 18.3 %collective-permute-start.17 = (f32[448,256]{1,0:T(8,128)S(1)}, f32[448,256]{1,0:T(8,128)S(1)}, u32[]{:S(2)}, u32[]{:S(2)}) collective-permute-start(f32[448,256]{1,0:T(8,128)S(1)} %get-tuple-element.63), channel_id=1, source_target_pairs={{0,3},{1,0},{2,1},{3,2},{4,7},{5,4},{6,5},{7,6},{8,11},{9,8},{10,9... | collective-permute-start | bytes 1376264 | tf_op jit(solution)/shard_map/ppermute | solution.py:345
  68.6 17.3 %collective-permute-start.16 = (f32[448,256]{1,0:T(8,128)S(1)}, f32[448,256]{1,0:T(8,128)S(1)}, u32[]{:S(2)}, u32[]{:S(2)}) collective-permute-start(f32[448,256]{1,0:T(8,128)S(1)} %get-tuple-element.62.refs_2_), channel_id=1, source_target_pairs={{0,1},{1,2},{2,3},{3,0},{4,5},{5,6},{6,7},{7,4},{8,9},{9,10},{10,1... | collective-permute-start | bytes 1376264 | tf_op jit(solution)/shard_map/ppermute | solution.py:345
  69.6 6.7 %collective-permute-start.21 = (f32[16,2048]{1,0:T(8,128)S(1)}, f32[16,2048]{1,0:T(8,128)S(1)}, u32[]{:S(2)}, u32[]{:S(2)}) collective-permute-start(f32[16,2048]{1,0:T(8,128)S(1)} %shard_map.108.refs_2_.refs_0_), channel_id=1, source_target_pairs={{0,96},{32,64},{64,32},{96,0},{1,97},{33,65},{65,33},{97,1},{2,98}... | collective-permute-start | bytes 393224 | tf_op jit(solution)/shard_map/ppermute | solution.py:353
  74.8 7.7 %collective-permute-start.20 = (f32[32,896]{1,0:T(8,128)S(1)}, f32[32,896]{1,0:T(8,128)S(1)}, u32[]{:S(2)}, u32[]{:S(2)}) collective-permute-start(f32[32,896]{1,0:T(8,128)S(1)} %get-tuple-element.65.refs_2_), channel_id=1, source_target_pairs={{0,32},{32,0},{64,96},{96,64},{1,33},{33,1},{65,97},{97,65},{2,34}... | collective-permute-start | bytes 344072 | tf_op jit(solution)/shard_map/ppermute | solution.py:353
  74.9 7.6 %collective-permute-start.19 = (f32[32,896]{1,0:T(8,128)S(1)}, f32[32,896]{1,0:T(8,128)S(1)}, u32[]{:S(2)}, u32[]{:S(2)}) collective-permute-start(f32[32,896]{1,0:T(8,128)S(1)} %get-tuple-element.64.refs_3_.refs_0_), channel_id=1, source_target_pairs={{0,96},{32,64},{64,32},{96,0},{1,97},{33,65},{65,33},{97,1},{2,98}... | collective-permute-start | bytes 344072 | tf_op jit(solution)/shard_map/ppermute | solution.py:353
  76.9 5.5 %collective-permute-start.22 = (f32[8,2048]{1,0:T(8,128)S(1)}, f32[8,2048]{1,0:T(8,128)S(1)}, u32[]{:S(2)}, u32[]{:S(2)}) collective-permute-start(f32[8,2048]{1,0:T(8,128)S(1)} %get-tuple-element.66.refs_0_), channel_id=1, source_target_pairs={{0,24},{4,28},{8,16},{12,20},{16,8},{20,12},{24,0},{28,4},{1,25},{... | collective-permute-start | bytes 196616 | tf_op jit(solution)/shard_map/ppermute | solution.py:357
  82.5 7.3 %collective-permute-start.24 = (f32[64,896]{1,0:T(8,128)S(1)}, f32[64,896]{1,0:T(8,128)S(1)}, u32[]{:S(2)}, u32[]{:S(2)}) collective-permute-start(f32[64,896]{1,0:T(8,128)S(1)} %get-tuple-element.69.refs_2_), channel_id=1, source_target_pairs={{0,96},{32,64},{64,32},{96,0},{1,97},{33,65},{65,33},{97,1},{2,98}... | collective-permute-start | bytes 688136 | tf_op jit(solution)/shard_map/ppermute | solution.py:353
  84.4 6.0 %collective-permute-start.23 = (f32[64,896]{1,0:T(8,128)S(1)}, f32[64,896]{1,0:T(8,128)S(1)}, u32[]{:S(2)}, u32[]{:S(2)}) collective-permute-start(f32[64,896]{1,0:T(8,128)S(1)} %get-tuple-element.67.refs_3_.refs_0_), channel_id=1, source_target_pairs={{0,32},{32,0},{64,96},{96,64},{1,33},{33,1},{65,97},{97,65},{2,34}... | collective-permute-start | bytes 688136 | tf_op jit(solution)/shard_map/ppermute | solution.py:353
  85.2 5.3 %collective-permute-start.25 = (f32[16,2048]{1,0:T(8,128)S(1)}, f32[16,2048]{1,0:T(8,128)S(1)}, u32[]{:S(2)}, u32[]{:S(2)}) collective-permute-start(f32[16,2048]{1,0:T(8,128)S(1)} %shard_map.112.refs_4_.refs_0_), channel_id=1, source_target_pairs={{0,8},{4,12},{8,0},{12,4},{16,24},{20,28},{24,16},{28,20},{1,9},{5... | collective-permute-start | bytes 393224 | tf_op jit(solution)/shard_map/ppermute | solution.py:357
  90.5 1.6 %collective-permute-start.26 = (f32[32,2048]{1,0:T(8,128)S(1)}, f32[32,2048]{1,0:T(8,128)S(1)}, u32[]{:S(2)}, u32[]{:S(2)}) collective-permute-start(f32[32,2048]{1,0:T(8,128)S(1)} %shard_map.116.refs_4_.refs_0_), channel_id=1, source_target_pairs={{0,4},{4,0},{8,12},{12,8},{16,20},{20,16},{24,28},{28,24},{1,5},{5... | collective-permute-start | bytes 786440 | tf_op jit(solution)/shard_map/ppermute | solution.py:361

commit v10 on v9

--- a/solution.py
+++ b/solution.py
@@ -398,13 +398,13 @@
         after=[send],
     )
     keep, send = halve(keep, swap_x(send, 0), far_bit, after=[pieces[0]])
-    pieces = [pieces[0]] + [ring(pieces[k], "dp", k) for k in (2, 1, 3)]
+    pieces = [pieces[0]] + [ring(pieces[k], "dp", k) for k in (1, 3, 2)]
     half = [out((far, toks))] * 2
     v_up, v_down = call(near_kernel, half, [VMEM] * 2, m, scaled, after=[send])
+    v_up, v_down = hold([v_up, v_down], [u0, u1])
+    v0, v1 = ring(v_up, "cols", 1), ring(v_down, "cols", 3)
     own = call(own_kernel, [out((rows // 4, toks))], [VMEM] * 2, m, scaled, after=[v_up])[0]
-    v_up, v_down = hold([v_up, v_down], [own, u0, u1])
-    v0, v1 = ring(v_up, "cols", 1), ring(v_down, "cols", 3)
-    up, down = call(relay_kernel, half, [VMEM] * 4, m, scaled, u0, u1, after=[v_up])
+    up, down = call(relay_kernel, half, [VMEM] * 4, m, scaled, u0, u1, after=[own])
 
     piece = add(*pieces, after=[up])
     stack = call(

time: 94.1 us -> 92.9 us (0.987)
  waiting for transfers between devices: 29.1 us -> 26.6 us
  starting transfers between devices: 31.5 us -> 32.8 us
    ppermute x8, waiting for transfers between devices: 11.1 us -> 8.72 us  [swap(): lax.ppermute(value, axis, [(i, i ^ 1 if step == 0 else 3 - i) for i in ra...]
    ppermute x8, starting transfers between devices: 7.96 us -> 9.92 us  [swap(): lax.ppermute(value, axis, [(i, i ^ 1 if step == 0 else 3 - i) for i in ra...]
    ppermute x9, starting transfers between devices: 14.7 us -> 13.6 us  [ring(): lax.ppermute(value, axis, [(i, (i + k) % count) for i in range(count)])]
  transfers between devices with their start and end apart: 27 -> 27, of which waited for: 16 -> 15; matrix products, arithmetic and copies ran while one was open for 0% -> 0% of each run, Pallas kernels for 14% -> 14%
where the time goes in v10:
time: 92.9 us; the launch traced here: 91.8 us
  starting transfers between devices  32.8 us (35%)
  Pallas kernels  31.4 us (34%)
  waiting for transfers between devices  26.6 us (29%)
    pallas_call x23, Pallas kernels, call(): pl.pallas_call(body, out_shape=outs, in_specs=list(specs) + [ANY] * len(a...  31.4 us
    ppermute x9, starting transfers between devices, ring(): lax.ppermute(value, axis, [(i, (i + k) % count) for i in range(count)])  13.6 us
    ppermute x8, starting transfers between devices, swap(): lax.ppermute(value, axis, [(i, i ^ 1 if step == 0 else 3 - i) for i in ra...  9.92 us
    ppermute x8, waiting for transfers between devices, swap(): lax.ppermute(value, axis, [(i, i ^ 1 if step == 0 else 3 - i) for i in ra...  8.72 us
    ppermute x4, waiting for transfers between devices, swap_x(): lax.ppermute(value, 'rows', [(i, i ^ 2 if step == 0 else 6 - 2 * (i // 2)...  7.25 us
    ppermute x3, starting transfers between devices, ring_x(): lax.ppermute(value, 'rows', [(i, (i + 2 * k) % count) for i in range(coun...  4.59 us
    ppermute x9, waiting for transfers between devices, ring(): lax.ppermute(value, axis, [(i, (i + k) % count) for i in range(count)])  4.52 us
    ppermute x4, starting transfers between devices, swap_x(): lax.ppermute(value, 'rows', [(i, i ^ 2 if step == 0 else 6 - 2 * (i // 2)...  4.43 us
  transfers between devices with their start and end apart: 27, of which 15 were waited for; matrix products, arithmetic and copies ran while one was open for 0% of the time, Pallas kernels for 14%

profile of v10, /device:TPU:0, one launch (start us, length us, event | category | flops | bytes accessed | tf_op | source)
XLA Modules:
  0.0 91.8 jit_solution(6409731628766627049)
XLA Ops:
  0.7 16.5 %shard_map.93 = (bf16[3584,2048]{1,0:T(8,128)(2,1)S(1)}, f32[2,2048]{1,0:T(2,128)S(1)}, f32[64,2048]{1,0:T(8,128)S(1)}) custom-call(bf16[3584,2048]{1,0:T(8,128)(2,1)} %refs_0_.1, bf16[256,3584]{1,0:T(8,128)(2,1)} %refs_3_.3, bf16[64,3584]{1,0:T(8,128)(2,1)} %bitcast.4, bf16[64,2048]{1,0:T(8,128)(2,1)} %refs_2_.3, bf16[256,2048]{1,0:T(8,128)(2,1)} %refs_1_.5), custom_call_target="tpu_custom_call" | custom-call | flops 5637144576 | bytes 14680064 | tf_op jit(solution)/shard_map/pallas_call | solution.py:49
  17.2 1.2 %collective-permute-done = f32[2,2048]{1,0:T(2,128)S(1)} collective-permute-done((f32[2,2048]{1,0:T(2,128)S(1)}, f32[2,2048]{1,0:T(2,128)S(1)}, u32[]{:S(2)}, u32[]{:S(2)}) %collective-permute-start) | collective-permute-done | bytes 16416 | tf_op jit(solution)/shard_map/ppermute | solution.py:361
  18.4 2.9 %collective-permute-start.3 = (f32[2,2048]{1,0:T(2,128)S(1)}, f32[2,2048]{1,0:T(2,128)S(1)}, u32[]{:S(2)}, u32[]{:S(2)}) collective-permute-start(f32[2,2048]{1,0:T(2,128)S(1)} %add.3.refs_0_), channel_id=1, source_target_pairs={{0,24},{4,28},{8,0},{12,4},{16,8},{20,12},{24,16},{28,20},{1,25},{... | collective-permute-start | bytes 49160 | tf_op jit(solution)/shard_map/ppermute | solution.py:349
  23.0 1.2 %shard_map.94.refs_7_.refs_1_ = f32[64,2048]{1,0:T(8,128)S(1)} custom-call(bf16[64,3584]{1,0:T(8,128)(2,1)S(1)} %bitcast.5, bf16[256,3584]{1,0:T(8,128)(2,1)S(1)} %copy-done.1, bf16[256,2048]{1,0:T(8,128)(2,1)S(1)} %copy-done, f32[2,2048]{1,0:T(2,128)S(1)} %get-tuple-element.40.refs_3_), custom_call_target="tpu_custom_call" | custom-call | flops 1 | bytes 1 | tf_op jit(solution)/shard_map/pallas_call | solution.py:49
  24.2 2.4 %collective-permute-done.2.refs_2_ = f32[2,2048]{1,0:T(2,128)S(1)} collective-permute-done((f32[2,2048]{1,0:T(2,128)S(1)}, f32[2,2048]{1,0:T(2,128)S(1)}, u32[]{:S(2)}, u32[]{:S(2)}) %collective-permute-start.2) | collective-permute-done | bytes 16416 | tf_op jit(solution)/shard_map/ppermute | solution.py:349
  27.1 1.2 %shard_map.95 = (f32[4,2048]{1,0:T(4,128)S(1)}, bf16[256,2048]{1,0:T(8,128)(2,1)S(1)}, f32[448,256]{1,0:T(8,128)S(1)}, f32[448,256]{1,0:T(8,128)S(1)}) custom-call(f32[2,2048]{1,0:T(2,128)S(1)} %add.3.refs_0_, f32[2,2048]{1,0:T(2,128)S(1)} %collective-permute-done.1.refs_1_, f32[2,2048]{1,0:T(2,128)S(1)} %collective-permute-done.2.refs_2_, ...), custom_call_target="tpu_custom_call" | custom-call | flops 1 | bytes 1 | tf_op jit(solution)/shard_map/pallas_call | solution.py:49
  28.3 1.6 %collective-permute-start.6 = (f32[448,256]{1,0:T(8,128)S(1)}, f32[448,256]{1,0:T(8,128)S(1)}, u32[]{:S(2)}, u32[]{:S(2)}) collective-permute-start(f32[448,256]{1,0:T(8,128)S(1)} %get-tuple-element.52), channel_id=1, source_target_pairs={{0,1},{1,2},{2,3},{3,0},{4,5},{5,6},{6,7},{7,4},{8,9},{9,10},{10,1... | collective-permute-start | bytes 1376264 | tf_op jit(solution)/shard_map/ppermute | solution.py:345
  29.9 1.7 %collective-permute-start.7 = (f32[448,256]{1,0:T(8,128)S(1)}, f32[448,256]{1,0:T(8,128)S(1)}, u32[]{:S(2)}, u32[]{:S(2)}) collective-permute-start(f32[448,256]{1,0:T(8,128)S(1)} %get-tuple-element.53), channel_id=1, source_target_pairs={{0,3},{1,0},{2,1},{3,2},{4,7},{5,4},{6,5},{7,6},{8,11},{9,8},{10,9... | collective-permute-start | bytes 1376264 | tf_op jit(solution)/shard_map/ppermute | solution.py:345
  31.9 1.5 %collective-permute-done.4.refs_1_ = f32[32,2048]{1,0:T(8,128)S(1)} collective-permute-done((f32[32,2048]{1,0:T(8,128)S(1)}, f32[32,2048]{1,0:T(8,128)S(1)}, u32[]{:S(2)}, u32[]{:S(2)}) %collective-permute-start.4) | collective-permute-done | bytes 262176 | tf_op jit(solution)/shard_map/ppermute | solution.py:361
  33.5 5.3 %shard_map.98 = (f32[64,896]{1,0:T(8,128)S(1)}, f32[64,896]{1,0:T(8,128)S(1)}, f32[64,896]{1,0:T(8,128)S(1)}, f32[64,896]{1,0:T(8,128)S(1)}) custom-call(f32[4,2048]{1,0:T(4,128)S(1)} %get-tuple-element.42.refs_0_.refs_2_, bf16[256,2048]{1,0:T(8,128)(2,1)S(1)} %copy-done, bf16[64,2048]{1,0:T(8,128)(2,1)S(1)} %copy-done.3, bf16[256,3584]{1,0:T(8,128)(2,1)S(1)} %copy-done.1, ...), custom_call_target="tpu_custom_call" | custom-call | flops 1 | bytes 1 | tf_op jit(solution)/shard_map/pallas_call | solution.py:49
  38.8 2.0 %collective-permute-start.11 = (f32[64,896]{1,0:T(8,128)S(1)}, f32[64,896]{1,0:T(8,128)S(1)}, u32[]{:S(2)}, u32[]{:S(2)}) collective-permute-start(f32[64,896]{1,0:T(8,128)S(1)} %get-tuple-element.57), channel_id=1, source_target_pairs={{0,32},{32,64},{64,96},{96,0},{1,33},{33,65},{65,97},{97,1},{2,34}... | collective-permute-start | bytes 688136 | tf_op jit(solution)/shard_map/ppermute | solution.py:345
  40.8 2.2 %collective-permute-start.12 = (f32[64,896]{1,0:T(8,128)S(1)}, f32[64,896]{1,0:T(8,128)S(1)}, u32[]{:S(2)}, u32[]{:S(2)}) collective-permute-start(f32[64,896]{1,0:T(8,128)S(1)} %get-tuple-element.58), channel_id=1, source_target_pairs={{0,96},{32,0},{64,32},{96,64},{1,97},{33,1},{65,33},{97,65},{2,98}... | collective-permute-start | bytes 688136 | tf_op jit(solution)/shard_map/ppermute | solution.py:345
  43.0 1.8 %collective-permute-start.13 = (f32[64,896]{1,0:T(8,128)S(1)}, f32[64,896]{1,0:T(8,128)S(1)}, u32[]{:S(2)}, u32[]{:S(2)}) collective-permute-start(f32[64,896]{1,0:T(8,128)S(1)} %get-tuple-element.59), channel_id=1, source_target_pairs={{0,64},{32,96},{64,0},{96,32},{1,65},{33,97},{65,1},{97,33},{2,66}... | collective-permute-start | bytes 688136 | tf_op jit(solution)/shard_map/ppermute | solution.py:345
  44.9 1.1 %shard_map.100 = (f32[448,256]{1,0:T(8,128)S(1)}, f32[448,256]{1,0:T(8,128)S(1)}) custom-call(bf16[3584,2048]{1,0:T(8,128)(2,1)S(1)} %get-tuple-element.39.refs_6_.refs_4_.refs_0_, bf16[256,2048]{1,0:T(8,128)(2,1)S(1)} %get-tuple-element.41.refs_1_, f32[8,2048]{1,0:T(8,128)S(1)} %get-tuple-element.49.refs_2_), custom_call_target="tpu_custom_call" | custom-call | flops 1 | bytes 1 | tf_op jit(solution)/shard_map/pallas_call | solution.py:49
  46.0 1.9 %collective-permute-start.9 = (f32[448,256]{1,0:T(8,128)S(1)}, f32[448,256]{1,0:T(8,128)S(1)}, u32[]{:S(2)}, u32[]{:S(2)}) collective-permute-start(f32[448,256]{1,0:T(8,128)S(1)} %get-tuple-element.55), channel_id=1, source_target_pairs={{0,3},{1,0},{2,1},{3,2},{4,7},{5,4},{6,5},{7,6},{8,11},{9,8},{10,9... | collective-permute-start | bytes 1376264 | tf_op jit(solution)/shard_map/ppermute | solution.py:345
  48.1 1.1 %shard_map.102.refs_4_.refs_0_ = f32[896,256]{1,0:T(8,128)S(1)} custom-call(bf16[3584,2048]{1,0:T(8,128)(2,1)S(1)} %get-tuple-element.39.refs_6_.refs_4_.refs_0_, bf16[256,2048]{1,0:T(8,128)(2,1)S(1)} %get-tuple-element.41.refs_1_, f32[448,256]{1,0:T(8,128)S(1)} %get-tuple-element.54.refs_2_), custom_call_target="tpu_custom_call" | custom-call | flops 1 | bytes 1 | tf_op jit(solution)/shard_map/pallas_call | solution.py:49
  49.3 1.1 %shard_map.103 = (f32[448,256]{1,0:T(8,128)S(1)}, f32[448,256]{1,0:T(8,128)S(1)}) custom-call(bf16[3584,2048]{1,0:T(8,128)(2,1)S(1)} %get-tuple-element.39.refs_6_.refs_4_.refs_0_, bf16[256,2048]{1,0:T(8,128)(2,1)S(1)} %get-tuple-element.41.refs_1_, f32[448,256]{1,0:T(8,128)S(1)} %collective-permute-done.6.refs_2_, ...), custom_call_target="tpu_custom_call" | custom-call | flops 1 | bytes 1 | tf_op jit(solution)/shard_map/pallas_call | solution.py:49
  50.4 2.7 %collective-permute-done.12.refs_2_ = f32[64,896]{1,0:T(8,128)S(1)} collective-permute-done((f32[64,896]{1,0:T(8,128)S(1)}, f32[64,896]{1,0:T(8,128)S(1)}, u32[]{:S(2)}, u32[]{:S(2)}) %collective-permute-start.12) | collective-permute-done | bytes 229408 | tf_op jit(solution)/shard_map/ppermute | solution.py:345
  53.1 1.8 %collective-permute-done.13.refs_3_ = f32[64,896]{1,0:T(8,128)S(1)} collective-permute-done((f32[64,896]{1,0:T(8,128)S(1)}, f32[64,896]{1,0:T(8,128)S(1)}, u32[]{:S(2)}, u32[]{:S(2)}) %collective-permute-start.13) | collective-permute-done | bytes 229408 | tf_op jit(solution)/shard_map/ppermute | solution.py:345
  55.4 1.8 %collective-permute-start.10 = (f32[8,2048]{1,0:T(8,128)S(1)}, f32[8,2048]{1,0:T(8,128)S(1)}, u32[]{:S(2)}, u32[]{:S(2)}) collective-permute-start(f32[8,2048]{1,0:T(8,128)S(1)} %get-tuple-element.49.refs_2_), channel_id=1, source_target_pairs={{0,24},{4,28},{8,16},{12,20},{16,8},{20,12},{24,0},{28,4},{1,25},{... | collective-permute-start | bytes 196616 | tf_op jit(solution)/shard_map/ppermute | solution.py:357
  57.2 3.7 %collective-permute-done.10.refs_1_ = f32[8,2048]{1,0:T(8,128)S(1)} collective-permute-done((f32[8,2048]{1,0:T(8,128)S(1)}, f32[8,2048]{1,0:T(8,128)S(1)}, u32[]{:S(2)}, u32[]{:S(2)}) %collective-permute-start.10) | collective-permute-done | bytes 65568 | tf_op jit(solution)/shard_map/ppermute | solution.py:357
  60.9 1.2 %collective-permute-start.14 = (f32[16,2048]{1,0:T(8,128)S(1)}, f32[16,2048]{1,0:T(8,128)S(1)}, u32[]{:S(2)}, u32[]{:S(2)}) collective-permute-start(f32[16,2048]{1,0:T(8,128)S(1)} %shard_map.105.refs_3_.refs_0_), channel_id=1, source_target_pairs={{0,32},{32,0},{64,96},{96,64},{1,33},{33,1},{65,97},{97,65},{2,34}... | collective-permute-start | bytes 393224 | tf_op jit(solution)/shard_map/ppermute | solution.py:353
  62.8 2.3 %collective-permute-start.18 = (f32[64,896]{1,0:T(8,128)S(1)}, f32[64,896]{1,0:T(8,128)S(1)}, u32[]{:S(2)}, u32[]{:S(2)}) collective-permute-start(f32[64,896]{1,0:T(8,128)S(1)} %shard_map.107.refs_2_.refs_0_), channel_id=1, source_target_pairs={{0,3},{1,2},{2,1},{3,0},{4,7},{5,6},{6,5},{7,4},{8,11},{9,10},{10,... | collective-permute-start | bytes 688136 | tf_op jit(solution)/shard_map/ppermute | solution.py:353
  66.0 2.3 %collective-permute-start.17 = (f32[448,256]{1,0:T(8,128)S(1)}, f32[448,256]{1,0:T(8,128)S(1)}, u32[]{:S(2)}, u32[]{:S(2)}) collective-permute-start(f32[448,256]{1,0:T(8,128)S(1)} %get-tuple-element.63), channel_id=1, source_target_pairs={{0,3},{1,0},{2,1},{3,2},{4,7},{5,4},{6,5},{7,6},{8,11},{9,8},{10,9... | collective-permute-start | bytes 1376264 | tf_op jit(solution)/shard_map/ppermute | solution.py:345
  68.3 1.9 %collective-permute-start.21 = (f32[16,2048]{1,0:T(8,128)S(1)}, f32[16,2048]{1,0:T(8,128)S(1)}, u32[]{:S(2)}, u32[]{:S(2)}) collective-permute-start(f32[16,2048]{1,0:T(8,128)S(1)} %shard_map.108.refs_2_.refs_0_), channel_id=1, source_target_pairs={{0,96},{32,64},{64,32},{96,0},{1,97},{33,65},{65,33},{97,1},{2,98}... | collective-permute-start | bytes 393224 | tf_op jit(solution)/shard_map/ppermute | solution.py:353
  70.1 2.5 %collective-permute-done.18.refs_1_ = f32[64,896]{1,0:T(8,128)S(1)} collective-permute-done((f32[64,896]{1,0:T(8,128)S(1)}, f32[64,896]{1,0:T(8,128)S(1)}, u32[]{:S(2)}, u32[]{:S(2)}) %collective-permute-start.18) | collective-permute-done | bytes 229408 | tf_op jit(solution)/shard_map/ppermute | solution.py:353
  72.6 1.1 %collective-permute-start.20 = (f32[32,896]{1,0:T(8,128)S(1)}, f32[32,896]{1,0:T(8,128)S(1)}, u32[]{:S(2)}, u32[]{:S(2)}) collective-permute-start(f32[32,896]{1,0:T(8,128)S(1)} %get-tuple-element.65.refs_2_), channel_id=1, source_target_pairs={{0,32},{32,0},{64,96},{96,64},{1,33},{33,1},{65,97},{97,65},{2,34}... | collective-permute-start | bytes 344072 | tf_op jit(solution)/shard_map/ppermute | solution.py:353
  73.7 1.3 %collective-permute-start.19 = (f32[32,896]{1,0:T(8,128)S(1)}, f32[32,896]{1,0:T(8,128)S(1)}, u32[]{:S(2)}, u32[]{:S(2)}) collective-permute-start(f32[32,896]{1,0:T(8,128)S(1)} %get-tuple-element.64.refs_3_.refs_0_), channel_id=1, source_target_pairs={{0,96},{32,64},{64,32},{96,0},{1,97},{33,65},{65,33},{97,1},{2,98}... | collective-permute-start | bytes 344072 | tf_op jit(solution)/shard_map/ppermute | solution.py:353
  76.0 1.9 %collective-permute-start.22 = (f32[8,2048]{1,0:T(8,128)S(1)}, f32[8,2048]{1,0:T(8,128)S(1)}, u32[]{:S(2)}, u32[]{:S(2)}) collective-permute-start(f32[8,2048]{1,0:T(8,128)S(1)} %get-tuple-element.66.refs_0_), channel_id=1, source_target_pairs={{0,24},{4,28},{8,16},{12,20},{16,8},{20,12},{24,0},{28,4},{1,25},{... | collective-permute-start | bytes 196616 | tf_op jit(solution)/shard_map/ppermute | solution.py:357
  78.0 3.6 %collective-permute-done.22.refs_1_ = f32[8,2048]{1,0:T(8,128)S(1)} collective-permute-done((f32[8,2048]{1,0:T(8,128)S(1)}, f32[8,2048]{1,0:T(8,128)S(1)}, u32[]{:S(2)}, u32[]{:S(2)}) %collective-permute-start.22) | collective-permute-done | bytes 65568 | tf_op jit(solution)/shard_map/ppermute | solution.py:357
  81.6 1.6 %collective-permute-start.24 = (f32[64,896]{1,0:T(8,128)S(1)}, f32[64,896]{1,0:T(8,128)S(1)}, u32[]{:S(2)}, u32[]{:S(2)}) collective-permute-start(f32[64,896]{1,0:T(8,128)S(1)} %get-tuple-element.69.refs_2_), channel_id=1, source_target_pairs={{0,96},{32,64},{64,32},{96,0},{1,97},{33,65},{65,33},{97,1},{2,98}... | collective-permute-start | bytes 688136 | tf_op jit(solution)/shard_map/ppermute | solution.py:353
  84.7 4.2 %collective-permute-done.24.refs_1_ = f32[64,896]{1,0:T(8,128)S(1)} collective-permute-done((f32[64,896]{1,0:T(8,128)S(1)}, f32[64,896]{1,0:T(8,128)S(1)}, u32[]{:S(2)}, u32[]{:S(2)}) %collective-permute-start.24) | collective-permute-done | bytes 229408 | tf_op jit(solution)/shard_map/ppermute | solution.py:353
  (59 shorter events, 10.4 us)
Async XLA Ops:
  0.6 22.4 %copy-start = (bf16[256,2048]{1,0:T(8,128)(2,1)S(1)}, bf16[256,2048]{1,0:T(8,128)(2,1)}, u32[]{:S(2)}) copy-start(bf16[256,2048]{1,0:T(8,128)(2,1)} %refs_1_.5) | copy-start | bytes 3145732
  0.6 22.4 %copy-start.1 = (bf16[256,3584]{1,0:T(8,128)(2,1)S(1)}, bf16[256,3584]{1,0:T(8,128)(2,1)}, u32[]{:S(2)}) copy-start(bf16[256,3584]{1,0:T(8,128)(2,1)} %refs_3_.3) | copy-start | bytes 5505028
  0.7 22.4 %copy-start.2 = (bf16[3584,64]{0,1:T(8,128)(2,1)S(1)}, bf16[3584,64]{0,1:T(8,128)(2,1)}, u32[]{:S(2)}) copy-start(bf16[3584,64]{0,1:T(8,128)(2,1)} %param.9) | copy-start | bytes 1376260
  0.7 26.4 %copy-start.4 = (f32[2048]{0:T(1024)S(1)}, f32[2048]{0:T(1024)}, u32[]{:S(2)}) copy-start(f32[2048]{0:T(1024)} %param.11) | copy-start | bytes 24580
  17.1 16.4 %copy-start.3 = (bf16[64,2048]{1,0:T(8,128)(2,1)S(1)}, bf16[64,2048]{1,0:T(8,128)(2,1)}, u32[]{:S(2)}) copy-start(bf16[64,2048]{1,0:T(8,128)(2,1)} %refs_2_.3) | copy-start | bytes 786436
  17.1 1.3 %collective-permute-start = (f32[2,2048]{1,0:T(2,128)S(1)}, f32[2,2048]{1,0:T(2,128)S(1)}, u32[]{:S(2)}, u32[]{:S(2)}) collective-permute-start(f32[2,2048]{1,0:T(2,128)S(1)} %get-tuple-element.40.refs_3_), channel_id=1, source_target_pairs={{0,4},{4,0},{8,12},{12,8},{16,20},{20,16},{24,28},{28,24},{1,5},{5... | collective-permute-start | bytes 49160 | tf_op jit(solution)/shard_map/ppermute | solution.py:361
  18.4 5.8 %collective-permute-start.3 = (f32[2,2048]{1,0:T(2,128)S(1)}, f32[2,2048]{1,0:T(2,128)S(1)}, u32[]{:S(2)}, u32[]{:S(2)}) collective-permute-start(f32[2,2048]{1,0:T(2,128)S(1)} %add.3.refs_0_), channel_id=1, source_target_pairs={{0,24},{4,28},{8,0},{12,4},{16,8},{20,12},{24,16},{28,20},{1,25},{... | collective-permute-start | bytes 49160 | tf_op jit(solution)/shard_map/ppermute | solution.py:349
  21.3 5.2 %collective-permute-start.2 = (f32[2,2048]{1,0:T(2,128)S(1)}, f32[2,2048]{1,0:T(2,128)S(1)}, u32[]{:S(2)}, u32[]{:S(2)}) collective-permute-start(f32[2,2048]{1,0:T(2,128)S(1)} %add.3.refs_0_), channel_id=1, source_target_pairs={{0,16},{4,20},{8,24},{12,28},{16,0},{20,4},{24,8},{28,12},{1,17},{... | collective-permute-start | bytes 49160 | tf_op jit(solution)/shard_map/ppermute | solution.py:349
  22.1 4.9 %collective-permute-start.1 = (f32[2,2048]{1,0:T(2,128)S(1)}, f32[2,2048]{1,0:T(2,128)S(1)}, u32[]{:S(2)}, u32[]{:S(2)}) collective-permute-start(f32[2,2048]{1,0:T(2,128)S(1)} %add.3.refs_0_), channel_id=1, source_target_pairs={{0,8},{4,12},{8,16},{12,20},{16,24},{20,28},{24,0},{28,4},{1,9},{5... | collective-permute-start | bytes 49160 | tf_op jit(solution)/shard_map/ppermute | solution.py:349
  28.3 17.7 %collective-permute-start.6 = (f32[448,256]{1,0:T(8,128)S(1)}, f32[448,256]{1,0:T(8,128)S(1)}, u32[]{:S(2)}, u32[]{:S(2)}) collective-permute-start(f32[448,256]{1,0:T(8,128)S(1)} %get-tuple-element.52), channel_id=1, source_target_pairs={{0,1},{1,2},{2,3},{3,0},{4,5},{5,6},{6,7},{7,4},{8,9},{9,10},{10,1... | collective-permute-start | bytes 1376264 | tf_op jit(solution)/shard_map/ppermute | solution.py:345
  29.9 16.1 %collective-permute-start.7 = (f32[448,256]{1,0:T(8,128)S(1)}, f32[448,256]{1,0:T(8,128)S(1)}, u32[]{:S(2)}, u32[]{:S(2)}) collective-permute-start(f32[448,256]{1,0:T(8,128)S(1)} %get-tuple-element.53), channel_id=1, source_target_pairs={{0,3},{1,0},{2,1},{3,2},{4,7},{5,4},{6,5},{7,6},{8,11},{9,8},{10,9... | collective-permute-start | bytes 1376264 | tf_op jit(solution)/shard_map/ppermute | solution.py:345
  31.8 1.6 %collective-permute-start.4 = (f32[32,2048]{1,0:T(8,128)S(1)}, f32[32,2048]{1,0:T(8,128)S(1)}, u32[]{:S(2)}, u32[]{:S(2)}) collective-permute-start(f32[32,2048]{1,0:T(8,128)S(1)} %get-tuple-element.45), channel_id=1, source_target_pairs={{0,4},{4,0},{8,12},{12,8},{16,20},{20,16},{24,28},{28,24},{1,5},{5... | collective-permute-start | bytes 786440 | tf_op jit(solution)/shard_map/ppermute | solution.py:361
  33.4 9.6 %collective-permute-start.5 = (f32[16,2048]{1,0:T(8,128)S(1)}, f32[16,2048]{1,0:T(8,128)S(1)}, u32[]{:S(2)}, u32[]{:S(2)}) collective-permute-start(f32[16,2048]{1,0:T(8,128)S(1)} %get-tuple-element.47.refs_5_), channel_id=1, source_target_pairs={{0,8},{4,12},{8,0},{12,4},{16,24},{20,28},{24,16},{28,20},{1,9},{5... | collective-permute-start | bytes 393224 | tf_op jit(solution)/shard_map/ppermute | solution.py:357
  38.8 11.6 %collective-permute-start.11 = (f32[64,896]{1,0:T(8,128)S(1)}, f32[64,896]{1,0:T(8,128)S(1)}, u32[]{:S(2)}, u32[]{:S(2)}) collective-permute-start(f32[64,896]{1,0:T(8,128)S(1)} %get-tuple-element.57), channel_id=1, source_target_pairs={{0,32},{32,64},{64,96},{96,0},{1,33},{33,65},{65,97},{97,1},{2,34}... | collective-permute-start | bytes 688136 | tf_op jit(solution)/shard_map/ppermute | solution.py:345
  40.8 12.3 %collective-permute-start.12 = (f32[64,896]{1,0:T(8,128)S(1)}, f32[64,896]{1,0:T(8,128)S(1)}, u32[]{:S(2)}, u32[]{:S(2)}) collective-permute-start(f32[64,896]{1,0:T(8,128)S(1)} %get-tuple-element.58), channel_id=1, source_target_pairs={{0,96},{32,0},{64,32},{96,64},{1,97},{33,1},{65,33},{97,65},{2,98}... | collective-permute-start | bytes 688136 | tf_op jit(solution)/shard_map/ppermute | solution.py:345
  43.0 11.9 %collective-permute-start.13 = (f32[64,896]{1,0:T(8,128)S(1)}, f32[64,896]{1,0:T(8,128)S(1)}, u32[]{:S(2)}, u32[]{:S(2)}) collective-permute-start(f32[64,896]{1,0:T(8,128)S(1)} %get-tuple-element.59), channel_id=1, source_target_pairs={{0,64},{32,96},{64,0},{96,32},{1,65},{33,97},{65,1},{97,33},{2,66}... | collective-permute-start | bytes 688136 | tf_op jit(solution)/shard_map/ppermute | solution.py:345
  46.0 16.1 %collective-permute-start.9 = (f32[448,256]{1,0:T(8,128)S(1)}, f32[448,256]{1,0:T(8,128)S(1)}, u32[]{:S(2)}, u32[]{:S(2)}) collective-permute-start(f32[448,256]{1,0:T(8,128)S(1)} %get-tuple-element.55), channel_id=1, source_target_pairs={{0,3},{1,0},{2,1},{3,2},{4,7},{5,4},{6,5},{7,6},{8,11},{9,8},{10,9... | collective-permute-start | bytes 1376264 | tf_op jit(solution)/shard_map/ppermute | solution.py:345
  47.9 14.3 %collective-permute-start.8 = (f32[448,256]{1,0:T(8,128)S(1)}, f32[448,256]{1,0:T(8,128)S(1)}, u32[]{:S(2)}, u32[]{:S(2)}) collective-permute-start(f32[448,256]{1,0:T(8,128)S(1)} %get-tuple-element.54.refs_2_), channel_id=1, source_target_pairs={{0,1},{1,2},{2,3},{3,0},{4,5},{5,6},{6,7},{7,4},{8,9},{9,10},{10,1... | collective-permute-start | bytes 1376264 | tf_op jit(solution)/shard_map/ppermute | solution.py:345
  55.0 7.7 %collective-permute-start.15 = (f32[64,896]{1,0:T(8,128)S(1)}, f32[64,896]{1,0:T(8,128)S(1)}, u32[]{:S(2)}, u32[]{:S(2)}) collective-permute-start(f32[64,896]{1,0:T(8,128)S(1)} %shard_map.104.refs_3_.refs_0_), channel_id=1, source_target_pairs={{0,1},{1,0},{2,3},{3,2},{4,5},{5,4},{6,7},{7,6},{8,9},{9,8},{10,11... | collective-permute-start | bytes 688136 | tf_op jit(solution)/shard_map/ppermute | solution.py:353
  55.4 5.5 %collective-permute-start.10 = (f32[8,2048]{1,0:T(8,128)S(1)}, f32[8,2048]{1,0:T(8,128)S(1)}, u32[]{:S(2)}, u32[]{:S(2)}) collective-permute-start(f32[8,2048]{1,0:T(8,128)S(1)} %get-tuple-element.49.refs_2_), channel_id=1, source_target_pairs={{0,24},{4,28},{8,16},{12,20},{16,8},{20,12},{24,0},{28,4},{1,25},{... | collective-permute-start | bytes 196616 | tf_op jit(solution)/shard_map/ppermute | solution.py:357
  60.9 5.0 %collective-permute-start.14 = (f32[16,2048]{1,0:T(8,128)S(1)}, f32[16,2048]{1,0:T(8,128)S(1)}, u32[]{:S(2)}, u32[]{:S(2)}) collective-permute-start(f32[16,2048]{1,0:T(8,128)S(1)} %shard_map.105.refs_3_.refs_0_), channel_id=1, source_target_pairs={{0,32},{32,0},{64,96},{96,64},{1,33},{33,1},{65,97},{97,65},{2,34}... | collective-permute-start | bytes 393224 | tf_op jit(solution)/shard_map/ppermute | solution.py:353
  62.8 9.8 %collective-permute-start.18 = (f32[64,896]{1,0:T(8,128)S(1)}, f32[64,896]{1,0:T(8,128)S(1)}, u32[]{:S(2)}, u32[]{:S(2)}) collective-permute-start(f32[64,896]{1,0:T(8,128)S(1)} %shard_map.107.refs_2_.refs_0_), channel_id=1, source_target_pairs={{0,3},{1,2},{2,1},{3,0},{4,7},{5,6},{6,5},{7,4},{8,11},{9,10},{10,... | collective-permute-start | bytes 688136 | tf_op jit(solution)/shard_map/ppermute | solution.py:353
  66.0 17.8 %collective-permute-start.17 = (f32[448,256]{1,0:T(8,128)S(1)}, f32[448,256]{1,0:T(8,128)S(1)}, u32[]{:S(2)}, u32[]{:S(2)}) collective-permute-start(f32[448,256]{1,0:T(8,128)S(1)} %get-tuple-element.63), channel_id=1, source_target_pairs={{0,3},{1,0},{2,1},{3,2},{4,7},{5,4},{6,5},{7,6},{8,11},{9,8},{10,9... | collective-permute-start | bytes 1376264 | tf_op jit(solution)/shard_map/ppermute | solution.py:345
  68.3 15.6 %collective-permute-start.16 = (f32[448,256]{1,0:T(8,128)S(1)}, f32[448,256]{1,0:T(8,128)S(1)}, u32[]{:S(2)}, u32[]{:S(2)}) collective-permute-start(f32[448,256]{1,0:T(8,128)S(1)} %get-tuple-element.62.refs_2_), channel_id=1, source_target_pairs={{0,1},{1,2},{2,3},{3,0},{4,5},{5,6},{6,7},{7,4},{8,9},{9,10},{10,1... | collective-permute-start | bytes 1376264 | tf_op jit(solution)/shard_map/ppermute | solution.py:345
  68.3 7.1 %collective-permute-start.21 = (f32[16,2048]{1,0:T(8,128)S(1)}, f32[16,2048]{1,0:T(8,128)S(1)}, u32[]{:S(2)}, u32[]{:S(2)}) collective-permute-start(f32[16,2048]{1,0:T(8,128)S(1)} %shard_map.108.refs_2_.refs_0_), channel_id=1, source_target_pairs={{0,96},{32,64},{64,32},{96,0},{1,97},{33,65},{65,33},{97,1},{2,98}... | collective-permute-start | bytes 393224 | tf_op jit(solution)/shard_map/ppermute | solution.py:353
  72.6 8.9 %collective-permute-start.20 = (f32[32,896]{1,0:T(8,128)S(1)}, f32[32,896]{1,0:T(8,128)S(1)}, u32[]{:S(2)}, u32[]{:S(2)}) collective-permute-start(f32[32,896]{1,0:T(8,128)S(1)} %get-tuple-element.65.refs_2_), channel_id=1, source_target_pairs={{0,32},{32,0},{64,96},{96,64},{1,33},{33,1},{65,97},{97,65},{2,34}... | collective-permute-start | bytes 344072 | tf_op jit(solution)/shard_map/ppermute | solution.py:353
  73.7 7.8 %collective-permute-start.19 = (f32[32,896]{1,0:T(8,128)S(1)}, f32[32,896]{1,0:T(8,128)S(1)}, u32[]{:S(2)}, u32[]{:S(2)}) collective-permute-start(f32[32,896]{1,0:T(8,128)S(1)} %get-tuple-element.64.refs_3_.refs_0_), channel_id=1, source_target_pairs={{0,96},{32,64},{64,32},{96,0},{1,97},{33,65},{65,33},{97,1},{2,98}... | collective-permute-start | bytes 344072 | tf_op jit(solution)/shard_map/ppermute | solution.py:353
  76.0 5.5 %collective-permute-start.22 = (f32[8,2048]{1,0:T(8,128)S(1)}, f32[8,2048]{1,0:T(8,128)S(1)}, u32[]{:S(2)}, u32[]{:S(2)}) collective-permute-start(f32[8,2048]{1,0:T(8,128)S(1)} %get-tuple-element.66.refs_0_), channel_id=1, source_target_pairs={{0,24},{4,28},{8,16},{12,20},{16,8},{20,12},{24,0},{28,4},{1,25},{... | collective-permute-start | bytes 196616 | tf_op jit(solution)/shard_map/ppermute | solution.py:357
  81.6 7.3 %collective-permute-start.24 = (f32[64,896]{1,0:T(8,128)S(1)}, f32[64,896]{1,0:T(8,128)S(1)}, u32[]{:S(2)}, u32[]{:S(2)}) collective-permute-start(f32[64,896]{1,0:T(8,128)S(1)} %get-tuple-element.69.refs_2_), channel_id=1, source_target_pairs={{0,96},{32,64},{64,32},{96,0},{1,97},{33,65},{65,33},{97,1},{2,98}... | collective-permute-start | bytes 688136 | tf_op jit(solution)/shard_map/ppermute | solution.py:353
  83.2 6.0 %collective-permute-start.23 = (f32[64,896]{1,0:T(8,128)S(1)}, f32[64,896]{1,0:T(8,128)S(1)}, u32[]{:S(2)}, u32[]{:S(2)}) collective-permute-start(f32[64,896]{1,0:T(8,128)S(1)} %get-tuple-element.67.refs_3_.refs_0_), channel_id=1, source_target_pairs={{0,32},{32,0},{64,96},{96,64},{1,33},{33,1},{65,97},{97,65},{2,34}... | collective-permute-start | bytes 688136 | tf_op jit(solution)/shard_map/ppermute | solution.py:353
  83.2 6.0 %collective-permute-start.25 = (f32[16,2048]{1,0:T(8,128)S(1)}, f32[16,2048]{1,0:T(8,128)S(1)}, u32[]{:S(2)}, u32[]{:S(2)}) collective-permute-start(f32[16,2048]{1,0:T(8,128)S(1)} %shard_map.112.refs_4_.refs_0_), channel_id=1, source_target_pairs={{0,8},{4,12},{8,0},{12,4},{16,24},{20,28},{24,16},{28,20},{1,9},{5... | collective-permute-start | bytes 393224 | tf_op jit(solution)/shard_map/ppermute | solution.py:357
  89.3 1.6 %collective-permute-start.26 = (f32[32,2048]{1,0:T(8,128)S(1)}, f32[32,2048]{1,0:T(8,128)S(1)}, u32[]{:S(2)}, u32[]{:S(2)}) collective-permute-start(f32[32,2048]{1,0:T(8,128)S(1)} %shard_map.116.refs_4_.refs_0_), channel_id=1, source_target_pairs={{0,4},{4,0},{8,12},{12,8},{16,20},{20,16},{24,28},{28,24},{1,5},{5... | collective-permute-start | bytes 786440 | tf_op jit(solution)/shard_map/ppermute | solution.py:361

commit v11 on v10

--- a/solution.py
+++ b/solution.py
@@ -388,7 +388,9 @@
         vec, bq, am,
         scratch=[pltpu.VMEM((rank, cols), F32)],
     )
-    keep, send = halve(keep, swap_core(send), near_bit)
+    half = [out((far, toks))] * 2
+    v_up, v_down = call(near_kernel, half, [VMEM] * 2, m, scaled, after=[send])
+    keep, send = halve(keep, swap_core(send), near_bit, after=[v_up])
     pieces = call(
         functools.partial(a_kernel, 2.0 * gamma),
         [out((rank, rows // 4))] * 4,
@@ -399,9 +401,7 @@
     )
     keep, send = halve(keep, swap_x(send, 0), far_bit, after=[pieces[0]])
     pieces = [pieces[0]] + [ring(pieces[k], "dp", k) for k in (1, 3, 2)]
-    half = [out((far, toks))] * 2
-    v_up, v_down = call(near_kernel, half, [VMEM] * 2, m, scaled, after=[send])
-    v_up, v_down = hold([v_up, v_down], [u0, u1])
+    v_up, v_down = hold([v_up, v_down], [send, u0, u1])
     v0, v1 = ring(v_up, "cols", 1), ring(v_down, "cols", 3)
     own = call(own_kernel, [out((rows // 4, toks))], [VMEM] * 2, m, scaled, after=[v_up])[0]
     up, down = call(relay_kernel, half, [VMEM] * 4, m, scaled, u0, u1, after=[own])

time: 92.9 us -> 92.2 us (level)
  waiting for transfers between devices: 26.6 us -> 24.6 us
  starting transfers between devices: 32.8 us -> 34.1 us
    ppermute x8, waiting for transfers between devices: 8.72 us -> 6.76 us  [swap(): lax.ppermute(value, axis, [(i, i ^ 1 if step == 0 else 3 - i) for i in ra...]
    ppermute x8, starting transfers between devices: 9.92 us -> 11.5 us  [swap(): lax.ppermute(value, axis, [(i, i ^ 1 if step == 0 else 3 - i) for i in ra...]
    ppermute x3, waiting for transfers between devices: 3.22 us -> 2.07 us  [swap_core(): return lax.ppermute(value, 'rows', [(i, i ^ 1) for i in range(count)])]
    ppermute x9, waiting for transfers between devices: 4.52 us -> 5.66 us  [ring(): lax.ppermute(value, axis, [(i, (i + k) % count) for i in range(count)])]
  transfers between devices with their start and end apart: 27 -> 27, of which waited for: 15 -> 13; matrix products, arithmetic and copies ran while one was open for 0% -> 0% of each run, Pallas kernels for 14% -> 14%
where the time goes in v11:
time: 92.2 us; the launch traced here: 91.1 us
  starting transfers between devices  34.1 us (37%)
  Pallas kernels  31.4 us (34%)
  waiting for transfers between devices  24.6 us (27%)
    pallas_call x23, Pallas kernels, call(): pl.pallas_call(body, out_shape=outs, in_specs=list(specs) + [ANY] * len(a...  31.4 us
    ppermute x9, starting transfers between devices, ring(): lax.ppermute(value, axis, [(i, (i + k) % count) for i in range(count)])  13.6 us
    ppermute x8, starting transfers between devices, swap(): lax.ppermute(value, axis, [(i, i ^ 1 if step == 0 else 3 - i) for i in ra...  11.5 us
    ppermute x4, waiting for transfers between devices, swap_x(): lax.ppermute(value, 'rows', [(i, i ^ 2 if step == 0 else 6 - 2 * (i // 2)...  7.26 us
    ppermute x8, waiting for transfers between devices, swap(): lax.ppermute(value, axis, [(i, i ^ 1 if step == 0 else 3 - i) for i in ra...  6.76 us
    ppermute x9, waiting for transfers between devices, ring(): lax.ppermute(value, axis, [(i, (i + k) % count) for i in range(count)])  5.66 us
    ppermute x3, starting transfers between devices, ring_x(): lax.ppermute(value, 'rows', [(i, (i + 2 * k) % count) for i in range(coun...  4.59 us
    ppermute x4, starting transfers between devices, swap_x(): lax.ppermute(value, 'rows', [(i, i ^ 2 if step == 0 else 6 - 2 * (i // 2)...  4.13 us
  transfers between devices with their start and end apart: 27, of which 13 were waited for; matrix products, arithmetic and copies ran while one was open for 0% of the time, Pallas kernels for 14%

profile of v11, /device:TPU:0, one launch (start us, length us, event | category | flops | bytes accessed | tf_op | source)
XLA Modules:
  0.0 91.1 jit_solution(13284690577532085434)
XLA Ops:
  0.7 16.5 %shard_map.93 = (bf16[3584,2048]{1,0:T(8,128)(2,1)S(1)}, f32[2,2048]{1,0:T(2,128)S(1)}, f32[64,2048]{1,0:T(8,128)S(1)}) custom-call(bf16[3584,2048]{1,0:T(8,128)(2,1)} %refs_0_.1, bf16[256,3584]{1,0:T(8,128)(2,1)} %refs_3_.3, bf16[64,3584]{1,0:T(8,128)(2,1)} %bitcast.4, bf16[64,2048]{1,0:T(8,128)(2,1)} %refs_2_.3, bf16[256,2048]{1,0:T(8,128)(2,1)} %refs_1_.5), custom_call_target="tpu_custom_call" | custom-call | flops 5637144576 | bytes 14680064 | tf_op jit(solution)/shard_map/pallas_call | solution.py:49
  17.2 1.2 %collective-permute-done = f32[2,2048]{1,0:T(2,128)S(1)} collective-permute-done((f32[2,2048]{1,0:T(2,128)S(1)}, f32[2,2048]{1,0:T(2,128)S(1)}, u32[]{:S(2)}, u32[]{:S(2)}) %collective-permute-start) | collective-permute-done | bytes 16416 | tf_op jit(solution)/shard_map/ppermute | solution.py:361
  18.4 2.9 %collective-permute-start.3 = (f32[2,2048]{1,0:T(2,128)S(1)}, f32[2,2048]{1,0:T(2,128)S(1)}, u32[]{:S(2)}, u32[]{:S(2)}) collective-permute-start(f32[2,2048]{1,0:T(2,128)S(1)} %add.3.refs_0_), channel_id=1, source_target_pairs={{0,24},{4,28},{8,0},{12,4},{16,8},{20,12},{24,16},{28,20},{1,25},{... | collective-permute-start | bytes 49160 | tf_op jit(solution)/shard_map/ppermute | solution.py:349
  23.0 1.2 %shard_map.94.refs_7_.refs_1_ = f32[64,2048]{1,0:T(8,128)S(1)} custom-call(bf16[64,3584]{1,0:T(8,128)(2,1)S(1)} %bitcast.5, bf16[256,3584]{1,0:T(8,128)(2,1)S(1)} %copy-done.1, bf16[256,2048]{1,0:T(8,128)(2,1)S(1)} %copy-done, f32[2,2048]{1,0:T(2,128)S(1)} %get-tuple-element.40.refs_3_), custom_call_target="tpu_custom_call" | custom-call | flops 1 | bytes 1 | tf_op jit(solution)/shard_map/pallas_call | solution.py:49
  24.2 2.4 %collective-permute-done.2.refs_2_ = f32[2,2048]{1,0:T(2,128)S(1)} collective-permute-done((f32[2,2048]{1,0:T(2,128)S(1)}, f32[2,2048]{1,0:T(2,128)S(1)}, u32[]{:S(2)}, u32[]{:S(2)}) %collective-permute-start.2) | collective-permute-done | bytes 16416 | tf_op jit(solution)/shard_map/ppermute | solution.py:349
  27.1 1.2 %shard_map.95 = (f32[4,2048]{1,0:T(4,128)S(1)}, bf16[256,2048]{1,0:T(8,128)(2,1)S(1)}, f32[448,256]{1,0:T(8,128)S(1)}, f32[448,256]{1,0:T(8,128)S(1)}) custom-call(f32[2,2048]{1,0:T(2,128)S(1)} %add.3.refs_0_, f32[2,2048]{1,0:T(2,128)S(1)} %collective-permute-done.1.refs_1_, f32[2,2048]{1,0:T(2,128)S(1)} %collective-permute-done.2.refs_2_, ...), custom_call_target="tpu_custom_call" | custom-call | flops 1 | bytes 1 | tf_op jit(solution)/shard_map/pallas_call | solution.py:49
  28.3 1.6 %collective-permute-start.6 = (f32[448,256]{1,0:T(8,128)S(1)}, f32[448,256]{1,0:T(8,128)S(1)}, u32[]{:S(2)}, u32[]{:S(2)}) collective-permute-start(f32[448,256]{1,0:T(8,128)S(1)} %get-tuple-element.52), channel_id=1, source_target_pairs={{0,1},{1,2},{2,3},{3,0},{4,5},{5,6},{6,7},{7,4},{8,9},{9,10},{10,1... | collective-permute-start | bytes 1376264 | tf_op jit(solution)/shard_map/ppermute | solution.py:345
  29.9 1.7 %collective-permute-start.7 = (f32[448,256]{1,0:T(8,128)S(1)}, f32[448,256]{1,0:T(8,128)S(1)}, u32[]{:S(2)}, u32[]{:S(2)}) collective-permute-start(f32[448,256]{1,0:T(8,128)S(1)} %get-tuple-element.53), channel_id=1, source_target_pairs={{0,3},{1,0},{2,1},{3,2},{4,7},{5,4},{6,5},{7,6},{8,11},{9,8},{10,9... | collective-permute-start | bytes 1376264 | tf_op jit(solution)/shard_map/ppermute | solution.py:345
  31.8 1.1 %shard_map.97 = (f32[448,256]{1,0:T(8,128)S(1)}, f32[448,256]{1,0:T(8,128)S(1)}) custom-call(bf16[3584,2048]{1,0:T(8,128)(2,1)S(1)} %get-tuple-element.39.refs_6_.refs_0_.refs_4_, bf16[256,2048]{1,0:T(8,128)(2,1)S(1)} %get-tuple-element.41.refs_1_, f32[32,2048]{1,0:T(8,128)S(1)} %get-tuple-element.44.refs_2_), custom_call_target="tpu_custom_call" | custom-call | flops 1 | bytes 1 | tf_op jit(solution)/shard_map/pallas_call | solution.py:49
  33.5 5.3 %shard_map.99 = (f32[64,896]{1,0:T(8,128)S(1)}, f32[64,896]{1,0:T(8,128)S(1)}, f32[64,896]{1,0:T(8,128)S(1)}, f32[64,896]{1,0:T(8,128)S(1)}) custom-call(f32[4,2048]{1,0:T(4,128)S(1)} %get-tuple-element.42.refs_0_.refs_2_, bf16[256,2048]{1,0:T(8,128)(2,1)S(1)} %copy-done, bf16[64,2048]{1,0:T(8,128)(2,1)S(1)} %copy-done.3, bf16[256,3584]{1,0:T(8,128)(2,1)S(1)} %copy-done.1, ...), custom_call_target="tpu_custom_call" | custom-call | flops 1 | bytes 1 | tf_op jit(solution)/shard_map/pallas_call | solution.py:49
  38.8 2.0 %collective-permute-start.11 = (f32[64,896]{1,0:T(8,128)S(1)}, f32[64,896]{1,0:T(8,128)S(1)}, u32[]{:S(2)}, u32[]{:S(2)}) collective-permute-start(f32[64,896]{1,0:T(8,128)S(1)} %get-tuple-element.57), channel_id=1, source_target_pairs={{0,32},{32,64},{64,96},{96,0},{1,33},{33,65},{65,97},{97,1},{2,34}... | collective-permute-start | bytes 688136 | tf_op jit(solution)/shard_map/ppermute | solution.py:345
  40.8 2.2 %collective-permute-start.12 = (f32[64,896]{1,0:T(8,128)S(1)}, f32[64,896]{1,0:T(8,128)S(1)}, u32[]{:S(2)}, u32[]{:S(2)}) collective-permute-start(f32[64,896]{1,0:T(8,128)S(1)} %get-tuple-element.58), channel_id=1, source_target_pairs={{0,96},{32,0},{64,32},{96,64},{1,97},{33,1},{65,33},{97,65},{2,98}... | collective-permute-start | bytes 688136 | tf_op jit(solution)/shard_map/ppermute | solution.py:345
  43.0 1.8 %collective-permute-start.13 = (f32[64,896]{1,0:T(8,128)S(1)}, f32[64,896]{1,0:T(8,128)S(1)}, u32[]{:S(2)}, u32[]{:S(2)}) collective-permute-start(f32[64,896]{1,0:T(8,128)S(1)} %get-tuple-element.59), channel_id=1, source_target_pairs={{0,64},{32,96},{64,0},{96,32},{1,65},{33,97},{65,1},{97,33},{2,66}... | collective-permute-start | bytes 688136 | tf_op jit(solution)/shard_map/ppermute | solution.py:345
  44.9 1.9 %collective-permute-start.9 = (f32[448,256]{1,0:T(8,128)S(1)}, f32[448,256]{1,0:T(8,128)S(1)}, u32[]{:S(2)}, u32[]{:S(2)}) collective-permute-start(f32[448,256]{1,0:T(8,128)S(1)} %get-tuple-element.55), channel_id=1, source_target_pairs={{0,3},{1,0},{2,1},{3,2},{4,7},{5,4},{6,5},{7,6},{8,11},{9,8},{10,9... | collective-permute-start | bytes 1376264 | tf_op jit(solution)/shard_map/ppermute | solution.py:345
  47.0 1.1 %shard_map.102.refs_4_.refs_0_ = f32[896,256]{1,0:T(8,128)S(1)} custom-call(bf16[3584,2048]{1,0:T(8,128)(2,1)S(1)} %get-tuple-element.39.refs_6_.refs_0_.refs_4_, bf16[256,2048]{1,0:T(8,128)(2,1)S(1)} %get-tuple-element.41.refs_1_, f32[448,256]{1,0:T(8,128)S(1)} %get-tuple-element.54.refs_2_), custom_call_target="tpu_custom_call" | custom-call | flops 1 | bytes 1 | tf_op jit(solution)/shard_map/pallas_call | solution.py:49
  48.1 1.1 %shard_map.103 = (f32[448,256]{1,0:T(8,128)S(1)}, f32[448,256]{1,0:T(8,128)S(1)}) custom-call(bf16[3584,2048]{1,0:T(8,128)(2,1)S(1)} %get-tuple-element.39.refs_6_.refs_0_.refs_4_, bf16[256,2048]{1,0:T(8,128)(2,1)S(1)} %get-tuple-element.41.refs_1_, f32[448,256]{1,0:T(8,128)S(1)} %collective-permute-done.6.refs_3_.refs_2_, ...), custom_call_target="tpu_custom_call" | custom-call | flops 1 | bytes 1 | tf_op jit(solution)/shard_map/pallas_call | solution.py:49
  49.3 3.8 %collective-permute-done.12.refs_2_ = f32[64,896]{1,0:T(8,128)S(1)} collective-permute-done((f32[64,896]{1,0:T(8,128)S(1)}, f32[64,896]{1,0:T(8,128)S(1)}, u32[]{:S(2)}, u32[]{:S(2)}) %collective-permute-start.12) | collective-permute-done | bytes 229408 | tf_op jit(solution)/shard_map/ppermute | solution.py:345
  53.1 1.8 %collective-permute-done.13.refs_3_ = f32[64,896]{1,0:T(8,128)S(1)} collective-permute-done((f32[64,896]{1,0:T(8,128)S(1)}, f32[64,896]{1,0:T(8,128)S(1)}, u32[]{:S(2)}, u32[]{:S(2)}) %collective-permute-start.13) | collective-permute-done | bytes 229408 | tf_op jit(solution)/shard_map/ppermute | solution.py:345
  55.4 1.8 %collective-permute-start.10 = (f32[8,2048]{1,0:T(8,128)S(1)}, f32[8,2048]{1,0:T(8,128)S(1)}, u32[]{:S(2)}, u32[]{:S(2)}) collective-permute-start(f32[8,2048]{1,0:T(8,128)S(1)} %get-tuple-element.51.refs_2_), channel_id=1, source_target_pairs={{0,24},{4,28},{8,16},{12,20},{16,8},{20,12},{24,0},{28,4},{1,25},{... | collective-permute-start | bytes 196616 | tf_op jit(solution)/shard_map/ppermute | solution.py:357
  57.2 3.7 %collective-permute-done.10.refs_1_ = f32[8,2048]{1,0:T(8,128)S(1)} collective-permute-done((f32[8,2048]{1,0:T(8,128)S(1)}, f32[8,2048]{1,0:T(8,128)S(1)}, u32[]{:S(2)}, u32[]{:S(2)}) %collective-permute-start.10) | collective-permute-done | bytes 65568 | tf_op jit(solution)/shard_map/ppermute | solution.py:357
  60.9 1.2 %collective-permute-start.14 = (f32[16,2048]{1,0:T(8,128)S(1)}, f32[16,2048]{1,0:T(8,128)S(1)}, u32[]{:S(2)}, u32[]{:S(2)}) collective-permute-start(f32[16,2048]{1,0:T(8,128)S(1)} %shard_map.105.refs_3_.refs_0_), channel_id=1, source_target_pairs={{0,32},{32,0},{64,96},{96,64},{1,33},{33,1},{65,97},{97,65},{2,34}... | collective-permute-start | bytes 393224 | tf_op jit(solution)/shard_map/ppermute | solution.py:353
  62.3 2.3 %collective-permute-start.18 = (f32[64,896]{1,0:T(8,128)S(1)}, f32[64,896]{1,0:T(8,128)S(1)}, u32[]{:S(2)}, u32[]{:S(2)}) collective-permute-start(f32[64,896]{1,0:T(8,128)S(1)} %shard_map.107.refs_2_.refs_0_), channel_id=1, source_target_pairs={{0,3},{1,2},{2,1},{3,0},{4,7},{5,6},{6,5},{7,4},{8,11},{9,10},{10,... | collective-permute-start | bytes 688136 | tf_op jit(solution)/shard_map/ppermute | solution.py:353
  64.6 1.4 %collective-permute-done.14.refs_1_ = f32[16,2048]{1,0:T(8,128)S(1)} collective-permute-done((f32[16,2048]{1,0:T(8,128)S(1)}, f32[16,2048]{1,0:T(8,128)S(1)}, u32[]{:S(2)}, u32[]{:S(2)}) %collective-permute-start.14) | collective-permute-done | bytes 131104 | tf_op jit(solution)/shard_map/ppermute | solution.py:353
  66.0 2.3 %collective-permute-start.17 = (f32[448,256]{1,0:T(8,128)S(1)}, f32[448,256]{1,0:T(8,128)S(1)}, u32[]{:S(2)}, u32[]{:S(2)}) collective-permute-start(f32[448,256]{1,0:T(8,128)S(1)} %get-tuple-element.63), channel_id=1, source_target_pairs={{0,3},{1,0},{2,1},{3,2},{4,7},{5,4},{6,5},{7,6},{8,11},{9,8},{10,9... | collective-permute-start | bytes 1376264 | tf_op jit(solution)/shard_map/ppermute | solution.py:345
  68.3 1.9 %collective-permute-start.21 = (f32[16,2048]{1,0:T(8,128)S(1)}, f32[16,2048]{1,0:T(8,128)S(1)}, u32[]{:S(2)}, u32[]{:S(2)}) collective-permute-start(f32[16,2048]{1,0:T(8,128)S(1)} %shard_map.108.refs_2_.refs_0_), channel_id=1, source_target_pairs={{0,96},{32,64},{64,32},{96,0},{1,97},{33,65},{65,33},{97,1},{2,98}... | collective-permute-start | bytes 393224 | tf_op jit(solution)/shard_map/ppermute | solution.py:353
  70.7 1.1 %collective-permute-start.20 = (f32[32,896]{1,0:T(8,128)S(1)}, f32[32,896]{1,0:T(8,128)S(1)}, u32[]{:S(2)}, u32[]{:S(2)}) collective-permute-start(f32[32,896]{1,0:T(8,128)S(1)} %get-tuple-element.65.refs_2_), channel_id=1, source_target_pairs={{0,32},{32,0},{64,96},{96,64},{1,33},{33,1},{65,97},{97,65},{2,34}... | collective-permute-start | bytes 344072 | tf_op jit(solution)/shard_map/ppermute | solution.py:353
  71.7 3.1 %collective-permute-start.19 = (f32[32,896]{1,0:T(8,128)S(1)}, f32[32,896]{1,0:T(8,128)S(1)}, u32[]{:S(2)}, u32[]{:S(2)}) collective-permute-start(f32[32,896]{1,0:T(8,128)S(1)} %get-tuple-element.64.refs_3_.refs_0_), channel_id=1, source_target_pairs={{0,96},{32,64},{64,32},{96,0},{1,97},{33,65},{65,33},{97,1},{2,98}... | collective-permute-start | bytes 344072 | tf_op jit(solution)/shard_map/ppermute | solution.py:353
  75.4 1.9 %collective-permute-start.22 = (f32[8,2048]{1,0:T(8,128)S(1)}, f32[8,2048]{1,0:T(8,128)S(1)}, u32[]{:S(2)}, u32[]{:S(2)}) collective-permute-start(f32[8,2048]{1,0:T(8,128)S(1)} %get-tuple-element.66.refs_0_), channel_id=1, source_target_pairs={{0,24},{4,28},{8,16},{12,20},{16,8},{20,12},{24,0},{28,4},{1,25},{... | collective-permute-start | bytes 196616 | tf_op jit(solution)/shard_map/ppermute | solution.py:357
  77.3 3.6 %collective-permute-done.22.refs_1_ = f32[8,2048]{1,0:T(8,128)S(1)} collective-permute-done((f32[8,2048]{1,0:T(8,128)S(1)}, f32[8,2048]{1,0:T(8,128)S(1)}, u32[]{:S(2)}, u32[]{:S(2)}) %collective-permute-start.22) | collective-permute-done | bytes 65568 | tf_op jit(solution)/shard_map/ppermute | solution.py:357
  81.0 1.6 %collective-permute-start.24 = (f32[64,896]{1,0:T(8,128)S(1)}, f32[64,896]{1,0:T(8,128)S(1)}, u32[]{:S(2)}, u32[]{:S(2)}) collective-permute-start(f32[64,896]{1,0:T(8,128)S(1)} %get-tuple-element.69.refs_2_), channel_id=1, source_target_pairs={{0,96},{32,64},{64,32},{96,0},{1,97},{33,65},{65,33},{97,1},{2,98}... | collective-permute-start | bytes 688136 | tf_op jit(solution)/shard_map/ppermute | solution.py:353
  83.8 4.5 %collective-permute-done.24.refs_1_ = f32[64,896]{1,0:T(8,128)S(1)} collective-permute-done((f32[64,896]{1,0:T(8,128)S(1)}, f32[64,896]{1,0:T(8,128)S(1)}, u32[]{:S(2)}, u32[]{:S(2)}) %collective-permute-start.24) | collective-permute-done | bytes 229408 | tf_op jit(solution)/shard_map/ppermute | solution.py:353
  88.7 1.0 %shard_map.117 = f32[64,3584]{1,0:T(8,128)} custom-call(f32[64,896]{1,0:T(8,128)S(1)} %get-tuple-element.67.refs_3_.refs_0_, f32[64,896]{1,0:T(8,128)S(1)} %get-tuple-element.71.refs_2_.refs_1_, f32[64,896]{1,0:T(8,128)S(1)} %get-tuple-element.69.refs_2_, f32[64,896]{1,0:T(8,128)S(1)} %get-tuple-element.72.refs_3_, f32[32,2048]{1,0:T(8,128)S(1)} %shard_map.116.refs_4_.refs_0_), custom_call_target="tpu_custom_call" | custom-call | flops 1 | bytes 1 | tf_op jit(solution)/shard_map/pallas_call | solution.py:49
  (59 shorter events, 8.2 us)
Async XLA Ops:
  0.6 22.4 %copy-start = (bf16[256,2048]{1,0:T(8,128)(2,1)S(1)}, bf16[256,2048]{1,0:T(8,128)(2,1)}, u32[]{:S(2)}) copy-start(bf16[256,2048]{1,0:T(8,128)(2,1)} %refs_1_.5) | copy-start | bytes 3145732
  0.6 22.4 %copy-start.1 = (bf16[256,3584]{1,0:T(8,128)(2,1)S(1)}, bf16[256,3584]{1,0:T(8,128)(2,1)}, u32[]{:S(2)}) copy-start(bf16[256,3584]{1,0:T(8,128)(2,1)} %refs_3_.3) | copy-start | bytes 5505028
  0.7 22.4 %copy-start.2 = (bf16[3584,64]{0,1:T(8,128)(2,1)S(1)}, bf16[3584,64]{0,1:T(8,128)(2,1)}, u32[]{:S(2)}) copy-start(bf16[3584,64]{0,1:T(8,128)(2,1)} %param.9) | copy-start | bytes 1376260
  0.7 26.4 %copy-start.4 = (f32[2048]{0:T(1024)S(1)}, f32[2048]{0:T(1024)}, u32[]{:S(2)}) copy-start(f32[2048]{0:T(1024)} %param.11) | copy-start | bytes 24580
  17.1 1.3 %collective-permute-start = (f32[2,2048]{1,0:T(2,128)S(1)}, f32[2,2048]{1,0:T(2,128)S(1)}, u32[]{:S(2)}, u32[]{:S(2)}) collective-permute-start(f32[2,2048]{1,0:T(2,128)S(1)} %get-tuple-element.40.refs_3_), channel_id=1, source_target_pairs={{0,4},{4,0},{8,12},{12,8},{16,20},{20,16},{24,28},{28,24},{1,5},{5... | collective-permute-start | bytes 49160 | tf_op jit(solution)/shard_map/ppermute | solution.py:361
  18.4 5.8 %collective-permute-start.3 = (f32[2,2048]{1,0:T(2,128)S(1)}, f32[2,2048]{1,0:T(2,128)S(1)}, u32[]{:S(2)}, u32[]{:S(2)}) collective-permute-start(f32[2,2048]{1,0:T(2,128)S(1)} %add.3.refs_0_), channel_id=1, source_target_pairs={{0,24},{4,28},{8,0},{12,4},{16,8},{20,12},{24,16},{28,20},{1,25},{... | collective-permute-start | bytes 49160 | tf_op jit(solution)/shard_map/ppermute | solution.py:349
  21.3 5.2 %collective-permute-start.2 = (f32[2,2048]{1,0:T(2,128)S(1)}, f32[2,2048]{1,0:T(2,128)S(1)}, u32[]{:S(2)}, u32[]{:S(2)}) collective-permute-start(f32[2,2048]{1,0:T(2,128)S(1)} %add.3.refs_0_), channel_id=1, source_target_pairs={{0,16},{4,20},{8,24},{12,28},{16,0},{20,4},{24,8},{28,12},{1,17},{... | collective-permute-start | bytes 49160 | tf_op jit(solution)/shard_map/ppermute | solution.py:349
  22.1 4.9 %collective-permute-start.1 = (f32[2,2048]{1,0:T(2,128)S(1)}, f32[2,2048]{1,0:T(2,128)S(1)}, u32[]{:S(2)}, u32[]{:S(2)}) collective-permute-start(f32[2,2048]{1,0:T(2,128)S(1)} %add.3.refs_0_), channel_id=1, source_target_pairs={{0,8},{4,12},{8,16},{12,20},{16,24},{20,28},{24,0},{28,4},{1,9},{5... | collective-permute-start | bytes 49160 | tf_op jit(solution)/shard_map/ppermute | solution.py:349
  27.1 6.4 %copy-start.3 = (bf16[64,2048]{1,0:T(8,128)(2,1)S(1)}, bf16[64,2048]{1,0:T(8,128)(2,1)}, u32[]{:S(2)}) copy-start(bf16[64,2048]{1,0:T(8,128)(2,1)} %refs_2_.3) | copy-start | bytes 786436
  28.3 16.6 %collective-permute-start.6 = (f32[448,256]{1,0:T(8,128)S(1)}, f32[448,256]{1,0:T(8,128)S(1)}, u32[]{:S(2)}, u32[]{:S(2)}) collective-permute-start(f32[448,256]{1,0:T(8,128)S(1)} %get-tuple-element.52), channel_id=1, source_target_pairs={{0,1},{1,2},{2,3},{3,0},{4,5},{5,6},{6,7},{7,4},{8,9},{9,10},{10,1... | collective-permute-start | bytes 1376264 | tf_op jit(solution)/shard_map/ppermute | solution.py:345
  29.9 15.0 %collective-permute-start.7 = (f32[448,256]{1,0:T(8,128)S(1)}, f32[448,256]{1,0:T(8,128)S(1)}, u32[]{:S(2)}, u32[]{:S(2)}) collective-permute-start(f32[448,256]{1,0:T(8,128)S(1)} %get-tuple-element.53), channel_id=1, source_target_pairs={{0,3},{1,0},{2,1},{3,2},{4,7},{5,4},{6,5},{7,6},{8,11},{9,8},{10,9... | collective-permute-start | bytes 1376264 | tf_op jit(solution)/shard_map/ppermute | solution.py:345
  31.8 1.6 %collective-permute-start.4 = (f32[32,2048]{1,0:T(8,128)S(1)}, f32[32,2048]{1,0:T(8,128)S(1)}, u32[]{:S(2)}, u32[]{:S(2)}) collective-permute-start(f32[32,2048]{1,0:T(8,128)S(1)} %get-tuple-element.44.refs_2_), channel_id=1, source_target_pairs={{0,4},{4,0},{8,12},{12,8},{16,20},{20,16},{24,28},{28,24},{1,5},{5... | collective-permute-start | bytes 786440 | tf_op jit(solution)/shard_map/ppermute | solution.py:361
  33.4 9.6 %collective-permute-start.5 = (f32[16,2048]{1,0:T(8,128)S(1)}, f32[16,2048]{1,0:T(8,128)S(1)}, u32[]{:S(2)}, u32[]{:S(2)}) collective-permute-start(f32[16,2048]{1,0:T(8,128)S(1)} %get-tuple-element.49.refs_5_), channel_id=1, source_target_pairs={{0,8},{4,12},{8,0},{12,4},{16,24},{20,28},{24,16},{28,20},{1,9},{5... | collective-permute-start | bytes 393224 | tf_op jit(solution)/shard_map/ppermute | solution.py:357
  38.8 10.5 %collective-permute-start.11 = (f32[64,896]{1,0:T(8,128)S(1)}, f32[64,896]{1,0:T(8,128)S(1)}, u32[]{:S(2)}, u32[]{:S(2)}) collective-permute-start(f32[64,896]{1,0:T(8,128)S(1)} %get-tuple-element.57), channel_id=1, source_target_pairs={{0,32},{32,64},{64,96},{96,0},{1,33},{33,65},{65,97},{97,1},{2,34}... | collective-permute-start | bytes 688136 | tf_op jit(solution)/shard_map/ppermute | solution.py:345
  40.8 12.3 %collective-permute-start.12 = (f32[64,896]{1,0:T(8,128)S(1)}, f32[64,896]{1,0:T(8,128)S(1)}, u32[]{:S(2)}, u32[]{:S(2)}) collective-permute-start(f32[64,896]{1,0:T(8,128)S(1)} %get-tuple-element.58), channel_id=1, source_target_pairs={{0,96},{32,0},{64,32},{96,64},{1,97},{33,1},{65,33},{97,65},{2,98}... | collective-permute-start | bytes 688136 | tf_op jit(solution)/shard_map/ppermute | solution.py:345
  43.0 11.9 %collective-permute-start.13 = (f32[64,896]{1,0:T(8,128)S(1)}, f32[64,896]{1,0:T(8,128)S(1)}, u32[]{:S(2)}, u32[]{:S(2)}) collective-permute-start(f32[64,896]{1,0:T(8,128)S(1)} %get-tuple-element.59), channel_id=1, source_target_pairs={{0,64},{32,96},{64,0},{96,32},{1,65},{33,97},{65,1},{97,33},{2,66}... | collective-permute-start | bytes 688136 | tf_op jit(solution)/shard_map/ppermute | solution.py:345
  44.9 17.3 %collective-permute-start.9 = (f32[448,256]{1,0:T(8,128)S(1)}, f32[448,256]{1,0:T(8,128)S(1)}, u32[]{:S(2)}, u32[]{:S(2)}) collective-permute-start(f32[448,256]{1,0:T(8,128)S(1)} %get-tuple-element.55), channel_id=1, source_target_pairs={{0,3},{1,0},{2,1},{3,2},{4,7},{5,4},{6,5},{7,6},{8,11},{9,8},{10,9... | collective-permute-start | bytes 1376264 | tf_op jit(solution)/shard_map/ppermute | solution.py:345
  46.7 15.4 %collective-permute-start.8 = (f32[448,256]{1,0:T(8,128)S(1)}, f32[448,256]{1,0:T(8,128)S(1)}, u32[]{:S(2)}, u32[]{:S(2)}) collective-permute-start(f32[448,256]{1,0:T(8,128)S(1)} %get-tuple-element.54.refs_2_), channel_id=1, source_target_pairs={{0,1},{1,2},{2,3},{3,0},{4,5},{5,6},{6,7},{7,4},{8,9},{9,10},{10,1... | collective-permute-start | bytes 1376264 | tf_op jit(solution)/shard_map/ppermute | solution.py:345
  55.0 7.3 %collective-permute-start.15 = (f32[64,896]{1,0:T(8,128)S(1)}, f32[64,896]{1,0:T(8,128)S(1)}, u32[]{:S(2)}, u32[]{:S(2)}) collective-permute-start(f32[64,896]{1,0:T(8,128)S(1)} %shard_map.104.refs_3_.refs_0_), channel_id=1, source_target_pairs={{0,1},{1,0},{2,3},{3,2},{4,5},{5,4},{6,7},{7,6},{8,9},{9,8},{10,11... | collective-permute-start | bytes 688136 | tf_op jit(solution)/shard_map/ppermute | solution.py:353
  55.4 5.5 %collective-permute-start.10 = (f32[8,2048]{1,0:T(8,128)S(1)}, f32[8,2048]{1,0:T(8,128)S(1)}, u32[]{:S(2)}, u32[]{:S(2)}) collective-permute-start(f32[8,2048]{1,0:T(8,128)S(1)} %get-tuple-element.51.refs_2_), channel_id=1, source_target_pairs={{0,24},{4,28},{8,16},{12,20},{16,8},{20,12},{24,0},{28,4},{1,25},{... | collective-permute-start | bytes 196616 | tf_op jit(solution)/shard_map/ppermute | solution.py:357
  60.9 5.0 %collective-permute-start.14 = (f32[16,2048]{1,0:T(8,128)S(1)}, f32[16,2048]{1,0:T(8,128)S(1)}, u32[]{:S(2)}, u32[]{:S(2)}) collective-permute-start(f32[16,2048]{1,0:T(8,128)S(1)} %shard_map.105.refs_3_.refs_0_), channel_id=1, source_target_pairs={{0,32},{32,0},{64,96},{96,64},{1,33},{33,1},{65,97},{97,65},{2,34}... | collective-permute-start | bytes 393224 | tf_op jit(solution)/shard_map/ppermute | solution.py:353
  62.3 8.3 %collective-permute-start.18 = (f32[64,896]{1,0:T(8,128)S(1)}, f32[64,896]{1,0:T(8,128)S(1)}, u32[]{:S(2)}, u32[]{:S(2)}) collective-permute-start(f32[64,896]{1,0:T(8,128)S(1)} %shard_map.107.refs_2_.refs_0_), channel_id=1, source_target_pairs={{0,3},{1,2},{2,1},{3,0},{4,7},{5,6},{6,5},{7,4},{8,11},{9,10},{10,... | collective-permute-start | bytes 688136 | tf_op jit(solution)/shard_map/ppermute | solution.py:353
  66.0 16.9 %collective-permute-start.17 = (f32[448,256]{1,0:T(8,128)S(1)}, f32[448,256]{1,0:T(8,128)S(1)}, u32[]{:S(2)}, u32[]{:S(2)}) collective-permute-start(f32[448,256]{1,0:T(8,128)S(1)} %get-tuple-element.63), channel_id=1, source_target_pairs={{0,3},{1,0},{2,1},{3,2},{4,7},{5,4},{6,5},{7,6},{8,11},{9,8},{10,9... | collective-permute-start | bytes 1376264 | tf_op jit(solution)/shard_map/ppermute | solution.py:345
  68.2 14.7 %collective-permute-start.16 = (f32[448,256]{1,0:T(8,128)S(1)}, f32[448,256]{1,0:T(8,128)S(1)}, u32[]{:S(2)}, u32[]{:S(2)}) collective-permute-start(f32[448,256]{1,0:T(8,128)S(1)} %get-tuple-element.62.refs_2_), channel_id=1, source_target_pairs={{0,1},{1,2},{2,3},{3,0},{4,5},{5,6},{6,7},{7,4},{8,9},{9,10},{10,1... | collective-permute-start | bytes 1376264 | tf_op jit(solution)/shard_map/ppermute | solution.py:345
  68.3 6.5 %collective-permute-start.21 = (f32[16,2048]{1,0:T(8,128)S(1)}, f32[16,2048]{1,0:T(8,128)S(1)}, u32[]{:S(2)}, u32[]{:S(2)}) collective-permute-start(f32[16,2048]{1,0:T(8,128)S(1)} %shard_map.108.refs_2_.refs_0_), channel_id=1, source_target_pairs={{0,96},{32,64},{64,32},{96,0},{1,97},{33,65},{65,33},{97,1},{2,98}... | collective-permute-start | bytes 393224 | tf_op jit(solution)/shard_map/ppermute | solution.py:353
  70.7 10.3 %collective-permute-start.20 = (f32[32,896]{1,0:T(8,128)S(1)}, f32[32,896]{1,0:T(8,128)S(1)}, u32[]{:S(2)}, u32[]{:S(2)}) collective-permute-start(f32[32,896]{1,0:T(8,128)S(1)} %get-tuple-element.65.refs_2_), channel_id=1, source_target_pairs={{0,32},{32,0},{64,96},{96,64},{1,33},{33,1},{65,97},{97,65},{2,34}... | collective-permute-start | bytes 344072 | tf_op jit(solution)/shard_map/ppermute | solution.py:353
  71.7 9.2 %collective-permute-start.19 = (f32[32,896]{1,0:T(8,128)S(1)}, f32[32,896]{1,0:T(8,128)S(1)}, u32[]{:S(2)}, u32[]{:S(2)}) collective-permute-start(f32[32,896]{1,0:T(8,128)S(1)} %get-tuple-element.64.refs_3_.refs_0_), channel_id=1, source_target_pairs={{0,96},{32,64},{64,32},{96,0},{1,97},{33,65},{65,33},{97,1},{2,98}... | collective-permute-start | bytes 344072 | tf_op jit(solution)/shard_map/ppermute | solution.py:353
  75.4 5.5 %collective-permute-start.22 = (f32[8,2048]{1,0:T(8,128)S(1)}, f32[8,2048]{1,0:T(8,128)S(1)}, u32[]{:S(2)}, u32[]{:S(2)}) collective-permute-start(f32[8,2048]{1,0:T(8,128)S(1)} %get-tuple-element.66.refs_0_), channel_id=1, source_target_pairs={{0,24},{4,28},{8,16},{12,20},{16,8},{20,12},{24,0},{28,4},{1,25},{... | collective-permute-start | bytes 196616 | tf_op jit(solution)/shard_map/ppermute | solution.py:357
  81.0 7.3 %collective-permute-start.24 = (f32[64,896]{1,0:T(8,128)S(1)}, f32[64,896]{1,0:T(8,128)S(1)}, u32[]{:S(2)}, u32[]{:S(2)}) collective-permute-start(f32[64,896]{1,0:T(8,128)S(1)} %get-tuple-element.69.refs_2_), channel_id=1, source_target_pairs={{0,96},{32,64},{64,32},{96,0},{1,97},{33,65},{65,33},{97,1},{2,98}... | collective-permute-start | bytes 688136 | tf_op jit(solution)/shard_map/ppermute | solution.py:353
  82.6 6.0 %collective-permute-start.23 = (f32[64,896]{1,0:T(8,128)S(1)}, f32[64,896]{1,0:T(8,128)S(1)}, u32[]{:S(2)}, u32[]{:S(2)}) collective-permute-start(f32[64,896]{1,0:T(8,128)S(1)} %get-tuple-element.67.refs_3_.refs_0_), channel_id=1, source_target_pairs={{0,32},{32,0},{64,96},{96,64},{1,33},{33,1},{65,97},{97,65},{2,34}... | collective-permute-start | bytes 688136 | tf_op jit(solution)/shard_map/ppermute | solution.py:353
  82.6 6.0 %collective-permute-start.25 = (f32[16,2048]{1,0:T(8,128)S(1)}, f32[16,2048]{1,0:T(8,128)S(1)}, u32[]{:S(2)}, u32[]{:S(2)}) collective-permute-start(f32[16,2048]{1,0:T(8,128)S(1)} %shard_map.112.refs_4_.refs_0_), channel_id=1, source_target_pairs={{0,8},{4,12},{8,0},{12,4},{16,24},{20,28},{24,16},{28,20},{1,9},{5... | collective-permute-start | bytes 393224 | tf_op jit(solution)/shard_map/ppermute | solution.py:357
  88.6 1.6 %collective-permute-start.26 = (f32[32,2048]{1,0:T(8,128)S(1)}, f32[32,2048]{1,0:T(8,128)S(1)}, u32[]{:S(2)}, u32[]{:S(2)}) collective-permute-start(f32[32,2048]{1,0:T(8,128)S(1)} %shard_map.116.refs_4_.refs_0_), channel_id=1, source_target_pairs={{0,4},{4,0},{8,12},{12,8},{16,20},{20,16},{24,28},{28,24},{1,5},{5... | collective-permute-start | bytes 786440 | tf_op jit(solution)/shard_map/ppermute | solution.py:361

commit v12 on v11

--- a/solution.py
+++ b/solution.py
@@ -204,19 +204,17 @@
     out_ref[half:] = (own_ref[half:] + w1_ref[...]).astype(BF16)
 
 
-def a_kernel(factor, vec_ref, dy_ref, b_ref, x_ref, m_ref, *refs):
-    outs, whole = refs[:-1], refs[-1]
+def a_kernel(factor, vec_ref, dy_ref, b_ref, x_ref, m_ref, *outs):
     scale = vec_ref[2:3] * factor
     wide = b_ref[...].astype(F32) * scale
     p_t = fold(nt(hi_lo(wide), dy_ref[...]))
     left = hi_lo(p_t)
     right = hi_lo(wide * (vec_ref[3:4] / vec_ref[0:1]))
-    rows = m_ref.shape[0]
-    tile = 512
-    for r in range(rows // tile):
-        at = slice(r * tile, (r + 1) * tile)
-        whole[:, at] = fold(nn(left, x_ref[:, at]) - nt(right, m_ref[at]))
-    split(whole, outs, lax.axis_index("dp"), 1)
+    count = len(outs)
+    size = m_ref.shape[0] // count
+    for k, ref in enumerate(outs):
+        start = pl.multiple_of(lax.rem(dp_index() + k, count) * size, 128)
+        ref[...] = fold(nn(left, x_ref[:, pl.ds(start, size)]) - nt(right, m_ref[pl.ds(start, size)]))
 
 
 def split(whole, outs, index, axis):
@@ -396,7 +394,6 @@
         [out((rank, rows // 4))] * 4,
         [VMEM] * 5,
         vec, dy, b, x, m,
-        scratch=[pltpu.VMEM((rank, rows), F32)],
         after=[send],
     )
     keep, send = halve(keep, swap_x(send, 0), far_bit, after=[pieces[0]])

time: 92.2 us -> 91.9 us (level)
  no operation moved by 1% of the time
where the time goes in v12:
time: 91.9 us; the launch traced here: 90.7 us
  starting transfers between devices  34.1 us (37%)
  Pallas kernels  31.1 us (34%)
  waiting for transfers between devices  24.6 us (27%)
    pallas_call x23, Pallas kernels, call(): pl.pallas_call(body, out_shape=outs, in_specs=list(specs) + [ANY] * len(a...  31.1 us
    ppermute x9, starting transfers between devices, ring(): lax.ppermute(value, axis, [(i, (i + k) % count) for i in range(count)])  13.6 us
    ppermute x8, starting transfers between devices, swap(): lax.ppermute(value, axis, [(i, i ^ 1 if step == 0 else 3 - i) for i in ra...  11.5 us
    ppermute x4, waiting for transfers between devices, swap_x(): lax.ppermute(value, 'rows', [(i, i ^ 2 if step == 0 else 6 - 2 * (i // 2)...  7.28 us
    ppermute x8, waiting for transfers between devices, swap(): lax.ppermute(value, axis, [(i, i ^ 1 if step == 0 else 3 - i) for i in ra...  6.75 us
    ppermute x9, waiting for transfers between devices, ring(): lax.ppermute(value, axis, [(i, (i + k) % count) for i in range(count)])  5.66 us
    ppermute x3, starting transfers between devices, ring_x(): lax.ppermute(value, 'rows', [(i, (i + 2 * k) % count) for i in range(coun...  4.59 us
    ppermute x4, starting transfers between devices, swap_x(): lax.ppermute(value, 'rows', [(i, i ^ 2 if step == 0 else 6 - 2 * (i // 2)...  4.12 us
  transfers between devices with their start and end apart: 27, of which 13 were waited for; matrix products, arithmetic and copies ran while one was open for 0% of the time, Pallas kernels for 14%

profile of v12, /device:TPU:0, one launch (start us, length us, event | category | flops | bytes accessed | tf_op | source)
XLA Modules:
  0.0 90.7 jit_solution(14285199089798694411)
XLA Ops:
  0.7 16.5 %shard_map.93 = (bf16[3584,2048]{1,0:T(8,128)(2,1)S(1)}, f32[2,2048]{1,0:T(2,128)S(1)}, f32[64,2048]{1,0:T(8,128)S(1)}) custom-call(bf16[3584,2048]{1,0:T(8,128)(2,1)} %refs_0_.1, bf16[256,3584]{1,0:T(8,128)(2,1)} %refs_3_.3, bf16[64,3584]{1,0:T(8,128)(2,1)} %bitcast.4, bf16[64,2048]{1,0:T(8,128)(2,1)} %refs_2_.3, bf16[256,2048]{1,0:T(8,128)(2,1)} %refs_1_.5), custom_call_target="tpu_custom_call" | custom-call | flops 5637144576 | bytes 14680064 | tf_op jit(solution)/shard_map/pallas_call | solution.py:49
  17.2 1.2 %collective-permute-done = f32[2,2048]{1,0:T(2,128)S(1)} collective-permute-done((f32[2,2048]{1,0:T(2,128)S(1)}, f32[2,2048]{1,0:T(2,128)S(1)}, u32[]{:S(2)}, u32[]{:S(2)}) %collective-permute-start) | collective-permute-done | bytes 16416 | tf_op jit(solution)/shard_map/ppermute | solution.py:359
  18.4 2.9 %collective-permute-start.3 = (f32[2,2048]{1,0:T(2,128)S(1)}, f32[2,2048]{1,0:T(2,128)S(1)}, u32[]{:S(2)}, u32[]{:S(2)}) collective-permute-start(f32[2,2048]{1,0:T(2,128)S(1)} %add.3.refs_0_), channel_id=1, source_target_pairs={{0,24},{4,28},{8,0},{12,4},{16,8},{20,12},{24,16},{28,20},{1,25},{... | collective-permute-start | bytes 49160 | tf_op jit(solution)/shard_map/ppermute | solution.py:347
  23.0 1.2 %shard_map.94.refs_7_.refs_1_ = f32[64,2048]{1,0:T(8,128)S(1)} custom-call(bf16[64,3584]{1,0:T(8,128)(2,1)S(1)} %bitcast.5, bf16[256,3584]{1,0:T(8,128)(2,1)S(1)} %copy-done.1, bf16[256,2048]{1,0:T(8,128)(2,1)S(1)} %copy-done, f32[2,2048]{1,0:T(2,128)S(1)} %get-tuple-element.40.refs_3_), custom_call_target="tpu_custom_call" | custom-call | flops 1 | bytes 1 | tf_op jit(solution)/shard_map/pallas_call | solution.py:49
  24.2 2.4 %collective-permute-done.2.refs_2_ = f32[2,2048]{1,0:T(2,128)S(1)} collective-permute-done((f32[2,2048]{1,0:T(2,128)S(1)}, f32[2,2048]{1,0:T(2,128)S(1)}, u32[]{:S(2)}, u32[]{:S(2)}) %collective-permute-start.2) | collective-permute-done | bytes 16416 | tf_op jit(solution)/shard_map/ppermute | solution.py:347
  27.1 1.2 %shard_map.95 = (f32[4,2048]{1,0:T(4,128)S(1)}, bf16[256,2048]{1,0:T(8,128)(2,1)S(1)}, f32[448,256]{1,0:T(8,128)S(1)}, f32[448,256]{1,0:T(8,128)S(1)}) custom-call(f32[2,2048]{1,0:T(2,128)S(1)} %add.3.refs_0_, f32[2,2048]{1,0:T(2,128)S(1)} %collective-permute-done.1.refs_1_, f32[2,2048]{1,0:T(2,128)S(1)} %collective-permute-done.2.refs_2_, ...), custom_call_target="tpu_custom_call" | custom-call | flops 1 | bytes 1 | tf_op jit(solution)/shard_map/pallas_call | solution.py:49
  28.3 1.6 %collective-permute-start.6 = (f32[448,256]{1,0:T(8,128)S(1)}, f32[448,256]{1,0:T(8,128)S(1)}, u32[]{:S(2)}, u32[]{:S(2)}) collective-permute-start(f32[448,256]{1,0:T(8,128)S(1)} %get-tuple-element.52), channel_id=1, source_target_pairs={{0,1},{1,2},{2,3},{3,0},{4,5},{5,6},{6,7},{7,4},{8,9},{9,10},{10,1... | collective-permute-start | bytes 1376264 | tf_op jit(solution)/shard_map/ppermute | solution.py:343
  29.9 1.7 %collective-permute-start.7 = (f32[448,256]{1,0:T(8,128)S(1)}, f32[448,256]{1,0:T(8,128)S(1)}, u32[]{:S(2)}, u32[]{:S(2)}) collective-permute-start(f32[448,256]{1,0:T(8,128)S(1)} %get-tuple-element.53), channel_id=1, source_target_pairs={{0,3},{1,0},{2,1},{3,2},{4,7},{5,4},{6,5},{7,6},{8,11},{9,8},{10,9... | collective-permute-start | bytes 1376264 | tf_op jit(solution)/shard_map/ppermute | solution.py:343
  31.8 1.1 %shard_map.97 = (f32[448,256]{1,0:T(8,128)S(1)}, f32[448,256]{1,0:T(8,128)S(1)}) custom-call(bf16[3584,2048]{1,0:T(8,128)(2,1)S(1)} %get-tuple-element.39.refs_6_.refs_0_.refs_4_, bf16[256,2048]{1,0:T(8,128)(2,1)S(1)} %get-tuple-element.41.refs_1_, f32[32,2048]{1,0:T(8,128)S(1)} %get-tuple-element.44.refs_2_), custom_call_target="tpu_custom_call" | custom-call | flops 1 | bytes 1 | tf_op jit(solution)/shard_map/pallas_call | solution.py:49
  33.5 5.0 %shard_map.99 = (f32[64,896]{1,0:T(8,128)S(1)}, f32[64,896]{1,0:T(8,128)S(1)}, f32[64,896]{1,0:T(8,128)S(1)}, f32[64,896]{1,0:T(8,128)S(1)}) custom-call(f32[4,2048]{1,0:T(4,128)S(1)} %get-tuple-element.42.refs_0_.refs_2_, bf16[256,2048]{1,0:T(8,128)(2,1)S(1)} %copy-done, bf16[64,2048]{1,0:T(8,128)(2,1)S(1)} %copy-done.3, bf16[256,3584]{1,0:T(8,128)(2,1)S(1)} %copy-done.1, ...), custom_call_target="tpu_custom_call" | custom-call | flops 1 | bytes 1 | tf_op jit(solution)/shard_map/pallas_call | solution.py:49
  38.5 2.0 %collective-permute-start.11 = (f32[64,896]{1,0:T(8,128)S(1)}, f32[64,896]{1,0:T(8,128)S(1)}, u32[]{:S(2)}, u32[]{:S(2)}) collective-permute-start(f32[64,896]{1,0:T(8,128)S(1)} %get-tuple-element.57), channel_id=1, source_target_pairs={{0,32},{32,64},{64,96},{96,0},{1,33},{33,65},{65,97},{97,1},{2,34}... | collective-permute-start | bytes 688136 | tf_op jit(solution)/shard_map/ppermute | solution.py:343
  40.5 2.2 %collective-permute-start.12 = (f32[64,896]{1,0:T(8,128)S(1)}, f32[64,896]{1,0:T(8,128)S(1)}, u32[]{:S(2)}, u32[]{:S(2)}) collective-permute-start(f32[64,896]{1,0:T(8,128)S(1)} %get-tuple-element.58), channel_id=1, source_target_pairs={{0,96},{32,0},{64,32},{96,64},{1,97},{33,1},{65,33},{97,65},{2,98}... | collective-permute-start | bytes 688136 | tf_op jit(solution)/shard_map/ppermute | solution.py:343
  42.7 1.8 %collective-permute-start.13 = (f32[64,896]{1,0:T(8,128)S(1)}, f32[64,896]{1,0:T(8,128)S(1)}, u32[]{:S(2)}, u32[]{:S(2)}) collective-permute-start(f32[64,896]{1,0:T(8,128)S(1)} %get-tuple-element.59), channel_id=1, source_target_pairs={{0,64},{32,96},{64,0},{96,32},{1,65},{33,97},{65,1},{97,33},{2,66}... | collective-permute-start | bytes 688136 | tf_op jit(solution)/shard_map/ppermute | solution.py:343
  44.5 1.9 %collective-permute-start.9 = (f32[448,256]{1,0:T(8,128)S(1)}, f32[448,256]{1,0:T(8,128)S(1)}, u32[]{:S(2)}, u32[]{:S(2)}) collective-permute-start(f32[448,256]{1,0:T(8,128)S(1)} %get-tuple-element.55), channel_id=1, source_target_pairs={{0,3},{1,0},{2,1},{3,2},{4,7},{5,4},{6,5},{7,6},{8,11},{9,8},{10,9... | collective-permute-start | bytes 1376264 | tf_op jit(solution)/shard_map/ppermute | solution.py:343
  46.6 1.1 %shard_map.102.refs_4_.refs_0_ = f32[896,256]{1,0:T(8,128)S(1)} custom-call(bf16[3584,2048]{1,0:T(8,128)(2,1)S(1)} %get-tuple-element.39.refs_6_.refs_0_.refs_4_, bf16[256,2048]{1,0:T(8,128)(2,1)S(1)} %get-tuple-element.41.refs_1_, f32[448,256]{1,0:T(8,128)S(1)} %get-tuple-element.54.refs_2_), custom_call_target="tpu_custom_call" | custom-call | flops 1 | bytes 1 | tf_op jit(solution)/shard_map/pallas_call | solution.py:49
  47.8 1.1 %shard_map.103 = (f32[448,256]{1,0:T(8,128)S(1)}, f32[448,256]{1,0:T(8,128)S(1)}) custom-call(bf16[3584,2048]{1,0:T(8,128)(2,1)S(1)} %get-tuple-element.39.refs_6_.refs_0_.refs_4_, bf16[256,2048]{1,0:T(8,128)(2,1)S(1)} %get-tuple-element.41.refs_1_, f32[448,256]{1,0:T(8,128)S(1)} %collective-permute-done.6.refs_3_.refs_2_, ...), custom_call_target="tpu_custom_call" | custom-call | flops 1 | bytes 1 | tf_op jit(solution)/shard_map/pallas_call | solution.py:49
  49.0 3.8 %collective-permute-done.12.refs_2_ = f32[64,896]{1,0:T(8,128)S(1)} collective-permute-done((f32[64,896]{1,0:T(8,128)S(1)}, f32[64,896]{1,0:T(8,128)S(1)}, u32[]{:S(2)}, u32[]{:S(2)}) %collective-permute-start.12) | collective-permute-done | bytes 229408 | tf_op jit(solution)/shard_map/ppermute | solution.py:343
  52.8 1.8 %collective-permute-done.13.refs_3_ = f32[64,896]{1,0:T(8,128)S(1)} collective-permute-done((f32[64,896]{1,0:T(8,128)S(1)}, f32[64,896]{1,0:T(8,128)S(1)}, u32[]{:S(2)}, u32[]{:S(2)}) %collective-permute-start.13) | collective-permute-done | bytes 229408 | tf_op jit(solution)/shard_map/ppermute | solution.py:343
  55.1 1.8 %collective-permute-start.10 = (f32[8,2048]{1,0:T(8,128)S(1)}, f32[8,2048]{1,0:T(8,128)S(1)}, u32[]{:S(2)}, u32[]{:S(2)}) collective-permute-start(f32[8,2048]{1,0:T(8,128)S(1)} %get-tuple-element.51.refs_2_), channel_id=1, source_target_pairs={{0,24},{4,28},{8,16},{12,20},{16,8},{20,12},{24,0},{28,4},{1,25},{... | collective-permute-start | bytes 196616 | tf_op jit(solution)/shard_map/ppermute | solution.py:355
  56.9 3.7 %collective-permute-done.10.refs_1_ = f32[8,2048]{1,0:T(8,128)S(1)} collective-permute-done((f32[8,2048]{1,0:T(8,128)S(1)}, f32[8,2048]{1,0:T(8,128)S(1)}, u32[]{:S(2)}, u32[]{:S(2)}) %collective-permute-start.10) | collective-permute-done | bytes 65568 | tf_op jit(solution)/shard_map/ppermute | solution.py:355
  60.6 1.2 %collective-permute-start.14 = (f32[16,2048]{1,0:T(8,128)S(1)}, f32[16,2048]{1,0:T(8,128)S(1)}, u32[]{:S(2)}, u32[]{:S(2)}) collective-permute-start(f32[16,2048]{1,0:T(8,128)S(1)} %shard_map.105.refs_3_.refs_0_), channel_id=1, source_target_pairs={{0,32},{32,0},{64,96},{96,64},{1,33},{33,1},{65,97},{97,65},{2,34}... | collective-permute-start | bytes 393224 | tf_op jit(solution)/shard_map/ppermute | solution.py:351
  62.0 2.3 %collective-permute-start.18 = (f32[64,896]{1,0:T(8,128)S(1)}, f32[64,896]{1,0:T(8,128)S(1)}, u32[]{:S(2)}, u32[]{:S(2)}) collective-permute-start(f32[64,896]{1,0:T(8,128)S(1)} %shard_map.107.refs_2_.refs_0_), channel_id=1, source_target_pairs={{0,3},{1,2},{2,1},{3,0},{4,7},{5,6},{6,5},{7,4},{8,11},{9,10},{10,... | collective-permute-start | bytes 688136 | tf_op jit(solution)/shard_map/ppermute | solution.py:351
  64.2 1.4 %collective-permute-done.14.refs_1_ = f32[16,2048]{1,0:T(8,128)S(1)} collective-permute-done((f32[16,2048]{1,0:T(8,128)S(1)}, f32[16,2048]{1,0:T(8,128)S(1)}, u32[]{:S(2)}, u32[]{:S(2)}) %collective-permute-start.14) | collective-permute-done | bytes 131104 | tf_op jit(solution)/shard_map/ppermute | solution.py:351
  65.7 2.3 %collective-permute-start.17 = (f32[448,256]{1,0:T(8,128)S(1)}, f32[448,256]{1,0:T(8,128)S(1)}, u32[]{:S(2)}, u32[]{:S(2)}) collective-permute-start(f32[448,256]{1,0:T(8,128)S(1)} %get-tuple-element.63), channel_id=1, source_target_pairs={{0,3},{1,0},{2,1},{3,2},{4,7},{5,4},{6,5},{7,6},{8,11},{9,8},{10,9... | collective-permute-start | bytes 1376264 | tf_op jit(solution)/shard_map/ppermute | solution.py:343
  67.9 1.9 %collective-permute-start.21 = (f32[16,2048]{1,0:T(8,128)S(1)}, f32[16,2048]{1,0:T(8,128)S(1)}, u32[]{:S(2)}, u32[]{:S(2)}) collective-permute-start(f32[16,2048]{1,0:T(8,128)S(1)} %shard_map.108.refs_2_.refs_0_), channel_id=1, source_target_pairs={{0,96},{32,64},{64,32},{96,0},{1,97},{33,65},{65,33},{97,1},{2,98}... | collective-permute-start | bytes 393224 | tf_op jit(solution)/shard_map/ppermute | solution.py:351
  70.3 1.1 %collective-permute-start.20 = (f32[32,896]{1,0:T(8,128)S(1)}, f32[32,896]{1,0:T(8,128)S(1)}, u32[]{:S(2)}, u32[]{:S(2)}) collective-permute-start(f32[32,896]{1,0:T(8,128)S(1)} %get-tuple-element.65.refs_2_), channel_id=1, source_target_pairs={{0,32},{32,0},{64,96},{96,64},{1,33},{33,1},{65,97},{97,65},{2,34}... | collective-permute-start | bytes 344072 | tf_op jit(solution)/shard_map/ppermute | solution.py:351
  71.4 3.1 %collective-permute-start.19 = (f32[32,896]{1,0:T(8,128)S(1)}, f32[32,896]{1,0:T(8,128)S(1)}, u32[]{:S(2)}, u32[]{:S(2)}) collective-permute-start(f32[32,896]{1,0:T(8,128)S(1)} %get-tuple-element.64.refs_3_.refs_0_), channel_id=1, source_target_pairs={{0,96},{32,64},{64,32},{96,0},{1,97},{33,65},{65,33},{97,1},{2,98}... | collective-permute-start | bytes 344072 | tf_op jit(solution)/shard_map/ppermute | solution.py:351
  75.1 1.9 %collective-permute-start.22 = (f32[8,2048]{1,0:T(8,128)S(1)}, f32[8,2048]{1,0:T(8,128)S(1)}, u32[]{:S(2)}, u32[]{:S(2)}) collective-permute-start(f32[8,2048]{1,0:T(8,128)S(1)} %get-tuple-element.66.refs_0_), channel_id=1, source_target_pairs={{0,24},{4,28},{8,16},{12,20},{16,8},{20,12},{24,0},{28,4},{1,25},{... | collective-permute-start | bytes 196616 | tf_op jit(solution)/shard_map/ppermute | solution.py:355
  77.0 3.6 %collective-permute-done.22.refs_1_ = f32[8,2048]{1,0:T(8,128)S(1)} collective-permute-done((f32[8,2048]{1,0:T(8,128)S(1)}, f32[8,2048]{1,0:T(8,128)S(1)}, u32[]{:S(2)}, u32[]{:S(2)}) %collective-permute-start.22) | collective-permute-done | bytes 65568 | tf_op jit(solution)/shard_map/ppermute | solution.py:355
  80.6 1.6 %collective-permute-start.24 = (f32[64,896]{1,0:T(8,128)S(1)}, f32[64,896]{1,0:T(8,128)S(1)}, u32[]{:S(2)}, u32[]{:S(2)}) collective-permute-start(f32[64,896]{1,0:T(8,128)S(1)} %get-tuple-element.69.refs_2_), channel_id=1, source_target_pairs={{0,96},{32,64},{64,32},{96,0},{1,97},{33,65},{65,33},{97,1},{2,98}... | collective-permute-start | bytes 688136 | tf_op jit(solution)/shard_map/ppermute | solution.py:351
  83.4 4.5 %collective-permute-done.24.refs_1_ = f32[64,896]{1,0:T(8,128)S(1)} collective-permute-done((f32[64,896]{1,0:T(8,128)S(1)}, f32[64,896]{1,0:T(8,128)S(1)}, u32[]{:S(2)}, u32[]{:S(2)}) %collective-permute-start.24) | collective-permute-done | bytes 229408 | tf_op jit(solution)/shard_map/ppermute | solution.py:351
  88.4 1.0 %shard_map.117 = f32[64,3584]{1,0:T(8,128)} custom-call(f32[64,896]{1,0:T(8,128)S(1)} %get-tuple-element.67.refs_3_.refs_0_, f32[64,896]{1,0:T(8,128)S(1)} %get-tuple-element.71.refs_2_.refs_1_, f32[64,896]{1,0:T(8,128)S(1)} %get-tuple-element.69.refs_2_, f32[64,896]{1,0:T(8,128)S(1)} %get-tuple-element.72.refs_3_, f32[32,2048]{1,0:T(8,128)S(1)} %shard_map.116.refs_4_.refs_0_), custom_call_target="tpu_custom_call" | custom-call | flops 1 | bytes 1 | tf_op jit(solution)/shard_map/pallas_call | solution.py:49
  (59 shorter events, 8.2 us)
Async XLA Ops:
  0.6 22.4 %copy-start = (bf16[256,2048]{1,0:T(8,128)(2,1)S(1)}, bf16[256,2048]{1,0:T(8,128)(2,1)}, u32[]{:S(2)}) copy-start(bf16[256,2048]{1,0:T(8,128)(2,1)} %refs_1_.5) | copy-start | bytes 3145732
  0.6 22.4 %copy-start.1 = (bf16[256,3584]{1,0:T(8,128)(2,1)S(1)}, bf16[256,3584]{1,0:T(8,128)(2,1)}, u32[]{:S(2)}) copy-start(bf16[256,3584]{1,0:T(8,128)(2,1)} %refs_3_.3) | copy-start | bytes 5505028
  0.7 22.4 %copy-start.2 = (bf16[3584,64]{0,1:T(8,128)(2,1)S(1)}, bf16[3584,64]{0,1:T(8,128)(2,1)}, u32[]{:S(2)}) copy-start(bf16[3584,64]{0,1:T(8,128)(2,1)} %param.9) | copy-start | bytes 1376260
  0.7 26.4 %copy-start.4 = (f32[2048]{0:T(1024)S(1)}, f32[2048]{0:T(1024)}, u32[]{:S(2)}) copy-start(f32[2048]{0:T(1024)} %param.11) | copy-start | bytes 24580
  17.1 1.3 %collective-permute-start = (f32[2,2048]{1,0:T(2,128)S(1)}, f32[2,2048]{1,0:T(2,128)S(1)}, u32[]{:S(2)}, u32[]{:S(2)}) collective-permute-start(f32[2,2048]{1,0:T(2,128)S(1)} %get-tuple-element.40.refs_3_), channel_id=1, source_target_pairs={{0,4},{4,0},{8,12},{12,8},{16,20},{20,16},{24,28},{28,24},{1,5},{5... | collective-permute-start | bytes 49160 | tf_op jit(solution)/shard_map/ppermute | solution.py:359
  18.4 5.8 %collective-permute-start.3 = (f32[2,2048]{1,0:T(2,128)S(1)}, f32[2,2048]{1,0:T(2,128)S(1)}, u32[]{:S(2)}, u32[]{:S(2)}) collective-permute-start(f32[2,2048]{1,0:T(2,128)S(1)} %add.3.refs_0_), channel_id=1, source_target_pairs={{0,24},{4,28},{8,0},{12,4},{16,8},{20,12},{24,16},{28,20},{1,25},{... | collective-permute-start | bytes 49160 | tf_op jit(solution)/shard_map/ppermute | solution.py:347
  21.3 5.2 %collective-permute-start.2 = (f32[2,2048]{1,0:T(2,128)S(1)}, f32[2,2048]{1,0:T(2,128)S(1)}, u32[]{:S(2)}, u32[]{:S(2)}) collective-permute-start(f32[2,2048]{1,0:T(2,128)S(1)} %add.3.refs_0_), channel_id=1, source_target_pairs={{0,16},{4,20},{8,24},{12,28},{16,0},{20,4},{24,8},{28,12},{1,17},{... | collective-permute-start | bytes 49160 | tf_op jit(solution)/shard_map/ppermute | solution.py:347
  22.1 4.9 %collective-permute-start.1 = (f32[2,2048]{1,0:T(2,128)S(1)}, f32[2,2048]{1,0:T(2,128)S(1)}, u32[]{:S(2)}, u32[]{:S(2)}) collective-permute-start(f32[2,2048]{1,0:T(2,128)S(1)} %add.3.refs_0_), channel_id=1, source_target_pairs={{0,8},{4,12},{8,16},{12,20},{16,24},{20,28},{24,0},{28,4},{1,9},{5... | collective-permute-start | bytes 49160 | tf_op jit(solution)/shard_map/ppermute | solution.py:347
  27.1 6.4 %copy-start.3 = (bf16[64,2048]{1,0:T(8,128)(2,1)S(1)}, bf16[64,2048]{1,0:T(8,128)(2,1)}, u32[]{:S(2)}) copy-start(bf16[64,2048]{1,0:T(8,128)(2,1)} %refs_2_.3) | copy-start | bytes 786436
  28.3 16.3 %collective-permute-start.6 = (f32[448,256]{1,0:T(8,128)S(1)}, f32[448,256]{1,0:T(8,128)S(1)}, u32[]{:S(2)}, u32[]{:S(2)}) collective-permute-start(f32[448,256]{1,0:T(8,128)S(1)} %get-tuple-element.52), channel_id=1, source_target_pairs={{0,1},{1,2},{2,3},{3,0},{4,5},{5,6},{6,7},{7,4},{8,9},{9,10},{10,1... | collective-permute-start | bytes 1376264 | tf_op jit(solution)/shard_map/ppermute | solution.py:343
  29.9 14.6 %collective-permute-start.7 = (f32[448,256]{1,0:T(8,128)S(1)}, f32[448,256]{1,0:T(8,128)S(1)}, u32[]{:S(2)}, u32[]{:S(2)}) collective-permute-start(f32[448,256]{1,0:T(8,128)S(1)} %get-tuple-element.53), channel_id=1, source_target_pairs={{0,3},{1,0},{2,1},{3,2},{4,7},{5,4},{6,5},{7,6},{8,11},{9,8},{10,9... | collective-permute-start | bytes 1376264 | tf_op jit(solution)/shard_map/ppermute | solution.py:343
  31.8 1.6 %collective-permute-start.4 = (f32[32,2048]{1,0:T(8,128)S(1)}, f32[32,2048]{1,0:T(8,128)S(1)}, u32[]{:S(2)}, u32[]{:S(2)}) collective-permute-start(f32[32,2048]{1,0:T(8,128)S(1)} %get-tuple-element.44.refs_2_), channel_id=1, source_target_pairs={{0,4},{4,0},{8,12},{12,8},{16,20},{20,16},{24,28},{28,24},{1,5},{5... | collective-permute-start | bytes 786440 | tf_op jit(solution)/shard_map/ppermute | solution.py:359
  33.4 9.3 %collective-permute-start.5 = (f32[16,2048]{1,0:T(8,128)S(1)}, f32[16,2048]{1,0:T(8,128)S(1)}, u32[]{:S(2)}, u32[]{:S(2)}) collective-permute-start(f32[16,2048]{1,0:T(8,128)S(1)} %get-tuple-element.49.refs_5_), channel_id=1, source_target_pairs={{0,8},{4,12},{8,0},{12,4},{16,24},{20,28},{24,16},{28,20},{1,9},{5... | collective-permute-start | bytes 393224 | tf_op jit(solution)/shard_map/ppermute | solution.py:355
  38.5 10.5 %collective-permute-start.11 = (f32[64,896]{1,0:T(8,128)S(1)}, f32[64,896]{1,0:T(8,128)S(1)}, u32[]{:S(2)}, u32[]{:S(2)}) collective-permute-start(f32[64,896]{1,0:T(8,128)S(1)} %get-tuple-element.57), channel_id=1, source_target_pairs={{0,32},{32,64},{64,96},{96,0},{1,33},{33,65},{65,97},{97,1},{2,34}... | collective-permute-start | bytes 688136 | tf_op jit(solution)/shard_map/ppermute | solution.py:343
  40.5 12.3 %collective-permute-start.12 = (f32[64,896]{1,0:T(8,128)S(1)}, f32[64,896]{1,0:T(8,128)S(1)}, u32[]{:S(2)}, u32[]{:S(2)}) collective-permute-start(f32[64,896]{1,0:T(8,128)S(1)} %get-tuple-element.58), channel_id=1, source_target_pairs={{0,96},{32,0},{64,32},{96,64},{1,97},{33,1},{65,33},{97,65},{2,98}... | collective-permute-start | bytes 688136 | tf_op jit(solution)/shard_map/ppermute | solution.py:343
  42.7 11.9 %collective-permute-start.13 = (f32[64,896]{1,0:T(8,128)S(1)}, f32[64,896]{1,0:T(8,128)S(1)}, u32[]{:S(2)}, u32[]{:S(2)}) collective-permute-start(f32[64,896]{1,0:T(8,128)S(1)} %get-tuple-element.59), channel_id=1, source_target_pairs={{0,64},{32,96},{64,0},{96,32},{1,65},{33,97},{65,1},{97,33},{2,66}... | collective-permute-start | bytes 688136 | tf_op jit(solution)/shard_map/ppermute | solution.py:343
  44.5 17.3 %collective-permute-start.9 = (f32[448,256]{1,0:T(8,128)S(1)}, f32[448,256]{1,0:T(8,128)S(1)}, u32[]{:S(2)}, u32[]{:S(2)}) collective-permute-start(f32[448,256]{1,0:T(8,128)S(1)} %get-tuple-element.55), channel_id=1, source_target_pairs={{0,3},{1,0},{2,1},{3,2},{4,7},{5,4},{6,5},{7,6},{8,11},{9,8},{10,9... | collective-permute-start | bytes 1376264 | tf_op jit(solution)/shard_map/ppermute | solution.py:343
  46.4 15.4 %collective-permute-start.8 = (f32[448,256]{1,0:T(8,128)S(1)}, f32[448,256]{1,0:T(8,128)S(1)}, u32[]{:S(2)}, u32[]{:S(2)}) collective-permute-start(f32[448,256]{1,0:T(8,128)S(1)} %get-tuple-element.54.refs_2_), channel_id=1, source_target_pairs={{0,1},{1,2},{2,3},{3,0},{4,5},{5,6},{6,7},{7,4},{8,9},{9,10},{10,1... | collective-permute-start | bytes 1376264 | tf_op jit(solution)/shard_map/ppermute | solution.py:343
  54.6 7.3 %collective-permute-start.15 = (f32[64,896]{1,0:T(8,128)S(1)}, f32[64,896]{1,0:T(8,128)S(1)}, u32[]{:S(2)}, u32[]{:S(2)}) collective-permute-start(f32[64,896]{1,0:T(8,128)S(1)} %shard_map.104.refs_3_.refs_0_), channel_id=1, source_target_pairs={{0,1},{1,0},{2,3},{3,2},{4,5},{5,4},{6,7},{7,6},{8,9},{9,8},{10,11... | collective-permute-start | bytes 688136 | tf_op jit(solution)/shard_map/ppermute | solution.py:351
  55.1 5.5 %collective-permute-start.10 = (f32[8,2048]{1,0:T(8,128)S(1)}, f32[8,2048]{1,0:T(8,128)S(1)}, u32[]{:S(2)}, u32[]{:S(2)}) collective-permute-start(f32[8,2048]{1,0:T(8,128)S(1)} %get-tuple-element.51.refs_2_), channel_id=1, source_target_pairs={{0,24},{4,28},{8,16},{12,20},{16,8},{20,12},{24,0},{28,4},{1,25},{... | collective-permute-start | bytes 196616 | tf_op jit(solution)/shard_map/ppermute | solution.py:355
  60.6 5.0 %collective-permute-start.14 = (f32[16,2048]{1,0:T(8,128)S(1)}, f32[16,2048]{1,0:T(8,128)S(1)}, u32[]{:S(2)}, u32[]{:S(2)}) collective-permute-start(f32[16,2048]{1,0:T(8,128)S(1)} %shard_map.105.refs_3_.refs_0_), channel_id=1, source_target_pairs={{0,32},{32,0},{64,96},{96,64},{1,33},{33,1},{65,97},{97,65},{2,34}... | collective-permute-start | bytes 393224 | tf_op jit(solution)/shard_map/ppermute | solution.py:351
  62.0 8.3 %collective-permute-start.18 = (f32[64,896]{1,0:T(8,128)S(1)}, f32[64,896]{1,0:T(8,128)S(1)}, u32[]{:S(2)}, u32[]{:S(2)}) collective-permute-start(f32[64,896]{1,0:T(8,128)S(1)} %shard_map.107.refs_2_.refs_0_), channel_id=1, source_target_pairs={{0,3},{1,2},{2,1},{3,0},{4,7},{5,6},{6,5},{7,4},{8,11},{9,10},{10,... | collective-permute-start | bytes 688136 | tf_op jit(solution)/shard_map/ppermute | solution.py:351
  65.7 16.9 %collective-permute-start.17 = (f32[448,256]{1,0:T(8,128)S(1)}, f32[448,256]{1,0:T(8,128)S(1)}, u32[]{:S(2)}, u32[]{:S(2)}) collective-permute-start(f32[448,256]{1,0:T(8,128)S(1)} %get-tuple-element.63), channel_id=1, source_target_pairs={{0,3},{1,0},{2,1},{3,2},{4,7},{5,4},{6,5},{7,6},{8,11},{9,8},{10,9... | collective-permute-start | bytes 1376264 | tf_op jit(solution)/shard_map/ppermute | solution.py:343
  67.9 14.7 %collective-permute-start.16 = (f32[448,256]{1,0:T(8,128)S(1)}, f32[448,256]{1,0:T(8,128)S(1)}, u32[]{:S(2)}, u32[]{:S(2)}) collective-permute-start(f32[448,256]{1,0:T(8,128)S(1)} %get-tuple-element.62.refs_2_), channel_id=1, source_target_pairs={{0,1},{1,2},{2,3},{3,0},{4,5},{5,6},{6,7},{7,4},{8,9},{9,10},{10,1... | collective-permute-start | bytes 1376264 | tf_op jit(solution)/shard_map/ppermute | solution.py:343
  67.9 6.6 %collective-permute-start.21 = (f32[16,2048]{1,0:T(8,128)S(1)}, f32[16,2048]{1,0:T(8,128)S(1)}, u32[]{:S(2)}, u32[]{:S(2)}) collective-permute-start(f32[16,2048]{1,0:T(8,128)S(1)} %shard_map.108.refs_2_.refs_0_), channel_id=1, source_target_pairs={{0,96},{32,64},{64,32},{96,0},{1,97},{33,65},{65,33},{97,1},{2,98}... | collective-permute-start | bytes 393224 | tf_op jit(solution)/shard_map/ppermute | solution.py:351
  70.3 10.3 %collective-permute-start.20 = (f32[32,896]{1,0:T(8,128)S(1)}, f32[32,896]{1,0:T(8,128)S(1)}, u32[]{:S(2)}, u32[]{:S(2)}) collective-permute-start(f32[32,896]{1,0:T(8,128)S(1)} %get-tuple-element.65.refs_2_), channel_id=1, source_target_pairs={{0,32},{32,0},{64,96},{96,64},{1,33},{33,1},{65,97},{97,65},{2,34}... | collective-permute-start | bytes 344072 | tf_op jit(solution)/shard_map/ppermute | solution.py:351
  71.4 9.2 %collective-permute-start.19 = (f32[32,896]{1,0:T(8,128)S(1)}, f32[32,896]{1,0:T(8,128)S(1)}, u32[]{:S(2)}, u32[]{:S(2)}) collective-permute-start(f32[32,896]{1,0:T(8,128)S(1)} %get-tuple-element.64.refs_3_.refs_0_), channel_id=1, source_target_pairs={{0,96},{32,64},{64,32},{96,0},{1,97},{33,65},{65,33},{97,1},{2,98}... | collective-permute-start | bytes 344072 | tf_op jit(solution)/shard_map/ppermute | solution.py:351
  75.1 5.5 %collective-permute-start.22 = (f32[8,2048]{1,0:T(8,128)S(1)}, f32[8,2048]{1,0:T(8,128)S(1)}, u32[]{:S(2)}, u32[]{:S(2)}) collective-permute-start(f32[8,2048]{1,0:T(8,128)S(1)} %get-tuple-element.66.refs_0_), channel_id=1, source_target_pairs={{0,24},{4,28},{8,16},{12,20},{16,8},{20,12},{24,0},{28,4},{1,25},{... | collective-permute-start | bytes 196616 | tf_op jit(solution)/shard_map/ppermute | solution.py:355
  80.6 7.3 %collective-permute-start.24 = (f32[64,896]{1,0:T(8,128)S(1)}, f32[64,896]{1,0:T(8,128)S(1)}, u32[]{:S(2)}, u32[]{:S(2)}) collective-permute-start(f32[64,896]{1,0:T(8,128)S(1)} %get-tuple-element.69.refs_2_), channel_id=1, source_target_pairs={{0,96},{32,64},{64,32},{96,0},{1,97},{33,65},{65,33},{97,1},{2,98}... | collective-permute-start | bytes 688136 | tf_op jit(solution)/shard_map/ppermute | solution.py:351
  82.2 6.0 %collective-permute-start.23 = (f32[64,896]{1,0:T(8,128)S(1)}, f32[64,896]{1,0:T(8,128)S(1)}, u32[]{:S(2)}, u32[]{:S(2)}) collective-permute-start(f32[64,896]{1,0:T(8,128)S(1)} %get-tuple-element.67.refs_3_.refs_0_), channel_id=1, source_target_pairs={{0,32},{32,0},{64,96},{96,64},{1,33},{33,1},{65,97},{97,65},{2,34}... | collective-permute-start | bytes 688136 | tf_op jit(solution)/shard_map/ppermute | solution.py:351
  82.2 6.0 %collective-permute-start.25 = (f32[16,2048]{1,0:T(8,128)S(1)}, f32[16,2048]{1,0:T(8,128)S(1)}, u32[]{:S(2)}, u32[]{:S(2)}) collective-permute-start(f32[16,2048]{1,0:T(8,128)S(1)} %shard_map.112.refs_4_.refs_0_), channel_id=1, source_target_pairs={{0,8},{4,12},{8,0},{12,4},{16,24},{20,28},{24,16},{28,20},{1,9},{5... | collective-permute-start | bytes 393224 | tf_op jit(solution)/shard_map/ppermute | solution.py:355
  88.3 1.6 %collective-permute-start.26 = (f32[32,2048]{1,0:T(8,128)S(1)}, f32[32,2048]{1,0:T(8,128)S(1)}, u32[]{:S(2)}, u32[]{:S(2)}) collective-permute-start(f32[32,2048]{1,0:T(8,128)S(1)} %shard_map.116.refs_4_.refs_0_), channel_id=1, source_target_pairs={{0,4},{4,0},{8,12},{12,8},{16,20},{20,16},{24,28},{28,24},{1,5},{5... | collective-permute-start | bytes 786440 | tf_op jit(solution)/shard_map/ppermute | solution.py:359
